TPU v7x, 32 devices: a whole 2x2x4 slice. The times are simulated.
32 devices in a mesh: ctx: 8 (over y, x, core), exp: 4 (over z).
Axes of the slice: x: 2, y: 2, z: 4, core: 2. Of those that a mesh axis runs over, the one named last changes fastest.
Arguments:
- queries: bfloat16 [512, 8192], P('ctx', 'exp'), may hold values from -52 to 52
- cache_keys: bfloat16 [1024, 512], P('ctx'), may hold values from -6 to 6
- cache_values: bfloat16 [1024, 512], P('ctx'), may hold values from -6 to 6
- block_keys: bfloat16 [512, 512], P('ctx'), may hold values from -6 to 6
- block_values: bfloat16 [512, 512], P('ctx'), may hold values from -6 to 6
- seg_starts: int32 [10], replicated, may hold values from 0 to 1408, as said below
- out_weight: bfloat16 [8192, 4096], P('exp', 'ctx'), may hold values from -0.5 to 0.5
- residual: bfloat16 [512, 4096], P('exp', 'ctx'), may hold values from -45 to 45
- norm_gain: float32 [4096], P('ctx'), may hold values from 0.1 to 1.9
- routes: int32 [512, 8], P('exp'), may hold values from 0 to 127, as said below
- gate_values: float32 [512, 8], P('exp'), may hold values from 0.05 to 0.5
- expert_in: bfloat16 [8, 4096, 3072], P('exp', 'ctx'), may hold values from -0.09375 to 0.09375
- expert_out: bfloat16 [8, 1536, 4096], P('exp', None, 'ctx'), may hold values from -0.15625 to 0.15625
Outputs:
- mixed: bfloat16 [512, 4096], P('exp', 'ctx')
- expert_sum: bfloat16 [512, 4096], P('exp', 'ctx')
Inputs may be any that keep to these rules, and one draw needn't show every extreme that they name: `routes`: 8 different experts in each row; within the rows of one index of exp (aligned blocks of 128 rows) no expert is named by more than 16 rows, and one expert numbered below 8 is named by exactly 16 rows in every block. `seg_starts`: strictly rising, the first 0; the last segment (the aggregator's part) starts inside the prefilled block.
All inputs are finite; a program needn't handle non-finite values.
Results may differ from a plain program's by a relative error of at most 0.029.
Values may be sent and summed in bfloat16 or wider, within the bound.
No kernel may reach another device: no remote copies, remote signals or barrier semaphores. Data moves between devices by JAX's collectives and lax.ppermute only.
A program may use at most 64 MiB of HBM per device.

v0:
```python
import math

import jax
import jax.numpy as jnp
from jax import lax
from jax.sharding import PartitionSpec as P

D = 4096
QHEADS = 64
KVH = 4
HEAD = 128
FFE = 1536
CAP = 16


neg_large = -1e30
eps_norm = 1e-06


def segment_of(positions, seg_starts):
    passed = (seg_starts[None, :] <= positions[:, None]).astype(jnp.int32)
    return jnp.sum(passed, axis=1) - 1


def body(
    queries,
    cache_keys,
    cache_values,
    block_keys,
    block_values,
    seg_starts,
    out_weight,
    residual,
    norm_gain,
    routes,
    gate_values,
    expert_in,
    expert_out,
):
    ctx_count = lax.axis_size("ctx")
    exp_count = lax.axis_size("exp")
    ctx_index = lax.axis_index("ctx")
    exp_index = lax.axis_index("exp")
    span_rows = queries.shape[0]
    local_heads = queries.shape[1] // HEAD
    cache_rows = cache_keys.shape[0]
    shard_rows = cache_rows + span_rows
    cache_total = cache_rows * ctx_count
    kv_index = exp_index * local_heads // (QHEADS // KVH)

    def head_cols(source):
        return lax.dynamic_slice_in_dim(source, kv_index * HEAD, HEAD, 1)

    local_kv = jnp.concatenate(
        [
            jnp.concatenate([head_cols(cache_keys), head_cols(cache_values)], axis=1),
            jnp.concatenate([head_cols(block_keys), head_cols(block_values)], axis=1),
        ],
        axis=0,
    )
    last_segment = seg_starts.shape[0] - 1
    score_scale = 1.0 / math.sqrt(HEAD)
    query_rows = local_heads * span_rows
    stacked_rows = (
        queries.reshape(span_rows, local_heads, HEAD).transpose(1, 0, 2).reshape(query_rows, HEAD)
    )
    query_pos = cache_total + ctx_index * span_rows + jnp.arange(span_rows, dtype=jnp.int32)
    query_seg = segment_of(query_pos, seg_starts)
    kv_piece = lax.all_gather(local_kv, "ctx", axis=0, tiled=True)
    running_max = jnp.full((query_rows,), neg_large, jnp.float32)
    piece_rows = kv_piece.shape[0]
    whole_index = jnp.arange(piece_rows, dtype=jnp.int32)
    key_owner = whole_index // shard_rows
    offset = whole_index % shard_rows
    key_pos = jnp.where(
        offset < cache_rows,
        key_owner * cache_rows + offset,
        cache_total + key_owner * span_rows + offset - cache_rows,
    )
    key_seg = segment_of(key_pos, seg_starts)
    allowed = (key_pos[None, :] <= query_pos[:, None]) & (
        (key_seg[None, :] == query_seg[:, None])
        | (key_seg[None, :] == 0)
        | (query_seg[:, None] == last_segment)
    )
    scores = (
        lax.dot_general(
            stacked_rows,
            kv_piece[:, :HEAD],
            (((1,), (1,)), ((), ())),
            preferred_element_type=jnp.float32,
        )
        * score_scale
    )
    scores = jnp.where(allowed[None], scores.reshape(local_heads, span_rows, piece_rows), neg_large)
    next_max = jnp.maximum(running_max, jnp.max(scores, axis=2).reshape(query_rows))
    weights_now = jnp.where(
        allowed[None], jnp.exp(scores - next_max.reshape(local_heads, span_rows)[:, :, None]), 0.0
    ).reshape(query_rows, piece_rows)
    running_sum = jnp.sum(weights_now, axis=1)
    weighted = jnp.dot(
        weights_now.astype(jnp.bfloat16), kv_piece[:, HEAD:], preferred_element_type=jnp.float32
    )
    heads_out = (weighted / running_sum[:, None]).astype(jnp.bfloat16)
    heads_out = (
        heads_out.reshape(local_heads, span_rows, HEAD)
        .transpose(1, 0, 2)
        .reshape(span_rows, local_heads * HEAD)
    )
    projected = jnp.dot(
        lax.all_gather(heads_out, "ctx", axis=0, tiled=True),
        out_weight,
        preferred_element_type=jnp.float32,
    )
    attn_part = lax.psum_scatter(
        projected.astype(jnp.bfloat16), "exp", scatter_dimension=0, tiled=True
    ).astype(jnp.float32)
    mixed = (residual.astype(jnp.float32) + attn_part).astype(jnp.bfloat16)
    mixed_wide = mixed.astype(jnp.float32)
    square_sum = lax.psum(jnp.sum(mixed_wide * mixed_wide, axis=1), "ctx")
    inverse = lax.rsqrt(square_sum / D + eps_norm)
    normed = (mixed_wide * inverse[:, None] * norm_gain[None, :]).astype(jnp.bfloat16)
    local_experts = expert_in.shape[0]
    flight = exp_count * local_experts
    expert_ids = jnp.arange(flight, dtype=jnp.int32)
    matched = routes[:, :, None] == expert_ids[None, None, :]
    member = jnp.sum(matched.astype(jnp.int32), axis=1)
    pair_gate = jnp.sum(jnp.where(matched, gate_values[:, :, None], 0.0), axis=1)
    slot_index = jnp.cumsum(member, axis=0) - member
    slot_ids = jnp.arange(CAP, dtype=jnp.int32)
    placed = (member.T[:, None, :] == 1) & (slot_index.T[:, None, :] == slot_ids[None, :, None])
    outgoing = jnp.einsum(
        "fct,td->fcd", placed.astype(jnp.bfloat16), normed, preferred_element_type=jnp.float32
    ).astype(jnp.bfloat16)
    outgoing = outgoing.reshape(exp_count, local_experts * CAP, outgoing.shape[2])
    arrived = lax.all_to_all(outgoing, "exp", split_axis=0, concat_axis=0, tiled=True)
    arrived = arrived.reshape(exp_count, local_experts, CAP, arrived.shape[2])
    gate_up = jnp.einsum("secd,edf->escf", arrived, expert_in, preferred_element_type=jnp.float32)
    summed = lax.psum(gate_up.astype(jnp.bfloat16), "ctx").astype(jnp.float32)
    active = (jax.nn.silu(summed[..., :FFE]) * summed[..., FFE:]).astype(jnp.bfloat16)
    produced = jnp.einsum(
        "escf,efd->escd", active, expert_out, preferred_element_type=jnp.float32
    ).astype(jnp.bfloat16)
    returned = lax.all_to_all(produced, "exp", split_axis=1, concat_axis=0, tiled=True)
    returned = returned.reshape(flight, CAP, returned.shape[3])
    mix_table = placed.astype(jnp.float32) * pair_gate.T[:, None, :]
    expert_sum = jnp.einsum(
        "fct,fcd->td", mix_table, returned.astype(jnp.float32), precision=lax.Precision.HIGHEST
    )
    return (mixed, expert_sum.astype(jnp.bfloat16))


def solution(mesh):
    placed = (
        P("ctx", "exp"),
        P("ctx", None),
        P("ctx", None),
        P("ctx", None),
        P("ctx", None),
        P(),
        P("exp", "ctx"),
        P("exp", "ctx"),
        P("ctx"),
        P("exp", None),
        P("exp", None),
        P("exp", "ctx", None),
        P("exp", None, "ctx"),
    )
    return jax.shard_map(
        body,
        mesh=mesh,
        in_specs=placed,
        out_specs=(P("exp", "ctx"), P("exp", "ctx")),
        check_vma=False,
    )
```

profile of v0, /device:TPU:0, one launch (start us, length us, event | category | flops | bytes accessed | tf_op | source)
XLA Modules:
  0.0 186.7 jit_solution(12227213875042583886)
XLA Ops:
  7.2 0.9 convert_reduce_fusion.2
  8.2 0.8 convert_reduce_fusion
  9.0 0.8 constant_dynamic-slice_fusion.2
  9.8 0.7 constant_dynamic-slice_fusion
  10.6 11.9 %all_gather.6 = bf16[1536,256]{1,0:T(8,128)(2,1)S(1)} all-gather(bf16[192,256]{1,0:T(8,128)(2,1)S(1)} %maximum_maximum_fusion), channel_id=1, replica_groups=mesh['ctx'=8,'exp'=4] {'ctx'}, dimensions={0}, use_global_device_ids=true | all-gather | bytes 884736 | tf_op jit(solution)/shard_map/all_gather | solution.py:69
  22.4 0.2 or_and_fusion
  22.6 0.6 broadcast_in_dim.30
  23.2 1.7 copy.50
  25.0 0.1 copy.48
  25.1 1.2 fusion.2
  26.3 1.8 fusion.3
  28.2 2.0 %fusion.19 = bf16[1024,128]{1,0:T(8,128)(2,1)S(1)} fusion(pred[1024,1536]{0,1:T(32,128)(4,1)S(1)} %copy.50, f32[1536,1024]{1,0:T(8,128)S(1)} %get-tuple-element.5, f32[1024]{0:T(1024)S(1)} %broadcast_maximum_fusion, bf16[1536,256]{1,0:T(8,128)(2,1)S(1)} %all_gather.6, f32[1024]{0:T(1024)S(1)} %fusion.3), kind=kOutput, calls=%fused_computation.17 | convolution fusion | flops 410779648 | bytes 8527872 | tf_op jit(solution)/shard_map/dot_general | solution.py:101
  30.1 0.2 copy.51
  30.3 0.8 copy.64
  31.2 0.0 reduce-scatter.2.cloned.1.call-start
  31.2 28.3 %all-gather.2.cloned.1.call-done = bf16[512,2048]{1,0:T(8,128)(2,1)} async-done(((bf16[64,2048]{1,0:T(8,128)(2,1)}), bf16[512,2048]{1,0:T(8,128)(2,1)}) %all-gather.2.cloned.1.call-update) | async-done | bytes 2097168 | tf_op jit(solution)/shard_map/all_gather | solution.py:111
  59.5 4.3 %convolution_convert_fusion = bf16[512,512]{1,0:T(8,128)(2,1)} fusion(bf16[512,2048]{1,0:T(8,128)(2,1)} %all-gather.2.cloned.1.call-done, bf16[2048,512]{1,0:T(8,128)(2,1)} %param.19), kind=kOutput, calls=%fused_computation.11 | convolution fusion | flops 1074003968 | bytes 4718592 | tf_op jit(solution)/shard_map/dot_general | solution.py:110
  63.9 0.1 copy.52
  64.0 0.2 reduce_window_sum.11
  64.2 21.4 %reduce-scatter.2.cloned.1.call-done = bf16[128,512]{1,0:T(8,128)(2,1)} async-done(((bf16[512,512]{1,0:T(8,128)(2,1)}), bf16[128,512]{1,0:T(8,128)(2,1)}) %reduce-scatter.2.cloned.1.call-update) | async-done | bytes 131088 | tf_op jit(solution)/shard_map/reduce_scatter | solution.py:115
  85.6 1.0 fusion.28
  86.6 11.9 %psum.14 = f32[128]{0:T(128)S(1)} all-reduce(f32[128]{0:T(128)S(1)} %get-tuple-element.2), channel_id=1, replica_groups=mesh['ctx'=8,'exp'=4] {'ctx'}, use_global_device_ids=true, to_apply=%region_9.10 | all-reduce | flops 128 | bytes 1024 | tf_op jit(solution)/shard_map/psum | solution.py:120
  98.5 0.3 convolution_convert_fusion.1
  98.8 8.6 %all_to_all.20 = bf16[4,32,512]{2,1,0:T(8,128)(2,1)S(1)} all-to-all(bf16[4,32,512]{2,1,0:T(8,128)(2,1)S(1)} %bitcast.71), channel_id=1, replica_groups=mesh['ctx'=8,'exp'=4] {'exp'}, dimensions={0} | all-to-all | bytes 262144 | tf_op jit(solution)/shard_map/all_to_all | solution.py:136
  107.4 4.9 %fusion.5 = bf16[2,4,16,3072]{3,2,1,0:T(8,128)(2,1)} fusion(bf16[2,512,3072]{2,1,0:T(8,128)(2,1)} %param.24, bf16[4,2,16,512]{3,2,1,0:T(8,128)(2,1)S(1)} %bitcast.65), kind=kOutput, calls=%fused_computation.7 | convolution fusion | flops 403046400 | bytes 7208960 | tf_op jit(solution)/shard_map/secd,edf->escf/dot_general | solution.py:138
  112.4 53.8 %all-reduce.2.cloned.1.call-done = bf16[2,4,16,3072]{3,2,1,0:T(8,128)(2,1)} async-done(((bf16[2,4,16,3072]{3,2,1,0:T(8,128)(2,1)}), bf16[2,4,16,3072]{3,2,1,0:T(8,128)(2,1)}) %all-reduce.2.cloned.1.call-update) | async-done | bytes 786448 | tf_op jit(solution)/shard_map/psum | solution.py:139
  166.2 1.3 convert_element_type.67
  167.5 0.7 fusion.13
  168.1 0.7 copy.56
  168.8 4.4 %all-to-all-start.1 = ((bf16[2,4,16,512]{3,2,0,1:T(8,128)(2,1)}), bf16[2,4,16,512]{3,2,0,1:T(8,128)(2,1)S(1)}, u32[]{:S(2)}, u32[]{:S(2)}) async-start(bf16[2,4,16,512]{3,2,0,1:T(8,128)(2,1)} %copy.56), calls=%async_computation.2 | async-start | bytes 262144 | tf_op jit(solution)/shard_map/all_to_all | solution.py:144
  173.3 5.9 %all-to-all-done.1 = bf16[2,4,16,512]{3,2,0,1:T(8,128)(2,1)S(1)} async-done(((bf16[2,4,16,512]{3,2,0,1:T(8,128)(2,1)}), bf16[2,4,16,512]{3,2,0,1:T(8,128)(2,1)S(1)}, u32[]{:S(2)}, u32[]{:S(2)}) %all-to-all-start.1) | async-done | bytes 131104 | tf_op jit(solution)/shard_map/all_to_all | solution.py:144
  179.2 1.0 fusion.12
  (34 shorter events, 0.4 us)
Async XLA Ops:
  7.2 160.3 %copy-start = (bf16[2,1536,512]{2,1,0:T(8,128)(2,1)S(1)}, bf16[2,1536,512]{2,1,0:T(8,128)(2,1)}, u32[]{:S(2)}) copy-start(bf16[2,1536,512]{2,1,0:T(8,128)(2,1)} %param.25) | copy-start | bytes 9437188
  7.2 52.3 %all-gather.2.cloned.1.call-start = ((), (), s32[]{:S(2)}) async-start(), calls=%async_computation.3 | async-start | bytes 2359296 | tf_op jit(solution)/shard_map/all_gather | solution.py:111
  8.9 16.0 %copy-start.2 = (bf16[64,2048]{1,0:T(8,128)(2,1)S(1)}, bf16[64,2048]{1,0:T(8,128)(2,1)}, u32[]{:S(2)}) copy-start(bf16[64,2048]{1,0:T(8,128)(2,1)} %param.13) | copy-start | bytes 786436
  31.1 32.7 %copy-start.4 = (s32[128,8]{0,1:T(8,128)S(1)}, s32[128,8]{0,1:T(8,128)}, u32[]{:S(2)}) copy-start(s32[128,8]{0,1:T(8,128)} %param.22) | copy-start | bytes 12292
  31.1 54.5 %copy-start.3 = (bf16[128,512]{1,0:T(8,128)(2,1)S(1)}, bf16[128,512]{1,0:T(8,128)(2,1)}, u32[]{:S(2)}) copy-start(bf16[128,512]{1,0:T(8,128)(2,1)} %param.20) | copy-start | bytes 393220
  31.2 67.4 %copy-start.6 = (f32[512]{0:T(512)S(1)}, f32[512]{0:T(512)}, u32[]{:S(2)}) copy-start(f32[512]{0:T(512)} %param.21) | copy-start | bytes 6148
  31.2 54.4 %reduce-scatter.2.cloned.1.call-start = ((), (), s32[]{:S(2)}) async-start(), calls=%async_computation.4 | async-start | bytes 655360 | tf_op jit(solution)/shard_map/reduce_scatter | solution.py:115
  63.8 102.4 %all-reduce.2.cloned.1.call-start = ((), (), s32[]{:S(2)}) async-start(), calls=%async_computation.5 | async-start | bytes 1572864 | tf_op jit(solution)/shard_map/psum | solution.py:139
  86.6 25.7 %copy-start.1 = (bf16[128,512]{1,0:T(8,128)(2,1)}, bf16[128,512]{1,0:T(8,128)(2,1)S(1)}, u32[]{:S(2)}) copy-start(bf16[128,512]{1,0:T(8,128)(2,1)S(1)} %get-tuple-element.3) | copy-start | bytes 393220
  167.5 5.8 %copy-start.5 = (f32[128,8]{0,1:T(8,128)S(1)}, f32[128,8]{0,1:T(8,128)}, u32[]{:S(2)}) copy-start(f32[128,8]{0,1:T(8,128)} %param.23) | copy-start | bytes 12292
  168.8 10.4 %all-to-all-start.1 = ((bf16[2,4,16,512]{3,2,0,1:T(8,128)(2,1)}), bf16[2,4,16,512]{3,2,0,1:T(8,128)(2,1)S(1)}, u32[]{:S(2)}, u32[]{:S(2)}) async-start(bf16[2,4,16,512]{3,2,0,1:T(8,128)(2,1)} %copy.56), calls=%async_computation.2 | async-start | bytes 262144 | tf_op jit(solution)/shard_map/all_to_all | solution.py:144
Sparse Core Ops, SparseCore 0:
  31.2 28.2 all-gather.1
  63.9 21.6 reduce-scatter.1
  112.5 53.6 all-reduce.1
where the time goes:
time: 187 us
  waiting for transfers between devices  109 us (58%)
  blocking collectives  32.4 us (17%)
  matrix products  14.3 us (8%)
  between operations  14 us (7%)
  other arithmetic  6.25 us (3%)
  local copies, waits for them, and re-layouts  5.79 us (3%)
  starting transfers between devices  4.57 us (2%)
    psum x1, waiting for transfers between devices, body(): summed = lax.psum(gate_up.astype(jnp.bfloat16), 'ctx').astype(jnp.float32)  53.8 us
    all_gather x1, waiting for transfers between devices, body(): lax.all_gather(heads_out, 'ctx', axis=0, tiled=True)  28.3 us
    reduce_scatter x1, waiting for transfers between devices, body(): lax.psum_scatter(projected.astype(jnp.bfloat16), 'exp', scatter_dimension...  21.4 us
    psum x1, blocking collectives, body(): square_sum = lax.psum(jnp.sum(mixed_wide * mixed_wide, axis=1), 'ctx')  11.9 us
    all_gather x1, blocking collectives, body(): kv_piece = lax.all_gather(local_kv, 'ctx', axis=0, tiled=True)  11.9 us
    all_to_all x1, blocking collectives, body(): lax.all_to_all(outgoing, 'exp', split_axis=0, concat_axis=0, tiled=True)  8.63 us
    all_to_all x1, waiting for transfers between devices, body(): lax.all_to_all(produced, 'exp', split_axis=1, concat_axis=0, tiled=True)  5.91 us
    dot_general x1, matrix products, body(): jnp.einsum('secd,edf->escf', arrived, expert_in, preferred_element_type=j...  4.93 us
  transfers between devices with their start and end apart: 4, of which 4 were waited for; matrix products, arithmetic and copies ran while one was open for 0% of the time, Pallas kernels for 0%

commit v1 on v0

v1 whole, which is shorter than its diff:
```python
import functools
import math

import jax
import jax.numpy as jnp
from jax import lax
from jax.experimental import pallas as pl
from jax.experimental.pallas import tpu as pltpu
from jax.sharding import PartitionSpec as P

QHEADS = 64
KVH = 4
HEAD = 128
CAP = 16
LANES = 128

neg_large = -1e30
eps_norm = 1e-06
bf16 = jnp.bfloat16
f32 = jnp.float32
MIB = 1024 * 1024

VMEM = pl.BlockSpec(memory_space=pltpu.VMEM)
SMEM = pl.BlockSpec(memory_space=pltpu.SMEM)
ANY = pl.BlockSpec(memory_space=pl.ANY)


def call(kernel, out_shape, in_specs, scratch=(), vmem=16, flops=0, nbytes=0):
    many = isinstance(out_shape, (list, tuple))
    return pl.pallas_call(
        kernel,
        out_shape=out_shape,
        in_specs=in_specs,
        out_specs=[VMEM] * len(out_shape) if many else VMEM,
        scratch_shapes=list(scratch),
        compiler_params=pltpu.CompilerParams(vmem_limit_bytes=vmem * MIB),
        cost_estimate=pl.CostEstimate(flops=flops, bytes_accessed=nbytes, transcendentals=0),
    )


def shape(dims, dtype):
    return jax.ShapeDtypeStruct(dims, dtype)


def dot(a, b):
    return lax.dot_general(a, b, (((1,), (0,)), ((), ())), preferred_element_type=f32)


def dot_t(a, b):
    return lax.dot_general(a, b, (((1,), (1,)), ((), ())), preferred_element_type=f32)


def rows_at(start, size, step):
    return pl.ds(pl.multiple_of(start, step), size)


def pick_kv(local_heads, ck, cv, bk, bv, out, sems):
    kv = lax.axis_index("exp") * local_heads // (QHEADS // KVH)
    cols = rows_at(kv * HEAD, HEAD, HEAD)
    cache, span = ck.shape[0], bk.shape[0]
    copies = []
    for n, (src, row, size, col) in enumerate(
        ((ck, 0, cache, 0), (cv, 0, cache, HEAD), (bk, cache, span, 0), (bv, cache, span, HEAD))
    ):
        copies.append(
            pltpu.make_async_copy(
                src.at[:, cols], out.at[pl.ds(row, size), pl.ds(col, HEAD)], sems.at[n]
            )
        )
    for copy in copies:
        copy.start()
    for copy in copies:
        copy.wait()


def rank_kernel(routes, gates, rank, gate):
    flight, tokens = rank.shape
    expert = lax.broadcasted_iota(jnp.int32, (flight, tokens), 0)
    member = jnp.zeros((flight, tokens), f32)
    weight = jnp.zeros((flight, tokens), f32)
    for k in range(routes.shape[0]):
        hit = routes[k : k + 1, :] == expert
        member = jnp.where(hit, 1.0, member)
        weight = weight + jnp.where(hit, gates[k : k + 1, :], 0.0)
    before = lax.broadcasted_iota(jnp.int32, (tokens, tokens), 0) < lax.broadcasted_iota(
        jnp.int32, (tokens, tokens), 1
    )
    count = dot(member.astype(bf16), jnp.where(before, 1.0, 0.0).astype(bf16))
    rank[...] = jnp.where(member > 0.5, count, -1.0)
    gate[...] = weight


def segment_of(position, seg_starts):
    passed = jnp.full(position.shape, -1, jnp.int32)
    for n in range(seg_starts.shape[0]):
        passed = passed + jnp.where(seg_starts[n] <= position, 1, 0)
    return passed


def visible(seg_starts, other, span, cache, pieces):
    ctx = lax.axis_index("ctx")
    cache_total = cache * lax.axis_size("ctx")
    piece_rows = cache + span
    keys = pieces * piece_rows
    index = lax.broadcasted_iota(jnp.int32, (1, keys), 1)
    key_pos = jnp.zeros((1, keys), jnp.int32)
    for k in range(pieces):
        owner = jnp.bitwise_xor(ctx, 2 * k + other)
        off = index - k * piece_rows
        pos = jnp.where(off < cache, owner * cache + off, cache_total + owner * span + off - cache)
        key_pos = pos if k == 0 else jnp.where(off >= 0, pos, key_pos)
    key_seg = segment_of(key_pos, seg_starts)
    query_pos = cache_total + ctx * span + lax.broadcasted_iota(jnp.int32, (span, 1), 0)
    query_seg = segment_of(query_pos, seg_starts)
    last = seg_starts.shape[0] - 1
    return (key_pos <= query_pos) & (
        (key_seg == query_seg) | (key_seg == 0) | (query_seg == last)
    )


GROUP = 4


def attend(seg_starts, q, kv, other, span, cache, heads, finish):
    pieces = kv.shape[0] // (cache + span)
    seen = visible(seg_starts, other, span, cache, pieces)
    scale = math.log2(math.e) / math.sqrt(HEAD)
    group = min(GROUP, heads)
    rows = group * span
    keys = kv[:, :HEAD]
    values = kv[:, HEAD:]
    for g in range(heads // group):
        stacked = jnp.concatenate(
            [q[:, (g * group + h) * HEAD : (g * group + h + 1) * HEAD] for h in range(group)], axis=0
        )
        scores = dot_t(stacked, keys)
        scores = jnp.where(
            seen[None], scores.reshape(group, span, kv.shape[0]), neg_large
        ).reshape(rows, kv.shape[0])
        top = jnp.max(scores, axis=1, keepdims=True)
        probs = jnp.exp2((scores - top) * scale)
        total = jnp.sum(probs, axis=1, keepdims=True)
        out = dot(probs.astype(bf16), values)
        finish(g, rows, group, out, top, total)


def attend_first(span, cache, heads, seg_starts, q, kv, o_out, m_out, l_out):
    def finish(g, rows, group, out, top, total):
        at = pl.ds(g * rows, rows)
        o_out[at, :] = out
        m_out[at, :] = jnp.broadcast_to(top, (rows, LANES))
        l_out[at, :] = jnp.broadcast_to(total, (rows, LANES))

    attend(seg_starts, q, kv, 0, span, cache, heads, finish)


def attend_second(span, cache, heads, seg_starts, q, kv, o_in, m_in, l_in, result):
    scale = math.log2(math.e) / math.sqrt(HEAD)

    def finish(g, rows, group, out, top, total):
        at = pl.ds(g * rows, rows)
        first = m_in[at, :]
        both = jnp.maximum(first, top)
        w_first = jnp.exp2((first - both) * scale)
        w_second = jnp.exp2((top - both) * scale)
        norm = l_in[at, :] * w_first + total * w_second
        merged = ((o_in[at, :] * w_first + out * w_second) / norm).astype(bf16)
        for h in range(group):
            col = (g * group + h) * HEAD
            result[:, col : col + HEAD] = merged[h * span : (h + 1) * span, :]

    attend(seg_starts, q, kv, 1, span, cache, heads, finish)


def project_first(heads_out, weight, out):
    out[...] = dot(heads_out[...], weight[...])


def project_second(n_exp, span, heads_out, weight, first, residual, *refs):
    ranks = refs[:n_exp]
    own_out = refs[n_exp]
    part_outs = refs[n_exp + 1 : 2 * n_exp]
    pick_outs = refs[2 * n_exp : 3 * n_exp]
    whole, picked = refs[3 * n_exp :]
    ctx, exp = lax.axis_index("ctx"), lax.axis_index("exp")
    second = dot(heads_out[...], weight[...])
    for k in range(heads_out.shape[0] // span):
        here = slice(k * span, (k + 1) * span)
        whole[rows_at(jnp.bitwise_xor(ctx, 2 * k) * span, span, span), :] = first[here, :]
        whole[rows_at(jnp.bitwise_xor(ctx, 2 * k + 1) * span, span, span), :] = second[here, :]
    tokens = residual.shape[0]
    flight = ranks[0].shape[0]
    local = flight // n_exp
    slot = lax.broadcasted_iota(jnp.int32, (CAP, tokens), 0).astype(f32)
    for k in range(n_exp):
        block = jnp.bitwise_xor(exp, k)
        part = whole[rows_at(block * tokens, tokens, tokens), :]
        if k == 0:
            part = part + residual[...].astype(f32)
            own_out[...] = part
        narrow = part.astype(bf16)
        if k > 0:
            part_outs[k - 1][...] = narrow
        rank = ranks[k][...]
        table = jnp.concatenate(
            [jnp.where(rank[e : e + 1, :] == slot, 1.0, 0.0) for e in range(flight)], axis=0
        ).astype(bf16)
        rows = dot(table, narrow).astype(bf16)
        for e in range(flight):
            at = (e % local) * n_exp * CAP + block * CAP
            picked[e // local, rows_at(at, CAP, CAP), :] = rows[e * CAP : (e + 1) * CAP, :]
    for k in range(n_exp):
        pick_outs[k][...] = picked[jnp.bitwise_xor(exp, k)]


def split_square(square):
    lane = lax.broadcasted_iota(jnp.int32, (square.shape[0], LANES), 1)
    high = square.astype(bf16).astype(f32)
    return jnp.where(lane == 0, high, jnp.where(lane == 1, square - high, 0.0))


def expert_in_kernel(n_exp, other, *refs):
    arrived = refs[:n_exp]
    gain, weight, out, held, sems = refs[n_exp:]
    expert = jnp.bitwise_xor(lax.axis_index("ctx") % 2, other)
    rows = out.shape[0]
    width = weight.shape[2]
    chunks = held.shape[0]
    step = width // chunks
    copies = [
        pltpu.make_async_copy(
            weight.at[expert, :, pl.ds(n * step, step)], held.at[n], sems.at[n]
        )
        for n in range(chunks)
    ]
    for copy in copies:
        copy.start()
    at = rows_at(expert * rows, rows, rows)
    total = arrived[0][at, :].astype(f32)
    for ref in arrived[1:]:
        total = total + ref[at, :].astype(f32)
    mixed = total.astype(bf16).astype(f32)
    out[:, width:] = split_square(jnp.sum(mixed * mixed, axis=1, keepdims=True)).astype(out.dtype)
    scaled = (mixed * gain[...]).astype(bf16)
    for n, copy in enumerate(copies):
        copy.wait()
        out[:, n * step : (n + 1) * step] = dot(scaled, held[n]).astype(out.dtype)


def chip_sum(mine, theirs, *outs):
    chip = lax.axis_index("ctx") // 2
    width = mine.shape[1] - LANES
    size = outs[0].shape[0]
    for k, out in enumerate(outs):
        at = rows_at(jnp.bitwise_xor(chip, k) * size, size, size)
        total = mine[at, :] + theirs[at, :].astype(f32)
        out[:, :width] = total[:, :width].astype(bf16)
        out[:, width:] = split_square(
            jnp.sum(total[:, width:], axis=1, keepdims=True)
        ).astype(bf16)


def activate(features, *refs):
    out = refs[-1]
    total = refs[0][...].astype(f32)
    for ref in refs[1:-1]:
        total = total + ref[...].astype(f32)
    hidden = out.shape[1]
    square = jnp.sum(total[:, 2 * hidden :], axis=1, keepdims=True)
    inverse = lax.rsqrt(square / features + eps_norm)
    gate = total[:, :hidden] * inverse
    up = total[:, hidden : 2 * hidden] * inverse
    out[...] = (gate / (1.0 + jnp.exp(-gate)) * up).astype(bf16)


def load_expert(weight, other, held, sem):
    expert = jnp.bitwise_xor(lax.axis_index("ctx") % 2, other)
    return pltpu.make_async_copy(weight.at[expert], held, sem)


def expert_out_first(active, weight, out, held, sem):
    copy = load_expert(weight, 0, held, sem)
    copy.start()
    copy.wait()
    out[...] = dot(active[...], held[...]).astype(bf16)


def expert_out_second(n_exp, active, weight, first, *refs):
    outs = refs[:n_exp]
    held, whole, sem = refs[n_exp:]
    copy = load_expert(weight, 1, held, sem)
    copy.start()
    ctx, exp = lax.axis_index("ctx"), lax.axis_index("exp")
    core, chip = ctx % 2, ctx // 2
    chips = lax.axis_size("ctx") // 2
    size = active.shape[0] // chips
    copy.wait()
    second = dot(active[...], held[...]).astype(bf16)
    for k in range(chips):
        at = rows_at(jnp.bitwise_xor(chip, k) * size, size, size)
        here = slice(k * size, (k + 1) * size)
        whole[core, at, :] = first[here, :]
        whole[1 - core, at, :] = second[here, :]
    for k in range(n_exp):
        at = rows_at(jnp.bitwise_xor(exp, k) * CAP, CAP, CAP)
        for j in range(whole.shape[0]):
            outs[k][j * CAP : (j + 1) * CAP, :] = whole[j, at, :]


def combine(n_exp, rank, gate, *refs):
    returned, out = refs[:n_exp], refs[n_exp]
    exp = lax.axis_index("exp")
    tokens = rank.shape[1]
    local = rank.shape[0] // n_exp
    slot = lax.broadcasted_iota(jnp.int32, (CAP, tokens), 0).astype(f32)
    tables = []
    for k in range(n_exp):
        for j in range(local):
            at = pl.ds(jnp.bitwise_xor(exp, k) * local + j, 1)
            tables.append(jnp.where(rank[at, :] == slot, gate[at, :], 0.0))
    table = jnp.concatenate(tables, axis=0).T
    rows = jnp.concatenate([ref[...] for ref in returned], axis=0)
    high = table.astype(bf16)
    low = (table - high.astype(f32)).astype(bf16)
    out[...] = (dot(high, rows) + dot(low, rows)).astype(bf16)


def permute(x, axis, k):
    n = lax.axis_size(axis)
    return lax.ppermute(x, axis, [(i, i ^ k) for i in range(n)])


def body(
    queries,
    cache_keys,
    cache_values,
    block_keys,
    block_values,
    seg_starts,
    out_weight,
    residual,
    norm_gain,
    routes,
    gate_values,
    expert_in,
    expert_out,
):
    n_ctx, n_exp = lax.axis_size("ctx"), lax.axis_size("exp")
    chips = n_ctx // 2
    span = queries.shape[0]
    heads = queries.shape[1] // HEAD
    cache = cache_keys.shape[0]
    tokens = routes.shape[0]
    local, features, width = expert_in.shape
    hidden = width // 2
    columns = out_weight.shape[1]
    flight = n_exp * local

    def over_chips(x):
        return [permute(x, "ctx", 2 * k) for k in range(1, chips)]

    def over_exp(xs):
        return [permute(x, "exp", k) for k, x in zip(range(1, n_exp), xs)]

    local_kv = call(
        functools.partial(pick_kv, heads),
        shape((cache + span, 2 * HEAD), bf16),
        [ANY] * 4,
        [pltpu.SemaphoreType.DMA((4,))],
        vmem=4,
    )(cache_keys, cache_values, block_keys, block_values)
    kv_same = jnp.concatenate([local_kv] + over_chips(local_kv), axis=0)
    kv_other = permute(kv_same, "ctx", 1)

    rank, gate = call(
        rank_kernel,
        [shape((flight, tokens), f32)] * 2,
        [VMEM] * 2,
        vmem=4,
    )(routes.T, gate_values.T)
    ranks = [rank] + over_exp([rank] * (n_exp - 1))

    rows = heads * span
    cost = dict(flops=4 * rows * kv_same.shape[0] * HEAD, nbytes=4 * MIB)
    stats = call(
        functools.partial(attend_first, span, cache, heads),
        [shape((rows, HEAD), f32), shape((rows, LANES), f32), shape((rows, LANES), f32)],
        [SMEM, VMEM, VMEM],
        vmem=24,
        **cost,
    )(seg_starts, queries, kv_same)
    heads_out = call(
        functools.partial(attend_second, span, cache, heads),
        shape((span, heads * HEAD), bf16),
        [SMEM] + [VMEM] * 5,
        vmem=24,
        **cost,
    )(seg_starts, queries, kv_other, *stats)

    heads_same = jnp.concatenate([heads_out] + over_chips(heads_out), axis=0)
    heads_other = permute(heads_same, "ctx", 1)
    cost = dict(
        flops=2 * heads_same.shape[0] * heads_same.shape[1] * columns, nbytes=4 * MIB
    )
    first = call(
        project_first,
        shape((heads_same.shape[0], columns), f32),
        [VMEM] * 2,
        vmem=16,
        **cost,
    )(heads_same, out_weight)
    per_exp = local * n_exp * CAP
    outs = call(
        functools.partial(project_second, n_exp, span),
        [shape((tokens, columns), f32)]
        + [shape((tokens, columns), bf16)] * (n_exp - 1)
        + [shape((per_exp, columns), bf16)] * n_exp,
        [VMEM] * (4 + n_exp),
        [
            pltpu.VMEM((n_ctx * span, columns), f32),
            pltpu.VMEM((n_exp, per_exp, columns), bf16),
        ],
        vmem=24,
        **cost,
    )(heads_other, out_weight, first, residual, *ranks)
    own, parts, picks = outs[0], outs[1:n_exp], outs[n_exp:]
    arrived = [picks[0]] + over_exp(picks[1:])

    gain = norm_gain.reshape(1, features)
    expert_rows = n_exp * CAP
    chunks = 6

    def gate_up(other, dtype):
        return call(
            functools.partial(expert_in_kernel, n_exp, other),
            shape((expert_rows, width + LANES), dtype),
            [VMEM] * (n_exp + 1) + [ANY],
            [
                pltpu.VMEM((chunks, features, width // chunks), bf16),
                pltpu.SemaphoreType.DMA((chunks,)),
            ],
            vmem=16,
            flops=2 * expert_rows * features * width,
            nbytes=4 * MIB,
        )(*arrived, gain, expert_in)

    sent = gate_up(1, bf16)
    theirs = permute(sent, "ctx", 1)
    mine = gate_up(0, f32)

    parts, mine = lax.optimization_barrier((parts, mine))
    part_sum = own
    for part in over_exp(parts):
        part_sum = part_sum + part.astype(f32)
    mixed = part_sum.astype(bf16)

    size = expert_rows // chips
    chunk = call(
        chip_sum,
        [shape((size, width + LANES), bf16)] * chips,
        [VMEM] * 2,
        vmem=8,
    )(mine, theirs)
    gathered = [chunk[0]] + [permute(chunk[k], "ctx", 2 * k) for k in range(1, chips)]
    active = call(
        functools.partial(activate, n_ctx * features),
        shape((size, hidden), bf16),
        [VMEM] * chips,
        vmem=8,
    )(*gathered)
    active_same = jnp.concatenate([active] + over_chips(active), axis=0)
    active_other = permute(active_same, "ctx", 1)
    held = pltpu.VMEM((hidden, columns), bf16)
    cost = dict(flops=2 * expert_rows * hidden * columns, nbytes=2 * MIB)
    made = call(
        expert_out_first,
        shape((expert_rows, columns), bf16),
        [VMEM, ANY],
        [held, pltpu.SemaphoreType.DMA],
        vmem=8,
        **cost,
    )(active_same, expert_out)
    produced = call(
        functools.partial(expert_out_second, n_exp),
        [shape((local * CAP, columns), bf16)] * n_exp,
        [VMEM, ANY, VMEM],
        [held, pltpu.VMEM((local, expert_rows, columns), bf16), pltpu.SemaphoreType.DMA],
        vmem=8,
        **cost,
    )(active_other, expert_out, made)
    returned = [produced[0]] + over_exp(produced[1:])
    expert_sum = call(
        functools.partial(combine, n_exp),
        shape((tokens, columns), bf16),
        [VMEM] * (2 + n_exp),
        vmem=8,
    )(rank, gate, *returned)
    return (mixed, expert_sum)


def solution(mesh):
    placed = (
        P("ctx", "exp"),
        P("ctx", None),
        P("ctx", None),
        P("ctx", None),
        P("ctx", None),
        P(),
        P("exp", "ctx"),
        P("exp", "ctx"),
        P("ctx"),
        P("exp", None),
        P("exp", None),
        P("exp", "ctx", None),
        P("exp", None, "ctx"),
    )
    return jax.shard_map(
        body,
        mesh=mesh,
        in_specs=placed,
        out_specs=(P("exp", "ctx"), P("exp", "ctx")),
        check_vma=False,
    )
```

time: 187 us -> 97.3 us (0.52)
  waiting for transfers between devices: 109 us -> 43.8 us
  blocking collectives: 32.4 us -> 0 us
  starting transfers between devices: 4.57 us -> 33.5 us
  matrix products: 14.3 us -> 0 us
  between operations: 14 us -> 0.88 us
  Pallas kernels: 0 us -> 12.9 us
  other arithmetic: 6.25 us -> 0.83 us
    psum x1 -> x0, waiting for transfers between devices: 53.8 us -> none  [body(): summed = lax.psum(gate_up.astype(jnp.bfloat16), 'ctx').astype(jnp.float32)]
    ppermute x0 -> x28, waiting for transfers between devices: none -> 43.8 us  [permute(): return lax.ppermute(x, axis, [(i, i ^ k) for i in range(n)])]
    ppermute x0 -> x28, starting transfers between devices: none -> 33.5 us  [permute(): return lax.ppermute(x, axis, [(i, i ^ k) for i in range(n)])]
    all_gather x1 -> x0, waiting for transfers between devices: 28.3 us -> none  [body(): lax.all_gather(heads_out, 'ctx', axis=0, tiled=True)]
    reduce_scatter x1 -> x0, waiting for transfers between devices: 21.4 us -> none  [body(): lax.psum_scatter(projected.astype(jnp.bfloat16), 'exp', scatter_dimension...]
    dot_general x7 -> x0, matrix products: 14.3 us -> none  [the longest x1 4.93 us: body(): jnp.einsum('secd,edf->escf', arrived, expert_in, preferred_element_type=j...]
    pallas_call x0 -> x13, Pallas kernels: none -> 12.9 us  [the longest x2 3.75 us: gate_up(): call(functools.partial(expert_in_kernel, n_exp, other), shape((expert_row...]
    psum x1 -> x0, blocking collectives: 11.9 us -> none  [body(): square_sum = lax.psum(jnp.sum(mixed_wide * mixed_wide, axis=1), 'ctx')]
  transfers between devices with their start and end apart: 4 -> 28, of which waited for: 4 -> 16; matrix products, arithmetic and copies ran while one was open for 0% -> 1% of each run, Pallas kernels for 0% -> 6%
where the time goes in v1:
time: 97.3 us; the launch traced here: 97.1 us
  waiting for transfers between devices  43.8 us (45%)
  starting transfers between devices  33.5 us (34%)
  Pallas kernels  12.9 us (13%)
  local copies, waits for them, and re-layouts  5.12 us (5%)
    ppermute x28, waiting for transfers between devices, permute(): return lax.ppermute(x, axis, [(i, i ^ k) for i in range(n)])  43.8 us
    ppermute x28, starting transfers between devices, permute(): return lax.ppermute(x, axis, [(i, i ^ k) for i in range(n)])  33.5 us
    unnamed x26, local copies, waits for them, and re-layouts  5.12 us
    pallas_call x2, Pallas kernels, gate_up(): call(functools.partial(expert_in_kernel, n_exp, other), shape((expert_row...  3.75 us
    pallas_call x1, Pallas kernels, body(): call(functools.partial(attend_second, span, cache, heads), shape((span, h...  2.53 us
    pallas_call x1, Pallas kernels, body(): call(functools.partial(attend_first, span, cache, heads), [shape((rows, H...  2.39 us
  transfers between devices with their start and end apart: 28, of which 16 were waited for; matrix products, arithmetic and copies ran while one was open for 1% of the time, Pallas kernels for 6%

profile of v1, /device:TPU:0, one launch (start us, length us, event | category | flops | bytes accessed | tf_op | source)
XLA Modules:
  0.0 97.1 jit_solution(29430315177708016)
XLA Ops:
  4.2 4.0 %collective-permute-start.2 = (bf16[192,256]{1,0:T(8,128)(2,1)S(1)}, bf16[192,256]{1,0:T(8,128)(2,1)S(1)}, u32[]{:S(2)}, u32[]{:S(2)}) collective-permute-start(bf16[192,256]{1,0:T(8,128)(2,1)S(1)} %shard_map.140), channel_id=1, source_target_pairs={{0,24},{4,28},{8,16},{12,20},{16,8},{20,12},{24,0},{28,4},{1,25},{... | collective-permute-start | bytes 294920 | tf_op jit(solution)/shard_map/ppermute | solution.py:330
  8.8 2.5 %collective-permute-done.2 = bf16[192,256]{1,0:T(8,128)(2,1)S(1)} collective-permute-done((bf16[192,256]{1,0:T(8,128)(2,1)S(1)}, bf16[192,256]{1,0:T(8,128)(2,1)S(1)}, u32[]{:S(2)}, u32[]{:S(2)}) %collective-permute-start.2) | collective-permute-done | bytes 98336 | tf_op jit(solution)/shard_map/ppermute | solution.py:330
  11.3 1.7 %collective-permute-done.1 = bf16[192,256]{1,0:T(8,128)(2,1)S(1)} collective-permute-done((bf16[192,256]{1,0:T(8,128)(2,1)S(1)}, bf16[192,256]{1,0:T(8,128)(2,1)S(1)}, u32[]{:S(2)}, u32[]{:S(2)}) %collective-permute-start.1) | collective-permute-done | bytes 98336 | tf_op jit(solution)/shard_map/ppermute | solution.py:330
  15.1 2.4 %shard_map.141 = (f32[1024,128]{1,0:T(8,128)S(1)}, f32[1024,128]{1,0:T(8,128)S(1)}, f32[1024,128]{1,0:T(8,128)S(1)}) custom-call(s32[10]{0:T(128)S(1)} %copy-done.12, bf16[64,2048]{1,0:T(8,128)(2,1)S(1)} %copy-done.3, bf16[768,256]{1,0:T(8,128)(2,1)S(1)} %pad_maximum_fusion.1.kv), custom_call_target="tpu_custom_call" | custom-call | flops 402653184 | bytes 4194304 | tf_op jit(solution)/shard_map/pallas_call | solution.py:385
  17.5 2.5 %shard_map.142 = bf16[64,2048]{1,0:T(8,128)(2,1)S(1)} custom-call(s32[10]{0:T(128)S(1)} %copy-done.12, bf16[64,2048]{1,0:T(8,128)(2,1)S(1)} %copy-done.3, bf16[768,256]{1,0:T(8,128)(2,1)S(1)} %collective-permute-done.3.kv, f32[1024,128]{1,0:T(8,128)S(1)} %get-tuple-element.27.o_in, f32[1024,128]{1,0:T(8,128)S(1)} %get-tuple-element.28.m_in, ...), custom_call_target="tpu_custom_call" | custom-call | flops 402653184 | bytes 4194304 | tf_op jit(solution)/shard_map/pallas_call | solution.py:392
  20.1 1.6 %collective-permute-start.6 = (bf16[64,2048]{1,0:T(8,128)(2,1)S(1)}, bf16[64,2048]{1,0:T(8,128)(2,1)S(1)}, u32[]{:S(2)}, u32[]{:S(2)}) collective-permute-start(bf16[64,2048]{1,0:T(8,128)(2,1)S(1)} %shard_map.142), channel_id=1, source_target_pairs={{0,24},{4,28},{8,16},{12,20},{16,8},{20,12},{24,0},{28,4},{1,25},{... | collective-permute-start | bytes 786440 | tf_op jit(solution)/shard_map/ppermute | solution.py:330
  21.6 1.4 %collective-permute-start.5 = (bf16[64,2048]{1,0:T(8,128)(2,1)S(1)}, bf16[64,2048]{1,0:T(8,128)(2,1)S(1)}, u32[]{:S(2)}, u32[]{:S(2)}) collective-permute-start(bf16[64,2048]{1,0:T(8,128)(2,1)S(1)} %shard_map.142), channel_id=1, source_target_pairs={{0,16},{4,20},{8,24},{12,28},{16,0},{20,4},{24,8},{28,12},{1,17},{... | collective-permute-start | bytes 786440 | tf_op jit(solution)/shard_map/ppermute | solution.py:330
  23.6 6.6 %collective-permute-done.6 = bf16[64,2048]{1,0:T(8,128)(2,1)S(1)} collective-permute-done((bf16[64,2048]{1,0:T(8,128)(2,1)S(1)}, bf16[64,2048]{1,0:T(8,128)(2,1)S(1)}, u32[]{:S(2)}, u32[]{:S(2)}) %collective-permute-start.6) | collective-permute-done | bytes 262176 | tf_op jit(solution)/shard_map/ppermute | solution.py:330
  30.2 5.2 %collective-permute-done.5 = bf16[64,2048]{1,0:T(8,128)(2,1)S(1)} collective-permute-done((bf16[64,2048]{1,0:T(8,128)(2,1)S(1)}, bf16[64,2048]{1,0:T(8,128)(2,1)S(1)}, u32[]{:S(2)}, u32[]{:S(2)}) %collective-permute-start.5) | collective-permute-done | bytes 262176 | tf_op jit(solution)/shard_map/ppermute | solution.py:330
  35.7 3.6 %collective-permute-start.10 = (f32[8,128]{1,0:T(8,128)S(1)}, f32[8,128]{1,0:T(8,128)S(1)}, u32[]{:S(2)}, u32[]{:S(2)}) collective-permute-start(f32[8,128]{1,0:T(8,128)S(1)} %get-tuple-element.30.refs_0_.rank), channel_id=1, source_target_pairs={{0,3},{1,2},{2,1},{3,0},{4,7},{5,6},{6,5},{7,4},{8,11},{9,10},{10,... | collective-permute-start | bytes 12296 | tf_op jit(solution)/shard_map/ppermute | solution.py:330
  41.1 2.7 %collective-permute-done.9.refs_2_ = f32[8,128]{1,0:T(8,128)S(1)} collective-permute-done((f32[8,128]{1,0:T(8,128)S(1)}, f32[8,128]{1,0:T(8,128)S(1)}, u32[]{:S(2)}, u32[]{:S(2)}) %collective-permute-start.9) | collective-permute-done | bytes 4128 | tf_op jit(solution)/shard_map/ppermute | solution.py:330
  43.8 1.1 %shard_map.145 = (f32[128,512]{1,0:T(8,128)S(1)}, bf16[128,512]{1,0:T(8,128)(2,1)S(1)}, bf16[128,512]{1,0:T(8,128)(2,1)S(1)}, bf16[128,512]{1,0:T(8,128)(2,1)S(1...) custom-call(bf16[256,2048]{1,0:T(8,128)(2,1)S(1)} %collective-permut, ...), custom_call_target="tpu_custom_call" | custom-call | flops 536870912 | bytes 4194304 | tf_op jit(solution)/shard_map/pallas_call | solution.py:413
  45.0 2.1 %collective-permute-start.12 = (bf16[128,512]{1,0:T(8,128)(2,1)S(1)}, bf16[128,512]{1,0:T(8,128)(2,1)S(1)}, u32[]{:S(2)}, u32[]{:S(2)}) collective-permute-start(bf16[128,512]{1,0:T(8,128)(2,1)S(1)} %get-tuple-element.37), channel_id=1, source_target_pairs={{0,2},{1,3},{2,0},{3,1},{4,6},{5,7},{6,4},{7,5},{8,10},{9,11},{10,... | collective-permute-start | bytes 393224 | tf_op jit(solution)/shard_map/ppermute | solution.py:330
  47.1 2.3 %collective-permute-start.13 = (bf16[128,512]{1,0:T(8,128)(2,1)S(1)}, bf16[128,512]{1,0:T(8,128)(2,1)S(1)}, u32[]{:S(2)}, u32[]{:S(2)}) collective-permute-start(bf16[128,512]{1,0:T(8,128)(2,1)S(1)} %get-tuple-element.38), channel_id=1, source_target_pairs={{0,3},{1,2},{2,1},{3,0},{4,7},{5,6},{6,5},{7,4},{8,11},{9,10},{10,... | collective-permute-start | bytes 393224 | tf_op jit(solution)/shard_map/ppermute | solution.py:330
  49.4 1.7 %collective-permute-done.11.refs_1_ = bf16[128,512]{1,0:T(8,128)(2,1)S(1)} collective-permute-done((bf16[128,512]{1,0:T(8,128)(2,1)S(1)}, bf16[128,512]{1,0:T(8,128)(2,1)S(1)}, u32[]{:S(2)}, u32[]{:S(2)}) %collective-permute-start.11) | collective-permute-done | bytes 131104 | tf_op jit(solution)/shard_map/ppermute | solution.py:330
  51.0 6.6 %collective-permute-done.12.refs_2_ = bf16[128,512]{1,0:T(8,128)(2,1)S(1)} collective-permute-done((bf16[128,512]{1,0:T(8,128)(2,1)S(1)}, bf16[128,512]{1,0:T(8,128)(2,1)S(1)}, u32[]{:S(2)}, u32[]{:S(2)}) %collective-permute-start.12) | collective-permute-done | bytes 131104 | tf_op jit(solution)/shard_map/ppermute | solution.py:330
  57.6 1.9 %shard_map.147 = bf16[64,3200]{1,0:T(8,128)(2,1)S(1)} custom-call(bf16[128,512]{1,0:T(8,128)(2,1)S(1)} %get-tuple-element.35.refs_0_, bf16[128,512]{1,0:T(8,128)(2,1)S(1)} %collective-permute-done.11.refs_1_, bf16[128,512]{1,0:T(8,128)(2,1)S(1)} %collective-permute-done.12.refs_2_, bf16[128,512]{1,0:T(8,128)(2,1)S(1)} %collective-permute-done.13.refs_3_, ...), custom_call_target="tpu_custom_call" | custom-call | flops 201326592 | bytes 4194304 | tf_op jit(solution)/shard_map/pallas_call | solution.py:434
  59.6 1.9 %shard_map.146.mine = f32[64,3200]{1,0:T(8,128)S(1)} custom-call(bf16[128,512]{1,0:T(8,128)(2,1)S(1)} %get-tuple-element.35.refs_0_, bf16[128,512]{1,0:T(8,128)(2,1)S(1)} %collective-permute-done.11.refs_1_, bf16[128,512]{1,0:T(8,128)(2,1)S(1)} %collective-permute-done.12.refs_2_, bf16[128,512]{1,0:T(8,128)(2,1)S(1)} %collective-permute-done.13.refs_3_, ...), custom_call_target="tpu_custom_call" | custom-call | flops 201326592 | bytes 4194304 | tf_op jit(solution)/shard_map/pallas_call | solution.py:434
  61.6 1.5 %collective-permute-start.18 = (bf16[16,3200]{1,0:T(8,128)(2,1)S(1)}, bf16[16,3200]{1,0:T(8,128)(2,1)S(1)}, u32[]{:S(2)}, u32[]{:S(2)}) collective-permute-start(bf16[16,3200]{1,0:T(8,128)(2,1)S(1)} %get-tuple-element.45), channel_id=1, source_target_pairs={{0,8},{4,12},{8,0},{12,4},{16,24},{20,28},{24,16},{28,20},{1,9},{5... | collective-permute-start | bytes 307208 | tf_op jit(solution)/shard_map/ppermute | solution.py:330
  63.9 1.3 %collective-permute-start.20 = (bf16[16,3200]{1,0:T(8,128)(2,1)S(1)}, bf16[16,3200]{1,0:T(8,128)(2,1)S(1)}, u32[]{:S(2)}, u32[]{:S(2)}) collective-permute-start(bf16[16,3200]{1,0:T(8,128)(2,1)S(1)} %get-tuple-element.47), channel_id=1, source_target_pairs={{0,24},{4,28},{8,16},{12,20},{16,8},{20,12},{24,0},{28,4},{1,25},{... | collective-permute-start | bytes 307208 | tf_op jit(solution)/shard_map/ppermute | solution.py:330
  65.2 1.8 %collective-permute-done.18.refs_1_ = bf16[16,3200]{1,0:T(8,128)(2,1)S(1)} collective-permute-done((bf16[16,3200]{1,0:T(8,128)(2,1)S(1)}, bf16[16,3200]{1,0:T(8,128)(2,1)S(1)}, u32[]{:S(2)}, u32[]{:S(2)}) %collective-permute-start.18) | collective-permute-done | bytes 102432 | tf_op jit(solution)/shard_map/ppermute | solution.py:330
  66.9 3.4 %collective-permute-done.19.refs_2_ = bf16[16,3200]{1,0:T(8,128)(2,1)S(1)} collective-permute-done((bf16[16,3200]{1,0:T(8,128)(2,1)S(1)}, bf16[16,3200]{1,0:T(8,128)(2,1)S(1)}, u32[]{:S(2)}, u32[]{:S(2)}) %collective-permute-start.19) | collective-permute-done | bytes 102432 | tf_op jit(solution)/shard_map/ppermute | solution.py:330
  70.4 1.5 %collective-permute-start.23 = (bf16[16,1536]{1,0:T(8,128)(2,1)S(1)}, bf16[16,1536]{1,0:T(8,128)(2,1)S(1)}, u32[]{:S(2)}, u32[]{:S(2)}) collective-permute-start(bf16[16,1536]{1,0:T(8,128)(2,1)S(1)} %shard_map.149), channel_id=1, source_target_pairs={{0,24},{4,28},{8,16},{12,20},{16,8},{20,12},{24,0},{28,4},{1,25},{... | collective-permute-start | bytes 147464 | tf_op jit(solution)/shard_map/ppermute | solution.py:330
  72.5 1.5 %collective-permute-start.21 = (bf16[16,1536]{1,0:T(8,128)(2,1)S(1)}, bf16[16,1536]{1,0:T(8,128)(2,1)S(1)}, u32[]{:S(2)}, u32[]{:S(2)}) collective-permute-start(bf16[16,1536]{1,0:T(8,128)(2,1)S(1)} %shard_map.149), channel_id=1, source_target_pairs={{0,8},{4,12},{8,0},{12,4},{16,24},{20,28},{24,16},{28,20},{1,9},{5... | collective-permute-start | bytes 147464 | tf_op jit(solution)/shard_map/ppermute | solution.py:330
  74.0 2.1 %collective-permute-done.23 = bf16[16,1536]{1,0:T(8,128)(2,1)S(1)} collective-permute-done((bf16[16,1536]{1,0:T(8,128)(2,1)S(1)}, bf16[16,1536]{1,0:T(8,128)(2,1)S(1)}, u32[]{:S(2)}, u32[]{:S(2)}) %collective-permute-start.23) | collective-permute-done | bytes 49184 | tf_op jit(solution)/shard_map/ppermute | solution.py:330
  76.7 2.0 %collective-permute-start.14 = (bf16[128,512]{1,0:T(8,128)(2,1)S(1)}, bf16[128,512]{1,0:T(8,128)(2,1)S(1)}, u32[]{:S(2)}, u32[]{:S(2)}) collective-permute-start(bf16[128,512]{1,0:T(8,128)(2,1)S(1)} %get-tuple-element.39), channel_id=1, source_target_pairs={{0,1},{1,0},{2,3},{3,2},{4,5},{5,4},{6,7},{7,6},{8,9},{9,8},{10,11... | collective-permute-start | bytes 393224 | tf_op jit(solution)/shard_map/ppermute | solution.py:330
  78.7 1.3 %collective-permute-start.15 = (bf16[128,512]{1,0:T(8,128)(2,1)S(1)}, bf16[128,512]{1,0:T(8,128)(2,1)S(1)}, u32[]{:S(2)}, u32[]{:S(2)}) collective-permute-start(bf16[128,512]{1,0:T(8,128)(2,1)S(1)} %get-tuple-element.40), channel_id=1, source_target_pairs={{0,2},{1,3},{2,0},{3,1},{4,6},{5,7},{6,4},{7,5},{8,10},{9,11},{10,... | collective-permute-start | bytes 393224 | tf_op jit(solution)/shard_map/ppermute | solution.py:330
  80.0 1.4 %collective-permute-start.16 = (bf16[128,512]{1,0:T(8,128)(2,1)S(1)}, bf16[128,512]{1,0:T(8,128)(2,1)S(1)}, u32[]{:S(2)}, u32[]{:S(2)}) collective-permute-start(bf16[128,512]{1,0:T(8,128)(2,1)S(1)} %get-tuple-element.41), channel_id=1, source_target_pairs={{0,3},{1,2},{2,1},{3,0},{4,7},{5,6},{6,5},{7,4},{8,11},{9,10},{10,... | collective-permute-start | bytes 393224 | tf_op jit(solution)/shard_map/ppermute | solution.py:330
  83.4 2.2 %collective-permute-start.26 = (bf16[32,512]{1,0:T(8,128)(2,1)S(1)}, bf16[32,512]{1,0:T(8,128)(2,1)S(1)}, u32[]{:S(2)}, u32[]{:S(2)}) collective-permute-start(bf16[32,512]{1,0:T(8,128)(2,1)S(1)} %get-tuple-element.50), channel_id=1, source_target_pairs={{0,2},{1,3},{2,0},{3,1},{4,6},{5,7},{6,4},{7,5},{8,10},{9,11},{10,... | collective-permute-start | bytes 98312 | tf_op jit(solution)/shard_map/ppermute | solution.py:330
  85.5 1.4 %collective-permute-start.27 = (bf16[32,512]{1,0:T(8,128)(2,1)S(1)}, bf16[32,512]{1,0:T(8,128)(2,1)S(1)}, u32[]{:S(2)}, u32[]{:S(2)}) collective-permute-start(bf16[32,512]{1,0:T(8,128)(2,1)S(1)} %get-tuple-element.51), channel_id=1, source_target_pairs={{0,3},{1,2},{2,1},{3,0},{4,7},{5,6},{6,5},{7,4},{8,11},{9,10},{10,... | collective-permute-start | bytes 98312 | tf_op jit(solution)/shard_map/ppermute | solution.py:330
  86.9 6.1 %collective-permute-done.15 = bf16[128,512]{1,0:T(8,128)(2,1)S(1)} collective-permute-done((bf16[128,512]{1,0:T(8,128)(2,1)S(1)}, bf16[128,512]{1,0:T(8,128)(2,1)S(1)}, u32[]{:S(2)}, u32[]{:S(2)}) %collective-permute-start.15) | collective-permute-done | bytes 131104 | tf_op jit(solution)/shard_map/ppermute | solution.py:330
  93.8 2.4 %collective-permute-done.26.refs_2_ = bf16[32,512]{1,0:T(8,128)(2,1)S(1)} collective-permute-done((bf16[32,512]{1,0:T(8,128)(2,1)S(1)}, bf16[32,512]{1,0:T(8,128)(2,1)S(1)}, u32[]{:S(2)}, u32[]{:S(2)}) %collective-permute-start.26) | collective-permute-done | bytes 32800 | tf_op jit(solution)/shard_map/ppermute | solution.py:330
  (67 shorter events, 14.9 us)
Async XLA Ops:
  4.2 7.1 %collective-permute-start.2 = (bf16[192,256]{1,0:T(8,128)(2,1)S(1)}, bf16[192,256]{1,0:T(8,128)(2,1)S(1)}, u32[]{:S(2)}, u32[]{:S(2)}) collective-permute-start(bf16[192,256]{1,0:T(8,128)(2,1)S(1)} %shard_map.140), channel_id=1, source_target_pairs={{0,24},{4,28},{8,16},{12,20},{16,8},{20,12},{24,0},{28,4},{1,25},{... | collective-permute-start | bytes 294920 | tf_op jit(solution)/shard_map/ppermute | solution.py:330
  8.2 4.9 %collective-permute-start.1 = (bf16[192,256]{1,0:T(8,128)(2,1)S(1)}, bf16[192,256]{1,0:T(8,128)(2,1)S(1)}, u32[]{:S(2)}, u32[]{:S(2)}) collective-permute-start(bf16[192,256]{1,0:T(8,128)(2,1)S(1)} %shard_map.140), channel_id=1, source_target_pairs={{0,16},{4,20},{8,24},{12,28},{16,0},{20,4},{24,8},{28,12},{1,17},{... | collective-permute-start | bytes 294920 | tf_op jit(solution)/shard_map/ppermute | solution.py:330
  8.7 4.7 %collective-permute-start = (bf16[192,256]{1,0:T(8,128)(2,1)S(1)}, bf16[192,256]{1,0:T(8,128)(2,1)S(1)}, u32[]{:S(2)}, u32[]{:S(2)}) collective-permute-start(bf16[192,256]{1,0:T(8,128)(2,1)S(1)} %shard_map.140), channel_id=1, source_target_pairs={{0,8},{4,12},{8,0},{12,4},{16,24},{20,28},{24,16},{28,20},{1,9},{5... | collective-permute-start | bytes 294920 | tf_op jit(solution)/shard_map/ppermute | solution.py:330
  13.4 4.1 %collective-permute-start.3 = (bf16[768,256]{1,0:T(8,128)(2,1)S(1)}, bf16[768,256]{1,0:T(8,128)(2,1)S(1)}, u32[]{:S(2)}, u32[]{:S(2)}) collective-permute-start(bf16[768,256]{1,0:T(8,128)(2,1)S(1)} %pad_maximum_fusion.1.kv), channel_id=1, source_target_pairs={{0,4},{4,0},{8,12},{12,8},{16,20},{20,16},{24,28},{28,24},{1,5},{5... | collective-permute-start | bytes 1179656 | tf_op jit(solution)/shard_map/ppermute | solution.py:330
  17.5 18.1 %copy-start.10 = (s32[128,8]{0,1:T(8,128)S(1)}, s32[128,8]{0,1:T(8,128)}, u32[]{:S(2)}) copy-start(s32[128,8]{0,1:T(8,128)} %param.22) | copy-start | bytes 12292
  17.5 18.0 %copy-start.11 = (f32[128,8]{0,1:T(8,128)S(1)}, f32[128,8]{0,1:T(8,128)}, u32[]{:S(2)}) copy-start(f32[128,8]{0,1:T(8,128)} %param.23) | copy-start | bytes 12292
  17.5 22.6 %copy-start.2 = (bf16[2048,512]{1,0:T(8,128)(2,1)S(1)}, bf16[2048,512]{1,0:T(8,128)(2,1)}, u32[]{:S(2)}) copy-start(bf16[2048,512]{1,0:T(8,128)(2,1)} %weight.5) | copy-start | bytes 6291460
  20.1 10.1 %collective-permute-start.6 = (bf16[64,2048]{1,0:T(8,128)(2,1)S(1)}, bf16[64,2048]{1,0:T(8,128)(2,1)S(1)}, u32[]{:S(2)}, u32[]{:S(2)}) collective-permute-start(bf16[64,2048]{1,0:T(8,128)(2,1)S(1)} %shard_map.142), channel_id=1, source_target_pairs={{0,24},{4,28},{8,16},{12,20},{16,8},{20,12},{24,0},{28,4},{1,25},{... | collective-permute-start | bytes 786440 | tf_op jit(solution)/shard_map/ppermute | solution.py:330
  21.6 13.7 %collective-permute-start.5 = (bf16[64,2048]{1,0:T(8,128)(2,1)S(1)}, bf16[64,2048]{1,0:T(8,128)(2,1)S(1)}, u32[]{:S(2)}, u32[]{:S(2)}) collective-permute-start(bf16[64,2048]{1,0:T(8,128)(2,1)S(1)} %shard_map.142), channel_id=1, source_target_pairs={{0,16},{4,20},{8,24},{12,28},{16,0},{20,4},{24,8},{28,12},{1,17},{... | collective-permute-start | bytes 786440 | tf_op jit(solution)/shard_map/ppermute | solution.py:330
  23.1 12.3 %collective-permute-start.4 = (bf16[64,2048]{1,0:T(8,128)(2,1)S(1)}, bf16[64,2048]{1,0:T(8,128)(2,1)S(1)}, u32[]{:S(2)}, u32[]{:S(2)}) collective-permute-start(bf16[64,2048]{1,0:T(8,128)(2,1)S(1)} %shard_map.142), channel_id=1, source_target_pairs={{0,8},{4,12},{8,0},{12,4},{16,24},{20,28},{24,16},{28,20},{1,9},{5... | collective-permute-start | bytes 786440 | tf_op jit(solution)/shard_map/ppermute | solution.py:330
  35.5 8.4 %collective-permute-start.7 = (bf16[256,2048]{1,0:T(8,128)(2,1)S(1)}, bf16[256,2048]{1,0:T(8,128)(2,1)S(1)}, u32[]{:S(2)}, u32[]{:S(2)}) collective-permute-start(bf16[256,2048]{1,0:T(8,128)(2,1)S(1)} %pad_maximum_fusion.heads_out), channel_id=1, source_target_pairs={{0,4},{4,0},{8,12},{12,8},{16,20},{20,16},{24,28},{28,24},{1,5},{5... | collective-permute-start | bytes 3145736 | tf_op jit(solution)/shard_map/ppermute | solution.py:330
  35.7 5.4 %collective-permute-start.10 = (f32[8,128]{1,0:T(8,128)S(1)}, f32[8,128]{1,0:T(8,128)S(1)}, u32[]{:S(2)}, u32[]{:S(2)}) collective-permute-start(f32[8,128]{1,0:T(8,128)S(1)} %get-tuple-element.30.refs_0_.rank), channel_id=1, source_target_pairs={{0,3},{1,2},{2,1},{3,0},{4,7},{5,6},{6,5},{7,4},{8,11},{9,10},{10,... | collective-permute-start | bytes 12296 | tf_op jit(solution)/shard_map/ppermute | solution.py:330
  39.3 4.5 %collective-permute-start.9 = (f32[8,128]{1,0:T(8,128)S(1)}, f32[8,128]{1,0:T(8,128)S(1)}, u32[]{:S(2)}, u32[]{:S(2)}) collective-permute-start(f32[8,128]{1,0:T(8,128)S(1)} %get-tuple-element.30.refs_0_.rank), channel_id=1, source_target_pairs={{0,2},{1,3},{2,0},{3,1},{4,6},{5,7},{6,4},{7,5},{8,10},{9,11},{10,... | collective-permute-start | bytes 12296 | tf_op jit(solution)/shard_map/ppermute | solution.py:330
  39.3 4.5 %collective-permute-start.8 = (f32[8,128]{1,0:T(8,128)S(1)}, f32[8,128]{1,0:T(8,128)S(1)}, u32[]{:S(2)}, u32[]{:S(2)}) collective-permute-start(f32[8,128]{1,0:T(8,128)S(1)} %get-tuple-element.30.refs_0_.rank), channel_id=1, source_target_pairs={{0,1},{1,0},{2,3},{3,2},{4,5},{5,4},{6,7},{7,6},{8,9},{9,8},{10,11... | collective-permute-start | bytes 12296 | tf_op jit(solution)/shard_map/ppermute | solution.py:330
  44.9 6.1 %collective-permute-start.11 = (bf16[128,512]{1,0:T(8,128)(2,1)S(1)}, bf16[128,512]{1,0:T(8,128)(2,1)S(1)}, u32[]{:S(2)}, u32[]{:S(2)}) collective-permute-start(bf16[128,512]{1,0:T(8,128)(2,1)S(1)} %get-tuple-element.36), channel_id=1, source_target_pairs={{0,1},{1,0},{2,3},{3,2},{4,5},{5,4},{6,7},{7,6},{8,9},{9,8},{10,11... | collective-permute-start | bytes 393224 | tf_op jit(solution)/shard_map/ppermute | solution.py:330
  45.0 12.6 %collective-permute-start.12 = (bf16[128,512]{1,0:T(8,128)(2,1)S(1)}, bf16[128,512]{1,0:T(8,128)(2,1)S(1)}, u32[]{:S(2)}, u32[]{:S(2)}) collective-permute-start(bf16[128,512]{1,0:T(8,128)(2,1)S(1)} %get-tuple-element.37), channel_id=1, source_target_pairs={{0,2},{1,3},{2,0},{3,1},{4,6},{5,7},{6,4},{7,5},{8,10},{9,11},{10,... | collective-permute-start | bytes 393224 | tf_op jit(solution)/shard_map/ppermute | solution.py:330
  47.1 10.5 %collective-permute-start.13 = (bf16[128,512]{1,0:T(8,128)(2,1)S(1)}, bf16[128,512]{1,0:T(8,128)(2,1)S(1)}, u32[]{:S(2)}, u32[]{:S(2)}) collective-permute-start(bf16[128,512]{1,0:T(8,128)(2,1)S(1)} %get-tuple-element.38), channel_id=1, source_target_pairs={{0,3},{1,2},{2,1},{3,0},{4,7},{5,6},{6,5},{7,4},{8,11},{9,10},{10,... | collective-permute-start | bytes 393224 | tf_op jit(solution)/shard_map/ppermute | solution.py:330
  59.5 2.0 %collective-permute-start.17 = (bf16[64,3200]{1,0:T(8,128)(2,1)S(1)}, bf16[64,3200]{1,0:T(8,128)(2,1)S(1)}, u32[]{:S(2)}, u32[]{:S(2)}) collective-permute-start(bf16[64,3200]{1,0:T(8,128)(2,1)S(1)} %shard_map.147), channel_id=1, source_target_pairs={{0,4},{4,0},{8,12},{12,8},{16,20},{20,16},{24,28},{28,24},{1,5},{5... | collective-permute-start | bytes 1228808 | tf_op jit(solution)/shard_map/ppermute | solution.py:330
  59.6 21.8 %copy-start.1 = (bf16[2,1536,512]{2,1,0:T(8,128)(2,1)S(1)}, bf16[2,1536,512]{2,1,0:T(8,128)(2,1)}, u32[]{:S(2)}) copy-start(bf16[2,1536,512]{2,1,0:T(8,128)(2,1)} %weight.7) | copy-start | bytes 9437188
  61.6 5.3 %collective-permute-start.18 = (bf16[16,3200]{1,0:T(8,128)(2,1)S(1)}, bf16[16,3200]{1,0:T(8,128)(2,1)S(1)}, u32[]{:S(2)}, u32[]{:S(2)}) collective-permute-start(bf16[16,3200]{1,0:T(8,128)(2,1)S(1)} %get-tuple-element.45), channel_id=1, source_target_pairs={{0,8},{4,12},{8,0},{12,4},{16,24},{20,28},{24,16},{28,20},{1,9},{5... | collective-permute-start | bytes 307208 | tf_op jit(solution)/shard_map/ppermute | solution.py:330
  63.1 7.2 %collective-permute-start.19 = (bf16[16,3200]{1,0:T(8,128)(2,1)S(1)}, bf16[16,3200]{1,0:T(8,128)(2,1)S(1)}, u32[]{:S(2)}, u32[]{:S(2)}) collective-permute-start(bf16[16,3200]{1,0:T(8,128)(2,1)S(1)} %get-tuple-element.46), channel_id=1, source_target_pairs={{0,16},{4,20},{8,24},{12,28},{16,0},{20,4},{24,8},{28,12},{1,17},{... | collective-permute-start | bytes 307208 | tf_op jit(solution)/shard_map/ppermute | solution.py:330
  63.9 6.4 %collective-permute-start.20 = (bf16[16,3200]{1,0:T(8,128)(2,1)S(1)}, bf16[16,3200]{1,0:T(8,128)(2,1)S(1)}, u32[]{:S(2)}, u32[]{:S(2)}) collective-permute-start(bf16[16,3200]{1,0:T(8,128)(2,1)S(1)} %get-tuple-element.47), channel_id=1, source_target_pairs={{0,24},{4,28},{8,16},{12,20},{16,8},{20,12},{24,0},{28,4},{1,25},{... | collective-permute-start | bytes 307208 | tf_op jit(solution)/shard_map/ppermute | solution.py:330
  70.4 5.6 %collective-permute-start.23 = (bf16[16,1536]{1,0:T(8,128)(2,1)S(1)}, bf16[16,1536]{1,0:T(8,128)(2,1)S(1)}, u32[]{:S(2)}, u32[]{:S(2)}) collective-permute-start(bf16[16,1536]{1,0:T(8,128)(2,1)S(1)} %shard_map.149), channel_id=1, source_target_pairs={{0,24},{4,28},{8,16},{12,20},{16,8},{20,12},{24,0},{28,4},{1,25},{... | collective-permute-start | bytes 147464 | tf_op jit(solution)/shard_map/ppermute | solution.py:330
  71.9 4.4 %collective-permute-start.22 = (bf16[16,1536]{1,0:T(8,128)(2,1)S(1)}, bf16[16,1536]{1,0:T(8,128)(2,1)S(1)}, u32[]{:S(2)}, u32[]{:S(2)}) collective-permute-start(bf16[16,1536]{1,0:T(8,128)(2,1)S(1)} %shard_map.149), channel_id=1, source_target_pairs={{0,16},{4,20},{8,24},{12,28},{16,0},{20,4},{24,8},{28,12},{1,17},{... | collective-permute-start | bytes 147464 | tf_op jit(solution)/shard_map/ppermute | solution.py:330
  72.5 4.1 %collective-permute-start.21 = (bf16[16,1536]{1,0:T(8,128)(2,1)S(1)}, bf16[16,1536]{1,0:T(8,128)(2,1)S(1)}, u32[]{:S(2)}, u32[]{:S(2)}) collective-permute-start(bf16[16,1536]{1,0:T(8,128)(2,1)S(1)} %shard_map.149), channel_id=1, source_target_pairs={{0,8},{4,12},{8,0},{12,4},{16,24},{20,28},{24,16},{28,20},{1,9},{5... | collective-permute-start | bytes 147464 | tf_op jit(solution)/shard_map/ppermute | solution.py:330
  76.6 5.3 %collective-permute-start.24 = (bf16[64,1536]{1,0:T(8,128)(2,1)S(1)}, bf16[64,1536]{1,0:T(8,128)(2,1)S(1)}, u32[]{:S(2)}, u32[]{:S(2)}) collective-permute-start(bf16[64,1536]{1,0:T(8,128)(2,1)S(1)} %pad_maximum_fusion.2.active), channel_id=1, source_target_pairs={{0,4},{4,0},{8,12},{12,8},{16,20},{20,16},{24,28},{28,24},{1,5},{5... | collective-permute-start | bytes 589832 | tf_op jit(solution)/shard_map/ppermute | solution.py:330
  76.7 8.8 %collective-permute-start.14 = (bf16[128,512]{1,0:T(8,128)(2,1)S(1)}, bf16[128,512]{1,0:T(8,128)(2,1)S(1)}, u32[]{:S(2)}, u32[]{:S(2)}) collective-permute-start(bf16[128,512]{1,0:T(8,128)(2,1)S(1)} %get-tuple-element.39), channel_id=1, source_target_pairs={{0,1},{1,0},{2,3},{3,2},{4,5},{5,4},{6,7},{7,6},{8,9},{9,8},{10,11... | collective-permute-start | bytes 393224 | tf_op jit(solution)/shard_map/ppermute | solution.py:330
  78.7 14.3 %collective-permute-start.15 = (bf16[128,512]{1,0:T(8,128)(2,1)S(1)}, bf16[128,512]{1,0:T(8,128)(2,1)S(1)}, u32[]{:S(2)}, u32[]{:S(2)}) collective-permute-start(bf16[128,512]{1,0:T(8,128)(2,1)S(1)} %get-tuple-element.40), channel_id=1, source_target_pairs={{0,2},{1,3},{2,0},{3,1},{4,6},{5,7},{6,4},{7,5},{8,10},{9,11},{10,... | collective-permute-start | bytes 393224 | tf_op jit(solution)/shard_map/ppermute | solution.py:330
  80.0 13.1 %collective-permute-start.16 = (bf16[128,512]{1,0:T(8,128)(2,1)S(1)}, bf16[128,512]{1,0:T(8,128)(2,1)S(1)}, u32[]{:S(2)}, u32[]{:S(2)}) collective-permute-start(bf16[128,512]{1,0:T(8,128)(2,1)S(1)} %get-tuple-element.41), channel_id=1, source_target_pairs={{0,3},{1,2},{2,1},{3,0},{4,7},{5,6},{6,5},{7,4},{8,11},{9,10},{10,... | collective-permute-start | bytes 393224 | tf_op jit(solution)/shard_map/ppermute | solution.py:330
  82.4 11.3 %collective-permute-start.25 = (bf16[32,512]{1,0:T(8,128)(2,1)S(1)}, bf16[32,512]{1,0:T(8,128)(2,1)S(1)}, u32[]{:S(2)}, u32[]{:S(2)}) collective-permute-start(bf16[32,512]{1,0:T(8,128)(2,1)S(1)} %get-tuple-element.49), channel_id=1, source_target_pairs={{0,1},{1,0},{2,3},{3,2},{4,5},{5,4},{6,7},{7,6},{8,9},{9,8},{10,11... | collective-permute-start | bytes 98312 | tf_op jit(solution)/shard_map/ppermute | solution.py:330
  83.4 12.8 %collective-permute-start.26 = (bf16[32,512]{1,0:T(8,128)(2,1)S(1)}, bf16[32,512]{1,0:T(8,128)(2,1)S(1)}, u32[]{:S(2)}, u32[]{:S(2)}) collective-permute-start(bf16[32,512]{1,0:T(8,128)(2,1)S(1)} %get-tuple-element.50), channel_id=1, source_target_pairs={{0,2},{1,3},{2,0},{3,1},{4,6},{5,7},{6,4},{7,5},{8,10},{9,11},{10,... | collective-permute-start | bytes 98312 | tf_op jit(solution)/shard_map/ppermute | solution.py:330
  85.5 10.6 %collective-permute-start.27 = (bf16[32,512]{1,0:T(8,128)(2,1)S(1)}, bf16[32,512]{1,0:T(8,128)(2,1)S(1)}, u32[]{:S(2)}, u32[]{:S(2)}) collective-permute-start(bf16[32,512]{1,0:T(8,128)(2,1)S(1)} %get-tuple-element.51), channel_id=1, source_target_pairs={{0,3},{1,2},{2,1},{3,0},{4,7},{5,6},{6,5},{7,4},{8,11},{9,10},{10,... | collective-permute-start | bytes 98312 | tf_op jit(solution)/shard_map/ppermute | solution.py:330
  (9 other events, 47.8 us)

commit v2 on v1

--- a/solution.py
+++ b/solution.py
@@ -19,10 +19,11 @@
 bf16 = jnp.bfloat16
 f32 = jnp.float32
 MIB = 1024 * 1024
+ALL_VMEM = 63.5
 
 VMEM = pl.BlockSpec(memory_space=pltpu.VMEM)
 SMEM = pl.BlockSpec(memory_space=pltpu.SMEM)
-ANY = pl.BlockSpec(memory_space=pl.ANY)
+HBM = pl.BlockSpec(memory_space=pltpu.HBM)
 
 
 def call(kernel, out_shape, in_specs, scratch=(), vmem=16, flops=0, nbytes=0):
@@ -33,7 +34,7 @@
         in_specs=in_specs,
         out_specs=[VMEM] * len(out_shape) if many else VMEM,
         scratch_shapes=list(scratch),
-        compiler_params=pltpu.CompilerParams(vmem_limit_bytes=vmem * MIB),
+        compiler_params=pltpu.CompilerParams(vmem_limit_bytes=int(vmem * MIB)),
         cost_estimate=pl.CostEstimate(flops=flops, bytes_accessed=nbytes, transcendentals=0),
     )
 
@@ -73,23 +74,6 @@
         copy.wait()
 
 
-def rank_kernel(routes, gates, rank, gate):
-    flight, tokens = rank.shape
-    expert = lax.broadcasted_iota(jnp.int32, (flight, tokens), 0)
-    member = jnp.zeros((flight, tokens), f32)
-    weight = jnp.zeros((flight, tokens), f32)
-    for k in range(routes.shape[0]):
-        hit = routes[k : k + 1, :] == expert
-        member = jnp.where(hit, 1.0, member)
-        weight = weight + jnp.where(hit, gates[k : k + 1, :], 0.0)
-    before = lax.broadcasted_iota(jnp.int32, (tokens, tokens), 0) < lax.broadcasted_iota(
-        jnp.int32, (tokens, tokens), 1
-    )
-    count = dot(member.astype(bf16), jnp.where(before, 1.0, 0.0).astype(bf16))
-    rank[...] = jnp.where(member > 0.5, count, -1.0)
-    gate[...] = weight
-
-
 def segment_of(position, seg_starts):
     passed = jnp.full(position.shape, -1, jnp.int32)
     for n in range(seg_starts.shape[0]):
@@ -97,7 +81,7 @@
     return passed
 
 
-def visible(seg_starts, other, span, cache, pieces):
+def mask_bias(seg_starts, other, span, cache, pieces):
     ctx = lax.axis_index("ctx")
     cache_total = cache * lax.axis_size("ctx")
     piece_rows = cache + span
@@ -113,48 +97,91 @@
     query_pos = cache_total + ctx * span + lax.broadcasted_iota(jnp.int32, (span, 1), 0)
     query_seg = segment_of(query_pos, seg_starts)
     last = seg_starts.shape[0] - 1
-    return (key_pos <= query_pos) & (
+    seen = (key_pos <= query_pos) & (
         (key_seg == query_seg) | (key_seg == 0) | (query_seg == last)
     )
+    return jnp.where(seen, 0.0, neg_large)
+
+
+def prepare(
+    n_exp, span, cache, seg_starts, q, routes, gates,
+    stacked, bias_same, bias_other, rank, high, low, q_vmem, routes_vmem, gates_vmem, sems,
+):
+    copies = [
+        pltpu.make_async_copy(src, dst, sems.at[n])
+        for n, (src, dst) in enumerate(
+            ((routes, routes_vmem), (gates, gates_vmem), (q, q_vmem))
+        )
+    ]
+    for copy in copies:
+        copy.start()
+    pieces = bias_same.shape[1] // (cache + span)
+    bias_same[...] = mask_bias(seg_starts, 0, span, cache, pieces)
+    bias_other[...] = mask_bias(seg_starts, 1, span, cache, pieces)
+    flight, tokens = rank.shape
+    local = flight // n_exp
+    expert = lax.broadcasted_iota(jnp.int32, (flight, tokens), 0)
+    member = jnp.zeros((flight, tokens), f32)
+    weight = jnp.zeros((flight, tokens), f32)
+    copies[0].wait()
+    copies[1].wait()
+    for k in range(routes.shape[0]):
+        hit = routes_vmem[k : k + 1, :] == expert
+        member = jnp.where(hit, 1.0, member)
+        weight = weight + jnp.where(hit, gates_vmem[k : k + 1, :], 0.0)
+    before = lax.broadcasted_iota(jnp.int32, (tokens, tokens), 0) < lax.broadcasted_iota(
+        jnp.int32, (tokens, tokens), 1
+    )
+    count = dot(member.astype(bf16), jnp.where(before, 1.0, 0.0).astype(bf16))
+    slots = jnp.where(member > 0.5, count, -1.0)
+    rank[...] = slots
+    exp = lax.axis_index("exp")
+    slot = lax.broadcasted_iota(jnp.int32, (CAP, tokens), 0).astype(f32)
+    tables = []
+    for e in range(flight):
+        tables.append(jnp.where(slots[e : e + 1, :] == slot, weight[e : e + 1, :], 0.0))
+    per = local * CAP
+    table = jnp.concatenate(tables, axis=0)
+    upper = table.astype(bf16)
+    lower = (table - upper.astype(f32)).astype(bf16)
+    for d in range(n_exp):
+        at = pl.ds(pl.multiple_of(jnp.bitwise_xor(exp, d) * per, per), per)
+        high[at, :] = upper[d * per : (d + 1) * per, :]
+        low[at, :] = lower[d * per : (d + 1) * per, :]
+    copies[2].wait()
+    for h in range(q.shape[1] // HEAD):
+        stacked[h * span : (h + 1) * span, :] = q_vmem[:, h * HEAD : (h + 1) * HEAD]
 
 
 GROUP = 4
 
 
-def attend(seg_starts, q, kv, other, span, cache, heads, finish):
-    pieces = kv.shape[0] // (cache + span)
-    seen = visible(seg_starts, other, span, cache, pieces)
+def attend(q, kv, bias, span, finish):
     scale = math.log2(math.e) / math.sqrt(HEAD)
-    group = min(GROUP, heads)
+    keys = kv.shape[0]
+    group = min(GROUP, q.shape[0] // span)
     rows = group * span
-    keys = kv[:, :HEAD]
-    values = kv[:, HEAD:]
-    for g in range(heads // group):
-        stacked = jnp.concatenate(
-            [q[:, (g * group + h) * HEAD : (g * group + h + 1) * HEAD] for h in range(group)], axis=0
-        )
-        scores = dot_t(stacked, keys)
-        scores = jnp.where(
-            seen[None], scores.reshape(group, span, kv.shape[0]), neg_large
-        ).reshape(rows, kv.shape[0])
+    for g in range(q.shape[0] // rows):
+        scores = dot_t(q[g * rows : (g + 1) * rows, :], kv[:, :HEAD])
+        scores = (scores.reshape(group, span, keys) + bias[...][None]).reshape(rows, keys)
         top = jnp.max(scores, axis=1, keepdims=True)
         probs = jnp.exp2((scores - top) * scale)
         total = jnp.sum(probs, axis=1, keepdims=True)
-        out = dot(probs.astype(bf16), values)
+        out = dot(probs.astype(bf16), kv[:, HEAD:])
         finish(g, rows, group, out, top, total)
 
 
-def attend_first(span, cache, heads, seg_starts, q, kv, o_out, m_out, l_out):
+def attend_first(span, q, kv, bias, o_out, m_out, l_out):
     def finish(g, rows, group, out, top, total):
         at = pl.ds(g * rows, rows)
         o_out[at, :] = out
         m_out[at, :] = jnp.broadcast_to(top, (rows, LANES))
         l_out[at, :] = jnp.broadcast_to(total, (rows, LANES))
 
-    attend(seg_starts, q, kv, 0, span, cache, heads, finish)
-
-
-def attend_second(span, cache, heads, seg_starts, q, kv, o_in, m_in, l_in, result):
+    attend(q, kv, bias, span, finish)
+
+
+def attend_second(span, q, kv, bias, o_in, m_in, l_in, result):
     scale = math.log2(math.e) / math.sqrt(HEAD)
 
     def finish(g, rows, group, out, top, total):
@@ -169,7 +196,7 @@
             col = (g * group + h) * HEAD
             result[:, col : col + HEAD] = merged[h * span : (h + 1) * span, :]
 
-    attend(seg_starts, q, kv, 1, span, cache, heads, finish)
+    attend(q, kv, bias, span, finish)
 
 
 def project_first(heads_out, weight, out):
@@ -221,20 +248,10 @@
 
 def expert_in_kernel(n_exp, other, *refs):
     arrived = refs[:n_exp]
-    gain, weight, out, held, sems = refs[n_exp:]
+    gain, weight, out = refs[n_exp:]
     expert = jnp.bitwise_xor(lax.axis_index("ctx") % 2, other)
     rows = out.shape[0]
     width = weight.shape[2]
-    chunks = held.shape[0]
-    step = width // chunks
-    copies = [
-        pltpu.make_async_copy(
-            weight.at[expert, :, pl.ds(n * step, step)], held.at[n], sems.at[n]
-        )
-        for n in range(chunks)
-    ]
-    for copy in copies:
-        copy.start()
     at = rows_at(expert * rows, rows, rows)
     total = arrived[0][at, :].astype(f32)
     for ref in arrived[1:]:
@@ -242,9 +259,9 @@
     mixed = total.astype(bf16).astype(f32)
     out[:, width:] = split_square(jnp.sum(mixed * mixed, axis=1, keepdims=True)).astype(out.dtype)
     scaled = (mixed * gain[...]).astype(bf16)
-    for n, copy in enumerate(copies):
-        copy.wait()
-        out[:, n * step : (n + 1) * step] = dot(scaled, held[n]).astype(out.dtype)
+    step = width // 6
+    for n in range(0, width, step):
+        out[:, n : n + step] = dot(scaled, weight[expert, :, n : n + step]).astype(out.dtype)
 
 
 def chip_sum(mine, theirs, *outs):
@@ -273,29 +290,17 @@
     out[...] = (gate / (1.0 + jnp.exp(-gate)) * up).astype(bf16)
 
 
-def load_expert(weight, other, held, sem):
-    expert = jnp.bitwise_xor(lax.axis_index("ctx") % 2, other)
-    return pltpu.make_async_copy(weight.at[expert], held, sem)
-
-
-def expert_out_first(active, weight, out, held, sem):
-    copy = load_expert(weight, 0, held, sem)
-    copy.start()
-    copy.wait()
-    out[...] = dot(active[...], held[...]).astype(bf16)
+def expert_out_first(active, weight, out):
+    out[...] = dot(active[...], weight[lax.axis_index("ctx") % 2]).astype(bf16)
 
 
 def expert_out_second(n_exp, active, weight, first, *refs):
-    outs = refs[:n_exp]
-    held, whole, sem = refs[n_exp:]
-    copy = load_expert(weight, 1, held, sem)
-    copy.start()
+    outs, whole = refs[:n_exp], refs[n_exp]
     ctx, exp = lax.axis_index("ctx"), lax.axis_index("exp")
     core, chip = ctx % 2, ctx // 2
     chips = lax.axis_size("ctx") // 2
     size = active.shape[0] // chips
-    copy.wait()
-    second = dot(active[...], held[...]).astype(bf16)
+    second = dot(active[...], weight[1 - core]).astype(bf16)
     for k in range(chips):
         at = rows_at(jnp.bitwise_xor(chip, k) * size, size, size)
         here = slice(k * size, (k + 1) * size)
@@ -307,22 +312,19 @@
             outs[k][j * CAP : (j + 1) * CAP, :] = whole[j, at, :]
 
 
-def combine(n_exp, rank, gate, *refs):
-    returned, out = refs[:n_exp], refs[n_exp]
-    exp = lax.axis_index("exp")
-    tokens = rank.shape[1]
-    local = rank.shape[0] // n_exp
-    slot = lax.broadcasted_iota(jnp.int32, (CAP, tokens), 0).astype(f32)
-    tables = []
-    for k in range(n_exp):
-        for j in range(local):
-            at = pl.ds(jnp.bitwise_xor(exp, k) * local + j, 1)
-            tables.append(jnp.where(rank[at, :] == slot, gate[at, :], 0.0))
-    table = jnp.concatenate(tables, axis=0).T
+def combine(n_exp, high, low, own, *refs):
+    parts, returned = refs[: n_exp - 1], refs[n_exp - 1 : -2]
+    mixed, out = refs[-2:]
+    total = own[...]
+    for part in parts:
+        total = total + part[...].astype(f32)
+    mixed[...] = total.astype(bf16)
     rows = jnp.concatenate([ref[...] for ref in returned], axis=0)
-    high = table.astype(bf16)
-    low = (table - high.astype(f32)).astype(bf16)
-    out[...] = (dot(high, rows) + dot(low, rows)).astype(bf16)
+    dims = (((0,), (0,)), ((), ()))
+    out[...] = (
+        lax.dot_general(high[...], rows, dims, preferred_element_type=f32)
+        + lax.dot_general(low[...], rows, dims, preferred_element_type=f32)
+    ).astype(bf16)
 
 
 def permute(x, axis, k):
@@ -365,37 +367,51 @@
     local_kv = call(
         functools.partial(pick_kv, heads),
         shape((cache + span, 2 * HEAD), bf16),
-        [ANY] * 4,
+        [HBM] * 4,
         [pltpu.SemaphoreType.DMA((4,))],
-        vmem=4,
+        vmem=ALL_VMEM,
     )(cache_keys, cache_values, block_keys, block_values)
-    kv_same = jnp.concatenate([local_kv] + over_chips(local_kv), axis=0)
+    kv_moved = over_chips(local_kv)
+
+    rows, keys = heads * span, chips * (cache + span)
+    stacked, bias_same, bias_other, rank, high, low = call(
+        functools.partial(prepare, n_exp, span, cache),
+        [shape((rows, HEAD), bf16)]
+        + [shape((span, keys), f32)] * 2
+        + [shape((flight, tokens), f32)]
+        + [shape((flight * CAP, tokens), bf16)] * 2,
+        [SMEM] + [HBM] * 3,
+        [
+            pltpu.VMEM(queries.shape, bf16),
+            pltpu.VMEM(routes.shape[::-1], jnp.int32),
+            pltpu.VMEM(routes.shape[::-1], f32),
+            pltpu.SemaphoreType.DMA((3,)),
+        ],
+        vmem=8,
+        nbytes=MIB,
+    )(seg_starts, queries, routes.T, gate_values.T)
+    moved = over_exp([rank] * (n_exp - 1))
+    kv_moved, stacked = lax.optimization_barrier((kv_moved, stacked))
+    kv_same = jnp.concatenate([local_kv] + kv_moved, axis=0)
     kv_other = permute(kv_same, "ctx", 1)
 
-    rank, gate = call(
-        rank_kernel,
-        [shape((flight, tokens), f32)] * 2,
-        [VMEM] * 2,
-        vmem=4,
-    )(routes.T, gate_values.T)
-    ranks = [rank] + over_exp([rank] * (n_exp - 1))
-
-    rows = heads * span
-    cost = dict(flops=4 * rows * kv_same.shape[0] * HEAD, nbytes=4 * MIB)
+    cost = dict(flops=4 * rows * keys * HEAD, nbytes=4 * MIB)
     stats = call(
-        functools.partial(attend_first, span, cache, heads),
+        functools.partial(attend_first, span),
         [shape((rows, HEAD), f32), shape((rows, LANES), f32), shape((rows, LANES), f32)],
-        [SMEM, VMEM, VMEM],
+        [VMEM] * 3,
         vmem=24,
         **cost,
-    )(seg_starts, queries, kv_same)
+    )(stacked, kv_same, bias_same)
+    kv_other, moved = lax.optimization_barrier((kv_other, moved))
+    ranks = [rank] + moved
     heads_out = call(
-        functools.partial(attend_second, span, cache, heads),
+        functools.partial(attend_second, span),
         shape((span, heads * HEAD), bf16),
-        [SMEM] + [VMEM] * 5,
+        [VMEM] * 6,
         vmem=24,
         **cost,
-    )(seg_starts, queries, kv_other, *stats)
+    )(stacked, kv_other, bias_other, *stats)
 
     heads_same = jnp.concatenate([heads_out] + over_chips(heads_out), axis=0)
     heads_other = permute(heads_same, "ctx", 1)
@@ -428,17 +444,12 @@
 
     gain = norm_gain.reshape(1, features)
     expert_rows = n_exp * CAP
-    chunks = 6
 
     def gate_up(other, dtype):
         return call(
             functools.partial(expert_in_kernel, n_exp, other),
             shape((expert_rows, width + LANES), dtype),
-            [VMEM] * (n_exp + 1) + [ANY],
-            [
-                pltpu.VMEM((chunks, features, width // chunks), bf16),
-                pltpu.SemaphoreType.DMA((chunks,)),
-            ],
+            [VMEM] * (n_exp + 2),
             vmem=16,
             flops=2 * expert_rows * features * width,
             nbytes=4 * MIB,
@@ -447,12 +458,6 @@
     sent = gate_up(1, bf16)
     theirs = permute(sent, "ctx", 1)
     mine = gate_up(0, f32)
-
-    parts, mine = lax.optimization_barrier((parts, mine))
-    part_sum = own
-    for part in over_exp(parts):
-        part_sum = part_sum + part.astype(f32)
-    mixed = part_sum.astype(bf16)
 
     size = expert_rows // chips
     chunk = call(
@@ -461,40 +466,53 @@
         [VMEM] * 2,
         vmem=8,
     )(mine, theirs)
-    gathered = [chunk[0]] + [permute(chunk[k], "ctx", 2 * k) for k in range(1, chips)]
+    order = [k for k in range(2, n_exp)] + [1]
+    share = -(-len(order) // 3)
+    turns = [order[:share], order[share : 2 * share], order[2 * share :]]
+    moved_parts = {}
+
+    def beside(turn, ready, step):
+        ready, sent = lax.optimization_barrier((ready, [parts[k - 1] for k in turns[turn]]))
+        got = [permute(x, "exp", k) for k, x in zip(turns[turn], sent)]
+        done, got = lax.optimization_barrier((step(ready), got))
+        moved_parts.update(zip(turns[turn], got))
+        return ready, done
+
+    chunk, gathered = beside(
+        0, chunk, lambda c: [permute(c[k], "ctx", 2 * k) for k in range(1, chips)]
+    )
     active = call(
         functools.partial(activate, n_ctx * features),
         shape((size, hidden), bf16),
         [VMEM] * chips,
         vmem=8,
-    )(*gathered)
-    active_same = jnp.concatenate([active] + over_chips(active), axis=0)
+    )(chunk[0], *gathered)
+    active, gathered = beside(1, active, over_chips)
+    active_same = jnp.concatenate([active] + gathered, axis=0)
     active_other = permute(active_same, "ctx", 1)
-    held = pltpu.VMEM((hidden, columns), bf16)
     cost = dict(flops=2 * expert_rows * hidden * columns, nbytes=2 * MIB)
     made = call(
         expert_out_first,
         shape((expert_rows, columns), bf16),
-        [VMEM, ANY],
-        [held, pltpu.SemaphoreType.DMA],
+        [VMEM] * 2,
         vmem=8,
         **cost,
     )(active_same, expert_out)
     produced = call(
         functools.partial(expert_out_second, n_exp),
         [shape((local * CAP, columns), bf16)] * n_exp,
-        [VMEM, ANY, VMEM],
-        [held, pltpu.VMEM((local, expert_rows, columns), bf16), pltpu.SemaphoreType.DMA],
+        [VMEM] * 3,
+        [pltpu.VMEM((local, expert_rows, columns), bf16)],
         vmem=8,
         **cost,
     )(active_other, expert_out, made)
-    returned = [produced[0]] + over_exp(produced[1:])
-    expert_sum = call(
+    produced, returned = beside(2, produced, lambda x: over_exp(x[1:]))
+    mixed, expert_sum = call(
         functools.partial(combine, n_exp),
-        shape((tokens, columns), bf16),
-        [VMEM] * (2 + n_exp),
+        [shape((tokens, columns), bf16)] * 2,
+        [VMEM] * (2 + 2 * n_exp),
         vmem=8,
-    )(rank, gate, *returned)
+    )(high, low, own, *[moved_parts[k] for k in range(1, n_exp)], produced[0], *returned)
     return (mixed, expert_sum)
 
 

time: 97.3 us -> 89.8 us (0.923)
  waiting for transfers between devices: 43.8 us -> 39.7 us
  local copies, waits for them, and re-layouts: 5.12 us -> 3.02 us
  Pallas kernels: 12.9 us -> 11.2 us
    ppermute x28, waiting for transfers between devices: 43.8 us -> 39.7 us  [permute(): return lax.ppermute(x, axis, [(i, i ^ k) for i in range(n)])]
    pallas_call x2, Pallas kernels: 3.75 us -> 1.37 us  [gate_up(): call(functools.partial(expert_in_kernel, n_exp, other), shape((expert_row...]
    unnamed x26 -> x21, local copies, waits for them, and re-layouts: 5.12 us -> 3.02 us
    pallas_call x1, Pallas kernels: 0.06 us -> 1.47 us  [body(): call(functools.partial(pick_kv, heads), shape((cache + span, 2 * HEAD), b...]
  transfers between devices with their start and end apart: 28 -> 28, of which waited for: 16 -> 18; matrix products, arithmetic and copies ran while one was open for 1% -> 0% of each run, Pallas kernels for 6% -> 5%
where the time goes in v2:
time: 89.8 us; the launch traced here: 89.5 us
  waiting for transfers between devices  39.7 us (44%)
  starting transfers between devices  33.7 us (38%)
  Pallas kernels  11.2 us (12%)
  local copies, waits for them, and re-layouts  3.02 us (3%)
  other arithmetic  1.01 us (1%)
    ppermute x28, waiting for transfers between devices, permute(): return lax.ppermute(x, axis, [(i, i ^ k) for i in range(n)])  39.7 us
    ppermute x28, starting transfers between devices, permute(): return lax.ppermute(x, axis, [(i, i ^ k) for i in range(n)])  33.7 us
    unnamed x21, local copies, waits for them, and re-layouts  3.02 us
    pallas_call x1, Pallas kernels, body(): call(functools.partial(attend_second, span), shape((span, heads * HEAD),...  1.89 us
  transfers between devices with their start and end apart: 28, of which 18 were waited for; matrix products, arithmetic and copies ran while one was open for 0% of the time, Pallas kernels for 5%

profile of v2, /device:TPU:0, one launch (start us, length us, event | category | flops | bytes accessed | tf_op | source)
XLA Modules:
  0.0 89.5 jit_solution(8048797610031981202)
XLA Ops:
  0.6 1.5 %shard_map.141 = bf16[192,256]{1,0:T(8,128)(2,1)} custom-call(bf16[128,512]{1,0:T(8,128)(2,1)} %ck.1, bf16[128,512]{1,0:T(8,128)(2,1)} %cv.1, bf16[64,512]{1,0:T(8,128)(2,1)} %bk.1, bf16[64,512]{1,0:T(8,128)(2,1)} %bv.1), custom_call_target="tpu_custom_call" | custom-call | tf_op jit(solution)/shard_map/pallas_call | solution.py:367
  2.1 4.0 %collective-permute-start.2 = (bf16[192,256]{1,0:T(8,128)(2,1)}, bf16[192,256]{1,0:T(8,128)(2,1)S(1)}, u32[]{:S(2)}, u32[]{:S(2)}) collective-permute-start(bf16[192,256]{1,0:T(8,128)(2,1)} %shard_map.141), channel_id=1, source_target_pairs={{0,24},{4,28},{8,16},{12,20},{16,8},{20,12},{24,0},{28,4},{1,25},{... | collective-permute-start | bytes 294920 | tf_op jit(solution)/shard_map/ppermute | solution.py:332
  6.7 0.9 %copy-done.3 = bf16[64,2048]{1,0:T(8,128)(2,1)S(1)} copy-done((bf16[64,2048]{1,0:T(8,128)(2,1)S(1)}, bf16[64,2048]{1,0:T(8,128)(2,1)}, u32[]{:S(2)}) %copy-start.3) | copy-done | bytes 262168
  9.7 1.0 %shard_map.140 = (bf16[1024,128]{1,0:T(8,128)(2,1)S(1)}, f32[64,768]{1,0:T(8,128)S(1)}, f32[64,768]{1,0:T(8,128)S(1)}, f32[8,128]{1,0:T(8,128)S(1)}, bf16[128,12...) custom-call(s32[10]{0:T(128)S(1)} %copy-done.8, bf16[64,2048]{1,0:T(8,128)(2,1)S(1)} %copy-done.3, s32[8,128]{1,0:T(8,128)S(1)} %bitcast.5, ...), custom_call_target="tpu_custom_call" | custom-call | bytes 1048576 | tf_op jit(solution)/shard_map/pallas_call | solution.py:377
  12.5 3.7 %collective-permute-start.6 = (f32[8,128]{1,0:T(8,128)S(1)}, f32[8,128]{1,0:T(8,128)S(1)}, u32[]{:S(2)}, u32[]{:S(2)}) collective-permute-start(f32[8,128]{1,0:T(8,128)S(1)} %get-tuple-element.66.refs_0_), channel_id=1, source_target_pairs={{0,3},{1,2},{2,1},{3,0},{4,7},{5,6},{6,5},{7,4},{8,11},{9,10},{10,... | collective-permute-start | bytes 12296 | tf_op jit(solution)/shard_map/ppermute | solution.py:332
  17.0 1.8 %shard_map.142 = (f32[1024,128]{1,0:T(8,128)S(1)}, f32[1024,128]{1,0:T(8,128)S(1)}, f32[1024,128]{1,0:T(8,128)S(1)}) custom-call(bf16[1024,128]{1,0:T(8,128)(2,1)S(1)} %get-tuple-element.62.q, bf16[768,256]{1,0:T(8,128)(2,1)S(1)} %pad_maximum_fusion.1.kv, f32[64,768]{1,0:T(8,128)S(1)} %get-tuple-element.69.bias), custom_call_target="tpu_custom_call" | custom-call | flops 402653184 | bytes 4194304 | tf_op jit(solution)/shard_map/pallas_call | solution.py:399
  18.7 1.9 %collective-permute-done.5.refs_2_ = f32[8,128]{1,0:T(8,128)S(1)} collective-permute-done((f32[8,128]{1,0:T(8,128)S(1)}, f32[8,128]{1,0:T(8,128)S(1)}, u32[]{:S(2)}, u32[]{:S(2)}) %collective-permute-start.5) | collective-permute-done | bytes 4128 | tf_op jit(solution)/shard_map/ppermute | solution.py:332
  20.7 1.9 %shard_map.143 = bf16[64,2048]{1,0:T(8,128)(2,1)S(1)} custom-call(bf16[1024,128]{1,0:T(8,128)(2,1)S(1)} %get-tuple-element.62.q, bf16[768,256]{1,0:T(8,128)(2,1)S(1)} %collective-permute-done.3.kv, f32[64,768]{1,0:T(8,128)S(1)} %get-tuple-element.68.bias, f32[1024,128]{1,0:T(8,128)S(1)} %get-tuple-element.70.o_in, f32[1024,128]{1,0:T(8,128)S(1)} %get-tuple-element.71.m_in, ...), custom_call_target="tpu_custom_call" | custom-call | flops 402653184 | bytes 4194304 | tf_op jit(solution)/shard_map/pallas_call | solution.py:408
  22.6 2.1 %collective-permute-start.9 = (bf16[64,2048]{1,0:T(8,128)(2,1)S(1)}, bf16[64,2048]{1,0:T(8,128)(2,1)S(1)}, u32[]{:S(2)}, u32[]{:S(2)}) collective-permute-start(bf16[64,2048]{1,0:T(8,128)(2,1)S(1)} %shard_map.143), channel_id=1, source_target_pairs={{0,24},{4,28},{8,16},{12,20},{16,8},{20,12},{24,0},{28,4},{1,25},{... | collective-permute-start | bytes 786440 | tf_op jit(solution)/shard_map/ppermute | solution.py:332
  26.1 6.7 %collective-permute-done.9 = bf16[64,2048]{1,0:T(8,128)(2,1)S(1)} collective-permute-done((bf16[64,2048]{1,0:T(8,128)(2,1)S(1)}, bf16[64,2048]{1,0:T(8,128)(2,1)S(1)}, u32[]{:S(2)}, u32[]{:S(2)}) %collective-permute-start.9) | collective-permute-done | bytes 262176 | tf_op jit(solution)/shard_map/ppermute | solution.py:332
  32.8 3.6 %collective-permute-done.8 = bf16[64,2048]{1,0:T(8,128)(2,1)S(1)} collective-permute-done((bf16[64,2048]{1,0:T(8,128)(2,1)S(1)}, bf16[64,2048]{1,0:T(8,128)(2,1)S(1)}, u32[]{:S(2)}, u32[]{:S(2)}) %collective-permute-start.8) | collective-permute-done | bytes 262176 | tf_op jit(solution)/shard_map/ppermute | solution.py:332
  37.3 1.9 %collective-permute-done.10.heads_out = bf16[256,2048]{1,0:T(8,128)(2,1)S(1)} collective-permute-done((bf16[256,2048]{1,0:T(8,128)(2,1)S(1)}, bf16[256,2048]{1,0:T(8,128)(2,1)S(1)}, u32[]{:S(2)}, u32[]{:S(2)}) %collective-permute-start.10) | collective-permute-done | bytes 1048608 | tf_op jit(solution)/shard_map/ppermute | solution.py:332
  39.2 1.1 %shard_map.145 = (f32[128,512]{1,0:T(8,128)S(1)}, bf16[128,512]{1,0:T(8,128)(2,1)S(1)}, bf16[128,512]{1,0:T(8,128)(2,1)S(1)}, bf16[128,512]{1,0:T(8,128)(2,1)S(1...) custom-call(bf16[256,2048]{1,0:T(8,128)(2,1)S(1)} %collective-permut, ...), custom_call_target="tpu_custom_call" | custom-call | flops 536870912 | bytes 4194304 | tf_op jit(solution)/shard_map/pallas_call | solution.py:429
  40.6 2.6 %collective-permute-start.12 = (bf16[128,512]{1,0:T(8,128)(2,1)S(1)}, bf16[128,512]{1,0:T(8,128)(2,1)S(1)}, u32[]{:S(2)}, u32[]{:S(2)}) collective-permute-start(bf16[128,512]{1,0:T(8,128)(2,1)S(1)} %get-tuple-element.79), channel_id=1, source_target_pairs={{0,2},{1,3},{2,0},{3,1},{4,6},{5,7},{6,4},{7,5},{8,10},{9,11},{10,... | collective-permute-start | bytes 393224 | tf_op jit(solution)/shard_map/ppermute | solution.py:332
  43.2 1.5 %collective-permute-start.13 = (bf16[128,512]{1,0:T(8,128)(2,1)S(1)}, bf16[128,512]{1,0:T(8,128)(2,1)S(1)}, u32[]{:S(2)}, u32[]{:S(2)}) collective-permute-start(bf16[128,512]{1,0:T(8,128)(2,1)S(1)} %get-tuple-element.80), channel_id=1, source_target_pairs={{0,3},{1,2},{2,1},{3,0},{4,7},{5,6},{6,5},{7,4},{8,11},{9,10},{10,... | collective-permute-start | bytes 393224 | tf_op jit(solution)/shard_map/ppermute | solution.py:332
  44.8 3.6 %collective-permute-done.11.refs_1_ = bf16[128,512]{1,0:T(8,128)(2,1)S(1)} collective-permute-done((bf16[128,512]{1,0:T(8,128)(2,1)S(1)}, bf16[128,512]{1,0:T(8,128)(2,1)S(1)}, u32[]{:S(2)}, u32[]{:S(2)}) %collective-permute-start.11) | collective-permute-done | bytes 131104 | tf_op jit(solution)/shard_map/ppermute | solution.py:332
  48.4 5.1 %collective-permute-done.12.refs_2_ = bf16[128,512]{1,0:T(8,128)(2,1)S(1)} collective-permute-done((bf16[128,512]{1,0:T(8,128)(2,1)S(1)}, bf16[128,512]{1,0:T(8,128)(2,1)S(1)}, u32[]{:S(2)}, u32[]{:S(2)}) %collective-permute-start.12) | collective-permute-done | bytes 131104 | tf_op jit(solution)/shard_map/ppermute | solution.py:332
  55.0 1.0 %collective-permute-done.14.theirs = bf16[64,3200]{1,0:T(8,128)(2,1)S(1)} collective-permute-done((bf16[64,3200]{1,0:T(8,128)(2,1)S(1)}, bf16[64,3200]{1,0:T(8,128)(2,1)S(1)}, u32[]{:S(2)}, u32[]{:S(2)}) %collective-permute-start.14) | collective-permute-done | bytes 409632 | tf_op jit(solution)/shard_map/ppermute | solution.py:332
  56.1 3.8 %collective-permute-start.18 = (bf16[128,512]{1,0:T(8,128)(2,1)S(1)}, bf16[128,512]{1,0:T(8,128)(2,1)S(1)}, u32[]{:S(2)}, u32[]{:S(2)}) collective-permute-start(bf16[128,512]{1,0:T(8,128)(2,1)S(1)} %get-tuple-element.90), channel_id=1, source_target_pairs={{0,2},{1,3},{2,0},{3,1},{4,6},{5,7},{6,4},{7,5},{8,10},{9,11},{10,... | collective-permute-start | bytes 393224 | tf_op jit(solution)/shard_map/ppermute | solution.py:332
  59.9 1.5 %collective-permute-start.15 = (bf16[16,3200]{1,0:T(8,128)(2,1)S(1)}, bf16[16,3200]{1,0:T(8,128)(2,1)S(1)}, u32[]{:S(2)}, u32[]{:S(2)}) collective-permute-start(bf16[16,3200]{1,0:T(8,128)(2,1)S(1)} %get-tuple-element.87), channel_id=1, source_target_pairs={{0,8},{4,12},{8,0},{12,4},{16,24},{20,28},{24,16},{28,20},{1,9},{5... | collective-permute-start | bytes 307208 | tf_op jit(solution)/shard_map/ppermute | solution.py:332
  62.2 1.2 %collective-permute-start.17 = (bf16[16,3200]{1,0:T(8,128)(2,1)S(1)}, bf16[16,3200]{1,0:T(8,128)(2,1)S(1)}, u32[]{:S(2)}, u32[]{:S(2)}) collective-permute-start(bf16[16,3200]{1,0:T(8,128)(2,1)S(1)} %get-tuple-element.89), channel_id=1, source_target_pairs={{0,24},{4,28},{8,16},{12,20},{16,8},{20,12},{24,0},{28,4},{1,25},{... | collective-permute-start | bytes 307208 | tf_op jit(solution)/shard_map/ppermute | solution.py:332
  63.4 1.2 %collective-permute-done.15.refs_1_ = bf16[16,3200]{1,0:T(8,128)(2,1)S(1)} collective-permute-done((bf16[16,3200]{1,0:T(8,128)(2,1)S(1)}, bf16[16,3200]{1,0:T(8,128)(2,1)S(1)}, u32[]{:S(2)}, u32[]{:S(2)}) %collective-permute-start.15) | collective-permute-done | bytes 102432 | tf_op jit(solution)/shard_map/ppermute | solution.py:332
  64.6 3.7 %collective-permute-done.16.refs_2_ = bf16[16,3200]{1,0:T(8,128)(2,1)S(1)} collective-permute-done((bf16[16,3200]{1,0:T(8,128)(2,1)S(1)}, bf16[16,3200]{1,0:T(8,128)(2,1)S(1)}, u32[]{:S(2)}, u32[]{:S(2)}) %collective-permute-start.16) | collective-permute-done | bytes 102432 | tf_op jit(solution)/shard_map/ppermute | solution.py:332
  68.4 1.4 %collective-permute-start.21 = (bf16[16,1536]{1,0:T(8,128)(2,1)S(1)}, bf16[16,1536]{1,0:T(8,128)(2,1)S(1)}, u32[]{:S(2)}, u32[]{:S(2)}) collective-permute-start(bf16[16,1536]{1,0:T(8,128)(2,1)S(1)} %shard_map.149), channel_id=1, source_target_pairs={{0,24},{4,28},{8,16},{12,20},{16,8},{20,12},{24,0},{28,4},{1,25},{... | collective-permute-start | bytes 147464 | tf_op jit(solution)/shard_map/ppermute | solution.py:332
  70.6 1.3 %collective-permute-start.19 = (bf16[16,1536]{1,0:T(8,128)(2,1)S(1)}, bf16[16,1536]{1,0:T(8,128)(2,1)S(1)}, u32[]{:S(2)}, u32[]{:S(2)}) collective-permute-start(bf16[16,1536]{1,0:T(8,128)(2,1)S(1)} %shard_map.149), channel_id=1, source_target_pairs={{0,8},{4,12},{8,0},{12,4},{16,24},{20,28},{24,16},{28,20},{1,9},{5... | collective-permute-start | bytes 147464 | tf_op jit(solution)/shard_map/ppermute | solution.py:332
  71.9 1.0 %collective-permute-start.22 = (bf16[128,512]{1,0:T(8,128)(2,1)S(1)}, bf16[128,512]{1,0:T(8,128)(2,1)S(1)}, u32[]{:S(2)}, u32[]{:S(2)}) collective-permute-start(bf16[128,512]{1,0:T(8,128)(2,1)S(1)} %get-tuple-element.96), channel_id=1, source_target_pairs={{0,3},{1,2},{2,1},{3,0},{4,7},{5,6},{6,5},{7,4},{8,11},{9,10},{10,... | collective-permute-start | bytes 393224 | tf_op jit(solution)/shard_map/ppermute | solution.py:332
  74.7 4.0 %collective-permute-done.22.refs_2_ = bf16[128,512]{1,0:T(8,128)(2,1)S(1)} collective-permute-done((bf16[128,512]{1,0:T(8,128)(2,1)S(1)}, bf16[128,512]{1,0:T(8,128)(2,1)S(1)}, u32[]{:S(2)}, u32[]{:S(2)}) %collective-permute-start.22) | collective-permute-done | bytes 131104 | tf_op jit(solution)/shard_map/ppermute | solution.py:332
  79.2 1.0 %collective-permute-done.23.active = bf16[64,1536]{1,0:T(8,128)(2,1)S(1)} collective-permute-done((bf16[64,1536]{1,0:T(8,128)(2,1)S(1)}, bf16[64,1536]{1,0:T(8,128)(2,1)S(1)}, u32[]{:S(2)}, u32[]{:S(2)}) %collective-permute-start.23) | collective-permute-done | bytes 196640 | tf_op jit(solution)/shard_map/ppermute | solution.py:332
  80.7 2.0 %collective-permute-start.24 = (bf16[32,512]{1,0:T(8,128)(2,1)S(1)}, bf16[32,512]{1,0:T(8,128)(2,1)S(1)}, u32[]{:S(2)}, u32[]{:S(2)}) collective-permute-start(bf16[32,512]{1,0:T(8,128)(2,1)S(1)} %get-tuple-element.105), channel_id=1, source_target_pairs={{0,1},{1,0},{2,3},{3,2},{4,5},{5,4},{6,7},{7,6},{8,9},{9,8},{10,11... | collective-permute-start | bytes 98312 | tf_op jit(solution)/shard_map/ppermute | solution.py:332
  82.7 2.4 %collective-permute-start.26 = (bf16[32,512]{1,0:T(8,128)(2,1)S(1)}, bf16[32,512]{1,0:T(8,128)(2,1)S(1)}, u32[]{:S(2)}, u32[]{:S(2)}) collective-permute-start(bf16[32,512]{1,0:T(8,128)(2,1)S(1)} %get-tuple-element.107), channel_id=1, source_target_pairs={{0,3},{1,2},{2,1},{3,0},{4,7},{5,6},{6,5},{7,4},{8,11},{9,10},{10,... | collective-permute-start | bytes 98312 | tf_op jit(solution)/shard_map/ppermute | solution.py:332
  85.2 2.8 %collective-permute-done.24.refs_4_ = bf16[32,512]{1,0:T(8,128)(2,1)S(1)} collective-permute-done((bf16[32,512]{1,0:T(8,128)(2,1)S(1)}, bf16[32,512]{1,0:T(8,128)(2,1)S(1)}, u32[]{:S(2)}, u32[]{:S(2)}) %collective-permute-start.24) | collective-permute-done | bytes 32800 | tf_op jit(solution)/shard_map/ppermute | solution.py:332
  88.6 1.0 %shard_map.152 = (bf16[128,512]{1,0:T(8,128)(2,1)}, bf16[128,512]{1,0:T(8,128)(2,1)}) custom-call(bf16[128,128]{1,0:T(8,128)(2,1)S(1)} %get-tuple-element.59.high, bf16[128,128]{1,0:T(8,128)(2,1)S(1)} %get-tuple-element.60.low, f32[128,512]{1,0:T(8,128)S(1)} %get-tuple-element.76.own, bf16[128,512]{1,0:T(8,128)(2,1)S(1)} %collective-permute-done.27.refs_0_, ...), custom_call_target="tpu_custom_call" | custom-call | tf_op jit(solution)/shard_map/pallas_call | solution.py:510
  (61 shorter events, 14.5 us)
Async XLA Ops:
  2.1 8.6 %collective-permute-start.2 = (bf16[192,256]{1,0:T(8,128)(2,1)}, bf16[192,256]{1,0:T(8,128)(2,1)S(1)}, u32[]{:S(2)}, u32[]{:S(2)}) collective-permute-start(bf16[192,256]{1,0:T(8,128)(2,1)} %shard_map.141), channel_id=1, source_target_pairs={{0,24},{4,28},{8,16},{12,20},{16,8},{20,12},{24,0},{28,4},{1,25},{... | collective-permute-start | bytes 294920 | tf_op jit(solution)/shard_map/ppermute | solution.py:332
  6.1 5.1 %collective-permute-start.1 = (bf16[192,256]{1,0:T(8,128)(2,1)}, bf16[192,256]{1,0:T(8,128)(2,1)S(1)}, u32[]{:S(2)}, u32[]{:S(2)}) collective-permute-start(bf16[192,256]{1,0:T(8,128)(2,1)} %shard_map.141), channel_id=1, source_target_pairs={{0,16},{4,20},{8,24},{12,28},{16,0},{20,4},{24,8},{28,12},{1,17},{... | collective-permute-start | bytes 294920 | tf_op jit(solution)/shard_map/ppermute | solution.py:332
  6.6 4.9 %collective-permute-start = (bf16[192,256]{1,0:T(8,128)(2,1)}, bf16[192,256]{1,0:T(8,128)(2,1)S(1)}, u32[]{:S(2)}, u32[]{:S(2)}) collective-permute-start(bf16[192,256]{1,0:T(8,128)(2,1)} %shard_map.141), channel_id=1, source_target_pairs={{0,8},{4,12},{8,0},{12,4},{16,24},{20,28},{24,16},{28,20},{1,9},{5... | collective-permute-start | bytes 294920 | tf_op jit(solution)/shard_map/ppermute | solution.py:332
  12.4 8.3 %collective-permute-start.3 = (bf16[768,256]{1,0:T(8,128)(2,1)S(1)}, bf16[768,256]{1,0:T(8,128)(2,1)S(1)}, u32[]{:S(2)}, u32[]{:S(2)}) collective-permute-start(bf16[768,256]{1,0:T(8,128)(2,1)S(1)} %pad_maximum_fusion.1.kv), channel_id=1, source_target_pairs={{0,4},{4,0},{8,12},{12,8},{16,20},{20,16},{24,28},{28,24},{1,5},{5... | collective-permute-start | bytes 1179656 | tf_op jit(solution)/shard_map/ppermute | solution.py:332
  12.5 6.2 %collective-permute-start.6 = (f32[8,128]{1,0:T(8,128)S(1)}, f32[8,128]{1,0:T(8,128)S(1)}, u32[]{:S(2)}, u32[]{:S(2)}) collective-permute-start(f32[8,128]{1,0:T(8,128)S(1)} %get-tuple-element.66.refs_0_), channel_id=1, source_target_pairs={{0,3},{1,2},{2,1},{3,0},{4,7},{5,6},{6,5},{7,4},{8,11},{9,10},{10,... | collective-permute-start | bytes 12296 | tf_op jit(solution)/shard_map/ppermute | solution.py:332
  16.2 4.5 %collective-permute-start.5 = (f32[8,128]{1,0:T(8,128)S(1)}, f32[8,128]{1,0:T(8,128)S(1)}, u32[]{:S(2)}, u32[]{:S(2)}) collective-permute-start(f32[8,128]{1,0:T(8,128)S(1)} %get-tuple-element.66.refs_0_), channel_id=1, source_target_pairs={{0,2},{1,3},{2,0},{3,1},{4,6},{5,7},{6,4},{7,5},{8,10},{9,11},{10,... | collective-permute-start | bytes 12296 | tf_op jit(solution)/shard_map/ppermute | solution.py:332
  16.2 4.5 %collective-permute-start.4 = (f32[8,128]{1,0:T(8,128)S(1)}, f32[8,128]{1,0:T(8,128)S(1)}, u32[]{:S(2)}, u32[]{:S(2)}) collective-permute-start(f32[8,128]{1,0:T(8,128)S(1)} %get-tuple-element.66.refs_0_), channel_id=1, source_target_pairs={{0,1},{1,0},{2,3},{3,2},{4,5},{5,4},{6,7},{7,6},{8,9},{9,8},{10,11... | collective-permute-start | bytes 12296 | tf_op jit(solution)/shard_map/ppermute | solution.py:332
  20.7 15.9 %copy-start.2 = (bf16[2048,512]{1,0:T(8,128)(2,1)S(1)}, bf16[2048,512]{1,0:T(8,128)(2,1)}, u32[]{:S(2)}) copy-start(bf16[2048,512]{1,0:T(8,128)(2,1)} %weight.5) | copy-start | bytes 6291460
  22.6 10.3 %collective-permute-start.9 = (bf16[64,2048]{1,0:T(8,128)(2,1)S(1)}, bf16[64,2048]{1,0:T(8,128)(2,1)S(1)}, u32[]{:S(2)}, u32[]{:S(2)}) collective-permute-start(bf16[64,2048]{1,0:T(8,128)(2,1)S(1)} %shard_map.143), channel_id=1, source_target_pairs={{0,24},{4,28},{8,16},{12,20},{16,8},{20,12},{24,0},{28,4},{1,25},{... | collective-permute-start | bytes 786440 | tf_op jit(solution)/shard_map/ppermute | solution.py:332
  24.7 11.7 %collective-permute-start.8 = (bf16[64,2048]{1,0:T(8,128)(2,1)S(1)}, bf16[64,2048]{1,0:T(8,128)(2,1)S(1)}, u32[]{:S(2)}, u32[]{:S(2)}) collective-permute-start(bf16[64,2048]{1,0:T(8,128)(2,1)S(1)} %shard_map.143), channel_id=1, source_target_pairs={{0,16},{4,20},{8,24},{12,28},{16,0},{20,4},{24,8},{28,12},{1,17},{... | collective-permute-start | bytes 786440 | tf_op jit(solution)/shard_map/ppermute | solution.py:332
  25.6 10.8 %collective-permute-start.7 = (bf16[64,2048]{1,0:T(8,128)(2,1)S(1)}, bf16[64,2048]{1,0:T(8,128)(2,1)S(1)}, u32[]{:S(2)}, u32[]{:S(2)}) collective-permute-start(bf16[64,2048]{1,0:T(8,128)(2,1)S(1)} %shard_map.143), channel_id=1, source_target_pairs={{0,8},{4,12},{8,0},{12,4},{16,24},{20,28},{24,16},{28,20},{1,9},{5... | collective-permute-start | bytes 786440 | tf_op jit(solution)/shard_map/ppermute | solution.py:332
  36.5 2.7 %collective-permute-start.10 = (bf16[256,2048]{1,0:T(8,128)(2,1)S(1)}, bf16[256,2048]{1,0:T(8,128)(2,1)S(1)}, u32[]{:S(2)}, u32[]{:S(2)}) collective-permute-start(bf16[256,2048]{1,0:T(8,128)(2,1)S(1)} %pad_maximum_fusion.heads_out), channel_id=1, source_target_pairs={{0,4},{4,0},{8,12},{12,8},{16,20},{20,16},{24,28},{28,24},{1,5},{5... | collective-permute-start | bytes 3145736 | tf_op jit(solution)/shard_map/ppermute | solution.py:332
  36.6 16.9 %copy-start = (bf16[2,512,3072]{2,1,0:T(8,128)(2,1)S(1)}, bf16[2,512,3072]{2,1,0:T(8,128)(2,1)}, u32[]{:S(2)}) copy-start(bf16[2,512,3072]{2,1,0:T(8,128)(2,1)} %refs_5_.3) | copy-start | bytes 18874372
  37.3 16.2 %copy-start.5 = (f32[512]{0:T(512)S(1)}, f32[512]{0:T(512)}, u32[]{:S(2)}) copy-start(f32[512]{0:T(512)} %param.21) | copy-start | bytes 6148
  40.3 8.1 %collective-permute-start.11 = (bf16[128,512]{1,0:T(8,128)(2,1)S(1)}, bf16[128,512]{1,0:T(8,128)(2,1)S(1)}, u32[]{:S(2)}, u32[]{:S(2)}) collective-permute-start(bf16[128,512]{1,0:T(8,128)(2,1)S(1)} %get-tuple-element.78), channel_id=1, source_target_pairs={{0,1},{1,0},{2,3},{3,2},{4,5},{5,4},{6,7},{7,6},{8,9},{9,8},{10,11... | collective-permute-start | bytes 393224 | tf_op jit(solution)/shard_map/ppermute | solution.py:332
  40.6 12.9 %collective-permute-start.12 = (bf16[128,512]{1,0:T(8,128)(2,1)S(1)}, bf16[128,512]{1,0:T(8,128)(2,1)S(1)}, u32[]{:S(2)}, u32[]{:S(2)}) collective-permute-start(bf16[128,512]{1,0:T(8,128)(2,1)S(1)} %get-tuple-element.79), channel_id=1, source_target_pairs={{0,2},{1,3},{2,0},{3,1},{4,6},{5,7},{6,4},{7,5},{8,10},{9,11},{10,... | collective-permute-start | bytes 393224 | tf_op jit(solution)/shard_map/ppermute | solution.py:332
  43.2 10.3 %collective-permute-start.13 = (bf16[128,512]{1,0:T(8,128)(2,1)S(1)}, bf16[128,512]{1,0:T(8,128)(2,1)S(1)}, u32[]{:S(2)}, u32[]{:S(2)}) collective-permute-start(bf16[128,512]{1,0:T(8,128)(2,1)S(1)} %get-tuple-element.80), channel_id=1, source_target_pairs={{0,3},{1,2},{2,1},{3,0},{4,7},{5,6},{6,5},{7,4},{8,11},{9,10},{10,... | collective-permute-start | bytes 393224 | tf_op jit(solution)/shard_map/ppermute | solution.py:332
  54.2 1.8 %collective-permute-start.14 = (bf16[64,3200]{1,0:T(8,128)(2,1)S(1)}, bf16[64,3200]{1,0:T(8,128)(2,1)S(1)}, u32[]{:S(2)}, u32[]{:S(2)}) collective-permute-start(bf16[64,3200]{1,0:T(8,128)(2,1)S(1)} %shard_map.147), channel_id=1, source_target_pairs={{0,4},{4,0},{8,12},{12,8},{16,20},{20,16},{24,28},{28,24},{1,5},{5... | collective-permute-start | bytes 1228808 | tf_op jit(solution)/shard_map/ppermute | solution.py:332
  54.3 24.5 %copy-start.1 = (bf16[2,1536,512]{2,1,0:T(8,128)(2,1)S(1)}, bf16[2,1536,512]{2,1,0:T(8,128)(2,1)}, u32[]{:S(2)}) copy-start(bf16[2,1536,512]{2,1,0:T(8,128)(2,1)} %weight.7) | copy-start | bytes 9437188
  56.1 12.1 %collective-permute-start.18 = (bf16[128,512]{1,0:T(8,128)(2,1)S(1)}, bf16[128,512]{1,0:T(8,128)(2,1)S(1)}, u32[]{:S(2)}, u32[]{:S(2)}) collective-permute-start(bf16[128,512]{1,0:T(8,128)(2,1)S(1)} %get-tuple-element.90), channel_id=1, source_target_pairs={{0,2},{1,3},{2,0},{3,1},{4,6},{5,7},{6,4},{7,5},{8,10},{9,11},{10,... | collective-permute-start | bytes 393224 | tf_op jit(solution)/shard_map/ppermute | solution.py:332
  59.9 4.7 %collective-permute-start.15 = (bf16[16,3200]{1,0:T(8,128)(2,1)S(1)}, bf16[16,3200]{1,0:T(8,128)(2,1)S(1)}, u32[]{:S(2)}, u32[]{:S(2)}) collective-permute-start(bf16[16,3200]{1,0:T(8,128)(2,1)S(1)} %get-tuple-element.87), channel_id=1, source_target_pairs={{0,8},{4,12},{8,0},{12,4},{16,24},{20,28},{24,16},{28,20},{1,9},{5... | collective-permute-start | bytes 307208 | tf_op jit(solution)/shard_map/ppermute | solution.py:332
  61.4 6.9 %collective-permute-start.16 = (bf16[16,3200]{1,0:T(8,128)(2,1)S(1)}, bf16[16,3200]{1,0:T(8,128)(2,1)S(1)}, u32[]{:S(2)}, u32[]{:S(2)}) collective-permute-start(bf16[16,3200]{1,0:T(8,128)(2,1)S(1)} %get-tuple-element.88), channel_id=1, source_target_pairs={{0,16},{4,20},{8,24},{12,28},{16,0},{20,4},{24,8},{28,12},{1,17},{... | collective-permute-start | bytes 307208 | tf_op jit(solution)/shard_map/ppermute | solution.py:332
  62.2 6.0 %collective-permute-start.17 = (bf16[16,3200]{1,0:T(8,128)(2,1)S(1)}, bf16[16,3200]{1,0:T(8,128)(2,1)S(1)}, u32[]{:S(2)}, u32[]{:S(2)}) collective-permute-start(bf16[16,3200]{1,0:T(8,128)(2,1)S(1)} %get-tuple-element.89), channel_id=1, source_target_pairs={{0,24},{4,28},{8,16},{12,20},{16,8},{20,12},{24,0},{28,4},{1,25},{... | collective-permute-start | bytes 307208 | tf_op jit(solution)/shard_map/ppermute | solution.py:332
  68.4 5.1 %collective-permute-start.21 = (bf16[16,1536]{1,0:T(8,128)(2,1)S(1)}, bf16[16,1536]{1,0:T(8,128)(2,1)S(1)}, u32[]{:S(2)}, u32[]{:S(2)}) collective-permute-start(bf16[16,1536]{1,0:T(8,128)(2,1)S(1)} %shard_map.149), channel_id=1, source_target_pairs={{0,24},{4,28},{8,16},{12,20},{16,8},{20,12},{24,0},{28,4},{1,25},{... | collective-permute-start | bytes 147464 | tf_op jit(solution)/shard_map/ppermute | solution.py:332
  69.7 4.2 %collective-permute-start.20 = (bf16[16,1536]{1,0:T(8,128)(2,1)S(1)}, bf16[16,1536]{1,0:T(8,128)(2,1)S(1)}, u32[]{:S(2)}, u32[]{:S(2)}) collective-permute-start(bf16[16,1536]{1,0:T(8,128)(2,1)S(1)} %shard_map.149), channel_id=1, source_target_pairs={{0,16},{4,20},{8,24},{12,28},{16,0},{20,4},{24,8},{28,12},{1,17},{... | collective-permute-start | bytes 147464 | tf_op jit(solution)/shard_map/ppermute | solution.py:332
  70.6 4.1 %collective-permute-start.19 = (bf16[16,1536]{1,0:T(8,128)(2,1)S(1)}, bf16[16,1536]{1,0:T(8,128)(2,1)S(1)}, u32[]{:S(2)}, u32[]{:S(2)}) collective-permute-start(bf16[16,1536]{1,0:T(8,128)(2,1)S(1)} %shard_map.149), channel_id=1, source_target_pairs={{0,8},{4,12},{8,0},{12,4},{16,24},{20,28},{24,16},{28,20},{1,9},{5... | collective-permute-start | bytes 147464 | tf_op jit(solution)/shard_map/ppermute | solution.py:332
  71.9 6.8 %collective-permute-start.22 = (bf16[128,512]{1,0:T(8,128)(2,1)S(1)}, bf16[128,512]{1,0:T(8,128)(2,1)S(1)}, u32[]{:S(2)}, u32[]{:S(2)}) collective-permute-start(bf16[128,512]{1,0:T(8,128)(2,1)S(1)} %get-tuple-element.96), channel_id=1, source_target_pairs={{0,3},{1,2},{2,1},{3,0},{4,7},{5,6},{6,5},{7,4},{8,11},{9,10},{10,... | collective-permute-start | bytes 393224 | tf_op jit(solution)/shard_map/ppermute | solution.py:332
  78.7 1.5 %collective-permute-start.23 = (bf16[64,1536]{1,0:T(8,128)(2,1)S(1)}, bf16[64,1536]{1,0:T(8,128)(2,1)S(1)}, u32[]{:S(2)}, u32[]{:S(2)}) collective-permute-start(bf16[64,1536]{1,0:T(8,128)(2,1)S(1)} %constant_dynamic-update-slice_fusion.active), channel_id=1, source_target_pairs={{0,4},{4,0},{8,12},{12,8},{16,20},{20,16},{24,28},{28,24},{1,5},{5... | collective-permute-start | bytes 589832 | tf_op jit(solution)/shard_map/ppermute | solution.py:332
  80.6 7.9 %collective-permute-start.27 = (bf16[128,512]{1,0:T(8,128)(2,1)S(1)}, bf16[128,512]{1,0:T(8,128)(2,1)S(1)}, u32[]{:S(2)}, u32[]{:S(2)}) collective-permute-start(bf16[128,512]{1,0:T(8,128)(2,1)S(1)} %get-tuple-element.108), channel_id=1, source_target_pairs={{0,1},{1,0},{2,3},{3,2},{4,5},{5,4},{6,7},{7,6},{8,9},{9,8},{10,11... | collective-permute-start | bytes 393224 | tf_op jit(solution)/shard_map/ppermute | solution.py:332
  80.7 7.3 %collective-permute-start.24 = (bf16[32,512]{1,0:T(8,128)(2,1)S(1)}, bf16[32,512]{1,0:T(8,128)(2,1)S(1)}, u32[]{:S(2)}, u32[]{:S(2)}) collective-permute-start(bf16[32,512]{1,0:T(8,128)(2,1)S(1)} %get-tuple-element.105), channel_id=1, source_target_pairs={{0,1},{1,0},{2,3},{3,2},{4,5},{5,4},{6,7},{7,6},{8,9},{9,8},{10,11... | collective-permute-start | bytes 98312 | tf_op jit(solution)/shard_map/ppermute | solution.py:332
  82.7 5.3 %collective-permute-start.25 = (bf16[32,512]{1,0:T(8,128)(2,1)S(1)}, bf16[32,512]{1,0:T(8,128)(2,1)S(1)}, u32[]{:S(2)}, u32[]{:S(2)}) collective-permute-start(bf16[32,512]{1,0:T(8,128)(2,1)S(1)} %get-tuple-element.106), channel_id=1, source_target_pairs={{0,2},{1,3},{2,0},{3,1},{4,6},{5,7},{6,4},{7,5},{8,10},{9,11},{10,... | collective-permute-start | bytes 98312 | tf_op jit(solution)/shard_map/ppermute | solution.py:332
  82.7 5.8 %collective-permute-start.26 = (bf16[32,512]{1,0:T(8,128)(2,1)S(1)}, bf16[32,512]{1,0:T(8,128)(2,1)S(1)}, u32[]{:S(2)}, u32[]{:S(2)}) collective-permute-start(bf16[32,512]{1,0:T(8,128)(2,1)S(1)} %get-tuple-element.107), channel_id=1, source_target_pairs={{0,3},{1,2},{2,1},{3,0},{4,7},{5,6},{6,5},{7,4},{8,11},{9,10},{10,... | collective-permute-start | bytes 98312 | tf_op jit(solution)/shard_map/ppermute | solution.py:332
  (5 other events, 5.7 us)

commit v3 on v2

--- a/solution.py
+++ b/solution.py
@@ -103,32 +103,22 @@
     return jnp.where(seen, 0.0, neg_large)
 
 
-def prepare(
-    n_exp, span, cache, seg_starts, q, routes, gates,
-    stacked, bias_same, bias_other, rank, high, low, q_vmem, routes_vmem, gates_vmem, sems,
-):
-    copies = [
-        pltpu.make_async_copy(src, dst, sems.at[n])
-        for n, (src, dst) in enumerate(
-            ((routes, routes_vmem), (gates, gates_vmem), (q, q_vmem))
-        )
-    ]
-    for copy in copies:
-        copy.start()
+def mask_kernel(span, cache, seg_starts, bias_same, bias_other):
     pieces = bias_same.shape[1] // (cache + span)
     bias_same[...] = mask_bias(seg_starts, 0, span, cache, pieces)
     bias_other[...] = mask_bias(seg_starts, 1, span, cache, pieces)
+
+
+def route_kernel(n_exp, routes, gates, rank, high, low):
     flight, tokens = rank.shape
     local = flight // n_exp
     expert = lax.broadcasted_iota(jnp.int32, (flight, tokens), 0)
     member = jnp.zeros((flight, tokens), f32)
     weight = jnp.zeros((flight, tokens), f32)
-    copies[0].wait()
-    copies[1].wait()
     for k in range(routes.shape[0]):
-        hit = routes_vmem[k : k + 1, :] == expert
+        hit = routes[k : k + 1, :] == expert
         member = jnp.where(hit, 1.0, member)
-        weight = weight + jnp.where(hit, gates_vmem[k : k + 1, :], 0.0)
+        weight = weight + jnp.where(hit, gates[k : k + 1, :], 0.0)
     before = lax.broadcasted_iota(jnp.int32, (tokens, tokens), 0) < lax.broadcasted_iota(
         jnp.int32, (tokens, tokens), 1
     )
@@ -148,9 +138,6 @@
         at = pl.ds(pl.multiple_of(jnp.bitwise_xor(exp, d) * per, per), per)
         high[at, :] = upper[d * per : (d + 1) * per, :]
         low[at, :] = lower[d * per : (d + 1) * per, :]
-    copies[2].wait()
-    for h in range(q.shape[1] // HEAD):
-        stacked[h * span : (h + 1) * span, :] = q_vmem[:, h * HEAD : (h + 1) * HEAD]
 
 
 GROUP = 4
@@ -181,8 +168,9 @@
     attend(q, kv, bias, span, finish)
 
 
-def attend_second(span, q, kv, bias, o_in, m_in, l_in, result):
+def attend_second(span, q, kv, bias, o_in, m_in, l_in, *results):
     scale = math.log2(math.e) / math.sqrt(HEAD)
+    half = results[0].shape[1] // HEAD
 
     def finish(g, rows, group, out, top, total):
         at = pl.ds(g * rows, rows)
@@ -193,7 +181,9 @@
         norm = l_in[at, :] * w_first + total * w_second
         merged = ((o_in[at, :] * w_first + out * w_second) / norm).astype(bf16)
         for h in range(group):
-            col = (g * group + h) * HEAD
+            head = g * group + h
+            result = results[head // half]
+            col = head % half * HEAD
             result[:, col : col + HEAD] = merged[h * span : (h + 1) * span, :]
 
     attend(q, kv, bias, span, finish)
@@ -203,12 +193,11 @@
     out[...] = dot(heads_out[...], weight[...])
 
 
-def project_second(n_exp, span, heads_out, weight, first, residual, *refs):
-    ranks = refs[:n_exp]
-    own_out = refs[n_exp]
-    part_outs = refs[n_exp + 1 : 2 * n_exp]
-    pick_outs = refs[2 * n_exp : 3 * n_exp]
-    whole, picked = refs[3 * n_exp :]
+def project_second(n_exp, span, heads_out, weight, first, residual, ranks, *refs):
+    own_out, odd_out = refs[:2]
+    even_outs = refs[2 : n_exp // 2 + 1]
+    pick_outs = refs[n_exp // 2 + 1 : -2]
+    whole, picked = refs[-2:]
     ctx, exp = lax.axis_index("ctx"), lax.axis_index("exp")
     second = dot(heads_out[...], weight[...])
     for k in range(heads_out.shape[0] // span):
@@ -216,7 +205,7 @@
         whole[rows_at(jnp.bitwise_xor(ctx, 2 * k) * span, span, span), :] = first[here, :]
         whole[rows_at(jnp.bitwise_xor(ctx, 2 * k + 1) * span, span, span), :] = second[here, :]
     tokens = residual.shape[0]
-    flight = ranks[0].shape[0]
+    flight = ranks.shape[0] // n_exp
     local = flight // n_exp
     slot = lax.broadcasted_iota(jnp.int32, (CAP, tokens), 0).astype(f32)
     for k in range(n_exp):
@@ -226,9 +215,11 @@
             part = part + residual[...].astype(f32)
             own_out[...] = part
         narrow = part.astype(bf16)
-        if k > 0:
-            part_outs[k - 1][...] = narrow
-        rank = ranks[k][...]
+        if k % 2:
+            odd_out[k // 2 * tokens : (k // 2 + 1) * tokens, :] = narrow
+        elif k:
+            even_outs[k // 2 - 1][...] = narrow
+        rank = ranks[k * flight : (k + 1) * flight, :]
         table = jnp.concatenate(
             [jnp.where(rank[e : e + 1, :] == slot, 1.0, 0.0) for e in range(flight)], axis=0
         ).astype(bf16)
@@ -312,10 +303,11 @@
             outs[k][j * CAP : (j + 1) * CAP, :] = whole[j, at, :]
 
 
-def combine(n_exp, high, low, own, *refs):
-    parts, returned = refs[: n_exp - 1], refs[n_exp - 1 : -2]
+def combine(high, low, own, odd, *refs):
+    n_exp = high.shape[0] // refs[0].shape[0]
+    returned, parts = refs[:n_exp], refs[n_exp:-2]
     mixed, out = refs[-2:]
-    total = own[...]
+    total = own[...] + odd[: own.shape[0], :].astype(f32)
     for part in parts:
         total = total + part[...].astype(f32)
     mixed[...] = total.astype(bf16)
@@ -330,6 +322,18 @@
 def permute(x, axis, k):
     n = lax.axis_size(axis)
     return lax.ppermute(x, axis, [(i, i ^ k) for i in range(n)])
+
+
+def gather_halves(halves, chips):
+    low, high = halves
+    if chips != 4:
+        return [[low, high]] + [
+            [permute(low, "ctx", 2 * k), permute(high, "ctx", 2 * k)] for k in range(1, chips)
+        ]
+    x_low, y_high = permute(low, "ctx", 2), permute(high, "ctx", 4)
+    x_high, y_low = permute(high, "ctx", 2), permute(low, "ctx", 4)
+    far_low, far_high = permute(x_low, "ctx", 4), permute(y_high, "ctx", 2)
+    return [[low, high], [x_low, x_high], [y_low, y_high], [far_low, far_high]]
 
 
 def body(
@@ -374,24 +378,23 @@
     kv_moved = over_chips(local_kv)
 
     rows, keys = heads * span, chips * (cache + span)
-    stacked, bias_same, bias_other, rank, high, low = call(
-        functools.partial(prepare, n_exp, span, cache),
-        [shape((rows, HEAD), bf16)]
-        + [shape((span, keys), f32)] * 2
-        + [shape((flight, tokens), f32)]
-        + [shape((flight * CAP, tokens), bf16)] * 2,
-        [SMEM] + [HBM] * 3,
-        [
-            pltpu.VMEM(queries.shape, bf16),
-            pltpu.VMEM(routes.shape[::-1], jnp.int32),
-            pltpu.VMEM(routes.shape[::-1], f32),
-            pltpu.SemaphoreType.DMA((3,)),
-        ],
+    bias_same, bias_other = call(
+        functools.partial(mask_kernel, span, cache),
+        [shape((span, keys), f32)] * 2,
+        [SMEM],
         vmem=8,
         nbytes=MIB,
-    )(seg_starts, queries, routes.T, gate_values.T)
-    moved = over_exp([rank] * (n_exp - 1))
-    kv_moved, stacked = lax.optimization_barrier((kv_moved, stacked))
+    )(seg_starts)
+    stacked = queries.reshape(span, heads, HEAD).transpose(1, 0, 2).reshape(rows, HEAD)
+    rank, high, low = call(
+        functools.partial(route_kernel, n_exp),
+        [shape((flight, tokens), f32)] + [shape((flight * CAP, tokens), bf16)] * 2,
+        [VMEM] * 2,
+        vmem=8,
+    )(routes.T, gate_values.T)
+    kv_moved, stacked, bias_same, bias_other, rank = lax.optimization_barrier(
+        (kv_moved, stacked, bias_same, bias_other, rank)
+    )
     kv_same = jnp.concatenate([local_kv] + kv_moved, axis=0)
     kv_other = permute(kv_same, "ctx", 1)
 
@@ -403,17 +406,22 @@
         vmem=24,
         **cost,
     )(stacked, kv_same, bias_same)
-    kv_other, moved = lax.optimization_barrier((kv_other, moved))
-    ranks = [rank] + moved
-    heads_out = call(
+    halves = call(
         functools.partial(attend_second, span),
-        shape((span, heads * HEAD), bf16),
+        [shape((span, rows // span * HEAD // 2), bf16)] * 2,
         [VMEM] * 6,
         vmem=24,
         **cost,
     )(stacked, kv_other, bias_other, *stats)
 
-    heads_same = jnp.concatenate([heads_out] + over_chips(heads_out), axis=0)
+    halves, ranks = lax.optimization_barrier((halves, rank))
+    step = 1
+    while step < n_exp:
+        ranks = jnp.concatenate([ranks, permute(ranks, "exp", step)], axis=0)
+        step *= 2
+    pieces = gather_halves(halves, chips)
+    pieces, ranks = lax.optimization_barrier((pieces, ranks))
+    heads_same = jnp.concatenate([jnp.concatenate(pair, axis=1) for pair in pieces], axis=0)
     heads_other = permute(heads_same, "ctx", 1)
     cost = dict(
         flops=2 * heads_same.shape[0] * heads_same.shape[1] * columns, nbytes=4 * MIB
@@ -429,27 +437,32 @@
     outs = call(
         functools.partial(project_second, n_exp, span),
         [shape((tokens, columns), f32)]
-        + [shape((tokens, columns), bf16)] * (n_exp - 1)
+        + [shape((n_exp // 2 * tokens, columns), bf16)]
+        + [shape((tokens, columns), bf16)] * (n_exp // 2 - 1)
         + [shape((per_exp, columns), bf16)] * n_exp,
-        [VMEM] * (4 + n_exp),
+        [VMEM] * 5,
         [
             pltpu.VMEM((n_ctx * span, columns), f32),
             pltpu.VMEM((n_exp, per_exp, columns), bf16),
         ],
         vmem=24,
         **cost,
-    )(heads_other, out_weight, first, residual, *ranks)
-    own, parts, picks = outs[0], outs[1:n_exp], outs[n_exp:]
-    arrived = [picks[0]] + over_exp(picks[1:])
+    )(heads_other, out_weight, first, residual, ranks)
+    own, odd, even, picks = outs[0], outs[1], outs[2 : n_exp // 2 + 1], outs[n_exp // 2 + 1 :]
+    passed = [permute(picks[2 * k + 1], "exp", 1) for k in range(1, n_exp // 2)]
+    arrived = [picks[0], permute(picks[1], "exp", 1)]
+    for k, got in enumerate(passed, 1):
+        pair = (picks[2 * k].astype(f32) + got.astype(f32)).astype(bf16)
+        arrived.append(permute(pair, "exp", 2 * k))
 
     gain = norm_gain.reshape(1, features)
     expert_rows = n_exp * CAP
 
     def gate_up(other, dtype):
         return call(
-            functools.partial(expert_in_kernel, n_exp, other),
+            functools.partial(expert_in_kernel, len(arrived), other),
             shape((expert_rows, width + LANES), dtype),
-            [VMEM] * (n_exp + 2),
+            [VMEM] * (len(arrived) + 2),
             vmem=16,
             flops=2 * expert_rows * features * width,
             nbytes=4 * MIB,
@@ -466,20 +479,15 @@
         [VMEM] * 2,
         vmem=8,
     )(mine, theirs)
-    order = [k for k in range(2, n_exp)] + [1]
-    share = -(-len(order) // 3)
-    turns = [order[:share], order[share : 2 * share], order[2 * share :]]
-    moved_parts = {}
-
-    def beside(turn, ready, step):
-        ready, sent = lax.optimization_barrier((ready, [parts[k - 1] for k in turns[turn]]))
-        got = [permute(x, "exp", k) for k, x in zip(turns[turn], sent)]
-        done, got = lax.optimization_barrier((step(ready), got))
-        moved_parts.update(zip(turns[turn], got))
-        return ready, done
-
-    chunk, gathered = beside(
-        0, chunk, lambda c: [permute(c[k], "ctx", 2 * k) for k in range(1, chips)]
+    def beside(ready, sent, step, exchange):
+        ready, sent = lax.optimization_barrier((ready, sent))
+        return (ready, *lax.optimization_barrier((step(ready), exchange(sent))))
+
+    chunk, gathered, odd = beside(
+        chunk,
+        odd,
+        lambda c: [permute(c[k], "ctx", 2 * k) for k in range(1, chips)],
+        lambda x: permute(x, "exp", 1),
     )
     active = call(
         functools.partial(activate, n_ctx * features),
@@ -487,7 +495,16 @@
         [VMEM] * chips,
         vmem=8,
     )(chunk[0], *gathered)
-    active, gathered = beside(1, active, over_chips)
+    even = [
+        (x.astype(f32) + odd[k * tokens : (k + 1) * tokens].astype(f32)).astype(bf16)
+        for k, x in enumerate(even, 1)
+    ]
+    active, gathered, even = beside(
+        active,
+        even,
+        over_chips,
+        lambda xs: [permute(x, "exp", 2 * k) for k, x in enumerate(xs, 1)],
+    )
     active_same = jnp.concatenate([active] + gathered, axis=0)
     active_other = permute(active_same, "ctx", 1)
     cost = dict(flops=2 * expert_rows * hidden * columns, nbytes=2 * MIB)
@@ -506,13 +523,13 @@
         vmem=8,
         **cost,
     )(active_other, expert_out, made)
-    produced, returned = beside(2, produced, lambda x: over_exp(x[1:]))
+    returned = over_exp(produced[1:])
     mixed, expert_sum = call(
-        functools.partial(combine, n_exp),
+        combine,
         [shape((tokens, columns), bf16)] * 2,
-        [VMEM] * (2 + 2 * n_exp),
-        vmem=8,
-    )(high, low, own, *[moved_parts[k] for k in range(1, n_exp)], produced[0], *returned)
+        [VMEM] * (4 + n_exp + len(even)),
+        vmem=8,
+    )(high, low, own, odd, produced[0], *returned, *even)
     return (mixed, expert_sum)
 
 

time: 89.8 us -> 83.5 us (0.930)
  waiting for transfers between devices: 39.7 us -> 33.2 us
  starting transfers between devices: 33.7 us -> 34.7 us
    ppermute x28 -> x29, waiting for transfers between devices: 39.7 us -> 33.2 us  [permute(): return lax.ppermute(x, axis, [(i, i ^ k) for i in range(n)])]
    ppermute x28 -> x29, starting transfers between devices: 33.7 us -> 34.7 us  [permute(): return lax.ppermute(x, axis, [(i, i ^ k) for i in range(n)])]
    unnamed x21 -> x23, local copies, waits for them, and re-layouts: 3.02 us -> 2.08 us
    pallas_call x5 -> x6, Pallas kernels: 5.2 us -> 5.06 us  [the longest x1 1.88 us: body(): call(functools.partial(attend_second, span), [shape((span, rows // span *...]
  transfers between devices with their start and end apart: 28 -> 29, of which waited for: 18 -> 17; matrix products, arithmetic and copies ran while one was open for 0% -> 0% of each run, Pallas kernels for 5% -> 5%
where the time goes in v3:
time: 83.5 us; the launch traced here: 83.2 us
  starting transfers between devices  34.7 us (42%)
  waiting for transfers between devices  33.2 us (40%)
  Pallas kernels  11.1 us (13%)
  local copies, waits for them, and re-layouts  2.15 us (3%)
  other arithmetic  1.07 us (1%)
  between operations  0.95 us (1%)
    ppermute x29, starting transfers between devices, permute(): return lax.ppermute(x, axis, [(i, i ^ k) for i in range(n)])  34.7 us
    ppermute x29, waiting for transfers between devices, permute(): return lax.ppermute(x, axis, [(i, i ^ k) for i in range(n)])  33.2 us
    unnamed x23, local copies, waits for them, and re-layouts  2.08 us
    pallas_call x1, Pallas kernels, body(): call(functools.partial(attend_second, span), [shape((span, rows // span *...  1.88 us
    pallas_call x1, Pallas kernels, body(): call(functools.partial(attend_first, span), [shape((rows, HEAD), f32), sh...  1.77 us
  transfers between devices with their start and end apart: 29, of which 17 were waited for; matrix products, arithmetic and copies ran while one was open for 0% of the time, Pallas kernels for 5%

profile of v3, /device:TPU:0, one launch (start us, length us, event | category | flops | bytes accessed | tf_op | source)
XLA Modules:
  0.0 83.2 jit_solution(6993125452664220006)
XLA Ops:
  0.6 1.5 %shard_map.141 = bf16[192,256]{1,0:T(8,128)(2,1)} custom-call(bf16[128,512]{1,0:T(8,128)(2,1)} %ck.1, bf16[128,512]{1,0:T(8,128)(2,1)} %cv.1, bf16[64,512]{1,0:T(8,128)(2,1)} %bk.1, bf16[64,512]{1,0:T(8,128)(2,1)} %bv.1), custom_call_target="tpu_custom_call" | custom-call | tf_op jit(solution)/shard_map/pallas_call | solution.py:371
  2.2 3.0 %collective-permute-start = (bf16[192,256]{1,0:T(8,128)(2,1)}, bf16[192,256]{1,0:T(8,128)(2,1)S(1)}, u32[]{:S(2)}, u32[]{:S(2)}) collective-permute-start(bf16[192,256]{1,0:T(8,128)(2,1)} %shard_map.141), channel_id=1, source_target_pairs={{0,8},{4,12},{8,0},{12,4},{16,24},{20,28},{24,16},{28,20},{1,9},{5... | collective-permute-start | bytes 294920 | tf_op jit(solution)/shard_map/ppermute | solution.py:324
  5.2 1.5 %collective-permute-start.1 = (bf16[192,256]{1,0:T(8,128)(2,1)}, bf16[192,256]{1,0:T(8,128)(2,1)S(1)}, u32[]{:S(2)}, u32[]{:S(2)}) collective-permute-start(bf16[192,256]{1,0:T(8,128)(2,1)} %shard_map.141), channel_id=1, source_target_pairs={{0,16},{4,20},{8,24},{12,28},{16,0},{20,4},{24,8},{28,12},{1,17},{... | collective-permute-start | bytes 294920 | tf_op jit(solution)/shard_map/ppermute | solution.py:324
  9.7 1.3 %collective-permute-done.1 = bf16[192,256]{1,0:T(8,128)(2,1)S(1)} collective-permute-done((bf16[192,256]{1,0:T(8,128)(2,1)}, bf16[192,256]{1,0:T(8,128)(2,1)S(1)}, u32[]{:S(2)}, u32[]{:S(2)}) %collective-permute-start.1) | collective-permute-done | bytes 98336 | tf_op jit(solution)/shard_map/ppermute | solution.py:324
  11.0 1.4 %collective-permute-done.2 = bf16[192,256]{1,0:T(8,128)(2,1)S(1)} collective-permute-done((bf16[192,256]{1,0:T(8,128)(2,1)}, bf16[192,256]{1,0:T(8,128)(2,1)S(1)}, u32[]{:S(2)}, u32[]{:S(2)}) %collective-permute-start.2) | collective-permute-done | bytes 98336 | tf_op jit(solution)/shard_map/ppermute | solution.py:324
  13.4 1.8 %shard_map.143 = (f32[1024,128]{1,0:T(8,128)S(1)}, f32[1024,128]{1,0:T(8,128)S(1)}, f32[1024,128]{1,0:T(8,128)S(1)}) custom-call(bf16[1024,128]{1,0:T(8,128)(2,1)S(1)} %bitcast.13, bf16[768,256]{1,0:T(8,128)(2,1)S(1)} %pad_maximum_fusion.kv, f32[64,768]{1,0:T(8,128)S(1)} %get-tuple-element.71.bias), custom_call_target="tpu_custom_call" | custom-call | flops 402653184 | bytes 4194304 | tf_op jit(solution)/shard_map/pallas_call | solution.py:402
  15.2 1.9 %shard_map.144 = (bf16[64,1024]{1,0:T(8,128)(2,1)S(1)}, bf16[64,1024]{1,0:T(8,128)(2,1)S(1)}) custom-call(bf16[1024,128]{1,0:T(8,128)(2,1)S(1)} %bitcast.14, bf16[768,256]{1,0:T(8,128)(2,1)S(1)} %collective-permute-done.3.kv, f32[64,768]{1,0:T(8,128)S(1)} %get-tuple-element.70.bias, f32[1024,128]{1,0:T(8,128)S(1)} %get-tuple-element.72.o_in, ...), custom_call_target="tpu_custom_call" | custom-call | flops 402653184 | bytes 4194304 | tf_op jit(solution)/shard_map/pallas_call | solution.py:409
  18.7 1.7 %collective-permute-start.10 = (f32[8,128]{1,0:T(8,128)S(1)}, f32[8,128]{1,0:T(8,128)S(1)}, u32[]{:S(2)}, u32[]{:S(2)}) collective-permute-start(f32[8,128]{1,0:T(8,128)S(1)} %get-tuple-element.80), channel_id=1, source_target_pairs={{0,1},{1,0},{2,3},{3,2},{4,5},{5,4},{6,7},{7,6},{8,9},{9,8},{10,11... | collective-permute-start | bytes 12296 | tf_op jit(solution)/shard_map/ppermute | solution.py:324
  20.3 1.4 %collective-permute-start.5 = (bf16[64,1024]{1,0:T(8,128)(2,1)S(1)}, bf16[64,1024]{1,0:T(8,128)(2,1)S(1)}, u32[]{:S(2)}, u32[]{:S(2)}) collective-permute-start(bf16[64,1024]{1,0:T(8,128)(2,1)S(1)} %get-tuple-element.82), channel_id=1, source_target_pairs={{0,8},{4,12},{8,0},{12,4},{16,24},{20,28},{24,16},{28,20},{1,9},{5... | collective-permute-start | bytes 393224 | tf_op jit(solution)/shard_map/ppermute | solution.py:324
  21.7 1.1 %collective-permute-start.6 = (bf16[64,1024]{1,0:T(8,128)(2,1)S(1)}, bf16[64,1024]{1,0:T(8,128)(2,1)S(1)}, u32[]{:S(2)}, u32[]{:S(2)}) collective-permute-start(bf16[64,1024]{1,0:T(8,128)(2,1)S(1)} %get-tuple-element.81), channel_id=1, source_target_pairs={{0,16},{4,20},{8,24},{12,28},{16,0},{20,4},{24,8},{28,12},{1,17},{... | collective-permute-start | bytes 393224 | tf_op jit(solution)/shard_map/ppermute | solution.py:324
  25.2 2.6 %collective-permute-start.11 = (f32[16,128]{1,0:T(8,128)S(1)}, f32[16,128]{1,0:T(8,128)S(1)}, u32[]{:S(2)}, u32[]{:S(2)}) collective-permute-start(f32[16,128]{1,0:T(8,128)S(1)} %pad_maximum_fusion.2), channel_id=1, source_target_pairs={{0,2},{1,3},{2,0},{3,1},{4,6},{5,7},{6,4},{7,5},{8,10},{9,11},{10,... | collective-permute-start | bytes 24584 | tf_op jit(solution)/shard_map/ppermute | solution.py:324
  27.8 1.9 %collective-permute-done.11 = f32[16,128]{1,0:T(8,128)S(1)} collective-permute-done((f32[16,128]{1,0:T(8,128)S(1)}, f32[16,128]{1,0:T(8,128)S(1)}, u32[]{:S(2)}, u32[]{:S(2)}) %collective-permute-start.11) | collective-permute-done | bytes 8224 | tf_op jit(solution)/shard_map/ppermute | solution.py:324
  30.7 1.9 %collective-permute-done.12.heads_out = bf16[256,2048]{1,0:T(8,128)(2,1)S(1)} collective-permute-done((bf16[256,2048]{1,0:T(8,128)(2,1)S(1)}, bf16[256,2048]{1,0:T(8,128)(2,1)S(1)}, u32[]{:S(2)}, u32[]{:S(2)}) %collective-permute-start.12) | collective-permute-done | bytes 1048608 | tf_op jit(solution)/shard_map/ppermute | solution.py:324
  32.6 1.1 %shard_map.146 = (f32[128,512]{1,0:T(8,128)S(1)}, bf16[256,512]{1,0:T(8,128)(2,1)S(1)}, bf16[128,512]{1,0:T(8,128)(2,1)S(1)}, bf16[128,512]{1,0:T(8,128)(2,1)S(1...) custom-call(bf16[256,2048]{1,0:T(8,128)(2,1)S(1)} %collective-permute-done.12.heads_out,, ...), custom_call_target="tpu_custom_call" | custom-call | flops 536870912 | bytes 4194304 | tf_op jit(solution)/shard_map/pallas_call | solution.py:437
  33.7 2.0 %collective-permute-start.14 = (bf16[128,512]{1,0:T(8,128)(2,1)S(1)}, bf16[128,512]{1,0:T(8,128)(2,1)S(1)}, u32[]{:S(2)}, u32[]{:S(2)}) collective-permute-start(bf16[128,512]{1,0:T(8,128)(2,1)S(1)} %get-tuple-element.94), channel_id=1, source_target_pairs={{0,1},{1,0},{2,3},{3,2},{4,5},{5,4},{6,7},{7,6},{8,9},{9,8},{10,11... | collective-permute-start | bytes 393224 | tf_op jit(solution)/shard_map/ppermute | solution.py:324
  35.8 4.3 %collective-permute-done.14 = bf16[128,512]{1,0:T(8,128)(2,1)S(1)} collective-permute-done((bf16[128,512]{1,0:T(8,128)(2,1)S(1)}, bf16[128,512]{1,0:T(8,128)(2,1)S(1)}, u32[]{:S(2)}, u32[]{:S(2)}) %collective-permute-start.14) | collective-permute-done | bytes 131104 | tf_op jit(solution)/shard_map/ppermute | solution.py:324
  40.1 2.7 %collective-permute-start.15 = (bf16[128,512]{1,0:T(8,128)(2,1)S(1)}, bf16[128,512]{1,0:T(8,128)(2,1)S(1)}, u32[]{:S(2)}, u32[]{:S(2)}) collective-permute-start(bf16[128,512]{1,0:T(8,128)(2,1)S(1)} %add_convert_fusion.1), channel_id=1, source_target_pairs={{0,2},{1,3},{2,0},{3,1},{4,6},{5,7},{6,4},{7,5},{8,10},{9,11},{10,... | collective-permute-start | bytes 393224 | tf_op jit(solution)/shard_map/ppermute | solution.py:324
  42.8 5.6 %collective-permute-done.15.refs_2_ = bf16[128,512]{1,0:T(8,128)(2,1)S(1)} collective-permute-done((bf16[128,512]{1,0:T(8,128)(2,1)S(1)}, bf16[128,512]{1,0:T(8,128)(2,1)S(1)}, u32[]{:S(2)}, u32[]{:S(2)}) %collective-permute-start.15) | collective-permute-done | bytes 131104 | tf_op jit(solution)/shard_map/ppermute | solution.py:324
  49.9 1.0 %collective-permute-done.16.theirs = bf16[64,3200]{1,0:T(8,128)(2,1)S(1)} collective-permute-done((bf16[64,3200]{1,0:T(8,128)(2,1)S(1)}, bf16[64,3200]{1,0:T(8,128)(2,1)S(1)}, u32[]{:S(2)}, u32[]{:S(2)}) %collective-permute-start.16) | collective-permute-done | bytes 409632 | tf_op jit(solution)/shard_map/ppermute | solution.py:324
  52.3 1.3 %collective-permute-start.18 = (bf16[16,3200]{1,0:T(8,128)(2,1)S(1)}, bf16[16,3200]{1,0:T(8,128)(2,1)S(1)}, u32[]{:S(2)}, u32[]{:S(2)}) collective-permute-start(bf16[16,3200]{1,0:T(8,128)(2,1)S(1)} %get-tuple-element.101), channel_id=1, source_target_pairs={{0,16},{4,20},{8,24},{12,28},{16,0},{20,4},{24,8},{28,12},{1,17},{... | collective-permute-start | bytes 307208 | tf_op jit(solution)/shard_map/ppermute | solution.py:324
  53.5 1.5 %collective-permute-start.19 = (bf16[16,3200]{1,0:T(8,128)(2,1)S(1)}, bf16[16,3200]{1,0:T(8,128)(2,1)S(1)}, u32[]{:S(2)}, u32[]{:S(2)}) collective-permute-start(bf16[16,3200]{1,0:T(8,128)(2,1)S(1)} %get-tuple-element.102), channel_id=1, source_target_pairs={{0,24},{4,28},{8,16},{12,20},{16,8},{20,12},{24,0},{28,4},{1,25},{... | collective-permute-start | bytes 307208 | tf_op jit(solution)/shard_map/ppermute | solution.py:324
  55.0 1.6 %collective-permute-done.17.refs_1_ = bf16[16,3200]{1,0:T(8,128)(2,1)S(1)} collective-permute-done((bf16[16,3200]{1,0:T(8,128)(2,1)S(1)}, bf16[16,3200]{1,0:T(8,128)(2,1)S(1)}, u32[]{:S(2)}, u32[]{:S(2)}) %collective-permute-start.17) | collective-permute-done | bytes 102432 | tf_op jit(solution)/shard_map/ppermute | solution.py:324
  56.7 1.8 %collective-permute-done.18.refs_2_ = bf16[16,3200]{1,0:T(8,128)(2,1)S(1)} collective-permute-done((bf16[16,3200]{1,0:T(8,128)(2,1)S(1)}, bf16[16,3200]{1,0:T(8,128)(2,1)S(1)}, u32[]{:S(2)}, u32[]{:S(2)}) %collective-permute-start.18) | collective-permute-done | bytes 102432 | tf_op jit(solution)/shard_map/ppermute | solution.py:324
  59.6 1.0 %collective-permute-start.21 = (bf16[16,1536]{1,0:T(8,128)(2,1)S(1)}, bf16[16,1536]{1,0:T(8,128)(2,1)S(1)}, u32[]{:S(2)}, u32[]{:S(2)}) collective-permute-start(bf16[16,1536]{1,0:T(8,128)(2,1)S(1)} %shard_map.150), channel_id=1, source_target_pairs={{0,8},{4,12},{8,0},{12,4},{16,24},{20,28},{24,16},{28,20},{1,9},{5... | collective-permute-start | bytes 147464 | tf_op jit(solution)/shard_map/ppermute | solution.py:324
  60.6 1.2 %collective-permute-start.22 = (bf16[16,1536]{1,0:T(8,128)(2,1)S(1)}, bf16[16,1536]{1,0:T(8,128)(2,1)S(1)}, u32[]{:S(2)}, u32[]{:S(2)}) collective-permute-start(bf16[16,1536]{1,0:T(8,128)(2,1)S(1)} %shard_map.150), channel_id=1, source_target_pairs={{0,16},{4,20},{8,24},{12,28},{16,0},{20,4},{24,8},{28,12},{1,17},{... | collective-permute-start | bytes 147464 | tf_op jit(solution)/shard_map/ppermute | solution.py:324
  61.8 1.3 %collective-permute-start.23 = (bf16[16,1536]{1,0:T(8,128)(2,1)S(1)}, bf16[16,1536]{1,0:T(8,128)(2,1)S(1)}, u32[]{:S(2)}, u32[]{:S(2)}) collective-permute-start(bf16[16,1536]{1,0:T(8,128)(2,1)S(1)} %shard_map.150), channel_id=1, source_target_pairs={{0,24},{4,28},{8,16},{12,20},{16,8},{20,12},{24,0},{28,4},{1,25},{... | collective-permute-start | bytes 147464 | tf_op jit(solution)/shard_map/ppermute | solution.py:324
  63.1 3.1 %collective-permute-start.24 = (bf16[128,512]{1,0:T(8,128)(2,1)S(1)}, bf16[128,512]{1,0:T(8,128)(2,1)S(1)}, u32[]{:S(2)}, u32[]{:S(2)}) collective-permute-start(bf16[128,512]{1,0:T(8,128)(2,1)S(1)} %add_convert_fusion), channel_id=1, source_target_pairs={{0,2},{1,3},{2,0},{3,1},{4,6},{5,7},{6,4},{7,5},{8,10},{9,11},{10,... | collective-permute-start | bytes 393224 | tf_op jit(solution)/shard_map/ppermute | solution.py:324
  66.8 3.9 %collective-permute-done.24.refs_4_ = bf16[128,512]{1,0:T(8,128)(2,1)S(1)} collective-permute-done((bf16[128,512]{1,0:T(8,128)(2,1)S(1)}, bf16[128,512]{1,0:T(8,128)(2,1)S(1)}, u32[]{:S(2)}, u32[]{:S(2)}) %collective-permute-start.24) | collective-permute-done | bytes 131104 | tf_op jit(solution)/shard_map/ppermute | solution.py:324
  71.2 1.0 %collective-permute-done.25.active = bf16[64,1536]{1,0:T(8,128)(2,1)S(1)} collective-permute-done((bf16[64,1536]{1,0:T(8,128)(2,1)S(1)}, bf16[64,1536]{1,0:T(8,128)(2,1)S(1)}, u32[]{:S(2)}, u32[]{:S(2)}) %collective-permute-start.25) | collective-permute-done | bytes 196640 | tf_op jit(solution)/shard_map/ppermute | solution.py:324
  73.2 3.4 %collective-permute-start.27 = (bf16[32,512]{1,0:T(8,128)(2,1)S(1)}, bf16[32,512]{1,0:T(8,128)(2,1)S(1)}, u32[]{:S(2)}, u32[]{:S(2)}) collective-permute-start(bf16[32,512]{1,0:T(8,128)(2,1)S(1)} %get-tuple-element.117), channel_id=1, source_target_pairs={{0,2},{1,3},{2,0},{3,1},{4,6},{5,7},{6,4},{7,5},{8,10},{9,11},{10,... | collective-permute-start | bytes 98312 | tf_op jit(solution)/shard_map/ppermute | solution.py:324
  77.1 1.4 %collective-permute-done.27.refs_2_ = bf16[32,512]{1,0:T(8,128)(2,1)S(1)} collective-permute-done((bf16[32,512]{1,0:T(8,128)(2,1)S(1)}, bf16[32,512]{1,0:T(8,128)(2,1)S(1)}, u32[]{:S(2)}, u32[]{:S(2)}) %collective-permute-start.27) | collective-permute-done | bytes 32800 | tf_op jit(solution)/shard_map/ppermute | solution.py:324
  78.5 3.7 %collective-permute-done.28.refs_3_ = bf16[32,512]{1,0:T(8,128)(2,1)S(1)} collective-permute-done((bf16[32,512]{1,0:T(8,128)(2,1)S(1)}, bf16[32,512]{1,0:T(8,128)(2,1)S(1)}, u32[]{:S(2)}, u32[]{:S(2)}) %collective-permute-start.28) | collective-permute-done | bytes 32800 | tf_op jit(solution)/shard_map/ppermute | solution.py:324
  (72 shorter events, 16.4 us)
Async XLA Ops:
  2.2 7.6 %collective-permute-start = (bf16[192,256]{1,0:T(8,128)(2,1)}, bf16[192,256]{1,0:T(8,128)(2,1)S(1)}, u32[]{:S(2)}, u32[]{:S(2)}) collective-permute-start(bf16[192,256]{1,0:T(8,128)(2,1)} %shard_map.141), channel_id=1, source_target_pairs={{0,8},{4,12},{8,0},{12,4},{16,24},{20,28},{24,16},{28,20},{1,9},{5... | collective-permute-start | bytes 294920 | tf_op jit(solution)/shard_map/ppermute | solution.py:324
  5.2 5.9 %collective-permute-start.1 = (bf16[192,256]{1,0:T(8,128)(2,1)}, bf16[192,256]{1,0:T(8,128)(2,1)S(1)}, u32[]{:S(2)}, u32[]{:S(2)}) collective-permute-start(bf16[192,256]{1,0:T(8,128)(2,1)} %shard_map.141), channel_id=1, source_target_pairs={{0,16},{4,20},{8,24},{12,28},{16,0},{20,4},{24,8},{28,12},{1,17},{... | collective-permute-start | bytes 294920 | tf_op jit(solution)/shard_map/ppermute | solution.py:324
  6.7 5.7 %collective-permute-start.2 = (bf16[192,256]{1,0:T(8,128)(2,1)}, bf16[192,256]{1,0:T(8,128)(2,1)S(1)}, u32[]{:S(2)}, u32[]{:S(2)}) collective-permute-start(bf16[192,256]{1,0:T(8,128)(2,1)} %shard_map.141), channel_id=1, source_target_pairs={{0,24},{4,28},{8,16},{12,20},{16,8},{20,12},{24,0},{28,4},{1,25},{... | collective-permute-start | bytes 294920 | tf_op jit(solution)/shard_map/ppermute | solution.py:324
  13.3 1.9 %collective-permute-start.3 = (bf16[768,256]{1,0:T(8,128)(2,1)S(1)}, bf16[768,256]{1,0:T(8,128)(2,1)S(1)}, u32[]{:S(2)}, u32[]{:S(2)}) collective-permute-start(bf16[768,256]{1,0:T(8,128)(2,1)S(1)} %pad_maximum_fusion.kv), channel_id=1, source_target_pairs={{0,4},{4,0},{8,12},{12,8},{16,20},{20,16},{24,28},{28,24},{1,5},{5... | collective-permute-start | bytes 1179656 | tf_op jit(solution)/shard_map/ppermute | solution.py:324
  15.2 33.2 %slice-start = ((s8[6291456]{0:T(1024)(128)(4,1)}), s8[4194304]{0:T(1024)(128)(4,1)S(1)}, s32[]{:S(2)}) async-start(s8[6291456]{0:T(1024)(128)(4,1)} %bitcast.11), calls=%async_computation | async-start | bytes 8388608
  17.1 6.4 %collective-permute-start.4 = (bf16[64,1024]{1,0:T(8,128)(2,1)S(1)}, bf16[64,1024]{1,0:T(8,128)(2,1)S(1)}, u32[]{:S(2)}, u32[]{:S(2)}) collective-permute-start(bf16[64,1024]{1,0:T(8,128)(2,1)S(1)} %get-tuple-element.81), channel_id=1, source_target_pairs={{0,8},{4,12},{8,0},{12,4},{16,24},{20,28},{24,16},{28,20},{1,9},{5... | collective-permute-start | bytes 393224 | tf_op jit(solution)/shard_map/ppermute | solution.py:324
  17.8 6.4 %collective-permute-start.7 = (bf16[64,1024]{1,0:T(8,128)(2,1)S(1)}, bf16[64,1024]{1,0:T(8,128)(2,1)S(1)}, u32[]{:S(2)}, u32[]{:S(2)}) collective-permute-start(bf16[64,1024]{1,0:T(8,128)(2,1)S(1)} %get-tuple-element.82), channel_id=1, source_target_pairs={{0,16},{4,20},{8,24},{12,28},{16,0},{20,4},{24,8},{28,12},{1,17},{... | collective-permute-start | bytes 393224 | tf_op jit(solution)/shard_map/ppermute | solution.py:324
  18.7 6.5 %collective-permute-start.10 = (f32[8,128]{1,0:T(8,128)S(1)}, f32[8,128]{1,0:T(8,128)S(1)}, u32[]{:S(2)}, u32[]{:S(2)}) collective-permute-start(f32[8,128]{1,0:T(8,128)S(1)} %get-tuple-element.80), channel_id=1, source_target_pairs={{0,1},{1,0},{2,3},{3,2},{4,5},{5,4},{6,7},{7,6},{8,9},{9,8},{10,11... | collective-permute-start | bytes 12296 | tf_op jit(solution)/shard_map/ppermute | solution.py:324
  20.3 9.4 %collective-permute-start.5 = (bf16[64,1024]{1,0:T(8,128)(2,1)S(1)}, bf16[64,1024]{1,0:T(8,128)(2,1)S(1)}, u32[]{:S(2)}, u32[]{:S(2)}) collective-permute-start(bf16[64,1024]{1,0:T(8,128)(2,1)S(1)} %get-tuple-element.82), channel_id=1, source_target_pairs={{0,8},{4,12},{8,0},{12,4},{16,24},{20,28},{24,16},{28,20},{1,9},{5... | collective-permute-start | bytes 393224 | tf_op jit(solution)/shard_map/ppermute | solution.py:324
  21.7 8.1 %collective-permute-start.6 = (bf16[64,1024]{1,0:T(8,128)(2,1)S(1)}, bf16[64,1024]{1,0:T(8,128)(2,1)S(1)}, u32[]{:S(2)}, u32[]{:S(2)}) collective-permute-start(bf16[64,1024]{1,0:T(8,128)(2,1)S(1)} %get-tuple-element.81), channel_id=1, source_target_pairs={{0,16},{4,20},{8,24},{12,28},{16,0},{20,4},{24,8},{28,12},{1,17},{... | collective-permute-start | bytes 393224 | tf_op jit(solution)/shard_map/ppermute | solution.py:324
  23.5 6.3 %collective-permute-start.8 = (bf16[64,1024]{1,0:T(8,128)(2,1)S(1)}, bf16[64,1024]{1,0:T(8,128)(2,1)S(1)}, u32[]{:S(2)}, u32[]{:S(2)}) collective-permute-start(bf16[64,1024]{1,0:T(8,128)(2,1)S(1)} %collective-permute-done.4), channel_id=1, source_target_pairs={{0,16},{4,20},{8,24},{12,28},{16,0},{20,4},{24,8},{28,12},{1,17},{... | collective-permute-start | bytes 393224 | tf_op jit(solution)/shard_map/ppermute | solution.py:324
  24.2 5.6 %collective-permute-start.9 = (bf16[64,1024]{1,0:T(8,128)(2,1)S(1)}, bf16[64,1024]{1,0:T(8,128)(2,1)S(1)}, u32[]{:S(2)}, u32[]{:S(2)}) collective-permute-start(bf16[64,1024]{1,0:T(8,128)(2,1)S(1)} %collective-permute-done.7), channel_id=1, source_target_pairs={{0,8},{4,12},{8,0},{12,4},{16,24},{20,28},{24,16},{28,20},{1,9},{5... | collective-permute-start | bytes 393224 | tf_op jit(solution)/shard_map/ppermute | solution.py:324
  25.2 4.6 %collective-permute-start.11 = (f32[16,128]{1,0:T(8,128)S(1)}, f32[16,128]{1,0:T(8,128)S(1)}, u32[]{:S(2)}, u32[]{:S(2)}) collective-permute-start(f32[16,128]{1,0:T(8,128)S(1)} %pad_maximum_fusion.2), channel_id=1, source_target_pairs={{0,2},{1,3},{2,0},{3,1},{4,6},{5,7},{6,4},{7,5},{8,10},{9,11},{10,... | collective-permute-start | bytes 24584 | tf_op jit(solution)/shard_map/ppermute | solution.py:324
  29.9 18.5 %slice-start.1 = ((s8[6291456]{0:T(1024)(128)(4,1)}), s8[2097152]{0:T(1024)(128)(4,1)S(1)}, s32[]{:S(2)}) async-start(s8[6291456]{0:T(1024)(128)(4,1)} %bitcast.11), calls=%async_computation.1 | async-start | bytes 4194304
  29.9 2.7 %collective-permute-start.12 = (bf16[256,2048]{1,0:T(8,128)(2,1)S(1)}, bf16[256,2048]{1,0:T(8,128)(2,1)S(1)}, u32[]{:S(2)}, u32[]{:S(2)}) collective-permute-start(bf16[256,2048]{1,0:T(8,128)(2,1)S(1)} %maximum_maximum_fusion.heads_out), channel_id=1, source_target_pairs={{0,4},{4,0},{8,12},{12,8},{16,20},{20,16},{24,28},{28,24},{1,5},{5... | collective-permute-start | bytes 3145736 | tf_op jit(solution)/shard_map/ppermute | solution.py:324
  33.7 6.4 %collective-permute-start.14 = (bf16[128,512]{1,0:T(8,128)(2,1)S(1)}, bf16[128,512]{1,0:T(8,128)(2,1)S(1)}, u32[]{:S(2)}, u32[]{:S(2)}) collective-permute-start(bf16[128,512]{1,0:T(8,128)(2,1)S(1)} %get-tuple-element.94), channel_id=1, source_target_pairs={{0,1},{1,0},{2,3},{3,2},{4,5},{5,4},{6,7},{7,6},{8,9},{9,8},{10,11... | collective-permute-start | bytes 393224 | tf_op jit(solution)/shard_map/ppermute | solution.py:324
  35.7 7.1 %collective-permute-start.13 = (bf16[128,512]{1,0:T(8,128)(2,1)S(1)}, bf16[128,512]{1,0:T(8,128)(2,1)S(1)}, u32[]{:S(2)}, u32[]{:S(2)}) collective-permute-start(bf16[128,512]{1,0:T(8,128)(2,1)S(1)} %get-tuple-element.92), channel_id=1, source_target_pairs={{0,1},{1,0},{2,3},{3,2},{4,5},{5,4},{6,7},{7,6},{8,9},{9,8},{10,11... | collective-permute-start | bytes 393224 | tf_op jit(solution)/shard_map/ppermute | solution.py:324
  40.1 8.2 %collective-permute-start.15 = (bf16[128,512]{1,0:T(8,128)(2,1)S(1)}, bf16[128,512]{1,0:T(8,128)(2,1)S(1)}, u32[]{:S(2)}, u32[]{:S(2)}) collective-permute-start(bf16[128,512]{1,0:T(8,128)(2,1)S(1)} %add_convert_fusion.1), channel_id=1, source_target_pairs={{0,2},{1,3},{2,0},{3,1},{4,6},{5,7},{6,4},{7,5},{8,10},{9,11},{10,... | collective-permute-start | bytes 393224 | tf_op jit(solution)/shard_map/ppermute | solution.py:324
  49.1 1.8 %collective-permute-start.16 = (bf16[64,3200]{1,0:T(8,128)(2,1)S(1)}, bf16[64,3200]{1,0:T(8,128)(2,1)S(1)}, u32[]{:S(2)}, u32[]{:S(2)}) collective-permute-start(bf16[64,3200]{1,0:T(8,128)(2,1)S(1)} %shard_map.148), channel_id=1, source_target_pairs={{0,4},{4,0},{8,12},{12,8},{16,20},{20,16},{24,28},{28,24},{1,5},{5... | collective-permute-start | bytes 1228808 | tf_op jit(solution)/shard_map/ppermute | solution.py:324
  49.2 21.7 %copy-start.1 = (bf16[2,1536,512]{2,1,0:T(8,128)(2,1)S(1)}, bf16[2,1536,512]{2,1,0:T(8,128)(2,1)}, u32[]{:S(2)}) copy-start(bf16[2,1536,512]{2,1,0:T(8,128)(2,1)} %weight.7) | copy-start | bytes 9437188
  51.0 8.4 %collective-permute-start.20 = (bf16[256,512]{1,0:T(8,128)(2,1)S(1)}, bf16[256,512]{1,0:T(8,128)(2,1)S(1)}, u32[]{:S(2)}, u32[]{:S(2)}) collective-permute-start(bf16[256,512]{1,0:T(8,128)(2,1)S(1)} %get-tuple-element.103), channel_id=1, source_target_pairs={{0,1},{1,0},{2,3},{3,2},{4,5},{5,4},{6,7},{7,6},{8,9},{9,8},{10,11... | collective-permute-start | bytes 786440 | tf_op jit(solution)/shard_map/ppermute | solution.py:324
  51.5 5.1 %collective-permute-start.17 = (bf16[16,3200]{1,0:T(8,128)(2,1)S(1)}, bf16[16,3200]{1,0:T(8,128)(2,1)S(1)}, u32[]{:S(2)}, u32[]{:S(2)}) collective-permute-start(bf16[16,3200]{1,0:T(8,128)(2,1)S(1)} %get-tuple-element.100), channel_id=1, source_target_pairs={{0,8},{4,12},{8,0},{12,4},{16,24},{20,28},{24,16},{28,20},{1,9},{5... | collective-permute-start | bytes 307208 | tf_op jit(solution)/shard_map/ppermute | solution.py:324
  52.3 6.2 %collective-permute-start.18 = (bf16[16,3200]{1,0:T(8,128)(2,1)S(1)}, bf16[16,3200]{1,0:T(8,128)(2,1)S(1)}, u32[]{:S(2)}, u32[]{:S(2)}) collective-permute-start(bf16[16,3200]{1,0:T(8,128)(2,1)S(1)} %get-tuple-element.101), channel_id=1, source_target_pairs={{0,16},{4,20},{8,24},{12,28},{16,0},{20,4},{24,8},{28,12},{1,17},{... | collective-permute-start | bytes 307208 | tf_op jit(solution)/shard_map/ppermute | solution.py:324
  53.5 5.6 %collective-permute-start.19 = (bf16[16,3200]{1,0:T(8,128)(2,1)S(1)}, bf16[16,3200]{1,0:T(8,128)(2,1)S(1)}, u32[]{:S(2)}, u32[]{:S(2)}) collective-permute-start(bf16[16,3200]{1,0:T(8,128)(2,1)S(1)} %get-tuple-element.102), channel_id=1, source_target_pairs={{0,24},{4,28},{8,16},{12,20},{16,8},{20,12},{24,0},{28,4},{1,25},{... | collective-permute-start | bytes 307208 | tf_op jit(solution)/shard_map/ppermute | solution.py:324
  59.6 6.6 %collective-permute-start.21 = (bf16[16,1536]{1,0:T(8,128)(2,1)S(1)}, bf16[16,1536]{1,0:T(8,128)(2,1)S(1)}, u32[]{:S(2)}, u32[]{:S(2)}) collective-permute-start(bf16[16,1536]{1,0:T(8,128)(2,1)S(1)} %shard_map.150), channel_id=1, source_target_pairs={{0,8},{4,12},{8,0},{12,4},{16,24},{20,28},{24,16},{28,20},{1,9},{5... | collective-permute-start | bytes 147464 | tf_op jit(solution)/shard_map/ppermute | solution.py:324
  60.6 5.6 %collective-permute-start.22 = (bf16[16,1536]{1,0:T(8,128)(2,1)S(1)}, bf16[16,1536]{1,0:T(8,128)(2,1)S(1)}, u32[]{:S(2)}, u32[]{:S(2)}) collective-permute-start(bf16[16,1536]{1,0:T(8,128)(2,1)S(1)} %shard_map.150), channel_id=1, source_target_pairs={{0,16},{4,20},{8,24},{12,28},{16,0},{20,4},{24,8},{28,12},{1,17},{... | collective-permute-start | bytes 147464 | tf_op jit(solution)/shard_map/ppermute | solution.py:324
  61.8 5.0 %collective-permute-start.23 = (bf16[16,1536]{1,0:T(8,128)(2,1)S(1)}, bf16[16,1536]{1,0:T(8,128)(2,1)S(1)}, u32[]{:S(2)}, u32[]{:S(2)}) collective-permute-start(bf16[16,1536]{1,0:T(8,128)(2,1)S(1)} %shard_map.150), channel_id=1, source_target_pairs={{0,24},{4,28},{8,16},{12,20},{16,8},{20,12},{24,0},{28,4},{1,25},{... | collective-permute-start | bytes 147464 | tf_op jit(solution)/shard_map/ppermute | solution.py:324
  63.1 7.6 %collective-permute-start.24 = (bf16[128,512]{1,0:T(8,128)(2,1)S(1)}, bf16[128,512]{1,0:T(8,128)(2,1)S(1)}, u32[]{:S(2)}, u32[]{:S(2)}) collective-permute-start(bf16[128,512]{1,0:T(8,128)(2,1)S(1)} %add_convert_fusion), channel_id=1, source_target_pairs={{0,2},{1,3},{2,0},{3,1},{4,6},{5,7},{6,4},{7,5},{8,10},{9,11},{10,... | collective-permute-start | bytes 393224 | tf_op jit(solution)/shard_map/ppermute | solution.py:324
  70.8 1.5 %collective-permute-start.25 = (bf16[64,1536]{1,0:T(8,128)(2,1)S(1)}, bf16[64,1536]{1,0:T(8,128)(2,1)S(1)}, u32[]{:S(2)}, u32[]{:S(2)}) collective-permute-start(bf16[64,1536]{1,0:T(8,128)(2,1)S(1)} %constant_dynamic-update-slice_fusion.active), channel_id=1, source_target_pairs={{0,4},{4,0},{8,12},{12,8},{16,20},{20,16},{24,28},{28,24},{1,5},{5... | collective-permute-start | bytes 589832 | tf_op jit(solution)/shard_map/ppermute | solution.py:324
  72.7 4.5 %collective-permute-start.26 = (bf16[32,512]{1,0:T(8,128)(2,1)S(1)}, bf16[32,512]{1,0:T(8,128)(2,1)S(1)}, u32[]{:S(2)}, u32[]{:S(2)}) collective-permute-start(bf16[32,512]{1,0:T(8,128)(2,1)S(1)} %get-tuple-element.116), channel_id=1, source_target_pairs={{0,1},{1,0},{2,3},{3,2},{4,5},{5,4},{6,7},{7,6},{8,9},{9,8},{10,11... | collective-permute-start | bytes 98312 | tf_op jit(solution)/shard_map/ppermute | solution.py:324
  73.2 5.3 %collective-permute-start.27 = (bf16[32,512]{1,0:T(8,128)(2,1)S(1)}, bf16[32,512]{1,0:T(8,128)(2,1)S(1)}, u32[]{:S(2)}, u32[]{:S(2)}) collective-permute-start(bf16[32,512]{1,0:T(8,128)(2,1)S(1)} %get-tuple-element.117), channel_id=1, source_target_pairs={{0,2},{1,3},{2,0},{3,1},{4,6},{5,7},{6,4},{7,5},{8,10},{9,11},{10,... | collective-permute-start | bytes 98312 | tf_op jit(solution)/shard_map/ppermute | solution.py:324
  76.6 5.7 %collective-permute-start.28 = (bf16[32,512]{1,0:T(8,128)(2,1)S(1)}, bf16[32,512]{1,0:T(8,128)(2,1)S(1)}, u32[]{:S(2)}, u32[]{:S(2)}) collective-permute-start(bf16[32,512]{1,0:T(8,128)(2,1)S(1)} %get-tuple-element.118), channel_id=1, source_target_pairs={{0,3},{1,2},{2,1},{3,0},{4,7},{5,6},{6,5},{7,4},{8,11},{9,10},{10,... | collective-permute-start | bytes 98312 | tf_op jit(solution)/shard_map/ppermute | solution.py:324
  (7 other events, 43.4 us)

commit v4 on v3

--- a/solution.py
+++ b/solution.py
@@ -103,7 +103,8 @@
     return jnp.where(seen, 0.0, neg_large)
 
 
-def mask_kernel(span, cache, seg_starts, bias_same, bias_other):
+def mask_kernel(span, cache, seg_starts, kv, bias_same, bias_other, kv_copy):
+    kv_copy[...] = kv[...]
     pieces = bias_same.shape[1] // (cache + span)
     bias_same[...] = mask_bias(seg_starts, 0, span, cache, pieces)
     bias_other[...] = mask_bias(seg_starts, 1, span, cache, pieces)
@@ -378,24 +379,25 @@
     kv_moved = over_chips(local_kv)
 
     rows, keys = heads * span, chips * (cache + span)
-    bias_same, bias_other = call(
+    bias_same, bias_other, own_kv = call(
         functools.partial(mask_kernel, span, cache),
-        [shape((span, keys), f32)] * 2,
-        [SMEM],
-        vmem=8,
-        nbytes=MIB,
-    )(seg_starts)
+        [shape((span, keys), f32)] * 2 + [shape(local_kv.shape, bf16)],
+        [SMEM, VMEM],
+        vmem=8,
+        nbytes=1 * MIB,
+    )(seg_starts, local_kv)
     stacked = queries.reshape(span, heads, HEAD).transpose(1, 0, 2).reshape(rows, HEAD)
     rank, high, low = call(
         functools.partial(route_kernel, n_exp),
         [shape((flight, tokens), f32)] + [shape((flight * CAP, tokens), bf16)] * 2,
         [VMEM] * 2,
         vmem=8,
+        nbytes=1 * MIB,
     )(routes.T, gate_values.T)
-    kv_moved, stacked, bias_same, bias_other, rank = lax.optimization_barrier(
-        (kv_moved, stacked, bias_same, bias_other, rank)
-    )
-    kv_same = jnp.concatenate([local_kv] + kv_moved, axis=0)
+    kv_moved, stacked, bias_same, bias_other, own_kv, rank = lax.optimization_barrier(
+        (kv_moved, stacked, bias_same, bias_other, own_kv, rank)
+    )
+    kv_same = jnp.concatenate([own_kv] + kv_moved, axis=0)
     kv_other = permute(kv_same, "ctx", 1)
 
     cost = dict(flops=4 * rows * keys * HEAD, nbytes=4 * MIB)
@@ -499,12 +501,8 @@
         (x.astype(f32) + odd[k * tokens : (k + 1) * tokens].astype(f32)).astype(bf16)
         for k, x in enumerate(even, 1)
     ]
-    active, gathered, even = beside(
-        active,
-        even,
-        over_chips,
-        lambda xs: [permute(x, "exp", 2 * k) for k, x in enumerate(xs, 1)],
-    )
+    even = [permute(x, "exp", 2 * k) for k, x in enumerate(even, 1)]
+    gathered, even = lax.optimization_barrier((over_chips(active), even))
     active_same = jnp.concatenate([active] + gathered, axis=0)
     active_other = permute(active_same, "ctx", 1)
     cost = dict(flops=2 * expert_rows * hidden * columns, nbytes=2 * MIB)

time: 83.5 us -> 79.9 us (0.957)
  waiting for transfers between devices: 33.2 us -> 29.3 us
  local copies, waits for them, and re-layouts: 2.15 us -> 3.07 us
  other arithmetic: 1.07 us -> 0.16 us
    ppermute x29, waiting for transfers between devices: 33.2 us -> 29.3 us  [permute(): return lax.ppermute(x, axis, [(i, i ^ k) for i in range(n)])]
    unnamed x23 -> x25, local copies, waits for them, and re-layouts: 2.08 us -> 3 us
    concatenate x1, other arithmetic: 0.92 us -> 0.01 us  [body(): active_same = jnp.concatenate([active] + gathered, axis=0)]
  transfers between devices with their start and end apart: 29 -> 29, of which waited for: 17 -> 17; matrix products, arithmetic and copies ran while one was open for 0% -> 0% of each run, Pallas kernels for 5% -> 6%
where the time goes in v4:
time: 79.9 us; the launch traced here: 79.6 us
  starting transfers between devices  35 us (44%)
  waiting for transfers between devices  29.3 us (37%)
  Pallas kernels  11.1 us (14%)
  local copies, waits for them, and re-layouts  3.07 us (4%)
  between operations  0.97 us (1%)
    ppermute x29, starting transfers between devices, permute(): return lax.ppermute(x, axis, [(i, i ^ k) for i in range(n)])  35 us
    ppermute x29, waiting for transfers between devices, permute(): return lax.ppermute(x, axis, [(i, i ^ k) for i in range(n)])  29.3 us
    unnamed x25, local copies, waits for them, and re-layouts  3 us
    pallas_call x1, Pallas kernels, body(): call(functools.partial(attend_second, span), [shape((span, rows // span *...  1.88 us
    pallas_call x1, Pallas kernels, body(): call(functools.partial(attend_first, span), [shape((rows, HEAD), f32), sh...  1.77 us
  transfers between devices with their start and end apart: 29, of which 17 were waited for; matrix products, arithmetic and copies ran while one was open for 0% of the time, Pallas kernels for 6%

profile of v4, /device:TPU:0, one launch (start us, length us, event | category | flops | bytes accessed | tf_op | source)
XLA Modules:
  0.0 79.6 jit_solution(3402525129731537164)
XLA Ops:
  0.6 1.5 %shard_map.141.kv = bf16[192,256]{1,0:T(8,128)(2,1)} custom-call(bf16[128,512]{1,0:T(8,128)(2,1)} %ck.1, bf16[128,512]{1,0:T(8,128)(2,1)} %cv.1, bf16[64,512]{1,0:T(8,128)(2,1)} %bk.1, bf16[64,512]{1,0:T(8,128)(2,1)} %bv.1), custom_call_target="tpu_custom_call" | custom-call | tf_op jit(solution)/shard_map/pallas_call | solution.py:372
  2.2 3.0 %collective-permute-start = (bf16[192,256]{1,0:T(8,128)(2,1)}, bf16[192,256]{1,0:T(8,128)(2,1)S(1)}, u32[]{:S(2)}, u32[]{:S(2)}) collective-permute-start(bf16[192,256]{1,0:T(8,128)(2,1)} %shard_map.141.kv), channel_id=1, source_target_pairs={{0,8},{4,12},{8,0},{12,4},{16,24},{20,28},{24,16},{28,20},{1,9},{5... | collective-permute-start | bytes 294920 | tf_op jit(solution)/shard_map/ppermute | solution.py:325
  5.2 1.5 %collective-permute-start.1 = (bf16[192,256]{1,0:T(8,128)(2,1)}, bf16[192,256]{1,0:T(8,128)(2,1)S(1)}, u32[]{:S(2)}, u32[]{:S(2)}) collective-permute-start(bf16[192,256]{1,0:T(8,128)(2,1)} %shard_map.141.kv), channel_id=1, source_target_pairs={{0,16},{4,20},{8,24},{12,28},{16,0},{20,4},{24,8},{28,12},{1,17},{... | collective-permute-start | bytes 294920 | tf_op jit(solution)/shard_map/ppermute | solution.py:325
  11.0 1.4 %collective-permute-done.2 = bf16[192,256]{1,0:T(8,128)(2,1)S(1)} collective-permute-done((bf16[192,256]{1,0:T(8,128)(2,1)}, bf16[192,256]{1,0:T(8,128)(2,1)S(1)}, u32[]{:S(2)}, u32[]{:S(2)}) %collective-permute-start.2) | collective-permute-done | bytes 98336 | tf_op jit(solution)/shard_map/ppermute | solution.py:325
  12.6 1.8 %shard_map.143 = (f32[1024,128]{1,0:T(8,128)S(1)}, f32[1024,128]{1,0:T(8,128)S(1)}, f32[1024,128]{1,0:T(8,128)S(1)}) custom-call(bf16[1024,128]{1,0:T(8,128)(2,1)S(1)} %bitcast.13, bf16[768,256]{1,0:T(8,128)(2,1)S(1)} %constant_dynamic-update-slice_fusion.kv, f32[64,768]{1,0:T(8,128)S(1)} %get-tuple-element.73.bias), custom_call_target="tpu_custom_call" | custom-call | flops 402653184 | bytes 4194304 | tf_op jit(solution)/shard_map/pallas_call | solution.py:404
  14.4 1.9 %shard_map.144 = (bf16[64,1024]{1,0:T(8,128)(2,1)S(1)}, bf16[64,1024]{1,0:T(8,128)(2,1)S(1)}) custom-call(bf16[1024,128]{1,0:T(8,128)(2,1)S(1)} %bitcast.14, bf16[768,256]{1,0:T(8,128)(2,1)S(1)} %collective-permute-done.3.kv, f32[64,768]{1,0:T(8,128)S(1)} %get-tuple-element.72.bias, f32[1024,128]{1,0:T(8,128)S(1)} %get-tuple-element.74.o_in, ...), custom_call_target="tpu_custom_call" | custom-call | flops 402653184 | bytes 4194304 | tf_op jit(solution)/shard_map/pallas_call | solution.py:411
  17.0 1.1 %collective-permute-start.7 = (bf16[64,1024]{1,0:T(8,128)(2,1)S(1)}, bf16[64,1024]{1,0:T(8,128)(2,1)S(1)}, u32[]{:S(2)}, u32[]{:S(2)}) collective-permute-start(bf16[64,1024]{1,0:T(8,128)(2,1)S(1)} %get-tuple-element.84), channel_id=1, source_target_pairs={{0,16},{4,20},{8,24},{12,28},{16,0},{20,4},{24,8},{28,12},{1,17},{... | collective-permute-start | bytes 393224 | tf_op jit(solution)/shard_map/ppermute | solution.py:325
  18.0 1.6 %collective-permute-start.10 = (f32[8,128]{1,0:T(8,128)S(1)}, f32[8,128]{1,0:T(8,128)S(1)}, u32[]{:S(2)}, u32[]{:S(2)}) collective-permute-start(f32[8,128]{1,0:T(8,128)S(1)} %get-tuple-element.82), channel_id=1, source_target_pairs={{0,1},{1,0},{2,3},{3,2},{4,5},{5,4},{6,7},{7,6},{8,9},{9,8},{10,11... | collective-permute-start | bytes 12296 | tf_op jit(solution)/shard_map/ppermute | solution.py:325
  19.6 1.3 %collective-permute-start.5 = (bf16[64,1024]{1,0:T(8,128)(2,1)S(1)}, bf16[64,1024]{1,0:T(8,128)(2,1)S(1)}, u32[]{:S(2)}, u32[]{:S(2)}) collective-permute-start(bf16[64,1024]{1,0:T(8,128)(2,1)S(1)} %get-tuple-element.84), channel_id=1, source_target_pairs={{0,8},{4,12},{8,0},{12,4},{16,24},{20,28},{24,16},{28,20},{1,9},{5... | collective-permute-start | bytes 393224 | tf_op jit(solution)/shard_map/ppermute | solution.py:325
  20.8 1.1 %collective-permute-start.6 = (bf16[64,1024]{1,0:T(8,128)(2,1)S(1)}, bf16[64,1024]{1,0:T(8,128)(2,1)S(1)}, u32[]{:S(2)}, u32[]{:S(2)}) collective-permute-start(bf16[64,1024]{1,0:T(8,128)(2,1)S(1)} %get-tuple-element.83), channel_id=1, source_target_pairs={{0,16},{4,20},{8,24},{12,28},{16,0},{20,4},{24,8},{28,12},{1,17},{... | collective-permute-start | bytes 393224 | tf_op jit(solution)/shard_map/ppermute | solution.py:325
  24.3 2.6 %collective-permute-start.11 = (f32[16,128]{1,0:T(8,128)S(1)}, f32[16,128]{1,0:T(8,128)S(1)}, u32[]{:S(2)}, u32[]{:S(2)}) collective-permute-start(f32[16,128]{1,0:T(8,128)S(1)} %pad_maximum_fusion.2), channel_id=1, source_target_pairs={{0,2},{1,3},{2,0},{3,1},{4,6},{5,7},{6,4},{7,5},{8,10},{9,11},{10,... | collective-permute-start | bytes 24584 | tf_op jit(solution)/shard_map/ppermute | solution.py:325
  26.9 1.9 %collective-permute-done.11 = f32[16,128]{1,0:T(8,128)S(1)} collective-permute-done((f32[16,128]{1,0:T(8,128)S(1)}, f32[16,128]{1,0:T(8,128)S(1)}, u32[]{:S(2)}, u32[]{:S(2)}) %collective-permute-start.11) | collective-permute-done | bytes 8224 | tf_op jit(solution)/shard_map/ppermute | solution.py:325
  29.8 1.9 %collective-permute-done.12.heads_out = bf16[256,2048]{1,0:T(8,128)(2,1)S(1)} collective-permute-done((bf16[256,2048]{1,0:T(8,128)(2,1)S(1)}, bf16[256,2048]{1,0:T(8,128)(2,1)S(1)}, u32[]{:S(2)}, u32[]{:S(2)}) %collective-permute-start.12) | collective-permute-done | bytes 1048608 | tf_op jit(solution)/shard_map/ppermute | solution.py:325
  31.7 1.1 %shard_map.146 = (f32[128,512]{1,0:T(8,128)S(1)}, bf16[256,512]{1,0:T(8,128)(2,1)S(1)}, bf16[128,512]{1,0:T(8,128)(2,1)S(1)}, bf16[128,512]{1,0:T(8,128)(2,1)S(1...) custom-call(bf16[256,2048]{1,0:T(8,128)(2,1)S(1)} %collective-permute-done.12.heads_out,, ...), custom_call_target="tpu_custom_call" | custom-call | flops 536870912 | bytes 4194304 | tf_op jit(solution)/shard_map/pallas_call | solution.py:439
  32.8 2.1 %collective-permute-start.14 = (bf16[128,512]{1,0:T(8,128)(2,1)S(1)}, bf16[128,512]{1,0:T(8,128)(2,1)S(1)}, u32[]{:S(2)}, u32[]{:S(2)}) collective-permute-start(bf16[128,512]{1,0:T(8,128)(2,1)S(1)} %get-tuple-element.96), channel_id=1, source_target_pairs={{0,1},{1,0},{2,3},{3,2},{4,5},{5,4},{6,7},{7,6},{8,9},{9,8},{10,11... | collective-permute-start | bytes 393224 | tf_op jit(solution)/shard_map/ppermute | solution.py:325
  34.9 4.2 %collective-permute-done.14 = bf16[128,512]{1,0:T(8,128)(2,1)S(1)} collective-permute-done((bf16[128,512]{1,0:T(8,128)(2,1)S(1)}, bf16[128,512]{1,0:T(8,128)(2,1)S(1)}, u32[]{:S(2)}, u32[]{:S(2)}) %collective-permute-start.14) | collective-permute-done | bytes 131104 | tf_op jit(solution)/shard_map/ppermute | solution.py:325
  39.2 2.7 %collective-permute-start.15 = (bf16[128,512]{1,0:T(8,128)(2,1)S(1)}, bf16[128,512]{1,0:T(8,128)(2,1)S(1)}, u32[]{:S(2)}, u32[]{:S(2)}) collective-permute-start(bf16[128,512]{1,0:T(8,128)(2,1)S(1)} %add_convert_fusion.1), channel_id=1, source_target_pairs={{0,2},{1,3},{2,0},{3,1},{4,6},{5,7},{6,4},{7,5},{8,10},{9,11},{10,... | collective-permute-start | bytes 393224 | tf_op jit(solution)/shard_map/ppermute | solution.py:325
  41.9 5.6 %collective-permute-done.15.refs_2_ = bf16[128,512]{1,0:T(8,128)(2,1)S(1)} collective-permute-done((bf16[128,512]{1,0:T(8,128)(2,1)S(1)}, bf16[128,512]{1,0:T(8,128)(2,1)S(1)}, u32[]{:S(2)}, u32[]{:S(2)}) %collective-permute-start.15) | collective-permute-done | bytes 131104 | tf_op jit(solution)/shard_map/ppermute | solution.py:325
  49.0 1.0 %collective-permute-done.16.theirs = bf16[64,3200]{1,0:T(8,128)(2,1)S(1)} collective-permute-done((bf16[64,3200]{1,0:T(8,128)(2,1)S(1)}, bf16[64,3200]{1,0:T(8,128)(2,1)S(1)}, u32[]{:S(2)}, u32[]{:S(2)}) %collective-permute-start.16) | collective-permute-done | bytes 409632 | tf_op jit(solution)/shard_map/ppermute | solution.py:325
  51.4 1.2 %collective-permute-start.18 = (bf16[16,3200]{1,0:T(8,128)(2,1)S(1)}, bf16[16,3200]{1,0:T(8,128)(2,1)S(1)}, u32[]{:S(2)}, u32[]{:S(2)}) collective-permute-start(bf16[16,3200]{1,0:T(8,128)(2,1)S(1)} %get-tuple-element.103), channel_id=1, source_target_pairs={{0,16},{4,20},{8,24},{12,28},{16,0},{20,4},{24,8},{28,12},{1,17},{... | collective-permute-start | bytes 307208 | tf_op jit(solution)/shard_map/ppermute | solution.py:325
  52.6 1.6 %collective-permute-start.19 = (bf16[16,3200]{1,0:T(8,128)(2,1)S(1)}, bf16[16,3200]{1,0:T(8,128)(2,1)S(1)}, u32[]{:S(2)}, u32[]{:S(2)}) collective-permute-start(bf16[16,3200]{1,0:T(8,128)(2,1)S(1)} %get-tuple-element.104), channel_id=1, source_target_pairs={{0,24},{4,28},{8,16},{12,20},{16,8},{20,12},{24,0},{28,4},{1,25},{... | collective-permute-start | bytes 307208 | tf_op jit(solution)/shard_map/ppermute | solution.py:325
  54.2 1.7 %collective-permute-done.17.refs_1_ = bf16[16,3200]{1,0:T(8,128)(2,1)S(1)} collective-permute-done((bf16[16,3200]{1,0:T(8,128)(2,1)S(1)}, bf16[16,3200]{1,0:T(8,128)(2,1)S(1)}, u32[]{:S(2)}, u32[]{:S(2)}) %collective-permute-start.17) | collective-permute-done | bytes 102432 | tf_op jit(solution)/shard_map/ppermute | solution.py:325
  55.9 2.3 %collective-permute-done.18.refs_2_ = bf16[16,3200]{1,0:T(8,128)(2,1)S(1)} collective-permute-done((bf16[16,3200]{1,0:T(8,128)(2,1)S(1)}, bf16[16,3200]{1,0:T(8,128)(2,1)S(1)}, u32[]{:S(2)}, u32[]{:S(2)}) %collective-permute-start.18) | collective-permute-done | bytes 102432 | tf_op jit(solution)/shard_map/ppermute | solution.py:325
  58.6 3.2 %collective-permute-start.24 = (bf16[128,512]{1,0:T(8,128)(2,1)S(1)}, bf16[128,512]{1,0:T(8,128)(2,1)S(1)}, u32[]{:S(2)}, u32[]{:S(2)}) collective-permute-start(bf16[128,512]{1,0:T(8,128)(2,1)S(1)} %add_convert_fusion), channel_id=1, source_target_pairs={{0,2},{1,3},{2,0},{3,1},{4,6},{5,7},{6,4},{7,5},{8,10},{9,11},{10,... | collective-permute-start | bytes 393224 | tf_op jit(solution)/shard_map/ppermute | solution.py:325
  61.9 1.4 %collective-permute-start.21 = (bf16[16,1536]{1,0:T(8,128)(2,1)S(1)}, bf16[16,1536]{1,0:T(8,128)(2,1)S(1)}, u32[]{:S(2)}, u32[]{:S(2)}) collective-permute-start(bf16[16,1536]{1,0:T(8,128)(2,1)S(1)} %shard_map.150), channel_id=1, source_target_pairs={{0,8},{4,12},{8,0},{12,4},{16,24},{20,28},{24,16},{28,20},{1,9},{5... | collective-permute-start | bytes 147464 | tf_op jit(solution)/shard_map/ppermute | solution.py:325
  64.3 1.2 %collective-permute-start.23 = (bf16[16,1536]{1,0:T(8,128)(2,1)S(1)}, bf16[16,1536]{1,0:T(8,128)(2,1)S(1)}, u32[]{:S(2)}, u32[]{:S(2)}) collective-permute-start(bf16[16,1536]{1,0:T(8,128)(2,1)S(1)} %shard_map.150), channel_id=1, source_target_pairs={{0,24},{4,28},{8,16},{12,20},{16,8},{20,12},{24,0},{28,4},{1,25},{... | collective-permute-start | bytes 147464 | tf_op jit(solution)/shard_map/ppermute | solution.py:325
  66.0 1.3 %collective-permute-done.22 = bf16[16,1536]{1,0:T(8,128)(2,1)S(1)} collective-permute-done((bf16[16,1536]{1,0:T(8,128)(2,1)S(1)}, bf16[16,1536]{1,0:T(8,128)(2,1)S(1)}, u32[]{:S(2)}, u32[]{:S(2)}) %collective-permute-start.22) | collective-permute-done | bytes 49184 | tf_op jit(solution)/shard_map/ppermute | solution.py:325
  67.4 1.9 %collective-permute-done.23 = bf16[16,1536]{1,0:T(8,128)(2,1)S(1)} collective-permute-done((bf16[16,1536]{1,0:T(8,128)(2,1)S(1)}, bf16[16,1536]{1,0:T(8,128)(2,1)S(1)}, u32[]{:S(2)}, u32[]{:S(2)}) %collective-permute-start.23) | collective-permute-done | bytes 49184 | tf_op jit(solution)/shard_map/ppermute | solution.py:325
  71.7 1.3 %collective-permute-start.27 = (bf16[32,512]{1,0:T(8,128)(2,1)S(1)}, bf16[32,512]{1,0:T(8,128)(2,1)S(1)}, u32[]{:S(2)}, u32[]{:S(2)}) collective-permute-start(bf16[32,512]{1,0:T(8,128)(2,1)S(1)} %get-tuple-element.117), channel_id=1, source_target_pairs={{0,2},{1,3},{2,0},{3,1},{4,6},{5,7},{6,4},{7,5},{8,10},{9,11},{10,... | collective-permute-start | bytes 98312 | tf_op jit(solution)/shard_map/ppermute | solution.py:325
  73.0 2.7 %collective-permute-start.28 = (bf16[32,512]{1,0:T(8,128)(2,1)S(1)}, bf16[32,512]{1,0:T(8,128)(2,1)S(1)}, u32[]{:S(2)}, u32[]{:S(2)}) collective-permute-start(bf16[32,512]{1,0:T(8,128)(2,1)S(1)} %get-tuple-element.118), channel_id=1, source_target_pairs={{0,3},{1,2},{2,1},{3,0},{4,7},{5,6},{6,5},{7,4},{8,11},{9,10},{10,... | collective-permute-start | bytes 98312 | tf_op jit(solution)/shard_map/ppermute | solution.py:325
  75.6 1.1 %collective-permute-done.27.refs_2_ = bf16[32,512]{1,0:T(8,128)(2,1)S(1)} collective-permute-done((bf16[32,512]{1,0:T(8,128)(2,1)S(1)}, bf16[32,512]{1,0:T(8,128)(2,1)S(1)}, u32[]{:S(2)}, u32[]{:S(2)}) %collective-permute-start.27) | collective-permute-done | bytes 32800 | tf_op jit(solution)/shard_map/ppermute | solution.py:325
  76.8 1.9 %collective-permute-done.28.refs_3_ = bf16[32,512]{1,0:T(8,128)(2,1)S(1)} collective-permute-done((bf16[32,512]{1,0:T(8,128)(2,1)S(1)}, bf16[32,512]{1,0:T(8,128)(2,1)S(1)}, u32[]{:S(2)}, u32[]{:S(2)}) %collective-permute-start.28) | collective-permute-done | bytes 32800 | tf_op jit(solution)/shard_map/ppermute | solution.py:325
  (74 shorter events, 16.6 us)
Async XLA Ops:
  2.2 8.5 %collective-permute-start = (bf16[192,256]{1,0:T(8,128)(2,1)}, bf16[192,256]{1,0:T(8,128)(2,1)S(1)}, u32[]{:S(2)}, u32[]{:S(2)}) collective-permute-start(bf16[192,256]{1,0:T(8,128)(2,1)} %shard_map.141.kv), channel_id=1, source_target_pairs={{0,8},{4,12},{8,0},{12,4},{16,24},{20,28},{24,16},{28,20},{1,9},{5... | collective-permute-start | bytes 294920 | tf_op jit(solution)/shard_map/ppermute | solution.py:325
  5.2 5.9 %collective-permute-start.1 = (bf16[192,256]{1,0:T(8,128)(2,1)}, bf16[192,256]{1,0:T(8,128)(2,1)S(1)}, u32[]{:S(2)}, u32[]{:S(2)}) collective-permute-start(bf16[192,256]{1,0:T(8,128)(2,1)} %shard_map.141.kv), channel_id=1, source_target_pairs={{0,16},{4,20},{8,24},{12,28},{16,0},{20,4},{24,8},{28,12},{1,17},{... | collective-permute-start | bytes 294920 | tf_op jit(solution)/shard_map/ppermute | solution.py:325
  6.7 5.7 %collective-permute-start.2 = (bf16[192,256]{1,0:T(8,128)(2,1)}, bf16[192,256]{1,0:T(8,128)(2,1)S(1)}, u32[]{:S(2)}, u32[]{:S(2)}) collective-permute-start(bf16[192,256]{1,0:T(8,128)(2,1)} %shard_map.141.kv), channel_id=1, source_target_pairs={{0,24},{4,28},{8,16},{12,20},{16,8},{20,12},{24,0},{28,4},{1,25},{... | collective-permute-start | bytes 294920 | tf_op jit(solution)/shard_map/ppermute | solution.py:325
  12.5 1.9 %collective-permute-start.3 = (bf16[768,256]{1,0:T(8,128)(2,1)S(1)}, bf16[768,256]{1,0:T(8,128)(2,1)S(1)}, u32[]{:S(2)}, u32[]{:S(2)}) collective-permute-start(bf16[768,256]{1,0:T(8,128)(2,1)S(1)} %constant_dynamic-update-slice_fusion.kv), channel_id=1, source_target_pairs={{0,4},{4,0},{8,12},{12,8},{16,20},{20,16},{24,28},{28,24},{1,5},{5... | collective-permute-start | bytes 1179656 | tf_op jit(solution)/shard_map/ppermute | solution.py:325
  14.3 33.2 %slice-start = ((s8[6291456]{0:T(1024)(128)(4,1)}), s8[4194304]{0:T(1024)(128)(4,1)S(1)}, s32[]{:S(2)}) async-start(s8[6291456]{0:T(1024)(128)(4,1)} %bitcast.11), calls=%async_computation | async-start | bytes 8388608
  16.3 6.3 %collective-permute-start.4 = (bf16[64,1024]{1,0:T(8,128)(2,1)S(1)}, bf16[64,1024]{1,0:T(8,128)(2,1)S(1)}, u32[]{:S(2)}, u32[]{:S(2)}) collective-permute-start(bf16[64,1024]{1,0:T(8,128)(2,1)S(1)} %get-tuple-element.83), channel_id=1, source_target_pairs={{0,8},{4,12},{8,0},{12,4},{16,24},{20,28},{24,16},{28,20},{1,9},{5... | collective-permute-start | bytes 393224 | tf_op jit(solution)/shard_map/ppermute | solution.py:325
  17.0 6.4 %collective-permute-start.7 = (bf16[64,1024]{1,0:T(8,128)(2,1)S(1)}, bf16[64,1024]{1,0:T(8,128)(2,1)S(1)}, u32[]{:S(2)}, u32[]{:S(2)}) collective-permute-start(bf16[64,1024]{1,0:T(8,128)(2,1)S(1)} %get-tuple-element.84), channel_id=1, source_target_pairs={{0,16},{4,20},{8,24},{12,28},{16,0},{20,4},{24,8},{28,12},{1,17},{... | collective-permute-start | bytes 393224 | tf_op jit(solution)/shard_map/ppermute | solution.py:325
  18.0 6.3 %collective-permute-start.10 = (f32[8,128]{1,0:T(8,128)S(1)}, f32[8,128]{1,0:T(8,128)S(1)}, u32[]{:S(2)}, u32[]{:S(2)}) collective-permute-start(f32[8,128]{1,0:T(8,128)S(1)} %get-tuple-element.82), channel_id=1, source_target_pairs={{0,1},{1,0},{2,3},{3,2},{4,5},{5,4},{6,7},{7,6},{8,9},{9,8},{10,11... | collective-permute-start | bytes 12296 | tf_op jit(solution)/shard_map/ppermute | solution.py:325
  19.6 9.2 %collective-permute-start.5 = (bf16[64,1024]{1,0:T(8,128)(2,1)S(1)}, bf16[64,1024]{1,0:T(8,128)(2,1)S(1)}, u32[]{:S(2)}, u32[]{:S(2)}) collective-permute-start(bf16[64,1024]{1,0:T(8,128)(2,1)S(1)} %get-tuple-element.84), channel_id=1, source_target_pairs={{0,8},{4,12},{8,0},{12,4},{16,24},{20,28},{24,16},{28,20},{1,9},{5... | collective-permute-start | bytes 393224 | tf_op jit(solution)/shard_map/ppermute | solution.py:325
  20.8 8.0 %collective-permute-start.6 = (bf16[64,1024]{1,0:T(8,128)(2,1)S(1)}, bf16[64,1024]{1,0:T(8,128)(2,1)S(1)}, u32[]{:S(2)}, u32[]{:S(2)}) collective-permute-start(bf16[64,1024]{1,0:T(8,128)(2,1)S(1)} %get-tuple-element.83), channel_id=1, source_target_pairs={{0,16},{4,20},{8,24},{12,28},{16,0},{20,4},{24,8},{28,12},{1,17},{... | collective-permute-start | bytes 393224 | tf_op jit(solution)/shard_map/ppermute | solution.py:325
  22.5 6.3 %collective-permute-start.8 = (bf16[64,1024]{1,0:T(8,128)(2,1)S(1)}, bf16[64,1024]{1,0:T(8,128)(2,1)S(1)}, u32[]{:S(2)}, u32[]{:S(2)}) collective-permute-start(bf16[64,1024]{1,0:T(8,128)(2,1)S(1)} %collective-permute-done.4), channel_id=1, source_target_pairs={{0,16},{4,20},{8,24},{12,28},{16,0},{20,4},{24,8},{28,12},{1,17},{... | collective-permute-start | bytes 393224 | tf_op jit(solution)/shard_map/ppermute | solution.py:325
  23.4 5.5 %collective-permute-start.9 = (bf16[64,1024]{1,0:T(8,128)(2,1)S(1)}, bf16[64,1024]{1,0:T(8,128)(2,1)S(1)}, u32[]{:S(2)}, u32[]{:S(2)}) collective-permute-start(bf16[64,1024]{1,0:T(8,128)(2,1)S(1)} %collective-permute-done.7), channel_id=1, source_target_pairs={{0,8},{4,12},{8,0},{12,4},{16,24},{20,28},{24,16},{28,20},{1,9},{5... | collective-permute-start | bytes 393224 | tf_op jit(solution)/shard_map/ppermute | solution.py:325
  24.3 4.6 %collective-permute-start.11 = (f32[16,128]{1,0:T(8,128)S(1)}, f32[16,128]{1,0:T(8,128)S(1)}, u32[]{:S(2)}, u32[]{:S(2)}) collective-permute-start(f32[16,128]{1,0:T(8,128)S(1)} %pad_maximum_fusion.2), channel_id=1, source_target_pairs={{0,2},{1,3},{2,0},{3,1},{4,6},{5,7},{6,4},{7,5},{8,10},{9,11},{10,... | collective-permute-start | bytes 24584 | tf_op jit(solution)/shard_map/ppermute | solution.py:325
  28.9 18.6 %slice-start.1 = ((s8[6291456]{0:T(1024)(128)(4,1)}), s8[2097152]{0:T(1024)(128)(4,1)S(1)}, s32[]{:S(2)}) async-start(s8[6291456]{0:T(1024)(128)(4,1)} %bitcast.11), calls=%async_computation.1 | async-start | bytes 4194304
  29.0 2.7 %collective-permute-start.12 = (bf16[256,2048]{1,0:T(8,128)(2,1)S(1)}, bf16[256,2048]{1,0:T(8,128)(2,1)S(1)}, u32[]{:S(2)}, u32[]{:S(2)}) collective-permute-start(bf16[256,2048]{1,0:T(8,128)(2,1)S(1)} %maximum_maximum_fusion.heads_out), channel_id=1, source_target_pairs={{0,4},{4,0},{8,12},{12,8},{16,20},{20,16},{24,28},{28,24},{1,5},{5... | collective-permute-start | bytes 3145736 | tf_op jit(solution)/shard_map/ppermute | solution.py:325
  32.8 6.4 %collective-permute-start.14 = (bf16[128,512]{1,0:T(8,128)(2,1)S(1)}, bf16[128,512]{1,0:T(8,128)(2,1)S(1)}, u32[]{:S(2)}, u32[]{:S(2)}) collective-permute-start(bf16[128,512]{1,0:T(8,128)(2,1)S(1)} %get-tuple-element.96), channel_id=1, source_target_pairs={{0,1},{1,0},{2,3},{3,2},{4,5},{5,4},{6,7},{7,6},{8,9},{9,8},{10,11... | collective-permute-start | bytes 393224 | tf_op jit(solution)/shard_map/ppermute | solution.py:325
  34.8 7.0 %collective-permute-start.13 = (bf16[128,512]{1,0:T(8,128)(2,1)S(1)}, bf16[128,512]{1,0:T(8,128)(2,1)S(1)}, u32[]{:S(2)}, u32[]{:S(2)}) collective-permute-start(bf16[128,512]{1,0:T(8,128)(2,1)S(1)} %get-tuple-element.94), channel_id=1, source_target_pairs={{0,1},{1,0},{2,3},{3,2},{4,5},{5,4},{6,7},{7,6},{8,9},{9,8},{10,11... | collective-permute-start | bytes 393224 | tf_op jit(solution)/shard_map/ppermute | solution.py:325
  39.2 8.3 %collective-permute-start.15 = (bf16[128,512]{1,0:T(8,128)(2,1)S(1)}, bf16[128,512]{1,0:T(8,128)(2,1)S(1)}, u32[]{:S(2)}, u32[]{:S(2)}) collective-permute-start(bf16[128,512]{1,0:T(8,128)(2,1)S(1)} %add_convert_fusion.1), channel_id=1, source_target_pairs={{0,2},{1,3},{2,0},{3,1},{4,6},{5,7},{6,4},{7,5},{8,10},{9,11},{10,... | collective-permute-start | bytes 393224 | tf_op jit(solution)/shard_map/ppermute | solution.py:325
  48.2 1.8 %collective-permute-start.16 = (bf16[64,3200]{1,0:T(8,128)(2,1)S(1)}, bf16[64,3200]{1,0:T(8,128)(2,1)S(1)}, u32[]{:S(2)}, u32[]{:S(2)}) collective-permute-start(bf16[64,3200]{1,0:T(8,128)(2,1)S(1)} %shard_map.148), channel_id=1, source_target_pairs={{0,4},{4,0},{8,12},{12,8},{16,20},{20,16},{24,28},{28,24},{1,5},{5... | collective-permute-start | bytes 1228808 | tf_op jit(solution)/shard_map/ppermute | solution.py:325
  48.3 21.1 %copy-start.1 = (bf16[2,1536,512]{2,1,0:T(8,128)(2,1)S(1)}, bf16[2,1536,512]{2,1,0:T(8,128)(2,1)}, u32[]{:S(2)}) copy-start(bf16[2,1536,512]{2,1,0:T(8,128)(2,1)} %weight.7) | copy-start | bytes 9437188
  50.1 8.4 %collective-permute-start.20 = (bf16[256,512]{1,0:T(8,128)(2,1)S(1)}, bf16[256,512]{1,0:T(8,128)(2,1)S(1)}, u32[]{:S(2)}, u32[]{:S(2)}) collective-permute-start(bf16[256,512]{1,0:T(8,128)(2,1)S(1)} %get-tuple-element.105), channel_id=1, source_target_pairs={{0,1},{1,0},{2,3},{3,2},{4,5},{5,4},{6,7},{7,6},{8,9},{9,8},{10,11... | collective-permute-start | bytes 786440 | tf_op jit(solution)/shard_map/ppermute | solution.py:325
  50.7 5.2 %collective-permute-start.17 = (bf16[16,3200]{1,0:T(8,128)(2,1)S(1)}, bf16[16,3200]{1,0:T(8,128)(2,1)S(1)}, u32[]{:S(2)}, u32[]{:S(2)}) collective-permute-start(bf16[16,3200]{1,0:T(8,128)(2,1)S(1)} %get-tuple-element.102), channel_id=1, source_target_pairs={{0,8},{4,12},{8,0},{12,4},{16,24},{20,28},{24,16},{28,20},{1,9},{5... | collective-permute-start | bytes 307208 | tf_op jit(solution)/shard_map/ppermute | solution.py:325
  51.4 6.8 %collective-permute-start.18 = (bf16[16,3200]{1,0:T(8,128)(2,1)S(1)}, bf16[16,3200]{1,0:T(8,128)(2,1)S(1)}, u32[]{:S(2)}, u32[]{:S(2)}) collective-permute-start(bf16[16,3200]{1,0:T(8,128)(2,1)S(1)} %get-tuple-element.103), channel_id=1, source_target_pairs={{0,16},{4,20},{8,24},{12,28},{16,0},{20,4},{24,8},{28,12},{1,17},{... | collective-permute-start | bytes 307208 | tf_op jit(solution)/shard_map/ppermute | solution.py:325
  52.6 5.6 %collective-permute-start.19 = (bf16[16,3200]{1,0:T(8,128)(2,1)S(1)}, bf16[16,3200]{1,0:T(8,128)(2,1)S(1)}, u32[]{:S(2)}, u32[]{:S(2)}) collective-permute-start(bf16[16,3200]{1,0:T(8,128)(2,1)S(1)} %get-tuple-element.104), channel_id=1, source_target_pairs={{0,24},{4,28},{8,16},{12,20},{16,8},{20,12},{24,0},{28,4},{1,25},{... | collective-permute-start | bytes 307208 | tf_op jit(solution)/shard_map/ppermute | solution.py:325
  58.6 10.7 %collective-permute-start.24 = (bf16[128,512]{1,0:T(8,128)(2,1)S(1)}, bf16[128,512]{1,0:T(8,128)(2,1)S(1)}, u32[]{:S(2)}, u32[]{:S(2)}) collective-permute-start(bf16[128,512]{1,0:T(8,128)(2,1)S(1)} %add_convert_fusion), channel_id=1, source_target_pairs={{0,2},{1,3},{2,0},{3,1},{4,6},{5,7},{6,4},{7,5},{8,10},{9,11},{10,... | collective-permute-start | bytes 393224 | tf_op jit(solution)/shard_map/ppermute | solution.py:325
  61.9 4.2 %collective-permute-start.21 = (bf16[16,1536]{1,0:T(8,128)(2,1)S(1)}, bf16[16,1536]{1,0:T(8,128)(2,1)S(1)}, u32[]{:S(2)}, u32[]{:S(2)}) collective-permute-start(bf16[16,1536]{1,0:T(8,128)(2,1)S(1)} %shard_map.150), channel_id=1, source_target_pairs={{0,8},{4,12},{8,0},{12,4},{16,24},{20,28},{24,16},{28,20},{1,9},{5... | collective-permute-start | bytes 147464 | tf_op jit(solution)/shard_map/ppermute | solution.py:325
  63.3 4.1 %collective-permute-start.22 = (bf16[16,1536]{1,0:T(8,128)(2,1)S(1)}, bf16[16,1536]{1,0:T(8,128)(2,1)S(1)}, u32[]{:S(2)}, u32[]{:S(2)}) collective-permute-start(bf16[16,1536]{1,0:T(8,128)(2,1)S(1)} %shard_map.150), channel_id=1, source_target_pairs={{0,16},{4,20},{8,24},{12,28},{16,0},{20,4},{24,8},{28,12},{1,17},{... | collective-permute-start | bytes 147464 | tf_op jit(solution)/shard_map/ppermute | solution.py:325
  64.3 5.0 %collective-permute-start.23 = (bf16[16,1536]{1,0:T(8,128)(2,1)S(1)}, bf16[16,1536]{1,0:T(8,128)(2,1)S(1)}, u32[]{:S(2)}, u32[]{:S(2)}) collective-permute-start(bf16[16,1536]{1,0:T(8,128)(2,1)S(1)} %shard_map.150), channel_id=1, source_target_pairs={{0,24},{4,28},{8,16},{12,20},{16,8},{20,12},{24,0},{28,4},{1,25},{... | collective-permute-start | bytes 147464 | tf_op jit(solution)/shard_map/ppermute | solution.py:325
  69.3 1.5 %collective-permute-start.25 = (bf16[64,1536]{1,0:T(8,128)(2,1)S(1)}, bf16[64,1536]{1,0:T(8,128)(2,1)S(1)}, u32[]{:S(2)}, u32[]{:S(2)}) collective-permute-start(bf16[64,1536]{1,0:T(8,128)(2,1)S(1)} %pad_maximum_fusion.active), channel_id=1, source_target_pairs={{0,4},{4,0},{8,12},{12,8},{16,20},{20,16},{24,28},{28,24},{1,5},{5... | collective-permute-start | bytes 589832 | tf_op jit(solution)/shard_map/ppermute | solution.py:325
  71.2 4.5 %collective-permute-start.26 = (bf16[32,512]{1,0:T(8,128)(2,1)S(1)}, bf16[32,512]{1,0:T(8,128)(2,1)S(1)}, u32[]{:S(2)}, u32[]{:S(2)}) collective-permute-start(bf16[32,512]{1,0:T(8,128)(2,1)S(1)} %get-tuple-element.116), channel_id=1, source_target_pairs={{0,1},{1,0},{2,3},{3,2},{4,5},{5,4},{6,7},{7,6},{8,9},{9,8},{10,11... | collective-permute-start | bytes 98312 | tf_op jit(solution)/shard_map/ppermute | solution.py:325
  71.7 5.1 %collective-permute-start.27 = (bf16[32,512]{1,0:T(8,128)(2,1)S(1)}, bf16[32,512]{1,0:T(8,128)(2,1)S(1)}, u32[]{:S(2)}, u32[]{:S(2)}) collective-permute-start(bf16[32,512]{1,0:T(8,128)(2,1)S(1)} %get-tuple-element.117), channel_id=1, source_target_pairs={{0,2},{1,3},{2,0},{3,1},{4,6},{5,7},{6,4},{7,5},{8,10},{9,11},{10,... | collective-permute-start | bytes 98312 | tf_op jit(solution)/shard_map/ppermute | solution.py:325
  73.0 5.7 %collective-permute-start.28 = (bf16[32,512]{1,0:T(8,128)(2,1)S(1)}, bf16[32,512]{1,0:T(8,128)(2,1)S(1)}, u32[]{:S(2)}, u32[]{:S(2)}) collective-permute-start(bf16[32,512]{1,0:T(8,128)(2,1)S(1)} %get-tuple-element.118), channel_id=1, source_target_pairs={{0,3},{1,2},{2,1},{3,0},{4,7},{5,6},{6,5},{7,4},{8,11},{9,10},{10,... | collective-permute-start | bytes 98312 | tf_op jit(solution)/shard_map/ppermute | solution.py:325
  (8 other events, 44.3 us)

commit v5 on v4

--- a/solution.py
+++ b/solution.py
@@ -141,7 +141,7 @@
         low[at, :] = lower[d * per : (d + 1) * per, :]
 
 
-GROUP = 4
+GROUP = 8
 
 
 def attend(q, kv, bias, span, finish):
@@ -197,21 +197,22 @@
 def project_second(n_exp, span, heads_out, weight, first, residual, ranks, *refs):
     own_out, odd_out = refs[:2]
     even_outs = refs[2 : n_exp // 2 + 1]
-    pick_outs = refs[n_exp // 2 + 1 : -2]
-    whole, picked = refs[-2:]
+    pick_outs, second = refs[n_exp // 2 + 1 : -1], refs[-1]
+    second[...] = dot(heads_out[...], weight[...])
     ctx, exp = lax.axis_index("ctx"), lax.axis_index("exp")
-    second = dot(heads_out[...], weight[...])
-    for k in range(heads_out.shape[0] // span):
-        here = slice(k * span, (k + 1) * span)
-        whole[rows_at(jnp.bitwise_xor(ctx, 2 * k) * span, span, span), :] = first[here, :]
-        whole[rows_at(jnp.bitwise_xor(ctx, 2 * k + 1) * span, span, span), :] = second[here, :]
-    tokens = residual.shape[0]
+    core, chip = ctx % 2, ctx // 2
+    tokens, columns = residual.shape
+    half = columns // 2
     flight = ranks.shape[0] // n_exp
     local = flight // n_exp
     slot = lax.broadcasted_iota(jnp.int32, (CAP, tokens), 0).astype(f32)
     for k in range(n_exp):
         block = jnp.bitwise_xor(exp, k)
-        part = whole[rows_at(block * tokens, tokens, tokens), :]
+        here = rows_at(jnp.bitwise_xor(chip, block) * span, span, span)
+        same, other = first[here, :], second[here, :]
+        part = jnp.concatenate(
+            [jnp.where(core == 0, same, other), jnp.where(core == 0, other, same)], axis=0
+        )
         if k == 0:
             part = part + residual[...].astype(f32)
             own_out[...] = part
@@ -220,16 +221,21 @@
             odd_out[k // 2 * tokens : (k // 2 + 1) * tokens, :] = narrow
         elif k:
             even_outs[k // 2 - 1][...] = narrow
-        rank = ranks[k * flight : (k + 1) * flight, :]
-        table = jnp.concatenate(
-            [jnp.where(rank[e : e + 1, :] == slot, 1.0, 0.0) for e in range(flight)], axis=0
-        ).astype(bf16)
-        rows = dot(table, narrow).astype(bf16)
-        for e in range(flight):
-            at = (e % local) * n_exp * CAP + block * CAP
-            picked[e // local, rows_at(at, CAP, CAP), :] = rows[e * CAP : (e + 1) * CAP, :]
-    for k in range(n_exp):
-        pick_outs[k][...] = picked[jnp.bitwise_xor(exp, k)]
+        table = []
+        for d in range(n_exp):
+            for j in range(local):
+                row = k * flight + jnp.bitwise_xor(exp, d) * local + j
+                table.append(jnp.where(ranks[pl.ds(row, 1), :] == slot, 1.0, 0.0))
+        rows = dot(jnp.concatenate(table, axis=0).astype(bf16), narrow).astype(bf16)
+        for d in range(n_exp):
+            for j in range(local):
+                at = rows_at(j * n_exp * CAP + block * CAP, CAP, CAP)
+                value = rows[(d * local + j) * CAP : (d * local + j + 1) * CAP, :]
+                if d < 2:
+                    pick_outs[d][at, :] = value
+                else:
+                    pick_outs[2 * d - 2][at, :] = value[:, :half]
+                    pick_outs[2 * d - 1][at, :] = value[:, half:]
 
 
 def split_square(square):
@@ -238,17 +244,18 @@
     return jnp.where(lane == 0, high, jnp.where(lane == 1, square - high, 0.0))
 
 
-def expert_in_kernel(n_exp, other, *refs):
-    arrived = refs[:n_exp]
-    gain, weight, out = refs[n_exp:]
+def expert_in_kernel(n_arrived, direct, other, *refs):
+    arrived = refs[:n_arrived]
+    gain, weight, out = refs[n_arrived:]
     expert = jnp.bitwise_xor(lax.axis_index("ctx") % 2, other)
     rows = out.shape[0]
     width = weight.shape[2]
     at = rows_at(expert * rows, rows, rows)
-    total = arrived[0][at, :].astype(f32)
-    for ref in arrived[1:]:
-        total = total + ref[at, :].astype(f32)
-    mixed = total.astype(bf16).astype(f32)
+    total = arrived[0][at, :].astype(f32) + arrived[1][at, :].astype(f32)
+    halves = [0.0, 0.0]
+    for n, ref in enumerate(arrived[2:]):
+        halves[n >= direct] = halves[n >= direct] + ref[at, :].astype(f32)
+    mixed = (total + jnp.concatenate(halves, axis=1)).astype(bf16).astype(f32)
     out[:, width:] = split_square(jnp.sum(mixed * mixed, axis=1, keepdims=True)).astype(out.dtype)
     scaled = (mixed * gain[...]).astype(bf16)
     step = width // 6
@@ -304,15 +311,9 @@
             outs[k][j * CAP : (j + 1) * CAP, :] = whole[j, at, :]
 
 
-def combine(high, low, own, odd, *refs):
-    n_exp = high.shape[0] // refs[0].shape[0]
-    returned, parts = refs[:n_exp], refs[n_exp:-2]
-    mixed, out = refs[-2:]
-    total = own[...] + odd[: own.shape[0], :].astype(f32)
-    for part in parts:
-        total = total + part[...].astype(f32)
-    mixed[...] = total.astype(bf16)
-    rows = jnp.concatenate([ref[...] for ref in returned], axis=0)
+def combine(high, low, *refs):
+    out = refs[-1]
+    rows = jnp.concatenate([ref[...] for ref in refs[:-1]], axis=0)
     dims = (((0,), (0,)), ((), ()))
     out[...] = (
         lax.dot_general(high[...], rows, dims, preferred_element_type=f32)
@@ -441,28 +442,27 @@
         [shape((tokens, columns), f32)]
         + [shape((n_exp // 2 * tokens, columns), bf16)]
         + [shape((tokens, columns), bf16)] * (n_exp // 2 - 1)
-        + [shape((per_exp, columns), bf16)] * n_exp,
+        + [shape((per_exp, columns), bf16)] * 2
+        + [shape((per_exp, columns // 2), bf16)] * (2 * n_exp - 4),
         [VMEM] * 5,
-        [
-            pltpu.VMEM((n_ctx * span, columns), f32),
-            pltpu.VMEM((n_exp, per_exp, columns), bf16),
-        ],
+        [pltpu.VMEM(first.shape, f32)],
         vmem=24,
         **cost,
     )(heads_other, out_weight, first, residual, ranks)
     own, odd, even, picks = outs[0], outs[1], outs[2 : n_exp // 2 + 1], outs[n_exp // 2 + 1 :]
-    passed = [permute(picks[2 * k + 1], "exp", 1) for k in range(1, n_exp // 2)]
-    arrived = [picks[0], permute(picks[1], "exp", 1)]
+    left, right = picks[2::2], picks[3::2]
+    passed = [permute(right[2 * k - 1], "exp", 1) for k in range(1, n_exp // 2)]
+    direct = [permute(x, "exp", k) for k, x in enumerate(left, 2)]
+    arrived = [picks[0], permute(picks[1], "exp", 1)] + direct
     for k, got in enumerate(passed, 1):
-        pair = (picks[2 * k].astype(f32) + got.astype(f32)).astype(bf16)
+        pair = (right[2 * k - 2].astype(f32) + got.astype(f32)).astype(bf16)
         arrived.append(permute(pair, "exp", 2 * k))
-
     gain = norm_gain.reshape(1, features)
     expert_rows = n_exp * CAP
 
     def gate_up(other, dtype):
         return call(
-            functools.partial(expert_in_kernel, len(arrived), other),
+            functools.partial(expert_in_kernel, len(arrived), len(direct), other),
             shape((expert_rows, width + LANES), dtype),
             [VMEM] * (len(arrived) + 2),
             vmem=16,
@@ -522,12 +522,16 @@
         **cost,
     )(active_other, expert_out, made)
     returned = over_exp(produced[1:])
-    mixed, expert_sum = call(
+    mixed = own + odd[:tokens].astype(f32)
+    for part in even:
+        mixed = mixed + part.astype(f32)
+    mixed = mixed.astype(bf16)
+    expert_sum = call(
         combine,
-        [shape((tokens, columns), bf16)] * 2,
-        [VMEM] * (4 + n_exp + len(even)),
-        vmem=8,
-    )(high, low, own, odd, produced[0], *returned, *even)
+        shape((tokens, columns), bf16),
+        [VMEM] * (2 + n_exp),
+        vmem=8,
+    )(high, low, produced[0], *returned)
     return (mixed, expert_sum)
 
 

time: 79.9 us -> 79.1 us (0.990)
  waiting for transfers between devices: 29.3 us -> 25.9 us
  starting transfers between devices: 35 us -> 37.3 us
    ppermute x29 -> x31, waiting for transfers between devices: 29.3 us -> 25.9 us  [permute(): return lax.ppermute(x, axis, [(i, i ^ k) for i in range(n)])]
    ppermute x29 -> x31, starting transfers between devices: 35 us -> 37.3 us  [permute(): return lax.ppermute(x, axis, [(i, i ^ k) for i in range(n)])]
  transfers between devices with their start and end apart: 29 -> 31, of which waited for: 17 -> 19; matrix products, arithmetic and copies ran while one was open for 0% -> 1% of each run, Pallas kernels for 6% -> 6%
where the time goes in v5:
time: 79.1 us; the launch traced here: 78.8 us
  starting transfers between devices  37.3 us (47%)
  waiting for transfers between devices  25.9 us (33%)
  Pallas kernels  10.7 us (14%)
  local copies, waits for them, and re-layouts  3.06 us (4%)
  between operations  0.96 us (1%)
  other arithmetic  0.84 us (1%)
    ppermute x31, starting transfers between devices, permute(): return lax.ppermute(x, axis, [(i, i ^ k) for i in range(n)])  37.3 us
    ppermute x31, waiting for transfers between devices, permute(): return lax.ppermute(x, axis, [(i, i ^ k) for i in range(n)])  25.9 us
    unnamed x25, local copies, waits for them, and re-layouts  2.99 us
    pallas_call x1, Pallas kernels, body(): call(functools.partial(attend_second, span), [shape((span, rows // span *...  1.7 us
    pallas_call x1, Pallas kernels, body(): call(functools.partial(attend_first, span), [shape((rows, HEAD), f32), sh...  1.62 us
  transfers between devices with their start and end apart: 31, of which 19 were waited for; matrix products, arithmetic and copies ran while one was open for 1% of the time, Pallas kernels for 6%

profile of v5, /device:TPU:0, one launch (start us, length us, event | category | flops | bytes accessed | tf_op | source)
XLA Modules:
  0.0 78.8 jit_solution(273251944296450515)
XLA Ops:
  0.6 1.5 %shard_map.140.kv = bf16[192,256]{1,0:T(8,128)(2,1)} custom-call(bf16[128,512]{1,0:T(8,128)(2,1)} %ck.1, bf16[128,512]{1,0:T(8,128)(2,1)} %cv.1, bf16[64,512]{1,0:T(8,128)(2,1)} %bk.1, bf16[64,512]{1,0:T(8,128)(2,1)} %bv.1), custom_call_target="tpu_custom_call" | custom-call | tf_op jit(solution)/shard_map/pallas_call | solution.py:373
  2.2 3.0 %collective-permute-start = (bf16[192,256]{1,0:T(8,128)(2,1)}, bf16[192,256]{1,0:T(8,128)(2,1)S(1)}, u32[]{:S(2)}, u32[]{:S(2)}) collective-permute-start(bf16[192,256]{1,0:T(8,128)(2,1)} %shard_map.140.kv), channel_id=1, source_target_pairs={{0,8},{4,12},{8,0},{12,4},{16,24},{20,28},{24,16},{28,20},{1,9},{5... | collective-permute-start | bytes 294920 | tf_op jit(solution)/shard_map/ppermute | solution.py:326
  5.2 1.5 %collective-permute-start.1 = (bf16[192,256]{1,0:T(8,128)(2,1)}, bf16[192,256]{1,0:T(8,128)(2,1)S(1)}, u32[]{:S(2)}, u32[]{:S(2)}) collective-permute-start(bf16[192,256]{1,0:T(8,128)(2,1)} %shard_map.140.kv), channel_id=1, source_target_pairs={{0,16},{4,20},{8,24},{12,28},{16,0},{20,4},{24,8},{28,12},{1,17},{... | collective-permute-start | bytes 294920 | tf_op jit(solution)/shard_map/ppermute | solution.py:326
  11.0 1.4 %collective-permute-done.2 = bf16[192,256]{1,0:T(8,128)(2,1)S(1)} collective-permute-done((bf16[192,256]{1,0:T(8,128)(2,1)}, bf16[192,256]{1,0:T(8,128)(2,1)S(1)}, u32[]{:S(2)}, u32[]{:S(2)}) %collective-permute-start.2) | collective-permute-done | bytes 98336 | tf_op jit(solution)/shard_map/ppermute | solution.py:326
  12.6 1.6 %shard_map.143 = (f32[1024,128]{1,0:T(8,128)S(1)}, f32[1024,128]{1,0:T(8,128)S(1)}, f32[1024,128]{1,0:T(8,128)S(1)}) custom-call(bf16[1024,128]{1,0:T(8,128)(2,1)S(1)} %bitcast.13, bf16[768,256]{1,0:T(8,128)(2,1)S(1)} %constant_dynamic-update-slice_fusion.kv, f32[64,768]{1,0:T(8,128)S(1)} %get-tuple-element.73.bias), custom_call_target="tpu_custom_call" | custom-call | flops 402653184 | bytes 4194304 | tf_op jit(solution)/shard_map/pallas_call | solution.py:405
  14.3 1.7 %shard_map.144 = (bf16[64,1024]{1,0:T(8,128)(2,1)S(1)}, bf16[64,1024]{1,0:T(8,128)(2,1)S(1)}) custom-call(bf16[1024,128]{1,0:T(8,128)(2,1)S(1)} %bitcast.14, bf16[768,256]{1,0:T(8,128)(2,1)S(1)} %collective-permute-done.3.kv, f32[64,768]{1,0:T(8,128)S(1)} %get-tuple-element.72.bias, f32[1024,128]{1,0:T(8,128)S(1)} %get-tuple-element.74.o_in, ...), custom_call_target="tpu_custom_call" | custom-call | flops 402653184 | bytes 4194304 | tf_op jit(solution)/shard_map/pallas_call | solution.py:412
  16.7 1.1 %collective-permute-start.7 = (bf16[64,1024]{1,0:T(8,128)(2,1)S(1)}, bf16[64,1024]{1,0:T(8,128)(2,1)S(1)}, u32[]{:S(2)}, u32[]{:S(2)}) collective-permute-start(bf16[64,1024]{1,0:T(8,128)(2,1)S(1)} %get-tuple-element.84), channel_id=1, source_target_pairs={{0,16},{4,20},{8,24},{12,28},{16,0},{20,4},{24,8},{28,12},{1,17},{... | collective-permute-start | bytes 393224 | tf_op jit(solution)/shard_map/ppermute | solution.py:326
  17.7 1.6 %collective-permute-start.10 = (f32[8,128]{1,0:T(8,128)S(1)}, f32[8,128]{1,0:T(8,128)S(1)}, u32[]{:S(2)}, u32[]{:S(2)}) collective-permute-start(f32[8,128]{1,0:T(8,128)S(1)} %get-tuple-element.82), channel_id=1, source_target_pairs={{0,1},{1,0},{2,3},{3,2},{4,5},{5,4},{6,7},{7,6},{8,9},{9,8},{10,11... | collective-permute-start | bytes 12296 | tf_op jit(solution)/shard_map/ppermute | solution.py:326
  19.3 1.2 %collective-permute-start.5 = (bf16[64,1024]{1,0:T(8,128)(2,1)S(1)}, bf16[64,1024]{1,0:T(8,128)(2,1)S(1)}, u32[]{:S(2)}, u32[]{:S(2)}) collective-permute-start(bf16[64,1024]{1,0:T(8,128)(2,1)S(1)} %get-tuple-element.84), channel_id=1, source_target_pairs={{0,8},{4,12},{8,0},{12,4},{16,24},{20,28},{24,16},{28,20},{1,9},{5... | collective-permute-start | bytes 393224 | tf_op jit(solution)/shard_map/ppermute | solution.py:326
  20.6 1.1 %collective-permute-start.6 = (bf16[64,1024]{1,0:T(8,128)(2,1)S(1)}, bf16[64,1024]{1,0:T(8,128)(2,1)S(1)}, u32[]{:S(2)}, u32[]{:S(2)}) collective-permute-start(bf16[64,1024]{1,0:T(8,128)(2,1)S(1)} %get-tuple-element.83), channel_id=1, source_target_pairs={{0,16},{4,20},{8,24},{12,28},{16,0},{20,4},{24,8},{28,12},{1,17},{... | collective-permute-start | bytes 393224 | tf_op jit(solution)/shard_map/ppermute | solution.py:326
  23.9 2.6 %collective-permute-start.11 = (f32[16,128]{1,0:T(8,128)S(1)}, f32[16,128]{1,0:T(8,128)S(1)}, u32[]{:S(2)}, u32[]{:S(2)}) collective-permute-start(f32[16,128]{1,0:T(8,128)S(1)} %pad_maximum_fusion.2), channel_id=1, source_target_pairs={{0,2},{1,3},{2,0},{3,1},{4,6},{5,7},{6,4},{7,5},{8,10},{9,11},{10,... | collective-permute-start | bytes 24584 | tf_op jit(solution)/shard_map/ppermute | solution.py:326
  26.5 2.0 %collective-permute-done.11 = f32[16,128]{1,0:T(8,128)S(1)} collective-permute-done((f32[16,128]{1,0:T(8,128)S(1)}, f32[16,128]{1,0:T(8,128)S(1)}, u32[]{:S(2)}, u32[]{:S(2)}) %collective-permute-start.11) | collective-permute-done | bytes 8224 | tf_op jit(solution)/shard_map/ppermute | solution.py:326
  29.4 1.9 %collective-permute-done.12.heads_out = bf16[256,2048]{1,0:T(8,128)(2,1)S(1)} collective-permute-done((bf16[256,2048]{1,0:T(8,128)(2,1)S(1)}, bf16[256,2048]{1,0:T(8,128)(2,1)S(1)}, u32[]{:S(2)}, u32[]{:S(2)}) %collective-permute-start.12) | collective-permute-done | bytes 1048608 | tf_op jit(solution)/shard_map/ppermute | solution.py:326
  32.4 2.1 %collective-permute-start.16 = (bf16[128,256]{1,0:T(8,128)(2,1)S(1)}, bf16[128,256]{1,0:T(8,128)(2,1)S(1)}, u32[]{:S(2)}, u32[]{:S(2)}) collective-permute-start(bf16[128,256]{1,0:T(8,128)(2,1)S(1)} %get-tuple-element.98), channel_id=1, source_target_pairs={{0,1},{1,0},{2,3},{3,2},{4,5},{5,4},{6,7},{7,6},{8,9},{9,8},{10,11... | collective-permute-start | bytes 196616 | tf_op jit(solution)/shard_map/ppermute | solution.py:326
  34.6 2.6 %collective-permute-start.14 = (bf16[128,256]{1,0:T(8,128)(2,1)S(1)}, bf16[128,256]{1,0:T(8,128)(2,1)S(1)}, u32[]{:S(2)}, u32[]{:S(2)}) collective-permute-start(bf16[128,256]{1,0:T(8,128)(2,1)S(1)} %get-tuple-element.95), channel_id=1, source_target_pairs={{0,2},{1,3},{2,0},{3,1},{4,6},{5,7},{6,4},{7,5},{8,10},{9,11},{10,... | collective-permute-start | bytes 196616 | tf_op jit(solution)/shard_map/ppermute | solution.py:326
  37.2 1.7 %collective-permute-start.15 = (bf16[128,256]{1,0:T(8,128)(2,1)S(1)}, bf16[128,256]{1,0:T(8,128)(2,1)S(1)}, u32[]{:S(2)}, u32[]{:S(2)}) collective-permute-start(bf16[128,256]{1,0:T(8,128)(2,1)S(1)} %get-tuple-element.96), channel_id=1, source_target_pairs={{0,3},{1,2},{2,1},{3,0},{4,7},{5,6},{6,5},{7,4},{8,11},{9,10},{10,... | collective-permute-start | bytes 196616 | tf_op jit(solution)/shard_map/ppermute | solution.py:326
  38.9 1.8 %collective-permute-start.17 = (bf16[128,256]{1,0:T(8,128)(2,1)S(1)}, bf16[128,256]{1,0:T(8,128)(2,1)S(1)}, u32[]{:S(2)}, u32[]{:S(2)}) collective-permute-start(bf16[128,256]{1,0:T(8,128)(2,1)S(1)} %add_convert_fusion.2), channel_id=1, source_target_pairs={{0,2},{1,3},{2,0},{3,1},{4,6},{5,7},{6,4},{7,5},{8,10},{9,11},{10,... | collective-permute-start | bytes 196616 | tf_op jit(solution)/shard_map/ppermute | solution.py:326
  41.2 4.2 %collective-permute-done.15.refs_3_ = bf16[128,256]{1,0:T(8,128)(2,1)S(1)} collective-permute-done((bf16[128,256]{1,0:T(8,128)(2,1)S(1)}, bf16[128,256]{1,0:T(8,128)(2,1)S(1)}, u32[]{:S(2)}, u32[]{:S(2)}) %collective-permute-start.15) | collective-permute-done | bytes 65568 | tf_op jit(solution)/shard_map/ppermute | solution.py:326
  45.4 2.1 %collective-permute-done.17.refs_4_ = bf16[128,256]{1,0:T(8,128)(2,1)S(1)} collective-permute-done((bf16[128,256]{1,0:T(8,128)(2,1)S(1)}, bf16[128,256]{1,0:T(8,128)(2,1)S(1)}, u32[]{:S(2)}, u32[]{:S(2)}) %collective-permute-start.17) | collective-permute-done | bytes 65568 | tf_op jit(solution)/shard_map/ppermute | solution.py:326
  49.0 1.0 %collective-permute-done.18.theirs = bf16[64,3200]{1,0:T(8,128)(2,1)S(1)} collective-permute-done((bf16[64,3200]{1,0:T(8,128)(2,1)S(1)}, bf16[64,3200]{1,0:T(8,128)(2,1)S(1)}, u32[]{:S(2)}, u32[]{:S(2)}) %collective-permute-start.18) | collective-permute-done | bytes 409632 | tf_op jit(solution)/shard_map/ppermute | solution.py:326
  51.1 1.1 %collective-permute-start.20 = (bf16[16,3200]{1,0:T(8,128)(2,1)S(1)}, bf16[16,3200]{1,0:T(8,128)(2,1)S(1)}, u32[]{:S(2)}, u32[]{:S(2)}) collective-permute-start(bf16[16,3200]{1,0:T(8,128)(2,1)S(1)} %get-tuple-element.105), channel_id=1, source_target_pairs={{0,16},{4,20},{8,24},{12,28},{16,0},{20,4},{24,8},{28,12},{1,17},{... | collective-permute-start | bytes 307208 | tf_op jit(solution)/shard_map/ppermute | solution.py:326
  52.3 1.5 %collective-permute-start.21 = (bf16[16,3200]{1,0:T(8,128)(2,1)S(1)}, bf16[16,3200]{1,0:T(8,128)(2,1)S(1)}, u32[]{:S(2)}, u32[]{:S(2)}) collective-permute-start(bf16[16,3200]{1,0:T(8,128)(2,1)S(1)} %get-tuple-element.106), channel_id=1, source_target_pairs={{0,24},{4,28},{8,16},{12,20},{16,8},{20,12},{24,0},{28,4},{1,25},{... | collective-permute-start | bytes 307208 | tf_op jit(solution)/shard_map/ppermute | solution.py:326
  53.7 1.9 %collective-permute-done.19.refs_1_ = bf16[16,3200]{1,0:T(8,128)(2,1)S(1)} collective-permute-done((bf16[16,3200]{1,0:T(8,128)(2,1)S(1)}, bf16[16,3200]{1,0:T(8,128)(2,1)S(1)}, u32[]{:S(2)}, u32[]{:S(2)}) %collective-permute-start.19) | collective-permute-done | bytes 102432 | tf_op jit(solution)/shard_map/ppermute | solution.py:326
  55.6 2.4 %collective-permute-done.20.refs_2_ = bf16[16,3200]{1,0:T(8,128)(2,1)S(1)} collective-permute-done((bf16[16,3200]{1,0:T(8,128)(2,1)S(1)}, bf16[16,3200]{1,0:T(8,128)(2,1)S(1)}, u32[]{:S(2)}, u32[]{:S(2)}) %collective-permute-start.20) | collective-permute-done | bytes 102432 | tf_op jit(solution)/shard_map/ppermute | solution.py:326
  58.6 2.6 %collective-permute-start.26 = (bf16[128,512]{1,0:T(8,128)(2,1)S(1)}, bf16[128,512]{1,0:T(8,128)(2,1)S(1)}, u32[]{:S(2)}, u32[]{:S(2)}) collective-permute-start(bf16[128,512]{1,0:T(8,128)(2,1)S(1)} %add_convert_fusion.1), channel_id=1, source_target_pairs={{0,2},{1,3},{2,0},{3,1},{4,6},{5,7},{6,4},{7,5},{8,10},{9,11},{10,... | collective-permute-start | bytes 393224 | tf_op jit(solution)/shard_map/ppermute | solution.py:326
  61.3 1.2 %collective-permute-start.23 = (bf16[16,1536]{1,0:T(8,128)(2,1)S(1)}, bf16[16,1536]{1,0:T(8,128)(2,1)S(1)}, u32[]{:S(2)}, u32[]{:S(2)}) collective-permute-start(bf16[16,1536]{1,0:T(8,128)(2,1)S(1)} %shard_map.150), channel_id=1, source_target_pairs={{0,8},{4,12},{8,0},{12,4},{16,24},{20,28},{24,16},{28,20},{1,9},{5... | collective-permute-start | bytes 147464 | tf_op jit(solution)/shard_map/ppermute | solution.py:326
  63.4 1.4 %collective-permute-start.25 = (bf16[16,1536]{1,0:T(8,128)(2,1)S(1)}, bf16[16,1536]{1,0:T(8,128)(2,1)S(1)}, u32[]{:S(2)}, u32[]{:S(2)}) collective-permute-start(bf16[16,1536]{1,0:T(8,128)(2,1)S(1)} %shard_map.150), channel_id=1, source_target_pairs={{0,24},{4,28},{8,16},{12,20},{16,8},{20,12},{24,0},{28,4},{1,25},{... | collective-permute-start | bytes 147464 | tf_op jit(solution)/shard_map/ppermute | solution.py:326
  65.5 1.1 %collective-permute-done.24 = bf16[16,1536]{1,0:T(8,128)(2,1)S(1)} collective-permute-done((bf16[16,1536]{1,0:T(8,128)(2,1)S(1)}, bf16[16,1536]{1,0:T(8,128)(2,1)S(1)}, u32[]{:S(2)}, u32[]{:S(2)}) %collective-permute-start.24) | collective-permute-done | bytes 49184 | tf_op jit(solution)/shard_map/ppermute | solution.py:326
  66.6 1.8 %collective-permute-done.25 = bf16[16,1536]{1,0:T(8,128)(2,1)S(1)} collective-permute-done((bf16[16,1536]{1,0:T(8,128)(2,1)S(1)}, bf16[16,1536]{1,0:T(8,128)(2,1)S(1)}, u32[]{:S(2)}, u32[]{:S(2)}) %collective-permute-start.25) | collective-permute-done | bytes 49184 | tf_op jit(solution)/shard_map/ppermute | solution.py:326
  70.9 1.3 %collective-permute-start.29 = (bf16[32,512]{1,0:T(8,128)(2,1)S(1)}, bf16[32,512]{1,0:T(8,128)(2,1)S(1)}, u32[]{:S(2)}, u32[]{:S(2)}) collective-permute-start(bf16[32,512]{1,0:T(8,128)(2,1)S(1)} %get-tuple-element.122), channel_id=1, source_target_pairs={{0,2},{1,3},{2,0},{3,1},{4,6},{5,7},{6,4},{7,5},{8,10},{9,11},{10,... | collective-permute-start | bytes 98312 | tf_op jit(solution)/shard_map/ppermute | solution.py:326
  72.2 2.6 %collective-permute-start.30 = (bf16[32,512]{1,0:T(8,128)(2,1)S(1)}, bf16[32,512]{1,0:T(8,128)(2,1)S(1)}, u32[]{:S(2)}, u32[]{:S(2)}) collective-permute-start(bf16[32,512]{1,0:T(8,128)(2,1)S(1)} %get-tuple-element.123), channel_id=1, source_target_pairs={{0,3},{1,2},{2,1},{3,0},{4,7},{5,6},{6,5},{7,4},{8,11},{9,10},{10,... | collective-permute-start | bytes 98312 | tf_op jit(solution)/shard_map/ppermute | solution.py:326
  75.9 2.0 %collective-permute-done.30.refs_3_ = bf16[32,512]{1,0:T(8,128)(2,1)S(1)} collective-permute-done((bf16[32,512]{1,0:T(8,128)(2,1)S(1)}, bf16[32,512]{1,0:T(8,128)(2,1)S(1)}, u32[]{:S(2)}, u32[]{:S(2)}) %collective-permute-start.30) | collective-permute-done | bytes 32800 | tf_op jit(solution)/shard_map/ppermute | solution.py:326
  (79 shorter events, 19.3 us)
Async XLA Ops:
  2.2 8.5 %collective-permute-start = (bf16[192,256]{1,0:T(8,128)(2,1)}, bf16[192,256]{1,0:T(8,128)(2,1)S(1)}, u32[]{:S(2)}, u32[]{:S(2)}) collective-permute-start(bf16[192,256]{1,0:T(8,128)(2,1)} %shard_map.140.kv), channel_id=1, source_target_pairs={{0,8},{4,12},{8,0},{12,4},{16,24},{20,28},{24,16},{28,20},{1,9},{5... | collective-permute-start | bytes 294920 | tf_op jit(solution)/shard_map/ppermute | solution.py:326
  5.2 5.9 %collective-permute-start.1 = (bf16[192,256]{1,0:T(8,128)(2,1)}, bf16[192,256]{1,0:T(8,128)(2,1)S(1)}, u32[]{:S(2)}, u32[]{:S(2)}) collective-permute-start(bf16[192,256]{1,0:T(8,128)(2,1)} %shard_map.140.kv), channel_id=1, source_target_pairs={{0,16},{4,20},{8,24},{12,28},{16,0},{20,4},{24,8},{28,12},{1,17},{... | collective-permute-start | bytes 294920 | tf_op jit(solution)/shard_map/ppermute | solution.py:326
  6.7 5.7 %collective-permute-start.2 = (bf16[192,256]{1,0:T(8,128)(2,1)}, bf16[192,256]{1,0:T(8,128)(2,1)S(1)}, u32[]{:S(2)}, u32[]{:S(2)}) collective-permute-start(bf16[192,256]{1,0:T(8,128)(2,1)} %shard_map.140.kv), channel_id=1, source_target_pairs={{0,24},{4,28},{8,16},{12,20},{16,8},{20,12},{24,0},{28,4},{1,25},{... | collective-permute-start | bytes 294920 | tf_op jit(solution)/shard_map/ppermute | solution.py:326
  12.5 1.8 %collective-permute-start.3 = (bf16[768,256]{1,0:T(8,128)(2,1)S(1)}, bf16[768,256]{1,0:T(8,128)(2,1)S(1)}, u32[]{:S(2)}, u32[]{:S(2)}) collective-permute-start(bf16[768,256]{1,0:T(8,128)(2,1)S(1)} %constant_dynamic-update-slice_fusion.kv), channel_id=1, source_target_pairs={{0,4},{4,0},{8,12},{12,8},{16,20},{20,16},{24,28},{28,24},{1,5},{5... | collective-permute-start | bytes 1179656 | tf_op jit(solution)/shard_map/ppermute | solution.py:326
  14.3 33.2 %slice-start = ((s8[6291456]{0:T(1024)(128)(4,1)}), s8[4194304]{0:T(1024)(128)(4,1)S(1)}, s32[]{:S(2)}) async-start(s8[6291456]{0:T(1024)(128)(4,1)} %bitcast.11), calls=%async_computation | async-start | bytes 8388608
  16.0 6.2 %collective-permute-start.4 = (bf16[64,1024]{1,0:T(8,128)(2,1)S(1)}, bf16[64,1024]{1,0:T(8,128)(2,1)S(1)}, u32[]{:S(2)}, u32[]{:S(2)}) collective-permute-start(bf16[64,1024]{1,0:T(8,128)(2,1)S(1)} %get-tuple-element.83), channel_id=1, source_target_pairs={{0,8},{4,12},{8,0},{12,4},{16,24},{20,28},{24,16},{28,20},{1,9},{5... | collective-permute-start | bytes 393224 | tf_op jit(solution)/shard_map/ppermute | solution.py:326
  16.7 6.4 %collective-permute-start.7 = (bf16[64,1024]{1,0:T(8,128)(2,1)S(1)}, bf16[64,1024]{1,0:T(8,128)(2,1)S(1)}, u32[]{:S(2)}, u32[]{:S(2)}) collective-permute-start(bf16[64,1024]{1,0:T(8,128)(2,1)S(1)} %get-tuple-element.84), channel_id=1, source_target_pairs={{0,16},{4,20},{8,24},{12,28},{16,0},{20,4},{24,8},{28,12},{1,17},{... | collective-permute-start | bytes 393224 | tf_op jit(solution)/shard_map/ppermute | solution.py:326
  17.7 6.2 %collective-permute-start.10 = (f32[8,128]{1,0:T(8,128)S(1)}, f32[8,128]{1,0:T(8,128)S(1)}, u32[]{:S(2)}, u32[]{:S(2)}) collective-permute-start(f32[8,128]{1,0:T(8,128)S(1)} %get-tuple-element.82), channel_id=1, source_target_pairs={{0,1},{1,0},{2,3},{3,2},{4,5},{5,4},{6,7},{7,6},{8,9},{9,8},{10,11... | collective-permute-start | bytes 12296 | tf_op jit(solution)/shard_map/ppermute | solution.py:326
  19.3 9.2 %collective-permute-start.5 = (bf16[64,1024]{1,0:T(8,128)(2,1)S(1)}, bf16[64,1024]{1,0:T(8,128)(2,1)S(1)}, u32[]{:S(2)}, u32[]{:S(2)}) collective-permute-start(bf16[64,1024]{1,0:T(8,128)(2,1)S(1)} %get-tuple-element.84), channel_id=1, source_target_pairs={{0,8},{4,12},{8,0},{12,4},{16,24},{20,28},{24,16},{28,20},{1,9},{5... | collective-permute-start | bytes 393224 | tf_op jit(solution)/shard_map/ppermute | solution.py:326
  20.6 7.9 %collective-permute-start.6 = (bf16[64,1024]{1,0:T(8,128)(2,1)S(1)}, bf16[64,1024]{1,0:T(8,128)(2,1)S(1)}, u32[]{:S(2)}, u32[]{:S(2)}) collective-permute-start(bf16[64,1024]{1,0:T(8,128)(2,1)S(1)} %get-tuple-element.83), channel_id=1, source_target_pairs={{0,16},{4,20},{8,24},{12,28},{16,0},{20,4},{24,8},{28,12},{1,17},{... | collective-permute-start | bytes 393224 | tf_op jit(solution)/shard_map/ppermute | solution.py:326
  22.2 6.3 %collective-permute-start.8 = (bf16[64,1024]{1,0:T(8,128)(2,1)S(1)}, bf16[64,1024]{1,0:T(8,128)(2,1)S(1)}, u32[]{:S(2)}, u32[]{:S(2)}) collective-permute-start(bf16[64,1024]{1,0:T(8,128)(2,1)S(1)} %collective-permute-done.4), channel_id=1, source_target_pairs={{0,16},{4,20},{8,24},{12,28},{16,0},{20,4},{24,8},{28,12},{1,17},{... | collective-permute-start | bytes 393224 | tf_op jit(solution)/shard_map/ppermute | solution.py:326
  23.1 5.5 %collective-permute-start.9 = (bf16[64,1024]{1,0:T(8,128)(2,1)S(1)}, bf16[64,1024]{1,0:T(8,128)(2,1)S(1)}, u32[]{:S(2)}, u32[]{:S(2)}) collective-permute-start(bf16[64,1024]{1,0:T(8,128)(2,1)S(1)} %collective-permute-done.7), channel_id=1, source_target_pairs={{0,8},{4,12},{8,0},{12,4},{16,24},{20,28},{24,16},{28,20},{1,9},{5... | collective-permute-start | bytes 393224 | tf_op jit(solution)/shard_map/ppermute | solution.py:326
  23.9 4.6 %collective-permute-start.11 = (f32[16,128]{1,0:T(8,128)S(1)}, f32[16,128]{1,0:T(8,128)S(1)}, u32[]{:S(2)}, u32[]{:S(2)}) collective-permute-start(f32[16,128]{1,0:T(8,128)S(1)} %pad_maximum_fusion.2), channel_id=1, source_target_pairs={{0,2},{1,3},{2,0},{3,1},{4,6},{5,7},{6,4},{7,5},{8,10},{9,11},{10,... | collective-permute-start | bytes 24584 | tf_op jit(solution)/shard_map/ppermute | solution.py:326
  28.6 2.7 %collective-permute-start.12 = (bf16[256,2048]{1,0:T(8,128)(2,1)S(1)}, bf16[256,2048]{1,0:T(8,128)(2,1)S(1)}, u32[]{:S(2)}, u32[]{:S(2)}) collective-permute-start(bf16[256,2048]{1,0:T(8,128)(2,1)S(1)} %maximum_maximum_fusion.heads_out), channel_id=1, source_target_pairs={{0,4},{4,0},{8,12},{12,8},{16,20},{20,16},{24,28},{28,24},{1,5},{5... | collective-permute-start | bytes 3145736 | tf_op jit(solution)/shard_map/ppermute | solution.py:326
  32.4 6.5 %collective-permute-start.16 = (bf16[128,256]{1,0:T(8,128)(2,1)S(1)}, bf16[128,256]{1,0:T(8,128)(2,1)S(1)}, u32[]{:S(2)}, u32[]{:S(2)}) collective-permute-start(bf16[128,256]{1,0:T(8,128)(2,1)S(1)} %get-tuple-element.98), channel_id=1, source_target_pairs={{0,1},{1,0},{2,3},{3,2},{4,5},{5,4},{6,7},{7,6},{8,9},{9,8},{10,11... | collective-permute-start | bytes 196616 | tf_op jit(solution)/shard_map/ppermute | solution.py:326
  34.5 13.0 %collective-permute-start.13 = (bf16[128,512]{1,0:T(8,128)(2,1)S(1)}, bf16[128,512]{1,0:T(8,128)(2,1)S(1)}, u32[]{:S(2)}, u32[]{:S(2)}) collective-permute-start(bf16[128,512]{1,0:T(8,128)(2,1)S(1)} %get-tuple-element.94), channel_id=1, source_target_pairs={{0,1},{1,0},{2,3},{3,2},{4,5},{5,4},{6,7},{7,6},{8,9},{9,8},{10,11... | collective-permute-start | bytes 393224 | tf_op jit(solution)/shard_map/ppermute | solution.py:326
  34.6 6.6 %collective-permute-start.14 = (bf16[128,256]{1,0:T(8,128)(2,1)S(1)}, bf16[128,256]{1,0:T(8,128)(2,1)S(1)}, u32[]{:S(2)}, u32[]{:S(2)}) collective-permute-start(bf16[128,256]{1,0:T(8,128)(2,1)S(1)} %get-tuple-element.95), channel_id=1, source_target_pairs={{0,2},{1,3},{2,0},{3,1},{4,6},{5,7},{6,4},{7,5},{8,10},{9,11},{10,... | collective-permute-start | bytes 196616 | tf_op jit(solution)/shard_map/ppermute | solution.py:326
  37.2 8.2 %collective-permute-start.15 = (bf16[128,256]{1,0:T(8,128)(2,1)S(1)}, bf16[128,256]{1,0:T(8,128)(2,1)S(1)}, u32[]{:S(2)}, u32[]{:S(2)}) collective-permute-start(bf16[128,256]{1,0:T(8,128)(2,1)S(1)} %get-tuple-element.96), channel_id=1, source_target_pairs={{0,3},{1,2},{2,1},{3,0},{4,7},{5,6},{6,5},{7,4},{8,11},{9,10},{10,... | collective-permute-start | bytes 196616 | tf_op jit(solution)/shard_map/ppermute | solution.py:326
  38.9 8.5 %collective-permute-start.17 = (bf16[128,256]{1,0:T(8,128)(2,1)S(1)}, bf16[128,256]{1,0:T(8,128)(2,1)S(1)}, u32[]{:S(2)}, u32[]{:S(2)}) collective-permute-start(bf16[128,256]{1,0:T(8,128)(2,1)S(1)} %add_convert_fusion.2), channel_id=1, source_target_pairs={{0,2},{1,3},{2,0},{3,1},{4,6},{5,7},{6,4},{7,5},{8,10},{9,11},{10,... | collective-permute-start | bytes 196616 | tf_op jit(solution)/shard_map/ppermute | solution.py:326
  48.2 1.8 %collective-permute-start.18 = (bf16[64,3200]{1,0:T(8,128)(2,1)S(1)}, bf16[64,3200]{1,0:T(8,128)(2,1)S(1)}, u32[]{:S(2)}, u32[]{:S(2)}) collective-permute-start(bf16[64,3200]{1,0:T(8,128)(2,1)S(1)} %shard_map.148), channel_id=1, source_target_pairs={{0,4},{4,0},{8,12},{12,8},{16,20},{20,16},{24,28},{28,24},{1,5},{5... | collective-permute-start | bytes 1228808 | tf_op jit(solution)/shard_map/ppermute | solution.py:326
  50.1 8.4 %collective-permute-start.22 = (bf16[256,512]{1,0:T(8,128)(2,1)S(1)}, bf16[256,512]{1,0:T(8,128)(2,1)S(1)}, u32[]{:S(2)}, u32[]{:S(2)}) collective-permute-start(bf16[256,512]{1,0:T(8,128)(2,1)S(1)} %get-tuple-element.107), channel_id=1, source_target_pairs={{0,1},{1,0},{2,3},{3,2},{4,5},{5,4},{6,7},{7,6},{8,9},{9,8},{10,11... | collective-permute-start | bytes 786440 | tf_op jit(solution)/shard_map/ppermute | solution.py:326
  50.2 5.4 %collective-permute-start.19 = (bf16[16,3200]{1,0:T(8,128)(2,1)S(1)}, bf16[16,3200]{1,0:T(8,128)(2,1)S(1)}, u32[]{:S(2)}, u32[]{:S(2)}) collective-permute-start(bf16[16,3200]{1,0:T(8,128)(2,1)S(1)} %get-tuple-element.104), channel_id=1, source_target_pairs={{0,8},{4,12},{8,0},{12,4},{16,24},{20,28},{24,16},{28,20},{1,9},{5... | collective-permute-start | bytes 307208 | tf_op jit(solution)/shard_map/ppermute | solution.py:326
  51.1 6.9 %collective-permute-start.20 = (bf16[16,3200]{1,0:T(8,128)(2,1)S(1)}, bf16[16,3200]{1,0:T(8,128)(2,1)S(1)}, u32[]{:S(2)}, u32[]{:S(2)}) collective-permute-start(bf16[16,3200]{1,0:T(8,128)(2,1)S(1)} %get-tuple-element.105), channel_id=1, source_target_pairs={{0,16},{4,20},{8,24},{12,28},{16,0},{20,4},{24,8},{28,12},{1,17},{... | collective-permute-start | bytes 307208 | tf_op jit(solution)/shard_map/ppermute | solution.py:326
  52.3 5.7 %collective-permute-start.21 = (bf16[16,3200]{1,0:T(8,128)(2,1)S(1)}, bf16[16,3200]{1,0:T(8,128)(2,1)S(1)}, u32[]{:S(2)}, u32[]{:S(2)}) collective-permute-start(bf16[16,3200]{1,0:T(8,128)(2,1)S(1)} %get-tuple-element.106), channel_id=1, source_target_pairs={{0,24},{4,28},{8,16},{12,20},{16,8},{20,12},{24,0},{28,4},{1,25},{... | collective-permute-start | bytes 307208 | tf_op jit(solution)/shard_map/ppermute | solution.py:326
  58.6 9.9 %collective-permute-start.26 = (bf16[128,512]{1,0:T(8,128)(2,1)S(1)}, bf16[128,512]{1,0:T(8,128)(2,1)S(1)}, u32[]{:S(2)}, u32[]{:S(2)}) collective-permute-start(bf16[128,512]{1,0:T(8,128)(2,1)S(1)} %add_convert_fusion.1), channel_id=1, source_target_pairs={{0,2},{1,3},{2,0},{3,1},{4,6},{5,7},{6,4},{7,5},{8,10},{9,11},{10,... | collective-permute-start | bytes 393224 | tf_op jit(solution)/shard_map/ppermute | solution.py:326
  61.3 4.2 %collective-permute-start.23 = (bf16[16,1536]{1,0:T(8,128)(2,1)S(1)}, bf16[16,1536]{1,0:T(8,128)(2,1)S(1)}, u32[]{:S(2)}, u32[]{:S(2)}) collective-permute-start(bf16[16,1536]{1,0:T(8,128)(2,1)S(1)} %shard_map.150), channel_id=1, source_target_pairs={{0,8},{4,12},{8,0},{12,4},{16,24},{20,28},{24,16},{28,20},{1,9},{5... | collective-permute-start | bytes 147464 | tf_op jit(solution)/shard_map/ppermute | solution.py:326
  62.5 4.1 %collective-permute-start.24 = (bf16[16,1536]{1,0:T(8,128)(2,1)S(1)}, bf16[16,1536]{1,0:T(8,128)(2,1)S(1)}, u32[]{:S(2)}, u32[]{:S(2)}) collective-permute-start(bf16[16,1536]{1,0:T(8,128)(2,1)S(1)} %shard_map.150), channel_id=1, source_target_pairs={{0,16},{4,20},{8,24},{12,28},{16,0},{20,4},{24,8},{28,12},{1,17},{... | collective-permute-start | bytes 147464 | tf_op jit(solution)/shard_map/ppermute | solution.py:326
  63.4 5.0 %collective-permute-start.25 = (bf16[16,1536]{1,0:T(8,128)(2,1)S(1)}, bf16[16,1536]{1,0:T(8,128)(2,1)S(1)}, u32[]{:S(2)}, u32[]{:S(2)}) collective-permute-start(bf16[16,1536]{1,0:T(8,128)(2,1)S(1)} %shard_map.150), channel_id=1, source_target_pairs={{0,24},{4,28},{8,16},{12,20},{16,8},{20,12},{24,0},{28,4},{1,25},{... | collective-permute-start | bytes 147464 | tf_op jit(solution)/shard_map/ppermute | solution.py:326
  68.4 1.5 %collective-permute-start.27 = (bf16[64,1536]{1,0:T(8,128)(2,1)S(1)}, bf16[64,1536]{1,0:T(8,128)(2,1)S(1)}, u32[]{:S(2)}, u32[]{:S(2)}) collective-permute-start(bf16[64,1536]{1,0:T(8,128)(2,1)S(1)} %pad_maximum_fusion.active), channel_id=1, source_target_pairs={{0,4},{4,0},{8,12},{12,8},{16,20},{20,16},{24,28},{28,24},{1,5},{5... | collective-permute-start | bytes 589832 | tf_op jit(solution)/shard_map/ppermute | solution.py:326
  70.4 5.2 %collective-permute-start.28 = (bf16[32,512]{1,0:T(8,128)(2,1)S(1)}, bf16[32,512]{1,0:T(8,128)(2,1)S(1)}, u32[]{:S(2)}, u32[]{:S(2)}) collective-permute-start(bf16[32,512]{1,0:T(8,128)(2,1)S(1)} %get-tuple-element.121), channel_id=1, source_target_pairs={{0,1},{1,0},{2,3},{3,2},{4,5},{5,4},{6,7},{7,6},{8,9},{9,8},{10,11... | collective-permute-start | bytes 98312 | tf_op jit(solution)/shard_map/ppermute | solution.py:326
  70.9 5.0 %collective-permute-start.29 = (bf16[32,512]{1,0:T(8,128)(2,1)S(1)}, bf16[32,512]{1,0:T(8,128)(2,1)S(1)}, u32[]{:S(2)}, u32[]{:S(2)}) collective-permute-start(bf16[32,512]{1,0:T(8,128)(2,1)S(1)} %get-tuple-element.122), channel_id=1, source_target_pairs={{0,2},{1,3},{2,0},{3,1},{4,6},{5,7},{6,4},{7,5},{8,10},{9,11},{10,... | collective-permute-start | bytes 98312 | tf_op jit(solution)/shard_map/ppermute | solution.py:326
  72.2 5.7 %collective-permute-start.30 = (bf16[32,512]{1,0:T(8,128)(2,1)S(1)}, bf16[32,512]{1,0:T(8,128)(2,1)S(1)}, u32[]{:S(2)}, u32[]{:S(2)}) collective-permute-start(bf16[32,512]{1,0:T(8,128)(2,1)S(1)} %get-tuple-element.123), channel_id=1, source_target_pairs={{0,3},{1,2},{2,1},{3,0},{4,7},{5,6},{6,5},{7,4},{8,11},{9,10},{10,... | collective-permute-start | bytes 98312 | tf_op jit(solution)/shard_map/ppermute | solution.py:326
  (10 other events, 83.5 us)

commit v6 on v5

--- a/solution.py
+++ b/solution.py
@@ -76,8 +76,8 @@
 
 def segment_of(position, seg_starts):
     passed = jnp.full(position.shape, -1, jnp.int32)
-    for n in range(seg_starts.shape[0]):
-        passed = passed + jnp.where(seg_starts[n] <= position, 1, 0)
+    for n in range(seg_starts.shape[1]):
+        passed = passed + jnp.where(seg_starts[:, n : n + 1] <= position, 1, 0)
     return passed
 
 
@@ -96,21 +96,21 @@
     key_seg = segment_of(key_pos, seg_starts)
     query_pos = cache_total + ctx * span + lax.broadcasted_iota(jnp.int32, (span, 1), 0)
     query_seg = segment_of(query_pos, seg_starts)
-    last = seg_starts.shape[0] - 1
+    last = seg_starts.shape[1] - 1
     seen = (key_pos <= query_pos) & (
         (key_seg == query_seg) | (key_seg == 0) | (query_seg == last)
     )
     return jnp.where(seen, 0.0, neg_large)
 
 
-def mask_kernel(span, cache, seg_starts, kv, bias_same, bias_other, kv_copy):
+def prepare(n_exp, top, segments, span, cache, small, kv, bias_same, bias_other, kv_copy, rank, high, low):
     kv_copy[...] = kv[...]
     pieces = bias_same.shape[1] // (cache + span)
+    seg_starts = small[2 * top : 2 * top + 1, :].astype(jnp.int32)[:, :segments]
     bias_same[...] = mask_bias(seg_starts, 0, span, cache, pieces)
     bias_other[...] = mask_bias(seg_starts, 1, span, cache, pieces)
-
-
-def route_kernel(n_exp, routes, gates, rank, high, low):
+    routes = small[:top, :].astype(jnp.int32)
+    gates = small[top : 2 * top, :]
     flight, tokens = rank.shape
     local = flight // n_exp
     expert = lax.broadcasted_iota(jnp.int32, (flight, tokens), 0)
@@ -251,9 +251,9 @@
     rows = out.shape[0]
     width = weight.shape[2]
     at = rows_at(expert * rows, rows, rows)
-    total = arrived[0][at, :].astype(f32) + arrived[1][at, :].astype(f32)
+    total = arrived[0][at, :].astype(f32) + arrived[1 + direct][at, :].astype(f32)
     halves = [0.0, 0.0]
-    for n, ref in enumerate(arrived[2:]):
+    for n, ref in enumerate(arrived[1 : 1 + direct] + arrived[2 + direct :]):
         halves[n >= direct] = halves[n >= direct] + ref[at, :].astype(f32)
     mixed = (total + jnp.concatenate(halves, axis=1)).astype(bf16).astype(f32)
     out[:, width:] = split_square(jnp.sum(mixed * mixed, axis=1, keepdims=True)).astype(out.dtype)
@@ -380,21 +380,26 @@
     kv_moved = over_chips(local_kv)
 
     rows, keys = heads * span, chips * (cache + span)
-    bias_same, bias_other, own_kv = call(
-        functools.partial(mask_kernel, span, cache),
-        [shape((span, keys), f32)] * 2 + [shape(local_kv.shape, bf16)],
-        [SMEM, VMEM],
-        vmem=8,
-        nbytes=1 * MIB,
-    )(seg_starts, local_kv)
-    stacked = queries.reshape(span, heads, HEAD).transpose(1, 0, 2).reshape(rows, HEAD)
-    rank, high, low = call(
-        functools.partial(route_kernel, n_exp),
-        [shape((flight, tokens), f32)] + [shape((flight * CAP, tokens), bf16)] * 2,
+    top, segments = routes.shape[1], seg_starts.shape[0]
+    small = jnp.concatenate(
+        [
+            routes.T.astype(f32),
+            gate_values.T,
+            jnp.pad(seg_starts.astype(f32)[None], ((0, 0), (0, tokens - segments))),
+        ],
+        axis=0,
+    )
+    bias_same, bias_other, own_kv, rank, high, low = call(
+        functools.partial(prepare, n_exp, top, segments, span, cache),
+        [shape((span, keys), f32)] * 2
+        + [shape(local_kv.shape, bf16)]
+        + [shape((flight, tokens), f32)]
+        + [shape((flight * CAP, tokens), bf16)] * 2,
         [VMEM] * 2,
         vmem=8,
-        nbytes=1 * MIB,
-    )(routes.T, gate_values.T)
+        nbytes=2 * MIB,
+    )(small, local_kv)
+    stacked = queries.reshape(span, heads, HEAD).transpose(1, 0, 2).reshape(rows, HEAD)
     kv_moved, stacked, bias_same, bias_other, own_kv, rank = lax.optimization_barrier(
         (kv_moved, stacked, bias_same, bias_other, own_kv, rank)
     )
@@ -453,7 +458,7 @@
     left, right = picks[2::2], picks[3::2]
     passed = [permute(right[2 * k - 1], "exp", 1) for k in range(1, n_exp // 2)]
     direct = [permute(x, "exp", k) for k, x in enumerate(left, 2)]
-    arrived = [picks[0], permute(picks[1], "exp", 1)] + direct
+    arrived = [picks[0]] + direct + [permute(picks[1], "exp", 1)]
     for k, got in enumerate(passed, 1):
         pair = (right[2 * k - 2].astype(f32) + got.astype(f32)).astype(bf16)
         arrived.append(permute(pair, "exp", 2 * k))
@@ -471,6 +476,8 @@
         )(*arrived, gain, expert_in)
 
     sent = gate_up(1, bf16)
+    sent, odd = lax.optimization_barrier((sent, odd))
+    odd = permute(odd, "exp", 1)
     theirs = permute(sent, "ctx", 1)
     mine = gate_up(0, f32)
 
@@ -485,12 +492,8 @@
         ready, sent = lax.optimization_barrier((ready, sent))
         return (ready, *lax.optimization_barrier((step(ready), exchange(sent))))
 
-    chunk, gathered, odd = beside(
-        chunk,
-        odd,
-        lambda c: [permute(c[k], "ctx", 2 * k) for k in range(1, chips)],
-        lambda x: permute(x, "exp", 1),
-    )
+    gathered = [permute(chunk[k], "ctx", 2 * k) for k in range(1, chips)]
+    gathered, odd = lax.optimization_barrier((gathered, odd))
     active = call(
         functools.partial(activate, n_ctx * features),
         shape((size, hidden), bf16),

time: 79.1 us -> 78.1 us (0.987)
  other arithmetic: 0.84 us -> 2.89 us
  local copies, waits for them, and re-layouts: 3.06 us -> 1.03 us
    unnamed x25 -> x19, local copies, waits for them, and re-layouts: 2.99 us -> 0.96 us
  transfers between devices with their start and end apart: 31 -> 31, of which waited for: 19 -> 18; matrix products, arithmetic and copies ran while one was open for 1% -> 4% of each run, Pallas kernels for 6% -> 5%
where the time goes in v6:
time: 78.1 us; the launch traced here: 77.9 us
  starting transfers between devices  36.8 us (47%)
  waiting for transfers between devices  26 us (33%)
  Pallas kernels  10.2 us (13%)
  other arithmetic  2.89 us (4%)
  local copies, waits for them, and re-layouts  1.03 us (1%)
  between operations  0.94 us (1%)
    ppermute x31, starting transfers between devices, permute(): return lax.ppermute(x, axis, [(i, i ^ k) for i in range(n)])  36.8 us
    ppermute x31, waiting for transfers between devices, permute(): return lax.ppermute(x, axis, [(i, i ^ k) for i in range(n)])  26 us
    pallas_call x1, Pallas kernels, body(): call(functools.partial(attend_second, span), [shape((span, rows // span *...  1.7 us
    pallas_call x1, Pallas kernels, body(): call(functools.partial(attend_first, span), [shape((rows, HEAD), f32), sh...  1.62 us
  transfers between devices with their start and end apart: 31, of which 18 were waited for; matrix products, arithmetic and copies ran while one was open for 4% of the time, Pallas kernels for 5%

profile of v6, /device:TPU:0, one launch (start us, length us, event | category | flops | bytes accessed | tf_op | source)
XLA Modules:
  0.0 77.9 jit_solution(2028157955637953677)
XLA Ops:
  0.6 1.5 %shard_map.140.kv = bf16[192,256]{1,0:T(8,128)(2,1)} custom-call(bf16[128,512]{1,0:T(8,128)(2,1)} %ck.1, bf16[128,512]{1,0:T(8,128)(2,1)} %cv.1, bf16[64,512]{1,0:T(8,128)(2,1)} %bk.1, bf16[64,512]{1,0:T(8,128)(2,1)} %bv.1), custom_call_target="tpu_custom_call" | custom-call | tf_op jit(solution)/shard_map/pallas_call | solution.py:373
  2.2 3.0 %collective-permute-start = (bf16[192,256]{1,0:T(8,128)(2,1)}, bf16[192,256]{1,0:T(8,128)(2,1)S(1)}, u32[]{:S(2)}, u32[]{:S(2)}) collective-permute-start(bf16[192,256]{1,0:T(8,128)(2,1)} %shard_map.140.kv), channel_id=1, source_target_pairs={{0,8},{4,12},{8,0},{12,4},{16,24},{20,28},{24,16},{28,20},{1,9},{5... | collective-permute-start | bytes 294920 | tf_op jit(solution)/shard_map/ppermute | solution.py:326
  5.2 1.5 %collective-permute-start.1 = (bf16[192,256]{1,0:T(8,128)(2,1)}, bf16[192,256]{1,0:T(8,128)(2,1)S(1)}, u32[]{:S(2)}, u32[]{:S(2)}) collective-permute-start(bf16[192,256]{1,0:T(8,128)(2,1)} %shard_map.140.kv), channel_id=1, source_target_pairs={{0,16},{4,20},{8,24},{12,28},{16,0},{20,4},{24,8},{28,12},{1,17},{... | collective-permute-start | bytes 294920 | tf_op jit(solution)/shard_map/ppermute | solution.py:326
  11.0 1.4 %collective-permute-done.2 = bf16[192,256]{1,0:T(8,128)(2,1)S(1)} collective-permute-done((bf16[192,256]{1,0:T(8,128)(2,1)}, bf16[192,256]{1,0:T(8,128)(2,1)S(1)}, u32[]{:S(2)}, u32[]{:S(2)}) %collective-permute-start.2) | collective-permute-done | bytes 98336 | tf_op jit(solution)/shard_map/ppermute | solution.py:326
  12.6 1.6 %shard_map.142 = (f32[1024,128]{1,0:T(8,128)S(1)}, f32[1024,128]{1,0:T(8,128)S(1)}, f32[1024,128]{1,0:T(8,128)S(1)}) custom-call(bf16[1024,128]{1,0:T(8,128)(2,1)S(1)} %bitcast.16, bf16[768,256]{1,0:T(8,128)(2,1)S(1)} %constant_dynamic-update-slice_fusion.kv, f32[64,768]{1,0:T(8,128)S(1)} %get-tuple-element.70.bias), custom_call_target="tpu_custom_call" | custom-call | flops 402653184 | bytes 4194304 | tf_op jit(solution)/shard_map/pallas_call | solution.py:410
  14.3 1.7 %shard_map.143 = (bf16[64,1024]{1,0:T(8,128)(2,1)S(1)}, bf16[64,1024]{1,0:T(8,128)(2,1)S(1)}) custom-call(bf16[1024,128]{1,0:T(8,128)(2,1)S(1)} %bitcast.17, bf16[768,256]{1,0:T(8,128)(2,1)S(1)} %collective-permute-done.3.kv, f32[64,768]{1,0:T(8,128)S(1)} %get-tuple-element.69.bias, f32[1024,128]{1,0:T(8,128)S(1)} %get-tuple-element.71.o_in, ...), custom_call_target="tpu_custom_call" | custom-call | flops 402653184 | bytes 4194304 | tf_op jit(solution)/shard_map/pallas_call | solution.py:417
  17.6 1.7 %collective-permute-start.10 = (f32[8,128]{1,0:T(8,128)S(1)}, f32[8,128]{1,0:T(8,128)S(1)}, u32[]{:S(2)}, u32[]{:S(2)}) collective-permute-start(f32[8,128]{1,0:T(8,128)S(1)} %get-tuple-element.79), channel_id=1, source_target_pairs={{0,1},{1,0},{2,3},{3,2},{4,5},{5,4},{6,7},{7,6},{8,9},{9,8},{10,11... | collective-permute-start | bytes 12296 | tf_op jit(solution)/shard_map/ppermute | solution.py:326
  19.2 1.3 %collective-permute-start.5 = (bf16[64,1024]{1,0:T(8,128)(2,1)S(1)}, bf16[64,1024]{1,0:T(8,128)(2,1)S(1)}, u32[]{:S(2)}, u32[]{:S(2)}) collective-permute-start(bf16[64,1024]{1,0:T(8,128)(2,1)S(1)} %get-tuple-element.81), channel_id=1, source_target_pairs={{0,8},{4,12},{8,0},{12,4},{16,24},{20,28},{24,16},{28,20},{1,9},{5... | collective-permute-start | bytes 393224 | tf_op jit(solution)/shard_map/ppermute | solution.py:326
  20.6 1.1 %collective-permute-start.6 = (bf16[64,1024]{1,0:T(8,128)(2,1)S(1)}, bf16[64,1024]{1,0:T(8,128)(2,1)S(1)}, u32[]{:S(2)}, u32[]{:S(2)}) collective-permute-start(bf16[64,1024]{1,0:T(8,128)(2,1)S(1)} %get-tuple-element.80), channel_id=1, source_target_pairs={{0,16},{4,20},{8,24},{12,28},{16,0},{20,4},{24,8},{28,12},{1,17},{... | collective-permute-start | bytes 393224 | tf_op jit(solution)/shard_map/ppermute | solution.py:326
  23.1 1.0 %collective-permute-start.9 = (bf16[64,1024]{1,0:T(8,128)(2,1)S(1)}, bf16[64,1024]{1,0:T(8,128)(2,1)S(1)}, u32[]{:S(2)}, u32[]{:S(2)}) collective-permute-start(bf16[64,1024]{1,0:T(8,128)(2,1)S(1)} %collective-permute-done.7), channel_id=1, source_target_pairs={{0,8},{4,12},{8,0},{12,4},{16,24},{20,28},{24,16},{28,20},{1,9},{5... | collective-permute-start | bytes 393224 | tf_op jit(solution)/shard_map/ppermute | solution.py:326
  24.0 2.6 %collective-permute-start.11 = (f32[16,128]{1,0:T(8,128)S(1)}, f32[16,128]{1,0:T(8,128)S(1)}, u32[]{:S(2)}, u32[]{:S(2)}) collective-permute-start(f32[16,128]{1,0:T(8,128)S(1)} %pad_maximum_fusion.2), channel_id=1, source_target_pairs={{0,2},{1,3},{2,0},{3,1},{4,6},{5,7},{6,4},{7,5},{8,10},{9,11},{10,... | collective-permute-start | bytes 24584 | tf_op jit(solution)/shard_map/ppermute | solution.py:326
  26.6 2.0 %collective-permute-done.11 = f32[16,128]{1,0:T(8,128)S(1)} collective-permute-done((f32[16,128]{1,0:T(8,128)S(1)}, f32[16,128]{1,0:T(8,128)S(1)}, u32[]{:S(2)}, u32[]{:S(2)}) %collective-permute-start.11) | collective-permute-done | bytes 8224 | tf_op jit(solution)/shard_map/ppermute | solution.py:326
  29.5 1.9 %collective-permute-done.12.heads_out = bf16[256,2048]{1,0:T(8,128)(2,1)S(1)} collective-permute-done((bf16[256,2048]{1,0:T(8,128)(2,1)S(1)}, bf16[256,2048]{1,0:T(8,128)(2,1)S(1)}, u32[]{:S(2)}, u32[]{:S(2)}) %collective-permute-start.12) | collective-permute-done | bytes 1048608 | tf_op jit(solution)/shard_map/ppermute | solution.py:326
  31.5 1.0 %shard_map.145 = (f32[128,512]{1,0:T(8,128)S(1)}, bf16[256,512]{1,0:T(8,128)(2,1)S(1)}, bf16[128,512]{1,0:T(8,128)(2,1)S(1)}, bf16[128,512]{1,0:T(8,128)(2,1)S(1...) custom-call(bf16[256,2048]{1,0:T(8,128)(2,1)S(1)} %collective-permut, ...), custom_call_target="tpu_custom_call" | custom-call | flops 536870912 | bytes 4194304 | tf_op jit(solution)/shard_map/pallas_call | solution.py:445
  32.5 2.0 %collective-permute-start.16 = (bf16[128,256]{1,0:T(8,128)(2,1)S(1)}, bf16[128,256]{1,0:T(8,128)(2,1)S(1)}, u32[]{:S(2)}, u32[]{:S(2)}) collective-permute-start(bf16[128,256]{1,0:T(8,128)(2,1)S(1)} %get-tuple-element.95), channel_id=1, source_target_pairs={{0,1},{1,0},{2,3},{3,2},{4,5},{5,4},{6,7},{7,6},{8,9},{9,8},{10,11... | collective-permute-start | bytes 196616 | tf_op jit(solution)/shard_map/ppermute | solution.py:326
  34.6 2.6 %collective-permute-start.13 = (bf16[128,256]{1,0:T(8,128)(2,1)S(1)}, bf16[128,256]{1,0:T(8,128)(2,1)S(1)}, u32[]{:S(2)}, u32[]{:S(2)}) collective-permute-start(bf16[128,256]{1,0:T(8,128)(2,1)S(1)} %get-tuple-element.91), channel_id=1, source_target_pairs={{0,2},{1,3},{2,0},{3,1},{4,6},{5,7},{6,4},{7,5},{8,10},{9,11},{10,... | collective-permute-start | bytes 196616 | tf_op jit(solution)/shard_map/ppermute | solution.py:326
  37.2 1.7 %collective-permute-start.14 = (bf16[128,256]{1,0:T(8,128)(2,1)S(1)}, bf16[128,256]{1,0:T(8,128)(2,1)S(1)}, u32[]{:S(2)}, u32[]{:S(2)}) collective-permute-start(bf16[128,256]{1,0:T(8,128)(2,1)S(1)} %get-tuple-element.92), channel_id=1, source_target_pairs={{0,3},{1,2},{2,1},{3,0},{4,7},{5,6},{6,5},{7,4},{8,11},{9,10},{10,... | collective-permute-start | bytes 196616 | tf_op jit(solution)/shard_map/ppermute | solution.py:326
  38.9 1.8 %collective-permute-start.17 = (bf16[128,256]{1,0:T(8,128)(2,1)S(1)}, bf16[128,256]{1,0:T(8,128)(2,1)S(1)}, u32[]{:S(2)}, u32[]{:S(2)}) collective-permute-start(bf16[128,256]{1,0:T(8,128)(2,1)S(1)} %add_convert_fusion.2), channel_id=1, source_target_pairs={{0,2},{1,3},{2,0},{3,1},{4,6},{5,7},{6,4},{7,5},{8,10},{9,11},{10,... | collective-permute-start | bytes 196616 | tf_op jit(solution)/shard_map/ppermute | solution.py:326
  41.2 4.2 %collective-permute-done.14.refs_2_ = bf16[128,256]{1,0:T(8,128)(2,1)S(1)} collective-permute-done((bf16[128,256]{1,0:T(8,128)(2,1)S(1)}, bf16[128,256]{1,0:T(8,128)(2,1)S(1)}, u32[]{:S(2)}, u32[]{:S(2)}) %collective-permute-start.14) | collective-permute-done | bytes 65568 | tf_op jit(solution)/shard_map/ppermute | solution.py:326
  45.4 2.1 %collective-permute-done.17.refs_4_ = bf16[128,256]{1,0:T(8,128)(2,1)S(1)} collective-permute-done((bf16[128,256]{1,0:T(8,128)(2,1)S(1)}, bf16[128,256]{1,0:T(8,128)(2,1)S(1)}, u32[]{:S(2)}, u32[]{:S(2)}) %collective-permute-start.17) | collective-permute-done | bytes 65568 | tf_op jit(solution)/shard_map/ppermute | solution.py:326
  51.1 1.3 %collective-permute-start.20 = (bf16[16,3200]{1,0:T(8,128)(2,1)S(1)}, bf16[16,3200]{1,0:T(8,128)(2,1)S(1)}, u32[]{:S(2)}, u32[]{:S(2)}) collective-permute-start(bf16[16,3200]{1,0:T(8,128)(2,1)S(1)} %get-tuple-element.99), channel_id=1, source_target_pairs={{0,16},{4,20},{8,24},{12,28},{16,0},{20,4},{24,8},{28,12},{1,17},{... | collective-permute-start | bytes 307208 | tf_op jit(solution)/shard_map/ppermute | solution.py:326
  52.3 1.3 %collective-permute-start.21 = (bf16[16,3200]{1,0:T(8,128)(2,1)S(1)}, bf16[16,3200]{1,0:T(8,128)(2,1)S(1)}, u32[]{:S(2)}, u32[]{:S(2)}) collective-permute-start(bf16[16,3200]{1,0:T(8,128)(2,1)S(1)} %get-tuple-element.100), channel_id=1, source_target_pairs={{0,24},{4,28},{8,16},{12,20},{16,8},{20,12},{24,0},{28,4},{1,25},{... | collective-permute-start | bytes 307208 | tf_op jit(solution)/shard_map/ppermute | solution.py:326
  53.7 3.3 %collective-permute-done.22 = bf16[256,512]{1,0:T(8,128)(2,1)S(1)} collective-permute-done((bf16[256,512]{1,0:T(8,128)(2,1)S(1)}, bf16[256,512]{1,0:T(8,128)(2,1)S(1)}, u32[]{:S(2)}, u32[]{:S(2)}) %collective-permute-start.22) | collective-permute-done | bytes 262176 | tf_op jit(solution)/shard_map/ppermute | solution.py:326
  58.0 2.2 %collective-permute-start.26 = (bf16[128,512]{1,0:T(8,128)(2,1)S(1)}, bf16[128,512]{1,0:T(8,128)(2,1)S(1)}, u32[]{:S(2)}, u32[]{:S(2)}) collective-permute-start(bf16[128,512]{1,0:T(8,128)(2,1)S(1)} %add_convert_fusion.1), channel_id=1, source_target_pairs={{0,2},{1,3},{2,0},{3,1},{4,6},{5,7},{6,4},{7,5},{8,10},{9,11},{10,... | collective-permute-start | bytes 393224 | tf_op jit(solution)/shard_map/ppermute | solution.py:326
  60.3 1.2 %collective-permute-start.23 = (bf16[16,1536]{1,0:T(8,128)(2,1)S(1)}, bf16[16,1536]{1,0:T(8,128)(2,1)S(1)}, u32[]{:S(2)}, u32[]{:S(2)}) collective-permute-start(bf16[16,1536]{1,0:T(8,128)(2,1)S(1)} %shard_map.149), channel_id=1, source_target_pairs={{0,8},{4,12},{8,0},{12,4},{16,24},{20,28},{24,16},{28,20},{1,9},{5... | collective-permute-start | bytes 147464 | tf_op jit(solution)/shard_map/ppermute | solution.py:326
  62.5 1.4 %collective-permute-start.25 = (bf16[16,1536]{1,0:T(8,128)(2,1)S(1)}, bf16[16,1536]{1,0:T(8,128)(2,1)S(1)}, u32[]{:S(2)}, u32[]{:S(2)}) collective-permute-start(bf16[16,1536]{1,0:T(8,128)(2,1)S(1)} %shard_map.149), channel_id=1, source_target_pairs={{0,24},{4,28},{8,16},{12,20},{16,8},{20,12},{24,0},{28,4},{1,25},{... | collective-permute-start | bytes 147464 | tf_op jit(solution)/shard_map/ppermute | solution.py:326
  64.5 1.1 %collective-permute-done.24 = bf16[16,1536]{1,0:T(8,128)(2,1)S(1)} collective-permute-done((bf16[16,1536]{1,0:T(8,128)(2,1)S(1)}, bf16[16,1536]{1,0:T(8,128)(2,1)S(1)}, u32[]{:S(2)}, u32[]{:S(2)}) %collective-permute-start.24) | collective-permute-done | bytes 49184 | tf_op jit(solution)/shard_map/ppermute | solution.py:326
  65.6 1.8 %collective-permute-done.25 = bf16[16,1536]{1,0:T(8,128)(2,1)S(1)} collective-permute-done((bf16[16,1536]{1,0:T(8,128)(2,1)S(1)}, bf16[16,1536]{1,0:T(8,128)(2,1)S(1)}, u32[]{:S(2)}, u32[]{:S(2)}) %collective-permute-start.25) | collective-permute-done | bytes 49184 | tf_op jit(solution)/shard_map/ppermute | solution.py:326
  68.0 1.0 %collective-permute-done.27.active = bf16[64,1536]{1,0:T(8,128)(2,1)S(1)} collective-permute-done((bf16[64,1536]{1,0:T(8,128)(2,1)S(1)}, bf16[64,1536]{1,0:T(8,128)(2,1)S(1)}, u32[]{:S(2)}, u32[]{:S(2)}) %collective-permute-start.27) | collective-permute-done | bytes 196640 | tf_op jit(solution)/shard_map/ppermute | solution.py:326
  69.4 1.0 %collective-permute-start.28 = (bf16[32,512]{1,0:T(8,128)(2,1)S(1)}, bf16[32,512]{1,0:T(8,128)(2,1)S(1)}, u32[]{:S(2)}, u32[]{:S(2)}) collective-permute-start(bf16[32,512]{1,0:T(8,128)(2,1)S(1)} %get-tuple-element.115), channel_id=1, source_target_pairs={{0,1},{1,0},{2,3},{3,2},{4,5},{5,4},{6,7},{7,6},{8,9},{9,8},{10,11... | collective-permute-start | bytes 98312 | tf_op jit(solution)/shard_map/ppermute | solution.py:326
  71.3 2.6 %collective-permute-start.30 = (bf16[32,512]{1,0:T(8,128)(2,1)S(1)}, bf16[32,512]{1,0:T(8,128)(2,1)S(1)}, u32[]{:S(2)}, u32[]{:S(2)}) collective-permute-start(bf16[32,512]{1,0:T(8,128)(2,1)S(1)} %get-tuple-element.117), channel_id=1, source_target_pairs={{0,3},{1,2},{2,1},{3,0},{4,7},{5,6},{6,5},{7,4},{8,11},{9,10},{10,... | collective-permute-start | bytes 98312 | tf_op jit(solution)/shard_map/ppermute | solution.py:326
  75.2 1.7 %collective-permute-done.30.refs_3_ = bf16[32,512]{1,0:T(8,128)(2,1)S(1)} collective-permute-done((bf16[32,512]{1,0:T(8,128)(2,1)S(1)}, bf16[32,512]{1,0:T(8,128)(2,1)S(1)}, u32[]{:S(2)}, u32[]{:S(2)}) %collective-permute-start.30) | collective-permute-done | bytes 32800 | tf_op jit(solution)/shard_map/ppermute | solution.py:326
  (75 shorter events, 19.2 us)
Async XLA Ops:
  2.2 7.9 %collective-permute-start = (bf16[192,256]{1,0:T(8,128)(2,1)}, bf16[192,256]{1,0:T(8,128)(2,1)S(1)}, u32[]{:S(2)}, u32[]{:S(2)}) collective-permute-start(bf16[192,256]{1,0:T(8,128)(2,1)} %shard_map.140.kv), channel_id=1, source_target_pairs={{0,8},{4,12},{8,0},{12,4},{16,24},{20,28},{24,16},{28,20},{1,9},{5... | collective-permute-start | bytes 294920 | tf_op jit(solution)/shard_map/ppermute | solution.py:326
  5.2 5.9 %collective-permute-start.1 = (bf16[192,256]{1,0:T(8,128)(2,1)}, bf16[192,256]{1,0:T(8,128)(2,1)S(1)}, u32[]{:S(2)}, u32[]{:S(2)}) collective-permute-start(bf16[192,256]{1,0:T(8,128)(2,1)} %shard_map.140.kv), channel_id=1, source_target_pairs={{0,16},{4,20},{8,24},{12,28},{16,0},{20,4},{24,8},{28,12},{1,17},{... | collective-permute-start | bytes 294920 | tf_op jit(solution)/shard_map/ppermute | solution.py:326
  6.7 5.7 %collective-permute-start.2 = (bf16[192,256]{1,0:T(8,128)(2,1)}, bf16[192,256]{1,0:T(8,128)(2,1)S(1)}, u32[]{:S(2)}, u32[]{:S(2)}) collective-permute-start(bf16[192,256]{1,0:T(8,128)(2,1)} %shard_map.140.kv), channel_id=1, source_target_pairs={{0,24},{4,28},{8,16},{12,20},{16,8},{20,12},{24,0},{28,4},{1,25},{... | collective-permute-start | bytes 294920 | tf_op jit(solution)/shard_map/ppermute | solution.py:326
  12.5 1.8 %collective-permute-start.3 = (bf16[768,256]{1,0:T(8,128)(2,1)S(1)}, bf16[768,256]{1,0:T(8,128)(2,1)S(1)}, u32[]{:S(2)}, u32[]{:S(2)}) collective-permute-start(bf16[768,256]{1,0:T(8,128)(2,1)S(1)} %constant_dynamic-update-slice_fusion.kv), channel_id=1, source_target_pairs={{0,4},{4,0},{8,12},{12,8},{16,20},{20,16},{24,28},{28,24},{1,5},{5... | collective-permute-start | bytes 1179656 | tf_op jit(solution)/shard_map/ppermute | solution.py:326
  14.3 33.2 %slice-start = ((s8[6291456]{0:T(1024)(128)(4,1)}), s8[4194304]{0:T(1024)(128)(4,1)S(1)}, s32[]{:S(2)}) async-start(s8[6291456]{0:T(1024)(128)(4,1)} %bitcast.14), calls=%async_computation | async-start | bytes 8388608
  16.0 6.4 %collective-permute-start.4 = (bf16[64,1024]{1,0:T(8,128)(2,1)S(1)}, bf16[64,1024]{1,0:T(8,128)(2,1)S(1)}, u32[]{:S(2)}, u32[]{:S(2)}) collective-permute-start(bf16[64,1024]{1,0:T(8,128)(2,1)S(1)} %get-tuple-element.80), channel_id=1, source_target_pairs={{0,8},{4,12},{8,0},{12,4},{16,24},{20,28},{24,16},{28,20},{1,9},{5... | collective-permute-start | bytes 393224 | tf_op jit(solution)/shard_map/ppermute | solution.py:326
  16.7 6.4 %collective-permute-start.7 = (bf16[64,1024]{1,0:T(8,128)(2,1)S(1)}, bf16[64,1024]{1,0:T(8,128)(2,1)S(1)}, u32[]{:S(2)}, u32[]{:S(2)}) collective-permute-start(bf16[64,1024]{1,0:T(8,128)(2,1)S(1)} %get-tuple-element.81), channel_id=1, source_target_pairs={{0,16},{4,20},{8,24},{12,28},{16,0},{20,4},{24,8},{28,12},{1,17},{... | collective-permute-start | bytes 393224 | tf_op jit(solution)/shard_map/ppermute | solution.py:326
  17.6 6.5 %collective-permute-start.10 = (f32[8,128]{1,0:T(8,128)S(1)}, f32[8,128]{1,0:T(8,128)S(1)}, u32[]{:S(2)}, u32[]{:S(2)}) collective-permute-start(f32[8,128]{1,0:T(8,128)S(1)} %get-tuple-element.79), channel_id=1, source_target_pairs={{0,1},{1,0},{2,3},{3,2},{4,5},{5,4},{6,7},{7,6},{8,9},{9,8},{10,11... | collective-permute-start | bytes 12296 | tf_op jit(solution)/shard_map/ppermute | solution.py:326
  19.2 9.4 %collective-permute-start.5 = (bf16[64,1024]{1,0:T(8,128)(2,1)S(1)}, bf16[64,1024]{1,0:T(8,128)(2,1)S(1)}, u32[]{:S(2)}, u32[]{:S(2)}) collective-permute-start(bf16[64,1024]{1,0:T(8,128)(2,1)S(1)} %get-tuple-element.81), channel_id=1, source_target_pairs={{0,8},{4,12},{8,0},{12,4},{16,24},{20,28},{24,16},{28,20},{1,9},{5... | collective-permute-start | bytes 393224 | tf_op jit(solution)/shard_map/ppermute | solution.py:326
  20.6 8.0 %collective-permute-start.6 = (bf16[64,1024]{1,0:T(8,128)(2,1)S(1)}, bf16[64,1024]{1,0:T(8,128)(2,1)S(1)}, u32[]{:S(2)}, u32[]{:S(2)}) collective-permute-start(bf16[64,1024]{1,0:T(8,128)(2,1)S(1)} %get-tuple-element.80), channel_id=1, source_target_pairs={{0,16},{4,20},{8,24},{12,28},{16,0},{20,4},{24,8},{28,12},{1,17},{... | collective-permute-start | bytes 393224 | tf_op jit(solution)/shard_map/ppermute | solution.py:326
  22.3 6.3 %collective-permute-start.8 = (bf16[64,1024]{1,0:T(8,128)(2,1)S(1)}, bf16[64,1024]{1,0:T(8,128)(2,1)S(1)}, u32[]{:S(2)}, u32[]{:S(2)}) collective-permute-start(bf16[64,1024]{1,0:T(8,128)(2,1)S(1)} %collective-permute-done.4), channel_id=1, source_target_pairs={{0,16},{4,20},{8,24},{12,28},{16,0},{20,4},{24,8},{28,12},{1,17},{... | collective-permute-start | bytes 393224 | tf_op jit(solution)/shard_map/ppermute | solution.py:326
  23.1 5.6 %collective-permute-start.9 = (bf16[64,1024]{1,0:T(8,128)(2,1)S(1)}, bf16[64,1024]{1,0:T(8,128)(2,1)S(1)}, u32[]{:S(2)}, u32[]{:S(2)}) collective-permute-start(bf16[64,1024]{1,0:T(8,128)(2,1)S(1)} %collective-permute-done.7), channel_id=1, source_target_pairs={{0,8},{4,12},{8,0},{12,4},{16,24},{20,28},{24,16},{28,20},{1,9},{5... | collective-permute-start | bytes 393224 | tf_op jit(solution)/shard_map/ppermute | solution.py:326
  24.0 4.6 %collective-permute-start.11 = (f32[16,128]{1,0:T(8,128)S(1)}, f32[16,128]{1,0:T(8,128)S(1)}, u32[]{:S(2)}, u32[]{:S(2)}) collective-permute-start(f32[16,128]{1,0:T(8,128)S(1)} %pad_maximum_fusion.2), channel_id=1, source_target_pairs={{0,2},{1,3},{2,0},{3,1},{4,6},{5,7},{6,4},{7,5},{8,10},{9,11},{10,... | collective-permute-start | bytes 24584 | tf_op jit(solution)/shard_map/ppermute | solution.py:326
  28.7 2.7 %collective-permute-start.12 = (bf16[256,2048]{1,0:T(8,128)(2,1)S(1)}, bf16[256,2048]{1,0:T(8,128)(2,1)S(1)}, u32[]{:S(2)}, u32[]{:S(2)}) collective-permute-start(bf16[256,2048]{1,0:T(8,128)(2,1)S(1)} %maximum_maximum_fusion.heads_out), channel_id=1, source_target_pairs={{0,4},{4,0},{8,12},{12,8},{16,20},{20,16},{24,28},{28,24},{1,5},{5... | collective-permute-start | bytes 3145736 | tf_op jit(solution)/shard_map/ppermute | solution.py:326
  32.5 6.4 %collective-permute-start.16 = (bf16[128,256]{1,0:T(8,128)(2,1)S(1)}, bf16[128,256]{1,0:T(8,128)(2,1)S(1)}, u32[]{:S(2)}, u32[]{:S(2)}) collective-permute-start(bf16[128,256]{1,0:T(8,128)(2,1)S(1)} %get-tuple-element.95), channel_id=1, source_target_pairs={{0,1},{1,0},{2,3},{3,2},{4,5},{5,4},{6,7},{7,6},{8,9},{9,8},{10,11... | collective-permute-start | bytes 196616 | tf_op jit(solution)/shard_map/ppermute | solution.py:326
  34.5 13.0 %collective-permute-start.15 = (bf16[128,512]{1,0:T(8,128)(2,1)S(1)}, bf16[128,512]{1,0:T(8,128)(2,1)S(1)}, u32[]{:S(2)}, u32[]{:S(2)}) collective-permute-start(bf16[128,512]{1,0:T(8,128)(2,1)S(1)} %get-tuple-element.93), channel_id=1, source_target_pairs={{0,1},{1,0},{2,3},{3,2},{4,5},{5,4},{6,7},{7,6},{8,9},{9,8},{10,11... | collective-permute-start | bytes 393224 | tf_op jit(solution)/shard_map/ppermute | solution.py:326
  34.6 6.6 %collective-permute-start.13 = (bf16[128,256]{1,0:T(8,128)(2,1)S(1)}, bf16[128,256]{1,0:T(8,128)(2,1)S(1)}, u32[]{:S(2)}, u32[]{:S(2)}) collective-permute-start(bf16[128,256]{1,0:T(8,128)(2,1)S(1)} %get-tuple-element.91), channel_id=1, source_target_pairs={{0,2},{1,3},{2,0},{3,1},{4,6},{5,7},{6,4},{7,5},{8,10},{9,11},{10,... | collective-permute-start | bytes 196616 | tf_op jit(solution)/shard_map/ppermute | solution.py:326
  37.2 8.2 %collective-permute-start.14 = (bf16[128,256]{1,0:T(8,128)(2,1)S(1)}, bf16[128,256]{1,0:T(8,128)(2,1)S(1)}, u32[]{:S(2)}, u32[]{:S(2)}) collective-permute-start(bf16[128,256]{1,0:T(8,128)(2,1)S(1)} %get-tuple-element.92), channel_id=1, source_target_pairs={{0,3},{1,2},{2,1},{3,0},{4,7},{5,6},{6,5},{7,4},{8,11},{9,10},{10,... | collective-permute-start | bytes 196616 | tf_op jit(solution)/shard_map/ppermute | solution.py:326
  38.9 8.5 %collective-permute-start.17 = (bf16[128,256]{1,0:T(8,128)(2,1)S(1)}, bf16[128,256]{1,0:T(8,128)(2,1)S(1)}, u32[]{:S(2)}, u32[]{:S(2)}) collective-permute-start(bf16[128,256]{1,0:T(8,128)(2,1)S(1)} %add_convert_fusion.2), channel_id=1, source_target_pairs={{0,2},{1,3},{2,0},{3,1},{4,6},{5,7},{6,4},{7,5},{8,10},{9,11},{10,... | collective-permute-start | bytes 196616 | tf_op jit(solution)/shard_map/ppermute | solution.py:326
  48.2 1.8 %collective-permute-start.18 = (bf16[64,3200]{1,0:T(8,128)(2,1)S(1)}, bf16[64,3200]{1,0:T(8,128)(2,1)S(1)}, u32[]{:S(2)}, u32[]{:S(2)}) collective-permute-start(bf16[64,3200]{1,0:T(8,128)(2,1)S(1)} %shard_map.147), channel_id=1, source_target_pairs={{0,4},{4,0},{8,12},{12,8},{16,20},{20,16},{24,28},{28,24},{1,5},{5... | collective-permute-start | bytes 1228808 | tf_op jit(solution)/shard_map/ppermute | solution.py:326
  48.3 8.7 %collective-permute-start.22 = (bf16[256,512]{1,0:T(8,128)(2,1)S(1)}, bf16[256,512]{1,0:T(8,128)(2,1)S(1)}, u32[]{:S(2)}, u32[]{:S(2)}) collective-permute-start(bf16[256,512]{1,0:T(8,128)(2,1)S(1)} %get-tuple-element.101), channel_id=1, source_target_pairs={{0,1},{1,0},{2,3},{3,2},{4,5},{5,4},{6,7},{7,6},{8,9},{9,8},{10,11... | collective-permute-start | bytes 786440 | tf_op jit(solution)/shard_map/ppermute | solution.py:326
  50.1 6.9 %collective-permute-start.19 = (bf16[16,3200]{1,0:T(8,128)(2,1)S(1)}, bf16[16,3200]{1,0:T(8,128)(2,1)S(1)}, u32[]{:S(2)}, u32[]{:S(2)}) collective-permute-start(bf16[16,3200]{1,0:T(8,128)(2,1)S(1)} %get-tuple-element.98), channel_id=1, source_target_pairs={{0,8},{4,12},{8,0},{12,4},{16,24},{20,28},{24,16},{28,20},{1,9},{5... | collective-permute-start | bytes 307208 | tf_op jit(solution)/shard_map/ppermute | solution.py:326
  51.1 5.9 %collective-permute-start.20 = (bf16[16,3200]{1,0:T(8,128)(2,1)S(1)}, bf16[16,3200]{1,0:T(8,128)(2,1)S(1)}, u32[]{:S(2)}, u32[]{:S(2)}) collective-permute-start(bf16[16,3200]{1,0:T(8,128)(2,1)S(1)} %get-tuple-element.99), channel_id=1, source_target_pairs={{0,16},{4,20},{8,24},{12,28},{16,0},{20,4},{24,8},{28,12},{1,17},{... | collective-permute-start | bytes 307208 | tf_op jit(solution)/shard_map/ppermute | solution.py:326
  52.3 5.6 %collective-permute-start.21 = (bf16[16,3200]{1,0:T(8,128)(2,1)S(1)}, bf16[16,3200]{1,0:T(8,128)(2,1)S(1)}, u32[]{:S(2)}, u32[]{:S(2)}) collective-permute-start(bf16[16,3200]{1,0:T(8,128)(2,1)S(1)} %get-tuple-element.100), channel_id=1, source_target_pairs={{0,24},{4,28},{8,16},{12,20},{16,8},{20,12},{24,0},{28,4},{1,25},{... | collective-permute-start | bytes 307208 | tf_op jit(solution)/shard_map/ppermute | solution.py:326
  58.0 9.5 %collective-permute-start.26 = (bf16[128,512]{1,0:T(8,128)(2,1)S(1)}, bf16[128,512]{1,0:T(8,128)(2,1)S(1)}, u32[]{:S(2)}, u32[]{:S(2)}) collective-permute-start(bf16[128,512]{1,0:T(8,128)(2,1)S(1)} %add_convert_fusion.1), channel_id=1, source_target_pairs={{0,2},{1,3},{2,0},{3,1},{4,6},{5,7},{6,4},{7,5},{8,10},{9,11},{10,... | collective-permute-start | bytes 393224 | tf_op jit(solution)/shard_map/ppermute | solution.py:326
  60.3 4.2 %collective-permute-start.23 = (bf16[16,1536]{1,0:T(8,128)(2,1)S(1)}, bf16[16,1536]{1,0:T(8,128)(2,1)S(1)}, u32[]{:S(2)}, u32[]{:S(2)}) collective-permute-start(bf16[16,1536]{1,0:T(8,128)(2,1)S(1)} %shard_map.149), channel_id=1, source_target_pairs={{0,8},{4,12},{8,0},{12,4},{16,24},{20,28},{24,16},{28,20},{1,9},{5... | collective-permute-start | bytes 147464 | tf_op jit(solution)/shard_map/ppermute | solution.py:326
  61.5 4.1 %collective-permute-start.24 = (bf16[16,1536]{1,0:T(8,128)(2,1)S(1)}, bf16[16,1536]{1,0:T(8,128)(2,1)S(1)}, u32[]{:S(2)}, u32[]{:S(2)}) collective-permute-start(bf16[16,1536]{1,0:T(8,128)(2,1)S(1)} %shard_map.149), channel_id=1, source_target_pairs={{0,16},{4,20},{8,24},{12,28},{16,0},{20,4},{24,8},{28,12},{1,17},{... | collective-permute-start | bytes 147464 | tf_op jit(solution)/shard_map/ppermute | solution.py:326
  62.5 5.0 %collective-permute-start.25 = (bf16[16,1536]{1,0:T(8,128)(2,1)S(1)}, bf16[16,1536]{1,0:T(8,128)(2,1)S(1)}, u32[]{:S(2)}, u32[]{:S(2)}) collective-permute-start(bf16[16,1536]{1,0:T(8,128)(2,1)S(1)} %shard_map.149), channel_id=1, source_target_pairs={{0,24},{4,28},{8,16},{12,20},{16,8},{20,12},{24,0},{28,4},{1,25},{... | collective-permute-start | bytes 147464 | tf_op jit(solution)/shard_map/ppermute | solution.py:326
  67.5 1.5 %collective-permute-start.27 = (bf16[64,1536]{1,0:T(8,128)(2,1)S(1)}, bf16[64,1536]{1,0:T(8,128)(2,1)S(1)}, u32[]{:S(2)}, u32[]{:S(2)}) collective-permute-start(bf16[64,1536]{1,0:T(8,128)(2,1)S(1)} %pad_maximum_fusion.active), channel_id=1, source_target_pairs={{0,4},{4,0},{8,12},{12,8},{16,20},{20,16},{24,28},{28,24},{1,5},{5... | collective-permute-start | bytes 589832 | tf_op jit(solution)/shard_map/ppermute | solution.py:326
  69.4 5.2 %collective-permute-start.28 = (bf16[32,512]{1,0:T(8,128)(2,1)S(1)}, bf16[32,512]{1,0:T(8,128)(2,1)S(1)}, u32[]{:S(2)}, u32[]{:S(2)}) collective-permute-start(bf16[32,512]{1,0:T(8,128)(2,1)S(1)} %get-tuple-element.115), channel_id=1, source_target_pairs={{0,1},{1,0},{2,3},{3,2},{4,5},{5,4},{6,7},{7,6},{8,9},{9,8},{10,11... | collective-permute-start | bytes 98312 | tf_op jit(solution)/shard_map/ppermute | solution.py:326
  70.4 4.8 %collective-permute-start.29 = (bf16[32,512]{1,0:T(8,128)(2,1)S(1)}, bf16[32,512]{1,0:T(8,128)(2,1)S(1)}, u32[]{:S(2)}, u32[]{:S(2)}) collective-permute-start(bf16[32,512]{1,0:T(8,128)(2,1)S(1)} %get-tuple-element.116), channel_id=1, source_target_pairs={{0,2},{1,3},{2,0},{3,1},{4,6},{5,7},{6,4},{7,5},{8,10},{9,11},{10,... | collective-permute-start | bytes 98312 | tf_op jit(solution)/shard_map/ppermute | solution.py:326
  71.3 5.7 %collective-permute-start.30 = (bf16[32,512]{1,0:T(8,128)(2,1)S(1)}, bf16[32,512]{1,0:T(8,128)(2,1)S(1)}, u32[]{:S(2)}, u32[]{:S(2)}) collective-permute-start(bf16[32,512]{1,0:T(8,128)(2,1)S(1)} %get-tuple-element.117), channel_id=1, source_target_pairs={{0,3},{1,2},{2,1},{3,0},{4,7},{5,6},{6,5},{7,4},{8,11},{9,10},{10,... | collective-permute-start | bytes 98312 | tf_op jit(solution)/shard_map/ppermute | solution.py:326
  (7 other events, 81.6 us)

commit v7 on v6

--- a/solution.py
+++ b/solution.py
@@ -49,6 +49,10 @@
 
 def dot_t(a, b):
     return lax.dot_general(a, b, (((1,), (1,)), ((), ())), preferred_element_type=f32)
+
+
+def turn(k, chips):
+    return (chips - k) % chips
 
 
 def rows_at(start, size, step):
@@ -89,7 +93,7 @@
     index = lax.broadcasted_iota(jnp.int32, (1, keys), 1)
     key_pos = jnp.zeros((1, keys), jnp.int32)
     for k in range(pieces):
-        owner = jnp.bitwise_xor(ctx, 2 * k + other)
+        owner = jnp.bitwise_xor(ctx, 2 * turn(k, pieces) + other)
         off = index - k * piece_rows
         pos = jnp.where(off < cache, owner * cache + off, cache_total + owner * span + off - cache)
         key_pos = pos if k == 0 else jnp.where(off >= 0, pos, key_pos)
@@ -301,7 +305,7 @@
     size = active.shape[0] // chips
     second = dot(active[...], weight[1 - core]).astype(bf16)
     for k in range(chips):
-        at = rows_at(jnp.bitwise_xor(chip, k) * size, size, size)
+        at = rows_at(jnp.bitwise_xor(chip, turn(k, chips)) * size, size, size)
         here = slice(k * size, (k + 1) * size)
         whole[core, at, :] = first[here, :]
         whole[1 - core, at, :] = second[here, :]
@@ -313,7 +317,7 @@
 
 def combine(high, low, *refs):
     out = refs[-1]
-    rows = jnp.concatenate([ref[...] for ref in refs[:-1]], axis=0)
+    rows = jnp.concatenate([ref[...] for ref in (refs[0], *refs[-2:0:-1])], axis=0)
     dims = (((0,), (0,)), ((), ()))
     out[...] = (
         lax.dot_general(high[...], rows, dims, preferred_element_type=f32)
@@ -365,7 +369,7 @@
     flight = n_exp * local
 
     def over_chips(x):
-        return [permute(x, "ctx", 2 * k) for k in range(1, chips)]
+        return [permute(x, "ctx", 2 * k) for k in reversed(range(1, chips))]
 
     def over_exp(xs):
         return [permute(x, "exp", k) for k, x in zip(range(1, n_exp), xs)]
@@ -457,7 +461,7 @@
     own, odd, even, picks = outs[0], outs[1], outs[2 : n_exp // 2 + 1], outs[n_exp // 2 + 1 :]
     left, right = picks[2::2], picks[3::2]
     passed = [permute(right[2 * k - 1], "exp", 1) for k in range(1, n_exp // 2)]
-    direct = [permute(x, "exp", k) for k, x in enumerate(left, 2)]
+    direct = [permute(x, "exp", k) for k, x in enumerate(left, 2)][::-1]
     arrived = [picks[0]] + direct + [permute(picks[1], "exp", 1)]
     for k, got in enumerate(passed, 1):
         pair = (right[2 * k - 2].astype(f32) + got.astype(f32)).astype(bf16)
@@ -524,7 +528,7 @@
         vmem=8,
         **cost,
     )(active_other, expert_out, made)
-    returned = over_exp(produced[1:])
+    returned = [permute(produced[k], "exp", k) for k in reversed(range(1, n_exp))]
     mixed = own + odd[:tokens].astype(f32)
     for part in even:
         mixed = mixed + part.astype(f32)

time: 78.1 us -> 76.1 us (0.974)
  waiting for transfers between devices: 26 us -> 23.6 us
    ppermute x31, waiting for transfers between devices: 26 us -> 23.6 us  [permute(): return lax.ppermute(x, axis, [(i, i ^ k) for i in range(n)])]
  transfers between devices with their start and end apart: 31 -> 31, of which waited for: 18 -> 20; matrix products, arithmetic and copies ran while one was open for 4% -> 4% of each run, Pallas kernels for 5% -> 5%
where the time goes in v7:
time: 76.1 us; the launch traced here: 75.9 us
  starting transfers between devices  37.2 us (49%)
  waiting for transfers between devices  23.6 us (31%)
  Pallas kernels  10.2 us (13%)
  other arithmetic  2.89 us (4%)
  local copies, waits for them, and re-layouts  1.03 us (1%)
  between operations  0.91 us (1%)
    ppermute x31, starting transfers between devices, permute(): return lax.ppermute(x, axis, [(i, i ^ k) for i in range(n)])  37.2 us
    ppermute x31, waiting for transfers between devices, permute(): return lax.ppermute(x, axis, [(i, i ^ k) for i in range(n)])  23.6 us
    pallas_call x1, Pallas kernels, body(): call(functools.partial(attend_second, span), [shape((span, rows // span *...  1.7 us
    pallas_call x1, Pallas kernels, body(): call(functools.partial(attend_first, span), [shape((rows, HEAD), f32), sh...  1.62 us
  transfers between devices with their start and end apart: 31, of which 20 were waited for; matrix products, arithmetic and copies ran while one was open for 4% of the time, Pallas kernels for 5%

profile of v7, /device:TPU:0, one launch (start us, length us, event | category | flops | bytes accessed | tf_op | source)
XLA Modules:
  0.0 75.9 jit_solution(14520586847215236077)
XLA Ops:
  0.6 1.5 %shard_map.140.kv = bf16[192,256]{1,0:T(8,128)(2,1)} custom-call(bf16[128,512]{1,0:T(8,128)(2,1)} %ck.1, bf16[128,512]{1,0:T(8,128)(2,1)} %cv.1, bf16[64,512]{1,0:T(8,128)(2,1)} %bk.1, bf16[64,512]{1,0:T(8,128)(2,1)} %bv.1), custom_call_target="tpu_custom_call" | custom-call | tf_op jit(solution)/shard_map/pallas_call | solution.py:377
  2.2 4.0 %collective-permute-start = (bf16[192,256]{1,0:T(8,128)(2,1)}, bf16[192,256]{1,0:T(8,128)(2,1)S(1)}, u32[]{:S(2)}, u32[]{:S(2)}) collective-permute-start(bf16[192,256]{1,0:T(8,128)(2,1)} %shard_map.140.kv), channel_id=1, source_target_pairs={{0,24},{4,28},{8,16},{12,20},{16,8},{20,12},{24,0},{28,4},{1,25},{... | collective-permute-start | bytes 294920 | tf_op jit(solution)/shard_map/ppermute | solution.py:330
  10.2 1.1 %collective-permute-done.1 = bf16[192,256]{1,0:T(8,128)(2,1)S(1)} collective-permute-done((bf16[192,256]{1,0:T(8,128)(2,1)}, bf16[192,256]{1,0:T(8,128)(2,1)S(1)}, u32[]{:S(2)}, u32[]{:S(2)}) %collective-permute-start.1) | collective-permute-done | bytes 98336 | tf_op jit(solution)/shard_map/ppermute | solution.py:330
  11.7 1.6 %shard_map.142 = (f32[1024,128]{1,0:T(8,128)S(1)}, f32[1024,128]{1,0:T(8,128)S(1)}, f32[1024,128]{1,0:T(8,128)S(1)}) custom-call(bf16[1024,128]{1,0:T(8,128)(2,1)S(1)} %bitcast.16, bf16[768,256]{1,0:T(8,128)(2,1)S(1)} %constant_dynamic-update-slice_fusion.kv, f32[64,768]{1,0:T(8,128)S(1)} %get-tuple-element.70.bias), custom_call_target="tpu_custom_call" | custom-call | flops 402653184 | bytes 4194304 | tf_op jit(solution)/shard_map/pallas_call | solution.py:414
  13.4 1.7 %shard_map.143 = (bf16[64,1024]{1,0:T(8,128)(2,1)S(1)}, bf16[64,1024]{1,0:T(8,128)(2,1)S(1)}) custom-call(bf16[1024,128]{1,0:T(8,128)(2,1)S(1)} %bitcast.17, bf16[768,256]{1,0:T(8,128)(2,1)S(1)} %collective-permute-done.3.kv, f32[64,768]{1,0:T(8,128)S(1)} %get-tuple-element.69.bias, f32[1024,128]{1,0:T(8,128)S(1)} %get-tuple-element.71.o_in, ...), custom_call_target="tpu_custom_call" | custom-call | flops 402653184 | bytes 4194304 | tf_op jit(solution)/shard_map/pallas_call | solution.py:421
  15.1 1.5 %collective-permute-start.4 = (bf16[64,1024]{1,0:T(8,128)(2,1)S(1)}, bf16[64,1024]{1,0:T(8,128)(2,1)S(1)}, u32[]{:S(2)}, u32[]{:S(2)}) collective-permute-start(bf16[64,1024]{1,0:T(8,128)(2,1)S(1)} %get-tuple-element.80), channel_id=1, source_target_pairs={{0,8},{4,12},{8,0},{12,4},{16,24},{20,28},{24,16},{28,20},{1,9},{5... | collective-permute-start | bytes 393224 | tf_op jit(solution)/shard_map/ppermute | solution.py:330
  17.2 1.7 %collective-permute-start.10 = (f32[8,128]{1,0:T(8,128)S(1)}, f32[8,128]{1,0:T(8,128)S(1)}, u32[]{:S(2)}, u32[]{:S(2)}) collective-permute-start(f32[8,128]{1,0:T(8,128)S(1)} %get-tuple-element.79), channel_id=1, source_target_pairs={{0,1},{1,0},{2,3},{3,2},{4,5},{5,4},{6,7},{7,6},{8,9},{9,8},{10,11... | collective-permute-start | bytes 12296 | tf_op jit(solution)/shard_map/ppermute | solution.py:330
  18.9 1.3 %collective-permute-start.5 = (bf16[64,1024]{1,0:T(8,128)(2,1)S(1)}, bf16[64,1024]{1,0:T(8,128)(2,1)S(1)}, u32[]{:S(2)}, u32[]{:S(2)}) collective-permute-start(bf16[64,1024]{1,0:T(8,128)(2,1)S(1)} %get-tuple-element.81), channel_id=1, source_target_pairs={{0,8},{4,12},{8,0},{12,4},{16,24},{20,28},{24,16},{28,20},{1,9},{5... | collective-permute-start | bytes 393224 | tf_op jit(solution)/shard_map/ppermute | solution.py:330
  21.0 1.4 %collective-permute-start.8 = (bf16[64,1024]{1,0:T(8,128)(2,1)S(1)}, bf16[64,1024]{1,0:T(8,128)(2,1)S(1)}, u32[]{:S(2)}, u32[]{:S(2)}) collective-permute-start(bf16[64,1024]{1,0:T(8,128)(2,1)S(1)} %collective-permute-done.4), channel_id=1, source_target_pairs={{0,16},{4,20},{8,24},{12,28},{16,0},{20,4},{24,8},{28,12},{1,17},{... | collective-permute-start | bytes 393224 | tf_op jit(solution)/shard_map/ppermute | solution.py:330
  23.1 2.8 %collective-permute-start.11 = (f32[16,128]{1,0:T(8,128)S(1)}, f32[16,128]{1,0:T(8,128)S(1)}, u32[]{:S(2)}, u32[]{:S(2)}) collective-permute-start(f32[16,128]{1,0:T(8,128)S(1)} %pad_maximum_fusion.2), channel_id=1, source_target_pairs={{0,2},{1,3},{2,0},{3,1},{4,6},{5,7},{6,4},{7,5},{8,10},{9,11},{10,... | collective-permute-start | bytes 24584 | tf_op jit(solution)/shard_map/ppermute | solution.py:330
  25.9 1.7 %collective-permute-done.11 = f32[16,128]{1,0:T(8,128)S(1)} collective-permute-done((f32[16,128]{1,0:T(8,128)S(1)}, f32[16,128]{1,0:T(8,128)S(1)}, u32[]{:S(2)}, u32[]{:S(2)}) %collective-permute-start.11) | collective-permute-done | bytes 8224 | tf_op jit(solution)/shard_map/ppermute | solution.py:330
  28.7 1.9 %collective-permute-done.12.heads_out = bf16[256,2048]{1,0:T(8,128)(2,1)S(1)} collective-permute-done((bf16[256,2048]{1,0:T(8,128)(2,1)S(1)}, bf16[256,2048]{1,0:T(8,128)(2,1)S(1)}, u32[]{:S(2)}, u32[]{:S(2)}) %collective-permute-start.12) | collective-permute-done | bytes 1048608 | tf_op jit(solution)/shard_map/ppermute | solution.py:330
  30.6 1.0 %shard_map.145 = (f32[128,512]{1,0:T(8,128)S(1)}, bf16[256,512]{1,0:T(8,128)(2,1)S(1)}, bf16[128,512]{1,0:T(8,128)(2,1)S(1)}, bf16[128,512]{1,0:T(8,128)(2,1)S(1...) custom-call(bf16[256,2048]{1,0:T(8,128)(2,1)S(1)} %collective-permut, ...), custom_call_target="tpu_custom_call" | custom-call | flops 536870912 | bytes 4194304 | tf_op jit(solution)/shard_map/pallas_call | solution.py:449
  31.7 2.1 %collective-permute-start.16 = (bf16[128,256]{1,0:T(8,128)(2,1)S(1)}, bf16[128,256]{1,0:T(8,128)(2,1)S(1)}, u32[]{:S(2)}, u32[]{:S(2)}) collective-permute-start(bf16[128,256]{1,0:T(8,128)(2,1)S(1)} %get-tuple-element.95), channel_id=1, source_target_pairs={{0,1},{1,0},{2,3},{3,2},{4,5},{5,4},{6,7},{7,6},{8,9},{9,8},{10,11... | collective-permute-start | bytes 196616 | tf_op jit(solution)/shard_map/ppermute | solution.py:330
  33.9 4.0 %collective-permute-start.13 = (bf16[128,256]{1,0:T(8,128)(2,1)S(1)}, bf16[128,256]{1,0:T(8,128)(2,1)S(1)}, u32[]{:S(2)}, u32[]{:S(2)}) collective-permute-start(bf16[128,256]{1,0:T(8,128)(2,1)S(1)} %get-tuple-element.91), channel_id=1, source_target_pairs={{0,3},{1,2},{2,1},{3,0},{4,7},{5,6},{6,5},{7,4},{8,11},{9,10},{10,... | collective-permute-start | bytes 196616 | tf_op jit(solution)/shard_map/ppermute | solution.py:330
  37.9 3.0 %collective-permute-start.17 = (bf16[128,256]{1,0:T(8,128)(2,1)S(1)}, bf16[128,256]{1,0:T(8,128)(2,1)S(1)}, u32[]{:S(2)}, u32[]{:S(2)}) collective-permute-start(bf16[128,256]{1,0:T(8,128)(2,1)S(1)} %add_convert_fusion.2), channel_id=1, source_target_pairs={{0,2},{1,3},{2,0},{3,1},{4,6},{5,7},{6,4},{7,5},{8,10},{9,11},{10,... | collective-permute-start | bytes 196616 | tf_op jit(solution)/shard_map/ppermute | solution.py:330
  40.8 2.8 %collective-permute-done.13.refs_1_ = bf16[128,256]{1,0:T(8,128)(2,1)S(1)} collective-permute-done((bf16[128,256]{1,0:T(8,128)(2,1)S(1)}, bf16[128,256]{1,0:T(8,128)(2,1)S(1)}, u32[]{:S(2)}, u32[]{:S(2)}) %collective-permute-start.13) | collective-permute-done | bytes 65568 | tf_op jit(solution)/shard_map/ppermute | solution.py:330
  43.7 2.9 %collective-permute-done.14.refs_2_ = bf16[128,256]{1,0:T(8,128)(2,1)S(1)} collective-permute-done((bf16[128,256]{1,0:T(8,128)(2,1)S(1)}, bf16[128,256]{1,0:T(8,128)(2,1)S(1)}, u32[]{:S(2)}, u32[]{:S(2)}) %collective-permute-start.14) | collective-permute-done | bytes 65568 | tf_op jit(solution)/shard_map/ppermute | solution.py:330
  48.9 1.0 %collective-permute-done.18.theirs = bf16[64,3200]{1,0:T(8,128)(2,1)S(1)} collective-permute-done((bf16[64,3200]{1,0:T(8,128)(2,1)S(1)}, bf16[64,3200]{1,0:T(8,128)(2,1)S(1)}, u32[]{:S(2)}, u32[]{:S(2)}) %collective-permute-start.18) | collective-permute-done | bytes 409632 | tf_op jit(solution)/shard_map/ppermute | solution.py:330
  49.9 1.4 %collective-permute-start.19 = (bf16[16,3200]{1,0:T(8,128)(2,1)S(1)}, bf16[16,3200]{1,0:T(8,128)(2,1)S(1)}, u32[]{:S(2)}, u32[]{:S(2)}) collective-permute-start(bf16[16,3200]{1,0:T(8,128)(2,1)S(1)} %get-tuple-element.98), channel_id=1, source_target_pairs={{0,8},{4,12},{8,0},{12,4},{16,24},{20,28},{24,16},{28,20},{1,9},{5... | collective-permute-start | bytes 307208 | tf_op jit(solution)/shard_map/ppermute | solution.py:330
  52.1 1.4 %collective-permute-start.21 = (bf16[16,3200]{1,0:T(8,128)(2,1)S(1)}, bf16[16,3200]{1,0:T(8,128)(2,1)S(1)}, u32[]{:S(2)}, u32[]{:S(2)}) collective-permute-start(bf16[16,3200]{1,0:T(8,128)(2,1)S(1)} %get-tuple-element.100), channel_id=1, source_target_pairs={{0,24},{4,28},{8,16},{12,20},{16,8},{20,12},{24,0},{28,4},{1,25},{... | collective-permute-start | bytes 307208 | tf_op jit(solution)/shard_map/ppermute | solution.py:330
  53.5 3.3 %collective-permute-done.22 = bf16[256,512]{1,0:T(8,128)(2,1)S(1)} collective-permute-done((bf16[256,512]{1,0:T(8,128)(2,1)S(1)}, bf16[256,512]{1,0:T(8,128)(2,1)S(1)}, u32[]{:S(2)}, u32[]{:S(2)}) %collective-permute-start.22) | collective-permute-done | bytes 262176 | tf_op jit(solution)/shard_map/ppermute | solution.py:330
  56.8 1.4 %collective-permute-done.20.refs_2_ = bf16[16,3200]{1,0:T(8,128)(2,1)S(1)} collective-permute-done((bf16[16,3200]{1,0:T(8,128)(2,1)S(1)}, bf16[16,3200]{1,0:T(8,128)(2,1)S(1)}, u32[]{:S(2)}, u32[]{:S(2)}) %collective-permute-start.20) | collective-permute-done | bytes 102432 | tf_op jit(solution)/shard_map/ppermute | solution.py:330
  58.2 1.0 %collective-permute-start.26 = (bf16[128,512]{1,0:T(8,128)(2,1)S(1)}, bf16[128,512]{1,0:T(8,128)(2,1)S(1)}, u32[]{:S(2)}, u32[]{:S(2)}) collective-permute-start(bf16[128,512]{1,0:T(8,128)(2,1)S(1)} %add_convert_fusion.1), channel_id=1, source_target_pairs={{0,2},{1,3},{2,0},{3,1},{4,6},{5,7},{6,4},{7,5},{8,10},{9,11},{10,... | collective-permute-start | bytes 393224 | tf_op jit(solution)/shard_map/ppermute | solution.py:330
  59.4 1.5 %collective-permute-start.23 = (bf16[16,1536]{1,0:T(8,128)(2,1)S(1)}, bf16[16,1536]{1,0:T(8,128)(2,1)S(1)}, u32[]{:S(2)}, u32[]{:S(2)}) collective-permute-start(bf16[16,1536]{1,0:T(8,128)(2,1)S(1)} %shard_map.149), channel_id=1, source_target_pairs={{0,24},{4,28},{8,16},{12,20},{16,8},{20,12},{24,0},{28,4},{1,25},{... | collective-permute-start | bytes 147464 | tf_op jit(solution)/shard_map/ppermute | solution.py:330
  61.6 1.4 %collective-permute-start.25 = (bf16[16,1536]{1,0:T(8,128)(2,1)S(1)}, bf16[16,1536]{1,0:T(8,128)(2,1)S(1)}, u32[]{:S(2)}, u32[]{:S(2)}) collective-permute-start(bf16[16,1536]{1,0:T(8,128)(2,1)S(1)} %shard_map.149), channel_id=1, source_target_pairs={{0,8},{4,12},{8,0},{12,4},{16,24},{20,28},{24,16},{28,20},{1,9},{5... | collective-permute-start | bytes 147464 | tf_op jit(solution)/shard_map/ppermute | solution.py:330
  62.9 1.5 %collective-permute-done.23 = bf16[16,1536]{1,0:T(8,128)(2,1)S(1)} collective-permute-done((bf16[16,1536]{1,0:T(8,128)(2,1)S(1)}, bf16[16,1536]{1,0:T(8,128)(2,1)S(1)}, u32[]{:S(2)}, u32[]{:S(2)}) %collective-permute-start.23) | collective-permute-done | bytes 49184 | tf_op jit(solution)/shard_map/ppermute | solution.py:330
  66.8 1.0 %collective-permute-done.27.active = bf16[64,1536]{1,0:T(8,128)(2,1)S(1)} collective-permute-done((bf16[64,1536]{1,0:T(8,128)(2,1)S(1)}, bf16[64,1536]{1,0:T(8,128)(2,1)S(1)}, u32[]{:S(2)}, u32[]{:S(2)}) %collective-permute-start.27) | collective-permute-done | bytes 196640 | tf_op jit(solution)/shard_map/ppermute | solution.py:330
  68.2 2.0 %collective-permute-start.28 = (bf16[32,512]{1,0:T(8,128)(2,1)S(1)}, bf16[32,512]{1,0:T(8,128)(2,1)S(1)}, u32[]{:S(2)}, u32[]{:S(2)}) collective-permute-start(bf16[32,512]{1,0:T(8,128)(2,1)S(1)} %get-tuple-element.115), channel_id=1, source_target_pairs={{0,3},{1,2},{2,1},{3,0},{4,7},{5,6},{6,5},{7,4},{8,11},{9,10},{10,... | collective-permute-start | bytes 98312 | tf_op jit(solution)/shard_map/ppermute | solution.py:330
  70.2 2.5 %collective-permute-start.30 = (bf16[32,512]{1,0:T(8,128)(2,1)S(1)}, bf16[32,512]{1,0:T(8,128)(2,1)S(1)}, u32[]{:S(2)}, u32[]{:S(2)}) collective-permute-start(bf16[32,512]{1,0:T(8,128)(2,1)S(1)} %get-tuple-element.117), channel_id=1, source_target_pairs={{0,1},{1,0},{2,3},{3,2},{4,5},{5,4},{6,7},{7,6},{8,9},{9,8},{10,11... | collective-permute-start | bytes 98312 | tf_op jit(solution)/shard_map/ppermute | solution.py:330
  74.1 0.9 %collective-permute-done.29.refs_2_ = bf16[32,512]{1,0:T(8,128)(2,1)S(1)} collective-permute-done((bf16[32,512]{1,0:T(8,128)(2,1)S(1)}, bf16[32,512]{1,0:T(8,128)(2,1)S(1)}, u32[]{:S(2)}, u32[]{:S(2)}) %collective-permute-start.29) | collective-permute-done | bytes 32800 | tf_op jit(solution)/shard_map/ppermute | solution.py:330
  75.0 0.9 %shard_map.152 = bf16[128,512]{1,0:T(8,128)(2,1)} custom-call(bf16[128,128]{1,0:T(8,128)(2,1)S(1)} %get-tuple-element.109.high, bf16[128,128]{1,0:T(8,128)(2,1)S(1)} %get-tuple-element.110.low, bf16[32,512]{1,0:T(8,128)(2,1)S(1)} %get-tuple-element.114.refs_0_, bf16[32,512]{1,0:T(8,128)(2,1)S(1)} %collective-permute-done.28.refs_1_, ...), custom_call_target="tpu_custom_call" | custom-call | tf_op jit(solution)/shard_map/pallas_call | solution.py:536
  (75 shorter events, 15.8 us)
Async XLA Ops:
  2.2 8.0 %collective-permute-start = (bf16[192,256]{1,0:T(8,128)(2,1)}, bf16[192,256]{1,0:T(8,128)(2,1)S(1)}, u32[]{:S(2)}, u32[]{:S(2)}) collective-permute-start(bf16[192,256]{1,0:T(8,128)(2,1)} %shard_map.140.kv), channel_id=1, source_target_pairs={{0,24},{4,28},{8,16},{12,20},{16,8},{20,12},{24,0},{28,4},{1,25},{... | collective-permute-start | bytes 294920 | tf_op jit(solution)/shard_map/ppermute | solution.py:330
  6.1 5.1 %collective-permute-start.1 = (bf16[192,256]{1,0:T(8,128)(2,1)}, bf16[192,256]{1,0:T(8,128)(2,1)S(1)}, u32[]{:S(2)}, u32[]{:S(2)}) collective-permute-start(bf16[192,256]{1,0:T(8,128)(2,1)} %shard_map.140.kv), channel_id=1, source_target_pairs={{0,16},{4,20},{8,24},{12,28},{16,0},{20,4},{24,8},{28,12},{1,17},{... | collective-permute-start | bytes 294920 | tf_op jit(solution)/shard_map/ppermute | solution.py:330
  6.6 4.9 %collective-permute-start.2 = (bf16[192,256]{1,0:T(8,128)(2,1)}, bf16[192,256]{1,0:T(8,128)(2,1)S(1)}, u32[]{:S(2)}, u32[]{:S(2)}) collective-permute-start(bf16[192,256]{1,0:T(8,128)(2,1)} %shard_map.140.kv), channel_id=1, source_target_pairs={{0,8},{4,12},{8,0},{12,4},{16,24},{20,28},{24,16},{28,20},{1,9},{5... | collective-permute-start | bytes 294920 | tf_op jit(solution)/shard_map/ppermute | solution.py:330
  11.6 1.8 %collective-permute-start.3 = (bf16[768,256]{1,0:T(8,128)(2,1)S(1)}, bf16[768,256]{1,0:T(8,128)(2,1)S(1)}, u32[]{:S(2)}, u32[]{:S(2)}) collective-permute-start(bf16[768,256]{1,0:T(8,128)(2,1)S(1)} %constant_dynamic-update-slice_fusion.kv), channel_id=1, source_target_pairs={{0,4},{4,0},{8,12},{12,8},{16,20},{20,16},{24,28},{28,24},{1,5},{5... | collective-permute-start | bytes 1179656 | tf_op jit(solution)/shard_map/ppermute | solution.py:330
  13.4 33.9 %slice-start = ((s8[6291456]{0:T(1024)(128)(4,1)}), s8[4194304]{0:T(1024)(128)(4,1)S(1)}, s32[]{:S(2)}) async-start(s8[6291456]{0:T(1024)(128)(4,1)} %bitcast.14), calls=%async_computation | async-start | bytes 8388608
  15.1 5.9 %collective-permute-start.4 = (bf16[64,1024]{1,0:T(8,128)(2,1)S(1)}, bf16[64,1024]{1,0:T(8,128)(2,1)S(1)}, u32[]{:S(2)}, u32[]{:S(2)}) collective-permute-start(bf16[64,1024]{1,0:T(8,128)(2,1)S(1)} %get-tuple-element.80), channel_id=1, source_target_pairs={{0,8},{4,12},{8,0},{12,4},{16,24},{20,28},{24,16},{28,20},{1,9},{5... | collective-permute-start | bytes 393224 | tf_op jit(solution)/shard_map/ppermute | solution.py:330
  16.6 5.8 %collective-permute-start.7 = (bf16[64,1024]{1,0:T(8,128)(2,1)S(1)}, bf16[64,1024]{1,0:T(8,128)(2,1)S(1)}, u32[]{:S(2)}, u32[]{:S(2)}) collective-permute-start(bf16[64,1024]{1,0:T(8,128)(2,1)S(1)} %get-tuple-element.81), channel_id=1, source_target_pairs={{0,16},{4,20},{8,24},{12,28},{16,0},{20,4},{24,8},{28,12},{1,17},{... | collective-permute-start | bytes 393224 | tf_op jit(solution)/shard_map/ppermute | solution.py:330
  17.2 5.9 %collective-permute-start.10 = (f32[8,128]{1,0:T(8,128)S(1)}, f32[8,128]{1,0:T(8,128)S(1)}, u32[]{:S(2)}, u32[]{:S(2)}) collective-permute-start(f32[8,128]{1,0:T(8,128)S(1)} %get-tuple-element.79), channel_id=1, source_target_pairs={{0,1},{1,0},{2,3},{3,2},{4,5},{5,4},{6,7},{7,6},{8,9},{9,8},{10,11... | collective-permute-start | bytes 12296 | tf_op jit(solution)/shard_map/ppermute | solution.py:330
  18.9 8.7 %collective-permute-start.5 = (bf16[64,1024]{1,0:T(8,128)(2,1)S(1)}, bf16[64,1024]{1,0:T(8,128)(2,1)S(1)}, u32[]{:S(2)}, u32[]{:S(2)}) collective-permute-start(bf16[64,1024]{1,0:T(8,128)(2,1)S(1)} %get-tuple-element.81), channel_id=1, source_target_pairs={{0,8},{4,12},{8,0},{12,4},{16,24},{20,28},{24,16},{28,20},{1,9},{5... | collective-permute-start | bytes 393224 | tf_op jit(solution)/shard_map/ppermute | solution.py:330
  20.2 7.5 %collective-permute-start.6 = (bf16[64,1024]{1,0:T(8,128)(2,1)S(1)}, bf16[64,1024]{1,0:T(8,128)(2,1)S(1)}, u32[]{:S(2)}, u32[]{:S(2)}) collective-permute-start(bf16[64,1024]{1,0:T(8,128)(2,1)S(1)} %get-tuple-element.80), channel_id=1, source_target_pairs={{0,16},{4,20},{8,24},{12,28},{16,0},{20,4},{24,8},{28,12},{1,17},{... | collective-permute-start | bytes 393224 | tf_op jit(solution)/shard_map/ppermute | solution.py:330
  21.0 6.8 %collective-permute-start.8 = (bf16[64,1024]{1,0:T(8,128)(2,1)S(1)}, bf16[64,1024]{1,0:T(8,128)(2,1)S(1)}, u32[]{:S(2)}, u32[]{:S(2)}) collective-permute-start(bf16[64,1024]{1,0:T(8,128)(2,1)S(1)} %collective-permute-done.4), channel_id=1, source_target_pairs={{0,16},{4,20},{8,24},{12,28},{16,0},{20,4},{24,8},{28,12},{1,17},{... | collective-permute-start | bytes 393224 | tf_op jit(solution)/shard_map/ppermute | solution.py:330
  22.4 5.4 %collective-permute-start.9 = (bf16[64,1024]{1,0:T(8,128)(2,1)S(1)}, bf16[64,1024]{1,0:T(8,128)(2,1)S(1)}, u32[]{:S(2)}, u32[]{:S(2)}) collective-permute-start(bf16[64,1024]{1,0:T(8,128)(2,1)S(1)} %collective-permute-done.7), channel_id=1, source_target_pairs={{0,8},{4,12},{8,0},{12,4},{16,24},{20,28},{24,16},{28,20},{1,9},{5... | collective-permute-start | bytes 393224 | tf_op jit(solution)/shard_map/ppermute | solution.py:330
  23.1 4.6 %collective-permute-start.11 = (f32[16,128]{1,0:T(8,128)S(1)}, f32[16,128]{1,0:T(8,128)S(1)}, u32[]{:S(2)}, u32[]{:S(2)}) collective-permute-start(f32[16,128]{1,0:T(8,128)S(1)} %pad_maximum_fusion.2), channel_id=1, source_target_pairs={{0,2},{1,3},{2,0},{3,1},{4,6},{5,7},{6,4},{7,5},{8,10},{9,11},{10,... | collective-permute-start | bytes 24584 | tf_op jit(solution)/shard_map/ppermute | solution.py:330
  27.9 2.7 %collective-permute-start.12 = (bf16[256,2048]{1,0:T(8,128)(2,1)S(1)}, bf16[256,2048]{1,0:T(8,128)(2,1)S(1)}, u32[]{:S(2)}, u32[]{:S(2)}) collective-permute-start(bf16[256,2048]{1,0:T(8,128)(2,1)S(1)} %maximum_maximum_fusion.heads_out), channel_id=1, source_target_pairs={{0,4},{4,0},{8,12},{12,8},{16,20},{20,16},{24,28},{28,24},{1,5},{5... | collective-permute-start | bytes 3145736 | tf_op jit(solution)/shard_map/ppermute | solution.py:330
  31.7 6.1 %collective-permute-start.16 = (bf16[128,256]{1,0:T(8,128)(2,1)S(1)}, bf16[128,256]{1,0:T(8,128)(2,1)S(1)}, u32[]{:S(2)}, u32[]{:S(2)}) collective-permute-start(bf16[128,256]{1,0:T(8,128)(2,1)S(1)} %get-tuple-element.95), channel_id=1, source_target_pairs={{0,1},{1,0},{2,3},{3,2},{4,5},{5,4},{6,7},{7,6},{8,9},{9,8},{10,11... | collective-permute-start | bytes 196616 | tf_op jit(solution)/shard_map/ppermute | solution.py:330
  33.8 13.5 %collective-permute-start.15 = (bf16[128,512]{1,0:T(8,128)(2,1)S(1)}, bf16[128,512]{1,0:T(8,128)(2,1)S(1)}, u32[]{:S(2)}, u32[]{:S(2)}) collective-permute-start(bf16[128,512]{1,0:T(8,128)(2,1)S(1)} %get-tuple-element.93), channel_id=1, source_target_pairs={{0,1},{1,0},{2,3},{3,2},{4,5},{5,4},{6,7},{7,6},{8,9},{9,8},{10,11... | collective-permute-start | bytes 393224 | tf_op jit(solution)/shard_map/ppermute | solution.py:330
  33.9 9.8 %collective-permute-start.13 = (bf16[128,256]{1,0:T(8,128)(2,1)S(1)}, bf16[128,256]{1,0:T(8,128)(2,1)S(1)}, u32[]{:S(2)}, u32[]{:S(2)}) collective-permute-start(bf16[128,256]{1,0:T(8,128)(2,1)S(1)} %get-tuple-element.91), channel_id=1, source_target_pairs={{0,3},{1,2},{2,1},{3,0},{4,7},{5,6},{6,5},{7,4},{8,11},{9,10},{10,... | collective-permute-start | bytes 196616 | tf_op jit(solution)/shard_map/ppermute | solution.py:330
  37.8 8.8 %collective-permute-start.14 = (bf16[128,256]{1,0:T(8,128)(2,1)S(1)}, bf16[128,256]{1,0:T(8,128)(2,1)S(1)}, u32[]{:S(2)}, u32[]{:S(2)}) collective-permute-start(bf16[128,256]{1,0:T(8,128)(2,1)S(1)} %get-tuple-element.92), channel_id=1, source_target_pairs={{0,2},{1,3},{2,0},{3,1},{4,6},{5,7},{6,4},{7,5},{8,10},{9,11},{10,... | collective-permute-start | bytes 196616 | tf_op jit(solution)/shard_map/ppermute | solution.py:330
  37.9 9.4 %collective-permute-start.17 = (bf16[128,256]{1,0:T(8,128)(2,1)S(1)}, bf16[128,256]{1,0:T(8,128)(2,1)S(1)}, u32[]{:S(2)}, u32[]{:S(2)}) collective-permute-start(bf16[128,256]{1,0:T(8,128)(2,1)S(1)} %add_convert_fusion.2), channel_id=1, source_target_pairs={{0,2},{1,3},{2,0},{3,1},{4,6},{5,7},{6,4},{7,5},{8,10},{9,11},{10,... | collective-permute-start | bytes 196616 | tf_op jit(solution)/shard_map/ppermute | solution.py:330
  48.0 1.8 %collective-permute-start.18 = (bf16[64,3200]{1,0:T(8,128)(2,1)S(1)}, bf16[64,3200]{1,0:T(8,128)(2,1)S(1)}, u32[]{:S(2)}, u32[]{:S(2)}) collective-permute-start(bf16[64,3200]{1,0:T(8,128)(2,1)S(1)} %shard_map.147), channel_id=1, source_target_pairs={{0,4},{4,0},{8,12},{12,8},{16,20},{20,16},{24,28},{28,24},{1,5},{5... | collective-permute-start | bytes 1228808 | tf_op jit(solution)/shard_map/ppermute | solution.py:330
  48.1 8.7 %collective-permute-start.22 = (bf16[256,512]{1,0:T(8,128)(2,1)S(1)}, bf16[256,512]{1,0:T(8,128)(2,1)S(1)}, u32[]{:S(2)}, u32[]{:S(2)}) collective-permute-start(bf16[256,512]{1,0:T(8,128)(2,1)S(1)} %get-tuple-element.101), channel_id=1, source_target_pairs={{0,1},{1,0},{2,3},{3,2},{4,5},{5,4},{6,7},{7,6},{8,9},{9,8},{10,11... | collective-permute-start | bytes 786440 | tf_op jit(solution)/shard_map/ppermute | solution.py:330
  49.9 6.9 %collective-permute-start.19 = (bf16[16,3200]{1,0:T(8,128)(2,1)S(1)}, bf16[16,3200]{1,0:T(8,128)(2,1)S(1)}, u32[]{:S(2)}, u32[]{:S(2)}) collective-permute-start(bf16[16,3200]{1,0:T(8,128)(2,1)S(1)} %get-tuple-element.98), channel_id=1, source_target_pairs={{0,8},{4,12},{8,0},{12,4},{16,24},{20,28},{24,16},{28,20},{1,9},{5... | collective-permute-start | bytes 307208 | tf_op jit(solution)/shard_map/ppermute | solution.py:330
  51.3 6.9 %collective-permute-start.20 = (bf16[16,3200]{1,0:T(8,128)(2,1)S(1)}, bf16[16,3200]{1,0:T(8,128)(2,1)S(1)}, u32[]{:S(2)}, u32[]{:S(2)}) collective-permute-start(bf16[16,3200]{1,0:T(8,128)(2,1)S(1)} %get-tuple-element.99), channel_id=1, source_target_pairs={{0,16},{4,20},{8,24},{12,28},{16,0},{20,4},{24,8},{28,12},{1,17},{... | collective-permute-start | bytes 307208 | tf_op jit(solution)/shard_map/ppermute | solution.py:330
  52.1 6.1 %collective-permute-start.21 = (bf16[16,3200]{1,0:T(8,128)(2,1)S(1)}, bf16[16,3200]{1,0:T(8,128)(2,1)S(1)}, u32[]{:S(2)}, u32[]{:S(2)}) collective-permute-start(bf16[16,3200]{1,0:T(8,128)(2,1)S(1)} %get-tuple-element.100), channel_id=1, source_target_pairs={{0,24},{4,28},{8,16},{12,20},{16,8},{20,12},{24,0},{28,4},{1,25},{... | collective-permute-start | bytes 307208 | tf_op jit(solution)/shard_map/ppermute | solution.py:330
  58.2 8.0 %collective-permute-start.26 = (bf16[128,512]{1,0:T(8,128)(2,1)S(1)}, bf16[128,512]{1,0:T(8,128)(2,1)S(1)}, u32[]{:S(2)}, u32[]{:S(2)}) collective-permute-start(bf16[128,512]{1,0:T(8,128)(2,1)S(1)} %add_convert_fusion.1), channel_id=1, source_target_pairs={{0,2},{1,3},{2,0},{3,1},{4,6},{5,7},{6,4},{7,5},{8,10},{9,11},{10,... | collective-permute-start | bytes 393224 | tf_op jit(solution)/shard_map/ppermute | solution.py:330
  59.4 5.1 %collective-permute-start.23 = (bf16[16,1536]{1,0:T(8,128)(2,1)S(1)}, bf16[16,1536]{1,0:T(8,128)(2,1)S(1)}, u32[]{:S(2)}, u32[]{:S(2)}) collective-permute-start(bf16[16,1536]{1,0:T(8,128)(2,1)S(1)} %shard_map.149), channel_id=1, source_target_pairs={{0,24},{4,28},{8,16},{12,20},{16,8},{20,12},{24,0},{28,4},{1,25},{... | collective-permute-start | bytes 147464 | tf_op jit(solution)/shard_map/ppermute | solution.py:330
  60.8 4.1 %collective-permute-start.24 = (bf16[16,1536]{1,0:T(8,128)(2,1)S(1)}, bf16[16,1536]{1,0:T(8,128)(2,1)S(1)}, u32[]{:S(2)}, u32[]{:S(2)}) collective-permute-start(bf16[16,1536]{1,0:T(8,128)(2,1)S(1)} %shard_map.149), channel_id=1, source_target_pairs={{0,16},{4,20},{8,24},{12,28},{16,0},{20,4},{24,8},{28,12},{1,17},{... | collective-permute-start | bytes 147464 | tf_op jit(solution)/shard_map/ppermute | solution.py:330
  61.6 4.1 %collective-permute-start.25 = (bf16[16,1536]{1,0:T(8,128)(2,1)S(1)}, bf16[16,1536]{1,0:T(8,128)(2,1)S(1)}, u32[]{:S(2)}, u32[]{:S(2)}) collective-permute-start(bf16[16,1536]{1,0:T(8,128)(2,1)S(1)} %shard_map.149), channel_id=1, source_target_pairs={{0,8},{4,12},{8,0},{12,4},{16,24},{20,28},{24,16},{28,20},{1,9},{5... | collective-permute-start | bytes 147464 | tf_op jit(solution)/shard_map/ppermute | solution.py:330
  66.3 1.5 %collective-permute-start.27 = (bf16[64,1536]{1,0:T(8,128)(2,1)S(1)}, bf16[64,1536]{1,0:T(8,128)(2,1)S(1)}, u32[]{:S(2)}, u32[]{:S(2)}) collective-permute-start(bf16[64,1536]{1,0:T(8,128)(2,1)S(1)} %pad_maximum_fusion.active), channel_id=1, source_target_pairs={{0,4},{4,0},{8,12},{12,8},{16,20},{20,16},{24,28},{28,24},{1,5},{5... | collective-permute-start | bytes 589832 | tf_op jit(solution)/shard_map/ppermute | solution.py:330
  68.2 5.9 %collective-permute-start.28 = (bf16[32,512]{1,0:T(8,128)(2,1)S(1)}, bf16[32,512]{1,0:T(8,128)(2,1)S(1)}, u32[]{:S(2)}, u32[]{:S(2)}) collective-permute-start(bf16[32,512]{1,0:T(8,128)(2,1)S(1)} %get-tuple-element.115), channel_id=1, source_target_pairs={{0,3},{1,2},{2,1},{3,0},{4,7},{5,6},{6,5},{7,4},{8,11},{9,10},{10,... | collective-permute-start | bytes 98312 | tf_op jit(solution)/shard_map/ppermute | solution.py:330
  70.2 4.8 %collective-permute-start.29 = (bf16[32,512]{1,0:T(8,128)(2,1)S(1)}, bf16[32,512]{1,0:T(8,128)(2,1)S(1)}, u32[]{:S(2)}, u32[]{:S(2)}) collective-permute-start(bf16[32,512]{1,0:T(8,128)(2,1)S(1)} %get-tuple-element.116), channel_id=1, source_target_pairs={{0,2},{1,3},{2,0},{3,1},{4,6},{5,7},{6,4},{7,5},{8,10},{9,11},{10,... | collective-permute-start | bytes 98312 | tf_op jit(solution)/shard_map/ppermute | solution.py:330
  70.2 4.8 %collective-permute-start.30 = (bf16[32,512]{1,0:T(8,128)(2,1)S(1)}, bf16[32,512]{1,0:T(8,128)(2,1)S(1)}, u32[]{:S(2)}, u32[]{:S(2)}) collective-permute-start(bf16[32,512]{1,0:T(8,128)(2,1)S(1)} %get-tuple-element.117), channel_id=1, source_target_pairs={{0,1},{1,0},{2,3},{3,2},{4,5},{5,4},{6,7},{7,6},{8,9},{9,8},{10,11... | collective-permute-start | bytes 98312 | tf_op jit(solution)/shard_map/ppermute | solution.py:330
  (7 other events, 82.0 us)

commit v8 on v7

--- a/solution.py
+++ b/solution.py
@@ -210,6 +210,9 @@
     flight = ranks.shape[0] // n_exp
     local = flight // n_exp
     slot = lax.broadcasted_iota(jnp.int32, (CAP, tokens), 0).astype(f32)
+    held, step = [0], n_exp // 2
+    while step:
+        held, step = held + [k ^ step for k in held], step // 2
     for k in range(n_exp):
         block = jnp.bitwise_xor(exp, k)
         here = rows_at(jnp.bitwise_xor(chip, block) * span, span, span)
@@ -228,18 +231,18 @@
         table = []
         for d in range(n_exp):
             for j in range(local):
-                row = k * flight + jnp.bitwise_xor(exp, d) * local + j
+                row = held.index(k) * flight + jnp.bitwise_xor(exp, d) * local + j
                 table.append(jnp.where(ranks[pl.ds(row, 1), :] == slot, 1.0, 0.0))
         rows = dot(jnp.concatenate(table, axis=0).astype(bf16), narrow).astype(bf16)
         for d in range(n_exp):
             for j in range(local):
                 at = rows_at(j * n_exp * CAP + block * CAP, CAP, CAP)
                 value = rows[(d * local + j) * CAP : (d * local + j + 1) * CAP, :]
-                if d < 2:
+                if d == 0:
                     pick_outs[d][at, :] = value
                 else:
-                    pick_outs[2 * d - 2][at, :] = value[:, :half]
-                    pick_outs[2 * d - 1][at, :] = value[:, half:]
+                    pick_outs[2 * d - 1][at, :] = value[:, :half]
+                    pick_outs[2 * d][at, :] = value[:, half:]
 
 
 def split_square(square):
@@ -255,9 +258,9 @@
     rows = out.shape[0]
     width = weight.shape[2]
     at = rows_at(expert * rows, rows, rows)
-    total = arrived[0][at, :].astype(f32) + arrived[1 + direct][at, :].astype(f32)
+    total = arrived[0][at, :].astype(f32)
     halves = [0.0, 0.0]
-    for n, ref in enumerate(arrived[1 : 1 + direct] + arrived[2 + direct :]):
+    for n, ref in enumerate(arrived[1:]):
         halves[n >= direct] = halves[n >= direct] + ref[at, :].astype(f32)
     mixed = (total + jnp.concatenate(halves, axis=1)).astype(bf16).astype(f32)
     out[:, width:] = split_square(jnp.sum(mixed * mixed, axis=1, keepdims=True)).astype(out.dtype)
@@ -427,10 +430,10 @@
     )(stacked, kv_other, bias_other, *stats)
 
     halves, ranks = lax.optimization_barrier((halves, rank))
-    step = 1
-    while step < n_exp:
+    step = n_exp // 2
+    while step:
         ranks = jnp.concatenate([ranks, permute(ranks, "exp", step)], axis=0)
-        step *= 2
+        step //= 2
     pieces = gather_halves(halves, chips)
     pieces, ranks = lax.optimization_barrier((pieces, ranks))
     heads_same = jnp.concatenate([jnp.concatenate(pair, axis=1) for pair in pieces], axis=0)
@@ -451,18 +454,19 @@
         [shape((tokens, columns), f32)]
         + [shape((n_exp // 2 * tokens, columns), bf16)]
         + [shape((tokens, columns), bf16)] * (n_exp // 2 - 1)
-        + [shape((per_exp, columns), bf16)] * 2
-        + [shape((per_exp, columns // 2), bf16)] * (2 * n_exp - 4),
+        + [shape((per_exp, columns), bf16)]
+        + [shape((per_exp, columns // 2), bf16)] * (2 * n_exp - 2),
         [VMEM] * 5,
         [pltpu.VMEM(first.shape, f32)],
         vmem=24,
         **cost,
     )(heads_other, out_weight, first, residual, ranks)
     own, odd, even, picks = outs[0], outs[1], outs[2 : n_exp // 2 + 1], outs[n_exp // 2 + 1 :]
-    left, right = picks[2::2], picks[3::2]
+    left, right = picks[3::2], picks[4::2]
     passed = [permute(right[2 * k - 1], "exp", 1) for k in range(1, n_exp // 2)]
     direct = [permute(x, "exp", k) for k, x in enumerate(left, 2)][::-1]
-    arrived = [picks[0]] + direct + [permute(picks[1], "exp", 1)]
+    direct.append(permute(picks[1], "exp", 1))
+    arrived = [picks[0]] + direct + [permute(picks[2], "exp", 1)]
     for k, got in enumerate(passed, 1):
         pair = (right[2 * k - 2].astype(f32) + got.astype(f32)).astype(bf16)
         arrived.append(permute(pair, "exp", 2 * k))

time: 76.1 us -> 75 us (0.986)
  waiting for transfers between devices: 23.6 us -> 21.8 us
  starting transfers between devices: 37.2 us -> 38 us
    ppermute x31 -> x32, waiting for transfers between devices: 23.6 us -> 21.8 us  [permute(): return lax.ppermute(x, axis, [(i, i ^ k) for i in range(n)])]
    ppermute x31 -> x32, starting transfers between devices: 37.2 us -> 38 us  [permute(): return lax.ppermute(x, axis, [(i, i ^ k) for i in range(n)])]
  transfers between devices with their start and end apart: 31 -> 32, of which waited for: 20 -> 20; matrix products, arithmetic and copies ran while one was open for 4% -> 4% of each run, Pallas kernels for 5% -> 5%
where the time goes in v8:
time: 75 us; the launch traced here: 74.8 us
  starting transfers between devices  38 us (51%)
  waiting for transfers between devices  21.8 us (29%)
  Pallas kernels  10.2 us (14%)
  other arithmetic  2.89 us (4%)
  local copies, waits for them, and re-layouts  1.02 us (1%)
  between operations  0.89 us (1%)
    ppermute x32, starting transfers between devices, permute(): return lax.ppermute(x, axis, [(i, i ^ k) for i in range(n)])  38 us
    ppermute x32, waiting for transfers between devices, permute(): return lax.ppermute(x, axis, [(i, i ^ k) for i in range(n)])  21.8 us
    pallas_call x1, Pallas kernels, body(): call(functools.partial(attend_second, span), [shape((span, rows // span *...  1.7 us
    pallas_call x1, Pallas kernels, body(): call(functools.partial(attend_first, span), [shape((rows, HEAD), f32), sh...  1.62 us
    pallas_call x1, Pallas kernels, body(): call(functools.partial(pick_kv, heads), shape((cache + span, 2 * HEAD), b...  1.51 us
  transfers between devices with their start and end apart: 32, of which 20 were waited for; matrix products, arithmetic and copies ran while one was open for 4% of the time, Pallas kernels for 5%

profile of v8, /device:TPU:0, one launch (start us, length us, event | category | flops | bytes accessed | tf_op | source)
XLA Modules:
  0.0 74.8 jit_solution(11249942969926504170)
XLA Ops:
  0.6 1.5 %shard_map.140.kv = bf16[192,256]{1,0:T(8,128)(2,1)} custom-call(bf16[128,512]{1,0:T(8,128)(2,1)} %ck.1, bf16[128,512]{1,0:T(8,128)(2,1)} %cv.1, bf16[64,512]{1,0:T(8,128)(2,1)} %bk.1, bf16[64,512]{1,0:T(8,128)(2,1)} %bv.1), custom_call_target="tpu_custom_call" | custom-call | tf_op jit(solution)/shard_map/pallas_call | solution.py:380
  2.2 4.0 %collective-permute-start = (bf16[192,256]{1,0:T(8,128)(2,1)}, bf16[192,256]{1,0:T(8,128)(2,1)S(1)}, u32[]{:S(2)}, u32[]{:S(2)}) collective-permute-start(bf16[192,256]{1,0:T(8,128)(2,1)} %shard_map.140.kv), channel_id=1, source_target_pairs={{0,24},{4,28},{8,16},{12,20},{16,8},{20,12},{24,0},{28,4},{1,25},{... | collective-permute-start | bytes 294920 | tf_op jit(solution)/shard_map/ppermute | solution.py:333
  10.2 1.1 %collective-permute-done.1 = bf16[192,256]{1,0:T(8,128)(2,1)S(1)} collective-permute-done((bf16[192,256]{1,0:T(8,128)(2,1)}, bf16[192,256]{1,0:T(8,128)(2,1)S(1)}, u32[]{:S(2)}, u32[]{:S(2)}) %collective-permute-start.1) | collective-permute-done | bytes 98336 | tf_op jit(solution)/shard_map/ppermute | solution.py:333
  11.7 1.6 %shard_map.142 = (f32[1024,128]{1,0:T(8,128)S(1)}, f32[1024,128]{1,0:T(8,128)S(1)}, f32[1024,128]{1,0:T(8,128)S(1)}) custom-call(bf16[1024,128]{1,0:T(8,128)(2,1)S(1)} %bitcast.16, bf16[768,256]{1,0:T(8,128)(2,1)S(1)} %constant_dynamic-update-slice_fusion.kv, f32[64,768]{1,0:T(8,128)S(1)} %get-tuple-element.71.bias), custom_call_target="tpu_custom_call" | custom-call | flops 402653184 | bytes 4194304 | tf_op jit(solution)/shard_map/pallas_call | solution.py:417
  13.4 1.7 %shard_map.143 = (bf16[64,1024]{1,0:T(8,128)(2,1)S(1)}, bf16[64,1024]{1,0:T(8,128)(2,1)S(1)}) custom-call(bf16[1024,128]{1,0:T(8,128)(2,1)S(1)} %bitcast.17, bf16[768,256]{1,0:T(8,128)(2,1)S(1)} %collective-permute-done.3.kv, f32[64,768]{1,0:T(8,128)S(1)} %get-tuple-element.70.bias, f32[1024,128]{1,0:T(8,128)S(1)} %get-tuple-element.72.o_in, ...), custom_call_target="tpu_custom_call" | custom-call | flops 402653184 | bytes 4194304 | tf_op jit(solution)/shard_map/pallas_call | solution.py:424
  15.1 1.5 %collective-permute-start.4 = (bf16[64,1024]{1,0:T(8,128)(2,1)S(1)}, bf16[64,1024]{1,0:T(8,128)(2,1)S(1)}, u32[]{:S(2)}, u32[]{:S(2)}) collective-permute-start(bf16[64,1024]{1,0:T(8,128)(2,1)S(1)} %get-tuple-element.81), channel_id=1, source_target_pairs={{0,8},{4,12},{8,0},{12,4},{16,24},{20,28},{24,16},{28,20},{1,9},{5... | collective-permute-start | bytes 393224 | tf_op jit(solution)/shard_map/ppermute | solution.py:333
  17.2 2.7 %collective-permute-start.10 = (f32[8,128]{1,0:T(8,128)S(1)}, f32[8,128]{1,0:T(8,128)S(1)}, u32[]{:S(2)}, u32[]{:S(2)}) collective-permute-start(f32[8,128]{1,0:T(8,128)S(1)} %get-tuple-element.80), channel_id=1, source_target_pairs={{0,2},{1,3},{2,0},{3,1},{4,6},{5,7},{6,4},{7,5},{8,10},{9,11},{10,... | collective-permute-start | bytes 12296 | tf_op jit(solution)/shard_map/ppermute | solution.py:333
  20.0 1.3 %collective-permute-start.5 = (bf16[64,1024]{1,0:T(8,128)(2,1)S(1)}, bf16[64,1024]{1,0:T(8,128)(2,1)S(1)}, u32[]{:S(2)}, u32[]{:S(2)}) collective-permute-start(bf16[64,1024]{1,0:T(8,128)(2,1)S(1)} %get-tuple-element.82), channel_id=1, source_target_pairs={{0,8},{4,12},{8,0},{12,4},{16,24},{20,28},{24,16},{28,20},{1,9},{5... | collective-permute-start | bytes 393224 | tf_op jit(solution)/shard_map/ppermute | solution.py:333
  21.8 1.4 %collective-permute-start.8 = (bf16[64,1024]{1,0:T(8,128)(2,1)S(1)}, bf16[64,1024]{1,0:T(8,128)(2,1)S(1)}, u32[]{:S(2)}, u32[]{:S(2)}) collective-permute-start(bf16[64,1024]{1,0:T(8,128)(2,1)S(1)} %collective-permute-done.4), channel_id=1, source_target_pairs={{0,16},{4,20},{8,24},{12,28},{16,0},{20,4},{24,8},{28,12},{1,17},{... | collective-permute-start | bytes 393224 | tf_op jit(solution)/shard_map/ppermute | solution.py:333
  24.0 1.6 %collective-permute-start.11 = (f32[16,128]{1,0:T(8,128)S(1)}, f32[16,128]{1,0:T(8,128)S(1)}, u32[]{:S(2)}, u32[]{:S(2)}) collective-permute-start(f32[16,128]{1,0:T(8,128)S(1)} %pad_maximum_fusion.2), channel_id=1, source_target_pairs={{0,1},{1,0},{2,3},{3,2},{4,5},{5,4},{6,7},{7,6},{8,9},{9,8},{10,11... | collective-permute-start | bytes 24584 | tf_op jit(solution)/shard_map/ppermute | solution.py:333
  25.6 2.1 %collective-permute-done.11 = f32[16,128]{1,0:T(8,128)S(1)} collective-permute-done((f32[16,128]{1,0:T(8,128)S(1)}, f32[16,128]{1,0:T(8,128)S(1)}, u32[]{:S(2)}, u32[]{:S(2)}) %collective-permute-start.11) | collective-permute-done | bytes 8224 | tf_op jit(solution)/shard_map/ppermute | solution.py:333
  27.7 1.1 %collective-permute-done.8 = bf16[64,1024]{1,0:T(8,128)(2,1)S(1)} collective-permute-done((bf16[64,1024]{1,0:T(8,128)(2,1)S(1)}, bf16[64,1024]{1,0:T(8,128)(2,1)S(1)}, u32[]{:S(2)}, u32[]{:S(2)}) %collective-permute-start.8) | collective-permute-done | bytes 131104 | tf_op jit(solution)/shard_map/ppermute | solution.py:333
  29.7 1.9 %collective-permute-done.12.heads_out = bf16[256,2048]{1,0:T(8,128)(2,1)S(1)} collective-permute-done((bf16[256,2048]{1,0:T(8,128)(2,1)S(1)}, bf16[256,2048]{1,0:T(8,128)(2,1)S(1)}, u32[]{:S(2)}, u32[]{:S(2)}) %collective-permute-start.12) | collective-permute-done | bytes 1048608 | tf_op jit(solution)/shard_map/ppermute | solution.py:333
  31.6 1.0 %shard_map.145 = (f32[128,512]{1,0:T(8,128)S(1)}, bf16[256,512]{1,0:T(8,128)(2,1)S(1)}, bf16[128,512]{1,0:T(8,128)(2,1)S(1)}, bf16[128,512]{1,0:T(8,128)(2,1)S(1...) custom-call(bf16[256,2048]{1,0:T(8,128)(2,1)S(1)} %collective-permut, ...), custom_call_target="tpu_custom_call" | custom-call | flops 536870912 | bytes 4194304 | tf_op jit(solution)/shard_map/pallas_call | solution.py:452
  32.6 1.6 %collective-permute-start.17 = (bf16[128,256]{1,0:T(8,128)(2,1)S(1)}, bf16[128,256]{1,0:T(8,128)(2,1)S(1)}, u32[]{:S(2)}, u32[]{:S(2)}) collective-permute-start(bf16[128,256]{1,0:T(8,128)(2,1)S(1)} %get-tuple-element.97), channel_id=1, source_target_pairs={{0,1},{1,0},{2,3},{3,2},{4,5},{5,4},{6,7},{7,6},{8,9},{9,8},{10,11... | collective-permute-start | bytes 196616 | tf_op jit(solution)/shard_map/ppermute | solution.py:333
  34.3 1.7 %collective-permute-start.13 = (bf16[128,256]{1,0:T(8,128)(2,1)S(1)}, bf16[128,256]{1,0:T(8,128)(2,1)S(1)}, u32[]{:S(2)}, u32[]{:S(2)}) collective-permute-start(bf16[128,256]{1,0:T(8,128)(2,1)S(1)} %get-tuple-element.92), channel_id=1, source_target_pairs={{0,3},{1,2},{2,1},{3,0},{4,7},{5,6},{6,5},{7,4},{8,11},{9,10},{10,... | collective-permute-start | bytes 196616 | tf_op jit(solution)/shard_map/ppermute | solution.py:333
  36.2 2.5 %collective-permute-start.15 = (bf16[128,256]{1,0:T(8,128)(2,1)S(1)}, bf16[128,256]{1,0:T(8,128)(2,1)S(1)}, u32[]{:S(2)}, u32[]{:S(2)}) collective-permute-start(bf16[128,256]{1,0:T(8,128)(2,1)S(1)} %get-tuple-element.94), channel_id=1, source_target_pairs={{0,1},{1,0},{2,3},{3,2},{4,5},{5,4},{6,7},{7,6},{8,9},{9,8},{10,11... | collective-permute-start | bytes 196616 | tf_op jit(solution)/shard_map/ppermute | solution.py:333
  38.7 2.3 %collective-permute-start.18 = (bf16[128,256]{1,0:T(8,128)(2,1)S(1)}, bf16[128,256]{1,0:T(8,128)(2,1)S(1)}, u32[]{:S(2)}, u32[]{:S(2)}) collective-permute-start(bf16[128,256]{1,0:T(8,128)(2,1)S(1)} %add_convert_fusion.2), channel_id=1, source_target_pairs={{0,2},{1,3},{2,0},{3,1},{4,6},{5,7},{6,4},{7,5},{8,10},{9,11},{10,... | collective-permute-start | bytes 196616 | tf_op jit(solution)/shard_map/ppermute | solution.py:333
  41.1 1.8 %collective-permute-done.14.refs_2_ = bf16[128,256]{1,0:T(8,128)(2,1)S(1)} collective-permute-done((bf16[128,256]{1,0:T(8,128)(2,1)S(1)}, bf16[128,256]{1,0:T(8,128)(2,1)S(1)}, u32[]{:S(2)}, u32[]{:S(2)}) %collective-permute-start.14) | collective-permute-done | bytes 65568 | tf_op jit(solution)/shard_map/ppermute | solution.py:333
  42.8 1.5 %collective-permute-done.15.refs_3_ = bf16[128,256]{1,0:T(8,128)(2,1)S(1)} collective-permute-done((bf16[128,256]{1,0:T(8,128)(2,1)S(1)}, bf16[128,256]{1,0:T(8,128)(2,1)S(1)}, u32[]{:S(2)}, u32[]{:S(2)}) %collective-permute-start.15) | collective-permute-done | bytes 65568 | tf_op jit(solution)/shard_map/ppermute | solution.py:333
  44.4 1.1 %collective-permute-done.16.refs_4_ = bf16[128,256]{1,0:T(8,128)(2,1)S(1)} collective-permute-done((bf16[128,256]{1,0:T(8,128)(2,1)S(1)}, bf16[128,256]{1,0:T(8,128)(2,1)S(1)}, u32[]{:S(2)}, u32[]{:S(2)}) %collective-permute-start.16) | collective-permute-done | bytes 65568 | tf_op jit(solution)/shard_map/ppermute | solution.py:333
  49.0 1.3 %collective-permute-start.21 = (bf16[16,3200]{1,0:T(8,128)(2,1)S(1)}, bf16[16,3200]{1,0:T(8,128)(2,1)S(1)}, u32[]{:S(2)}, u32[]{:S(2)}) collective-permute-start(bf16[16,3200]{1,0:T(8,128)(2,1)S(1)} %get-tuple-element.101), channel_id=1, source_target_pairs={{0,16},{4,20},{8,24},{12,28},{16,0},{20,4},{24,8},{28,12},{1,17},{... | collective-permute-start | bytes 307208 | tf_op jit(solution)/shard_map/ppermute | solution.py:333
  50.3 1.4 %collective-permute-start.22 = (bf16[16,3200]{1,0:T(8,128)(2,1)S(1)}, bf16[16,3200]{1,0:T(8,128)(2,1)S(1)}, u32[]{:S(2)}, u32[]{:S(2)}) collective-permute-start(bf16[16,3200]{1,0:T(8,128)(2,1)S(1)} %get-tuple-element.102), channel_id=1, source_target_pairs={{0,24},{4,28},{8,16},{12,20},{16,8},{20,12},{24,0},{28,4},{1,25},{... | collective-permute-start | bytes 307208 | tf_op jit(solution)/shard_map/ppermute | solution.py:333
  51.7 3.3 %collective-permute-done.23 = bf16[256,512]{1,0:T(8,128)(2,1)S(1)} collective-permute-done((bf16[256,512]{1,0:T(8,128)(2,1)S(1)}, bf16[256,512]{1,0:T(8,128)(2,1)S(1)}, u32[]{:S(2)}, u32[]{:S(2)}) %collective-permute-start.23) | collective-permute-done | bytes 262176 | tf_op jit(solution)/shard_map/ppermute | solution.py:333
  55.9 2.2 %collective-permute-start.27 = (bf16[128,512]{1,0:T(8,128)(2,1)S(1)}, bf16[128,512]{1,0:T(8,128)(2,1)S(1)}, u32[]{:S(2)}, u32[]{:S(2)}) collective-permute-start(bf16[128,512]{1,0:T(8,128)(2,1)S(1)} %add_convert_fusion.1), channel_id=1, source_target_pairs={{0,2},{1,3},{2,0},{3,1},{4,6},{5,7},{6,4},{7,5},{8,10},{9,11},{10,... | collective-permute-start | bytes 393224 | tf_op jit(solution)/shard_map/ppermute | solution.py:333
  58.2 1.5 %collective-permute-start.24 = (bf16[16,1536]{1,0:T(8,128)(2,1)S(1)}, bf16[16,1536]{1,0:T(8,128)(2,1)S(1)}, u32[]{:S(2)}, u32[]{:S(2)}) collective-permute-start(bf16[16,1536]{1,0:T(8,128)(2,1)S(1)} %shard_map.149), channel_id=1, source_target_pairs={{0,24},{4,28},{8,16},{12,20},{16,8},{20,12},{24,0},{28,4},{1,25},{... | collective-permute-start | bytes 147464 | tf_op jit(solution)/shard_map/ppermute | solution.py:333
  59.7 1.3 %collective-permute-start.25 = (bf16[16,1536]{1,0:T(8,128)(2,1)S(1)}, bf16[16,1536]{1,0:T(8,128)(2,1)S(1)}, u32[]{:S(2)}, u32[]{:S(2)}) collective-permute-start(bf16[16,1536]{1,0:T(8,128)(2,1)S(1)} %shard_map.149), channel_id=1, source_target_pairs={{0,16},{4,20},{8,24},{12,28},{16,0},{20,4},{24,8},{28,12},{1,17},{... | collective-permute-start | bytes 147464 | tf_op jit(solution)/shard_map/ppermute | solution.py:333
  61.7 1.5 %collective-permute-done.24 = bf16[16,1536]{1,0:T(8,128)(2,1)S(1)} collective-permute-done((bf16[16,1536]{1,0:T(8,128)(2,1)S(1)}, bf16[16,1536]{1,0:T(8,128)(2,1)S(1)}, u32[]{:S(2)}, u32[]{:S(2)}) %collective-permute-start.24) | collective-permute-done | bytes 49184 | tf_op jit(solution)/shard_map/ppermute | solution.py:333
  63.8 1.3 %collective-permute-done.26 = bf16[16,1536]{1,0:T(8,128)(2,1)S(1)} collective-permute-done((bf16[16,1536]{1,0:T(8,128)(2,1)S(1)}, bf16[16,1536]{1,0:T(8,128)(2,1)S(1)}, u32[]{:S(2)}, u32[]{:S(2)}) %collective-permute-start.26) | collective-permute-done | bytes 49184 | tf_op jit(solution)/shard_map/ppermute | solution.py:333
  67.0 1.4 %collective-permute-start.29 = (bf16[32,512]{1,0:T(8,128)(2,1)S(1)}, bf16[32,512]{1,0:T(8,128)(2,1)S(1)}, u32[]{:S(2)}, u32[]{:S(2)}) collective-permute-start(bf16[32,512]{1,0:T(8,128)(2,1)S(1)} %get-tuple-element.117), channel_id=1, source_target_pairs={{0,3},{1,2},{2,1},{3,0},{4,7},{5,6},{6,5},{7,4},{8,11},{9,10},{10,... | collective-permute-start | bytes 98312 | tf_op jit(solution)/shard_map/ppermute | solution.py:333
  68.4 1.1 %collective-permute-start.30 = (bf16[32,512]{1,0:T(8,128)(2,1)S(1)}, bf16[32,512]{1,0:T(8,128)(2,1)S(1)}, u32[]{:S(2)}, u32[]{:S(2)}) collective-permute-start(bf16[32,512]{1,0:T(8,128)(2,1)S(1)} %get-tuple-element.118), channel_id=1, source_target_pairs={{0,2},{1,3},{2,0},{3,1},{4,6},{5,7},{6,4},{7,5},{8,10},{9,11},{10,... | collective-permute-start | bytes 98312 | tf_op jit(solution)/shard_map/ppermute | solution.py:333
  69.5 2.0 %collective-permute-start.31 = (bf16[32,512]{1,0:T(8,128)(2,1)S(1)}, bf16[32,512]{1,0:T(8,128)(2,1)S(1)}, u32[]{:S(2)}, u32[]{:S(2)}) collective-permute-start(bf16[32,512]{1,0:T(8,128)(2,1)S(1)} %get-tuple-element.119), channel_id=1, source_target_pairs={{0,1},{1,0},{2,3},{3,2},{4,5},{5,4},{6,7},{7,6},{8,9},{9,8},{10,11... | collective-permute-start | bytes 98312 | tf_op jit(solution)/shard_map/ppermute | solution.py:333
  (77 shorter events, 18.7 us)
Async XLA Ops:
  2.2 8.0 %collective-permute-start = (bf16[192,256]{1,0:T(8,128)(2,1)}, bf16[192,256]{1,0:T(8,128)(2,1)S(1)}, u32[]{:S(2)}, u32[]{:S(2)}) collective-permute-start(bf16[192,256]{1,0:T(8,128)(2,1)} %shard_map.140.kv), channel_id=1, source_target_pairs={{0,24},{4,28},{8,16},{12,20},{16,8},{20,12},{24,0},{28,4},{1,25},{... | collective-permute-start | bytes 294920 | tf_op jit(solution)/shard_map/ppermute | solution.py:333
  6.1 5.1 %collective-permute-start.1 = (bf16[192,256]{1,0:T(8,128)(2,1)}, bf16[192,256]{1,0:T(8,128)(2,1)S(1)}, u32[]{:S(2)}, u32[]{:S(2)}) collective-permute-start(bf16[192,256]{1,0:T(8,128)(2,1)} %shard_map.140.kv), channel_id=1, source_target_pairs={{0,16},{4,20},{8,24},{12,28},{16,0},{20,4},{24,8},{28,12},{1,17},{... | collective-permute-start | bytes 294920 | tf_op jit(solution)/shard_map/ppermute | solution.py:333
  6.6 4.9 %collective-permute-start.2 = (bf16[192,256]{1,0:T(8,128)(2,1)}, bf16[192,256]{1,0:T(8,128)(2,1)S(1)}, u32[]{:S(2)}, u32[]{:S(2)}) collective-permute-start(bf16[192,256]{1,0:T(8,128)(2,1)} %shard_map.140.kv), channel_id=1, source_target_pairs={{0,8},{4,12},{8,0},{12,4},{16,24},{20,28},{24,16},{28,20},{1,9},{5... | collective-permute-start | bytes 294920 | tf_op jit(solution)/shard_map/ppermute | solution.py:333
  11.6 1.8 %collective-permute-start.3 = (bf16[768,256]{1,0:T(8,128)(2,1)S(1)}, bf16[768,256]{1,0:T(8,128)(2,1)S(1)}, u32[]{:S(2)}, u32[]{:S(2)}) collective-permute-start(bf16[768,256]{1,0:T(8,128)(2,1)S(1)} %constant_dynamic-update-slice_fusion.kv), channel_id=1, source_target_pairs={{0,4},{4,0},{8,12},{12,8},{16,20},{20,16},{24,28},{28,24},{1,5},{5... | collective-permute-start | bytes 1179656 | tf_op jit(solution)/shard_map/ppermute | solution.py:333
  15.1 6.7 %collective-permute-start.4 = (bf16[64,1024]{1,0:T(8,128)(2,1)S(1)}, bf16[64,1024]{1,0:T(8,128)(2,1)S(1)}, u32[]{:S(2)}, u32[]{:S(2)}) collective-permute-start(bf16[64,1024]{1,0:T(8,128)(2,1)S(1)} %get-tuple-element.81), channel_id=1, source_target_pairs={{0,8},{4,12},{8,0},{12,4},{16,24},{20,28},{24,16},{28,20},{1,9},{5... | collective-permute-start | bytes 393224 | tf_op jit(solution)/shard_map/ppermute | solution.py:333
  16.6 6.6 %collective-permute-start.7 = (bf16[64,1024]{1,0:T(8,128)(2,1)S(1)}, bf16[64,1024]{1,0:T(8,128)(2,1)S(1)}, u32[]{:S(2)}, u32[]{:S(2)}) collective-permute-start(bf16[64,1024]{1,0:T(8,128)(2,1)S(1)} %get-tuple-element.82), channel_id=1, source_target_pairs={{0,16},{4,20},{8,24},{12,28},{16,0},{20,4},{24,8},{28,12},{1,17},{... | collective-permute-start | bytes 393224 | tf_op jit(solution)/shard_map/ppermute | solution.py:333
  17.2 6.8 %collective-permute-start.10 = (f32[8,128]{1,0:T(8,128)S(1)}, f32[8,128]{1,0:T(8,128)S(1)}, u32[]{:S(2)}, u32[]{:S(2)}) collective-permute-start(f32[8,128]{1,0:T(8,128)S(1)} %get-tuple-element.80), channel_id=1, source_target_pairs={{0,2},{1,3},{2,0},{3,1},{4,6},{5,7},{6,4},{7,5},{8,10},{9,11},{10,... | collective-permute-start | bytes 12296 | tf_op jit(solution)/shard_map/ppermute | solution.py:333
  20.0 7.7 %collective-permute-start.5 = (bf16[64,1024]{1,0:T(8,128)(2,1)S(1)}, bf16[64,1024]{1,0:T(8,128)(2,1)S(1)}, u32[]{:S(2)}, u32[]{:S(2)}) collective-permute-start(bf16[64,1024]{1,0:T(8,128)(2,1)S(1)} %get-tuple-element.82), channel_id=1, source_target_pairs={{0,8},{4,12},{8,0},{12,4},{16,24},{20,28},{24,16},{28,20},{1,9},{5... | collective-permute-start | bytes 393224 | tf_op jit(solution)/shard_map/ppermute | solution.py:333
  21.2 6.5 %collective-permute-start.6 = (bf16[64,1024]{1,0:T(8,128)(2,1)S(1)}, bf16[64,1024]{1,0:T(8,128)(2,1)S(1)}, u32[]{:S(2)}, u32[]{:S(2)}) collective-permute-start(bf16[64,1024]{1,0:T(8,128)(2,1)S(1)} %get-tuple-element.81), channel_id=1, source_target_pairs={{0,16},{4,20},{8,24},{12,28},{16,0},{20,4},{24,8},{28,12},{1,17},{... | collective-permute-start | bytes 393224 | tf_op jit(solution)/shard_map/ppermute | solution.py:333
  21.8 6.9 %collective-permute-start.8 = (bf16[64,1024]{1,0:T(8,128)(2,1)S(1)}, bf16[64,1024]{1,0:T(8,128)(2,1)S(1)}, u32[]{:S(2)}, u32[]{:S(2)}) collective-permute-start(bf16[64,1024]{1,0:T(8,128)(2,1)S(1)} %collective-permute-done.4), channel_id=1, source_target_pairs={{0,16},{4,20},{8,24},{12,28},{16,0},{20,4},{24,8},{28,12},{1,17},{... | collective-permute-start | bytes 393224 | tf_op jit(solution)/shard_map/ppermute | solution.py:333
  23.2 5.5 %collective-permute-start.9 = (bf16[64,1024]{1,0:T(8,128)(2,1)S(1)}, bf16[64,1024]{1,0:T(8,128)(2,1)S(1)}, u32[]{:S(2)}, u32[]{:S(2)}) collective-permute-start(bf16[64,1024]{1,0:T(8,128)(2,1)S(1)} %collective-permute-done.7), channel_id=1, source_target_pairs={{0,8},{4,12},{8,0},{12,4},{16,24},{20,28},{24,16},{28,20},{1,9},{5... | collective-permute-start | bytes 393224 | tf_op jit(solution)/shard_map/ppermute | solution.py:333
  24.0 3.7 %collective-permute-start.11 = (f32[16,128]{1,0:T(8,128)S(1)}, f32[16,128]{1,0:T(8,128)S(1)}, u32[]{:S(2)}, u32[]{:S(2)}) collective-permute-start(f32[16,128]{1,0:T(8,128)S(1)} %pad_maximum_fusion.2), channel_id=1, source_target_pairs={{0,1},{1,0},{2,3},{3,2},{4,5},{5,4},{6,7},{7,6},{8,9},{9,8},{10,11... | collective-permute-start | bytes 24584 | tf_op jit(solution)/shard_map/ppermute | solution.py:333
  28.8 2.7 %collective-permute-start.12 = (bf16[256,2048]{1,0:T(8,128)(2,1)S(1)}, bf16[256,2048]{1,0:T(8,128)(2,1)S(1)}, u32[]{:S(2)}, u32[]{:S(2)}) collective-permute-start(bf16[256,2048]{1,0:T(8,128)(2,1)S(1)} %maximum_maximum_fusion.heads_out), channel_id=1, source_target_pairs={{0,4},{4,0},{8,12},{12,8},{16,20},{20,16},{24,28},{28,24},{1,5},{5... | collective-permute-start | bytes 3145736 | tf_op jit(solution)/shard_map/ppermute | solution.py:333
  32.6 6.1 %collective-permute-start.17 = (bf16[128,256]{1,0:T(8,128)(2,1)S(1)}, bf16[128,256]{1,0:T(8,128)(2,1)S(1)}, u32[]{:S(2)}, u32[]{:S(2)}) collective-permute-start(bf16[128,256]{1,0:T(8,128)(2,1)S(1)} %get-tuple-element.97), channel_id=1, source_target_pairs={{0,1},{1,0},{2,3},{3,2},{4,5},{5,4},{6,7},{7,6},{8,9},{9,8},{10,11... | collective-permute-start | bytes 196616 | tf_op jit(solution)/shard_map/ppermute | solution.py:333
  34.3 6.8 %collective-permute-start.13 = (bf16[128,256]{1,0:T(8,128)(2,1)S(1)}, bf16[128,256]{1,0:T(8,128)(2,1)S(1)}, u32[]{:S(2)}, u32[]{:S(2)}) collective-permute-start(bf16[128,256]{1,0:T(8,128)(2,1)S(1)} %get-tuple-element.92), channel_id=1, source_target_pairs={{0,3},{1,2},{2,1},{3,0},{4,7},{5,6},{6,5},{7,4},{8,11},{9,10},{10,... | collective-permute-start | bytes 196616 | tf_op jit(solution)/shard_map/ppermute | solution.py:333
  35.9 6.9 %collective-permute-start.14 = (bf16[128,256]{1,0:T(8,128)(2,1)S(1)}, bf16[128,256]{1,0:T(8,128)(2,1)S(1)}, u32[]{:S(2)}, u32[]{:S(2)}) collective-permute-start(bf16[128,256]{1,0:T(8,128)(2,1)S(1)} %get-tuple-element.93), channel_id=1, source_target_pairs={{0,2},{1,3},{2,0},{3,1},{4,6},{5,7},{6,4},{7,5},{8,10},{9,11},{10,... | collective-permute-start | bytes 196616 | tf_op jit(solution)/shard_map/ppermute | solution.py:333
  36.2 8.2 %collective-permute-start.15 = (bf16[128,256]{1,0:T(8,128)(2,1)S(1)}, bf16[128,256]{1,0:T(8,128)(2,1)S(1)}, u32[]{:S(2)}, u32[]{:S(2)}) collective-permute-start(bf16[128,256]{1,0:T(8,128)(2,1)S(1)} %get-tuple-element.94), channel_id=1, source_target_pairs={{0,1},{1,0},{2,3},{3,2},{4,5},{5,4},{6,7},{7,6},{8,9},{9,8},{10,11... | collective-permute-start | bytes 196616 | tf_op jit(solution)/shard_map/ppermute | solution.py:333
  38.6 6.9 %collective-permute-start.16 = (bf16[128,256]{1,0:T(8,128)(2,1)S(1)}, bf16[128,256]{1,0:T(8,128)(2,1)S(1)}, u32[]{:S(2)}, u32[]{:S(2)}) collective-permute-start(bf16[128,256]{1,0:T(8,128)(2,1)S(1)} %get-tuple-element.95), channel_id=1, source_target_pairs={{0,1},{1,0},{2,3},{3,2},{4,5},{5,4},{6,7},{7,6},{8,9},{9,8},{10,11... | collective-permute-start | bytes 196616 | tf_op jit(solution)/shard_map/ppermute | solution.py:333
  38.7 6.8 %collective-permute-start.18 = (bf16[128,256]{1,0:T(8,128)(2,1)S(1)}, bf16[128,256]{1,0:T(8,128)(2,1)S(1)}, u32[]{:S(2)}, u32[]{:S(2)}) collective-permute-start(bf16[128,256]{1,0:T(8,128)(2,1)S(1)} %add_convert_fusion.2), channel_id=1, source_target_pairs={{0,2},{1,3},{2,0},{3,1},{4,6},{5,7},{6,4},{7,5},{8,10},{9,11},{10,... | collective-permute-start | bytes 196616 | tf_op jit(solution)/shard_map/ppermute | solution.py:333
  46.2 1.8 %collective-permute-start.19 = (bf16[64,3200]{1,0:T(8,128)(2,1)S(1)}, bf16[64,3200]{1,0:T(8,128)(2,1)S(1)}, u32[]{:S(2)}, u32[]{:S(2)}) collective-permute-start(bf16[64,3200]{1,0:T(8,128)(2,1)S(1)} %shard_map.147), channel_id=1, source_target_pairs={{0,4},{4,0},{8,12},{12,8},{16,20},{20,16},{24,28},{28,24},{1,5},{5... | collective-permute-start | bytes 1228808 | tf_op jit(solution)/shard_map/ppermute | solution.py:333
  46.3 8.7 %collective-permute-start.23 = (bf16[256,512]{1,0:T(8,128)(2,1)S(1)}, bf16[256,512]{1,0:T(8,128)(2,1)S(1)}, u32[]{:S(2)}, u32[]{:S(2)}) collective-permute-start(bf16[256,512]{1,0:T(8,128)(2,1)S(1)} %get-tuple-element.103), channel_id=1, source_target_pairs={{0,1},{1,0},{2,3},{3,2},{4,5},{5,4},{6,7},{7,6},{8,9},{9,8},{10,11... | collective-permute-start | bytes 786440 | tf_op jit(solution)/shard_map/ppermute | solution.py:333
  48.2 6.9 %collective-permute-start.20 = (bf16[16,3200]{1,0:T(8,128)(2,1)S(1)}, bf16[16,3200]{1,0:T(8,128)(2,1)S(1)}, u32[]{:S(2)}, u32[]{:S(2)}) collective-permute-start(bf16[16,3200]{1,0:T(8,128)(2,1)S(1)} %get-tuple-element.100), channel_id=1, source_target_pairs={{0,8},{4,12},{8,0},{12,4},{16,24},{20,28},{24,16},{28,20},{1,9},{5... | collective-permute-start | bytes 307208 | tf_op jit(solution)/shard_map/ppermute | solution.py:333
  49.0 6.1 %collective-permute-start.21 = (bf16[16,3200]{1,0:T(8,128)(2,1)S(1)}, bf16[16,3200]{1,0:T(8,128)(2,1)S(1)}, u32[]{:S(2)}, u32[]{:S(2)}) collective-permute-start(bf16[16,3200]{1,0:T(8,128)(2,1)S(1)} %get-tuple-element.101), channel_id=1, source_target_pairs={{0,16},{4,20},{8,24},{12,28},{16,0},{20,4},{24,8},{28,12},{1,17},{... | collective-permute-start | bytes 307208 | tf_op jit(solution)/shard_map/ppermute | solution.py:333
  50.3 5.6 %collective-permute-start.22 = (bf16[16,3200]{1,0:T(8,128)(2,1)S(1)}, bf16[16,3200]{1,0:T(8,128)(2,1)S(1)}, u32[]{:S(2)}, u32[]{:S(2)}) collective-permute-start(bf16[16,3200]{1,0:T(8,128)(2,1)S(1)} %get-tuple-element.102), channel_id=1, source_target_pairs={{0,24},{4,28},{8,16},{12,20},{16,8},{20,12},{24,0},{28,4},{1,25},{... | collective-permute-start | bytes 307208 | tf_op jit(solution)/shard_map/ppermute | solution.py:333
  55.9 9.2 %collective-permute-start.27 = (bf16[128,512]{1,0:T(8,128)(2,1)S(1)}, bf16[128,512]{1,0:T(8,128)(2,1)S(1)}, u32[]{:S(2)}, u32[]{:S(2)}) collective-permute-start(bf16[128,512]{1,0:T(8,128)(2,1)S(1)} %add_convert_fusion.1), channel_id=1, source_target_pairs={{0,2},{1,3},{2,0},{3,1},{4,6},{5,7},{6,4},{7,5},{8,10},{9,11},{10,... | collective-permute-start | bytes 393224 | tf_op jit(solution)/shard_map/ppermute | solution.py:333
  58.2 5.1 %collective-permute-start.24 = (bf16[16,1536]{1,0:T(8,128)(2,1)S(1)}, bf16[16,1536]{1,0:T(8,128)(2,1)S(1)}, u32[]{:S(2)}, u32[]{:S(2)}) collective-permute-start(bf16[16,1536]{1,0:T(8,128)(2,1)S(1)} %shard_map.149), channel_id=1, source_target_pairs={{0,24},{4,28},{8,16},{12,20},{16,8},{20,12},{24,0},{28,4},{1,25},{... | collective-permute-start | bytes 147464 | tf_op jit(solution)/shard_map/ppermute | solution.py:333
  59.7 4.1 %collective-permute-start.25 = (bf16[16,1536]{1,0:T(8,128)(2,1)S(1)}, bf16[16,1536]{1,0:T(8,128)(2,1)S(1)}, u32[]{:S(2)}, u32[]{:S(2)}) collective-permute-start(bf16[16,1536]{1,0:T(8,128)(2,1)S(1)} %shard_map.149), channel_id=1, source_target_pairs={{0,16},{4,20},{8,24},{12,28},{16,0},{20,4},{24,8},{28,12},{1,17},{... | collective-permute-start | bytes 147464 | tf_op jit(solution)/shard_map/ppermute | solution.py:333
  61.0 4.1 %collective-permute-start.26 = (bf16[16,1536]{1,0:T(8,128)(2,1)S(1)}, bf16[16,1536]{1,0:T(8,128)(2,1)S(1)}, u32[]{:S(2)}, u32[]{:S(2)}) collective-permute-start(bf16[16,1536]{1,0:T(8,128)(2,1)S(1)} %shard_map.149), channel_id=1, source_target_pairs={{0,8},{4,12},{8,0},{12,4},{16,24},{20,28},{24,16},{28,20},{1,9},{5... | collective-permute-start | bytes 147464 | tf_op jit(solution)/shard_map/ppermute | solution.py:333
  65.1 1.5 %collective-permute-start.28 = (bf16[64,1536]{1,0:T(8,128)(2,1)S(1)}, bf16[64,1536]{1,0:T(8,128)(2,1)S(1)}, u32[]{:S(2)}, u32[]{:S(2)}) collective-permute-start(bf16[64,1536]{1,0:T(8,128)(2,1)S(1)} %pad_maximum_fusion.active), channel_id=1, source_target_pairs={{0,4},{4,0},{8,12},{12,8},{16,20},{20,16},{24,28},{28,24},{1,5},{5... | collective-permute-start | bytes 589832 | tf_op jit(solution)/shard_map/ppermute | solution.py:333
  67.0 5.8 %collective-permute-start.29 = (bf16[32,512]{1,0:T(8,128)(2,1)S(1)}, bf16[32,512]{1,0:T(8,128)(2,1)S(1)}, u32[]{:S(2)}, u32[]{:S(2)}) collective-permute-start(bf16[32,512]{1,0:T(8,128)(2,1)S(1)} %get-tuple-element.117), channel_id=1, source_target_pairs={{0,3},{1,2},{2,1},{3,0},{4,7},{5,6},{6,5},{7,4},{8,11},{9,10},{10,... | collective-permute-start | bytes 98312 | tf_op jit(solution)/shard_map/ppermute | solution.py:333
  68.4 5.3 %collective-permute-start.30 = (bf16[32,512]{1,0:T(8,128)(2,1)S(1)}, bf16[32,512]{1,0:T(8,128)(2,1)S(1)}, u32[]{:S(2)}, u32[]{:S(2)}) collective-permute-start(bf16[32,512]{1,0:T(8,128)(2,1)S(1)} %get-tuple-element.118), channel_id=1, source_target_pairs={{0,2},{1,3},{2,0},{3,1},{4,6},{5,7},{6,4},{7,5},{8,10},{9,11},{10,... | collective-permute-start | bytes 98312 | tf_op jit(solution)/shard_map/ppermute | solution.py:333
  69.5 4.4 %collective-permute-start.31 = (bf16[32,512]{1,0:T(8,128)(2,1)S(1)}, bf16[32,512]{1,0:T(8,128)(2,1)S(1)}, u32[]{:S(2)}, u32[]{:S(2)}) collective-permute-start(bf16[32,512]{1,0:T(8,128)(2,1)S(1)} %get-tuple-element.119), channel_id=1, source_target_pairs={{0,1},{1,0},{2,3},{3,2},{4,5},{5,4},{6,7},{7,6},{8,9},{9,8},{10,11... | collective-permute-start | bytes 98312 | tf_op jit(solution)/shard_map/ppermute | solution.py:333
  (8 other events, 109.6 us)

commit v9 on v8

--- a/solution.py
+++ b/solution.py
@@ -320,7 +320,7 @@
 
 def combine(high, low, *refs):
     out = refs[-1]
-    rows = jnp.concatenate([ref[...] for ref in (refs[0], *refs[-2:0:-1])], axis=0)
+    rows = jnp.concatenate([ref[...] for ref in (refs[0], *refs[2:-1], refs[1])], axis=0)
     dims = (((0,), (0,)), ((), ()))
     out[...] = (
         lax.dot_general(high[...], rows, dims, preferred_element_type=f32)
@@ -532,7 +532,7 @@
         vmem=8,
         **cost,
     )(active_other, expert_out, made)
-    returned = [permute(produced[k], "exp", k) for k in reversed(range(1, n_exp))]
+    returned = [permute(produced[k], "exp", k) for k in (n_exp - 1, *range(1, n_exp - 1))]
     mixed = own + odd[:tokens].astype(f32)
     for part in even:
         mixed = mixed + part.astype(f32)

time: 75 us -> 74.8 us (level)
  no operation moved by 1% of the time
where the time goes in v9:
time: 74.8 us; the launch traced here: 74.6 us
  starting transfers between devices  38 us (51%)
  waiting for transfers between devices  21.6 us (29%)
  Pallas kernels  10.2 us (14%)
  other arithmetic  2.89 us (4%)
  local copies, waits for them, and re-layouts  1.02 us (1%)
  between operations  0.89 us (1%)
    ppermute x32, starting transfers between devices, permute(): return lax.ppermute(x, axis, [(i, i ^ k) for i in range(n)])  38 us
    ppermute x32, waiting for transfers between devices, permute(): return lax.ppermute(x, axis, [(i, i ^ k) for i in range(n)])  21.6 us
    pallas_call x1, Pallas kernels, body(): call(functools.partial(attend_second, span), [shape((span, rows // span *...  1.7 us
    pallas_call x1, Pallas kernels, body(): call(functools.partial(attend_first, span), [shape((rows, HEAD), f32), sh...  1.62 us
    pallas_call x1, Pallas kernels, body(): call(functools.partial(pick_kv, heads), shape((cache + span, 2 * HEAD), b...  1.51 us
  transfers between devices with their start and end apart: 32, of which 20 were waited for; matrix products, arithmetic and copies ran while one was open for 4% of the time, Pallas kernels for 5%

profile of v9, /device:TPU:0, one launch (start us, length us, event | category | flops | bytes accessed | tf_op | source)
XLA Modules:
  0.0 74.6 jit_solution(6128476064755256496)
XLA Ops:
  0.6 1.5 %shard_map.140.kv = bf16[192,256]{1,0:T(8,128)(2,1)} custom-call(bf16[128,512]{1,0:T(8,128)(2,1)} %ck.1, bf16[128,512]{1,0:T(8,128)(2,1)} %cv.1, bf16[64,512]{1,0:T(8,128)(2,1)} %bk.1, bf16[64,512]{1,0:T(8,128)(2,1)} %bv.1), custom_call_target="tpu_custom_call" | custom-call | tf_op jit(solution)/shard_map/pallas_call | solution.py:380
  2.2 4.0 %collective-permute-start = (bf16[192,256]{1,0:T(8,128)(2,1)}, bf16[192,256]{1,0:T(8,128)(2,1)S(1)}, u32[]{:S(2)}, u32[]{:S(2)}) collective-permute-start(bf16[192,256]{1,0:T(8,128)(2,1)} %shard_map.140.kv), channel_id=1, source_target_pairs={{0,24},{4,28},{8,16},{12,20},{16,8},{20,12},{24,0},{28,4},{1,25},{... | collective-permute-start | bytes 294920 | tf_op jit(solution)/shard_map/ppermute | solution.py:333
  10.2 1.1 %collective-permute-done.1 = bf16[192,256]{1,0:T(8,128)(2,1)S(1)} collective-permute-done((bf16[192,256]{1,0:T(8,128)(2,1)}, bf16[192,256]{1,0:T(8,128)(2,1)S(1)}, u32[]{:S(2)}, u32[]{:S(2)}) %collective-permute-start.1) | collective-permute-done | bytes 98336 | tf_op jit(solution)/shard_map/ppermute | solution.py:333
  11.7 1.6 %shard_map.142 = (f32[1024,128]{1,0:T(8,128)S(1)}, f32[1024,128]{1,0:T(8,128)S(1)}, f32[1024,128]{1,0:T(8,128)S(1)}) custom-call(bf16[1024,128]{1,0:T(8,128)(2,1)S(1)} %bitcast.16, bf16[768,256]{1,0:T(8,128)(2,1)S(1)} %constant_dynamic-update-slice_fusion.kv, f32[64,768]{1,0:T(8,128)S(1)} %get-tuple-element.71.bias), custom_call_target="tpu_custom_call" | custom-call | flops 402653184 | bytes 4194304 | tf_op jit(solution)/shard_map/pallas_call | solution.py:417
  13.4 1.7 %shard_map.143 = (bf16[64,1024]{1,0:T(8,128)(2,1)S(1)}, bf16[64,1024]{1,0:T(8,128)(2,1)S(1)}) custom-call(bf16[1024,128]{1,0:T(8,128)(2,1)S(1)} %bitcast.17, bf16[768,256]{1,0:T(8,128)(2,1)S(1)} %collective-permute-done.3.kv, f32[64,768]{1,0:T(8,128)S(1)} %get-tuple-element.70.bias, f32[1024,128]{1,0:T(8,128)S(1)} %get-tuple-element.72.o_in, ...), custom_call_target="tpu_custom_call" | custom-call | flops 402653184 | bytes 4194304 | tf_op jit(solution)/shard_map/pallas_call | solution.py:424
  15.1 1.5 %collective-permute-start.4 = (bf16[64,1024]{1,0:T(8,128)(2,1)S(1)}, bf16[64,1024]{1,0:T(8,128)(2,1)S(1)}, u32[]{:S(2)}, u32[]{:S(2)}) collective-permute-start(bf16[64,1024]{1,0:T(8,128)(2,1)S(1)} %get-tuple-element.81), channel_id=1, source_target_pairs={{0,8},{4,12},{8,0},{12,4},{16,24},{20,28},{24,16},{28,20},{1,9},{5... | collective-permute-start | bytes 393224 | tf_op jit(solution)/shard_map/ppermute | solution.py:333
  17.2 2.7 %collective-permute-start.10 = (f32[8,128]{1,0:T(8,128)S(1)}, f32[8,128]{1,0:T(8,128)S(1)}, u32[]{:S(2)}, u32[]{:S(2)}) collective-permute-start(f32[8,128]{1,0:T(8,128)S(1)} %get-tuple-element.80), channel_id=1, source_target_pairs={{0,2},{1,3},{2,0},{3,1},{4,6},{5,7},{6,4},{7,5},{8,10},{9,11},{10,... | collective-permute-start | bytes 12296 | tf_op jit(solution)/shard_map/ppermute | solution.py:333
  20.0 1.3 %collective-permute-start.5 = (bf16[64,1024]{1,0:T(8,128)(2,1)S(1)}, bf16[64,1024]{1,0:T(8,128)(2,1)S(1)}, u32[]{:S(2)}, u32[]{:S(2)}) collective-permute-start(bf16[64,1024]{1,0:T(8,128)(2,1)S(1)} %get-tuple-element.82), channel_id=1, source_target_pairs={{0,8},{4,12},{8,0},{12,4},{16,24},{20,28},{24,16},{28,20},{1,9},{5... | collective-permute-start | bytes 393224 | tf_op jit(solution)/shard_map/ppermute | solution.py:333
  21.8 1.4 %collective-permute-start.8 = (bf16[64,1024]{1,0:T(8,128)(2,1)S(1)}, bf16[64,1024]{1,0:T(8,128)(2,1)S(1)}, u32[]{:S(2)}, u32[]{:S(2)}) collective-permute-start(bf16[64,1024]{1,0:T(8,128)(2,1)S(1)} %collective-permute-done.4), channel_id=1, source_target_pairs={{0,16},{4,20},{8,24},{12,28},{16,0},{20,4},{24,8},{28,12},{1,17},{... | collective-permute-start | bytes 393224 | tf_op jit(solution)/shard_map/ppermute | solution.py:333
  24.0 1.6 %collective-permute-start.11 = (f32[16,128]{1,0:T(8,128)S(1)}, f32[16,128]{1,0:T(8,128)S(1)}, u32[]{:S(2)}, u32[]{:S(2)}) collective-permute-start(f32[16,128]{1,0:T(8,128)S(1)} %pad_maximum_fusion.2), channel_id=1, source_target_pairs={{0,1},{1,0},{2,3},{3,2},{4,5},{5,4},{6,7},{7,6},{8,9},{9,8},{10,11... | collective-permute-start | bytes 24584 | tf_op jit(solution)/shard_map/ppermute | solution.py:333
  25.6 2.1 %collective-permute-done.11 = f32[16,128]{1,0:T(8,128)S(1)} collective-permute-done((f32[16,128]{1,0:T(8,128)S(1)}, f32[16,128]{1,0:T(8,128)S(1)}, u32[]{:S(2)}, u32[]{:S(2)}) %collective-permute-start.11) | collective-permute-done | bytes 8224 | tf_op jit(solution)/shard_map/ppermute | solution.py:333
  27.7 1.1 %collective-permute-done.8 = bf16[64,1024]{1,0:T(8,128)(2,1)S(1)} collective-permute-done((bf16[64,1024]{1,0:T(8,128)(2,1)S(1)}, bf16[64,1024]{1,0:T(8,128)(2,1)S(1)}, u32[]{:S(2)}, u32[]{:S(2)}) %collective-permute-start.8) | collective-permute-done | bytes 131104 | tf_op jit(solution)/shard_map/ppermute | solution.py:333
  29.7 1.9 %collective-permute-done.12.heads_out = bf16[256,2048]{1,0:T(8,128)(2,1)S(1)} collective-permute-done((bf16[256,2048]{1,0:T(8,128)(2,1)S(1)}, bf16[256,2048]{1,0:T(8,128)(2,1)S(1)}, u32[]{:S(2)}, u32[]{:S(2)}) %collective-permute-start.12) | collective-permute-done | bytes 1048608 | tf_op jit(solution)/shard_map/ppermute | solution.py:333
  31.6 1.0 %shard_map.145 = (f32[128,512]{1,0:T(8,128)S(1)}, bf16[256,512]{1,0:T(8,128)(2,1)S(1)}, bf16[128,512]{1,0:T(8,128)(2,1)S(1)}, bf16[128,512]{1,0:T(8,128)(2,1)S(1...) custom-call(bf16[256,2048]{1,0:T(8,128)(2,1)S(1)} %collective-permut, ...), custom_call_target="tpu_custom_call" | custom-call | flops 536870912 | bytes 4194304 | tf_op jit(solution)/shard_map/pallas_call | solution.py:452
  32.6 1.6 %collective-permute-start.17 = (bf16[128,256]{1,0:T(8,128)(2,1)S(1)}, bf16[128,256]{1,0:T(8,128)(2,1)S(1)}, u32[]{:S(2)}, u32[]{:S(2)}) collective-permute-start(bf16[128,256]{1,0:T(8,128)(2,1)S(1)} %get-tuple-element.97), channel_id=1, source_target_pairs={{0,1},{1,0},{2,3},{3,2},{4,5},{5,4},{6,7},{7,6},{8,9},{9,8},{10,11... | collective-permute-start | bytes 196616 | tf_op jit(solution)/shard_map/ppermute | solution.py:333
  34.3 1.7 %collective-permute-start.13 = (bf16[128,256]{1,0:T(8,128)(2,1)S(1)}, bf16[128,256]{1,0:T(8,128)(2,1)S(1)}, u32[]{:S(2)}, u32[]{:S(2)}) collective-permute-start(bf16[128,256]{1,0:T(8,128)(2,1)S(1)} %get-tuple-element.92), channel_id=1, source_target_pairs={{0,3},{1,2},{2,1},{3,0},{4,7},{5,6},{6,5},{7,4},{8,11},{9,10},{10,... | collective-permute-start | bytes 196616 | tf_op jit(solution)/shard_map/ppermute | solution.py:333
  36.2 2.5 %collective-permute-start.15 = (bf16[128,256]{1,0:T(8,128)(2,1)S(1)}, bf16[128,256]{1,0:T(8,128)(2,1)S(1)}, u32[]{:S(2)}, u32[]{:S(2)}) collective-permute-start(bf16[128,256]{1,0:T(8,128)(2,1)S(1)} %get-tuple-element.94), channel_id=1, source_target_pairs={{0,1},{1,0},{2,3},{3,2},{4,5},{5,4},{6,7},{7,6},{8,9},{9,8},{10,11... | collective-permute-start | bytes 196616 | tf_op jit(solution)/shard_map/ppermute | solution.py:333
  38.7 2.3 %collective-permute-start.18 = (bf16[128,256]{1,0:T(8,128)(2,1)S(1)}, bf16[128,256]{1,0:T(8,128)(2,1)S(1)}, u32[]{:S(2)}, u32[]{:S(2)}) collective-permute-start(bf16[128,256]{1,0:T(8,128)(2,1)S(1)} %add_convert_fusion.2), channel_id=1, source_target_pairs={{0,2},{1,3},{2,0},{3,1},{4,6},{5,7},{6,4},{7,5},{8,10},{9,11},{10,... | collective-permute-start | bytes 196616 | tf_op jit(solution)/shard_map/ppermute | solution.py:333
  41.1 1.8 %collective-permute-done.14.refs_2_ = bf16[128,256]{1,0:T(8,128)(2,1)S(1)} collective-permute-done((bf16[128,256]{1,0:T(8,128)(2,1)S(1)}, bf16[128,256]{1,0:T(8,128)(2,1)S(1)}, u32[]{:S(2)}, u32[]{:S(2)}) %collective-permute-start.14) | collective-permute-done | bytes 65568 | tf_op jit(solution)/shard_map/ppermute | solution.py:333
  42.8 1.5 %collective-permute-done.15.refs_3_ = bf16[128,256]{1,0:T(8,128)(2,1)S(1)} collective-permute-done((bf16[128,256]{1,0:T(8,128)(2,1)S(1)}, bf16[128,256]{1,0:T(8,128)(2,1)S(1)}, u32[]{:S(2)}, u32[]{:S(2)}) %collective-permute-start.15) | collective-permute-done | bytes 65568 | tf_op jit(solution)/shard_map/ppermute | solution.py:333
  44.4 1.1 %collective-permute-done.16.refs_4_ = bf16[128,256]{1,0:T(8,128)(2,1)S(1)} collective-permute-done((bf16[128,256]{1,0:T(8,128)(2,1)S(1)}, bf16[128,256]{1,0:T(8,128)(2,1)S(1)}, u32[]{:S(2)}, u32[]{:S(2)}) %collective-permute-start.16) | collective-permute-done | bytes 65568 | tf_op jit(solution)/shard_map/ppermute | solution.py:333
  49.0 1.3 %collective-permute-start.21 = (bf16[16,3200]{1,0:T(8,128)(2,1)S(1)}, bf16[16,3200]{1,0:T(8,128)(2,1)S(1)}, u32[]{:S(2)}, u32[]{:S(2)}) collective-permute-start(bf16[16,3200]{1,0:T(8,128)(2,1)S(1)} %get-tuple-element.101), channel_id=1, source_target_pairs={{0,16},{4,20},{8,24},{12,28},{16,0},{20,4},{24,8},{28,12},{1,17},{... | collective-permute-start | bytes 307208 | tf_op jit(solution)/shard_map/ppermute | solution.py:333
  50.3 1.4 %collective-permute-start.22 = (bf16[16,3200]{1,0:T(8,128)(2,1)S(1)}, bf16[16,3200]{1,0:T(8,128)(2,1)S(1)}, u32[]{:S(2)}, u32[]{:S(2)}) collective-permute-start(bf16[16,3200]{1,0:T(8,128)(2,1)S(1)} %get-tuple-element.102), channel_id=1, source_target_pairs={{0,24},{4,28},{8,16},{12,20},{16,8},{20,12},{24,0},{28,4},{1,25},{... | collective-permute-start | bytes 307208 | tf_op jit(solution)/shard_map/ppermute | solution.py:333
  51.7 3.3 %collective-permute-done.23 = bf16[256,512]{1,0:T(8,128)(2,1)S(1)} collective-permute-done((bf16[256,512]{1,0:T(8,128)(2,1)S(1)}, bf16[256,512]{1,0:T(8,128)(2,1)S(1)}, u32[]{:S(2)}, u32[]{:S(2)}) %collective-permute-start.23) | collective-permute-done | bytes 262176 | tf_op jit(solution)/shard_map/ppermute | solution.py:333
  55.9 2.2 %collective-permute-start.27 = (bf16[128,512]{1,0:T(8,128)(2,1)S(1)}, bf16[128,512]{1,0:T(8,128)(2,1)S(1)}, u32[]{:S(2)}, u32[]{:S(2)}) collective-permute-start(bf16[128,512]{1,0:T(8,128)(2,1)S(1)} %add_convert_fusion.1), channel_id=1, source_target_pairs={{0,2},{1,3},{2,0},{3,1},{4,6},{5,7},{6,4},{7,5},{8,10},{9,11},{10,... | collective-permute-start | bytes 393224 | tf_op jit(solution)/shard_map/ppermute | solution.py:333
  58.2 1.5 %collective-permute-start.24 = (bf16[16,1536]{1,0:T(8,128)(2,1)S(1)}, bf16[16,1536]{1,0:T(8,128)(2,1)S(1)}, u32[]{:S(2)}, u32[]{:S(2)}) collective-permute-start(bf16[16,1536]{1,0:T(8,128)(2,1)S(1)} %shard_map.149), channel_id=1, source_target_pairs={{0,24},{4,28},{8,16},{12,20},{16,8},{20,12},{24,0},{28,4},{1,25},{... | collective-permute-start | bytes 147464 | tf_op jit(solution)/shard_map/ppermute | solution.py:333
  59.7 1.3 %collective-permute-start.25 = (bf16[16,1536]{1,0:T(8,128)(2,1)S(1)}, bf16[16,1536]{1,0:T(8,128)(2,1)S(1)}, u32[]{:S(2)}, u32[]{:S(2)}) collective-permute-start(bf16[16,1536]{1,0:T(8,128)(2,1)S(1)} %shard_map.149), channel_id=1, source_target_pairs={{0,16},{4,20},{8,24},{12,28},{16,0},{20,4},{24,8},{28,12},{1,17},{... | collective-permute-start | bytes 147464 | tf_op jit(solution)/shard_map/ppermute | solution.py:333
  61.7 1.5 %collective-permute-done.24 = bf16[16,1536]{1,0:T(8,128)(2,1)S(1)} collective-permute-done((bf16[16,1536]{1,0:T(8,128)(2,1)S(1)}, bf16[16,1536]{1,0:T(8,128)(2,1)S(1)}, u32[]{:S(2)}, u32[]{:S(2)}) %collective-permute-start.24) | collective-permute-done | bytes 49184 | tf_op jit(solution)/shard_map/ppermute | solution.py:333
  63.8 1.3 %collective-permute-done.26 = bf16[16,1536]{1,0:T(8,128)(2,1)S(1)} collective-permute-done((bf16[16,1536]{1,0:T(8,128)(2,1)S(1)}, bf16[16,1536]{1,0:T(8,128)(2,1)S(1)}, u32[]{:S(2)}, u32[]{:S(2)}) %collective-permute-start.26) | collective-permute-done | bytes 49184 | tf_op jit(solution)/shard_map/ppermute | solution.py:333
  65.6 1.0 %collective-permute-done.28.active = bf16[64,1536]{1,0:T(8,128)(2,1)S(1)} collective-permute-done((bf16[64,1536]{1,0:T(8,128)(2,1)S(1)}, bf16[64,1536]{1,0:T(8,128)(2,1)S(1)}, u32[]{:S(2)}, u32[]{:S(2)}) %collective-permute-start.28) | collective-permute-done | bytes 196640 | tf_op jit(solution)/shard_map/ppermute | solution.py:333
  67.0 1.4 %collective-permute-start.29 = (bf16[32,512]{1,0:T(8,128)(2,1)S(1)}, bf16[32,512]{1,0:T(8,128)(2,1)S(1)}, u32[]{:S(2)}, u32[]{:S(2)}) collective-permute-start(bf16[32,512]{1,0:T(8,128)(2,1)S(1)} %get-tuple-element.117), channel_id=1, source_target_pairs={{0,3},{1,2},{2,1},{3,0},{4,7},{5,6},{6,5},{7,4},{8,11},{9,10},{10,... | collective-permute-start | bytes 98312 | tf_op jit(solution)/shard_map/ppermute | solution.py:333
  68.5 3.0 %collective-permute-start.31 = (bf16[32,512]{1,0:T(8,128)(2,1)S(1)}, bf16[32,512]{1,0:T(8,128)(2,1)S(1)}, u32[]{:S(2)}, u32[]{:S(2)}) collective-permute-start(bf16[32,512]{1,0:T(8,128)(2,1)S(1)} %get-tuple-element.119), channel_id=1, source_target_pairs={{0,2},{1,3},{2,0},{3,1},{4,6},{5,7},{6,4},{7,5},{8,10},{9,11},{10,... | collective-permute-start | bytes 98312 | tf_op jit(solution)/shard_map/ppermute | solution.py:333
  (77 shorter events, 17.5 us)
Async XLA Ops:
  2.2 8.0 %collective-permute-start = (bf16[192,256]{1,0:T(8,128)(2,1)}, bf16[192,256]{1,0:T(8,128)(2,1)S(1)}, u32[]{:S(2)}, u32[]{:S(2)}) collective-permute-start(bf16[192,256]{1,0:T(8,128)(2,1)} %shard_map.140.kv), channel_id=1, source_target_pairs={{0,24},{4,28},{8,16},{12,20},{16,8},{20,12},{24,0},{28,4},{1,25},{... | collective-permute-start | bytes 294920 | tf_op jit(solution)/shard_map/ppermute | solution.py:333
  6.1 5.1 %collective-permute-start.1 = (bf16[192,256]{1,0:T(8,128)(2,1)}, bf16[192,256]{1,0:T(8,128)(2,1)S(1)}, u32[]{:S(2)}, u32[]{:S(2)}) collective-permute-start(bf16[192,256]{1,0:T(8,128)(2,1)} %shard_map.140.kv), channel_id=1, source_target_pairs={{0,16},{4,20},{8,24},{12,28},{16,0},{20,4},{24,8},{28,12},{1,17},{... | collective-permute-start | bytes 294920 | tf_op jit(solution)/shard_map/ppermute | solution.py:333
  6.6 4.9 %collective-permute-start.2 = (bf16[192,256]{1,0:T(8,128)(2,1)}, bf16[192,256]{1,0:T(8,128)(2,1)S(1)}, u32[]{:S(2)}, u32[]{:S(2)}) collective-permute-start(bf16[192,256]{1,0:T(8,128)(2,1)} %shard_map.140.kv), channel_id=1, source_target_pairs={{0,8},{4,12},{8,0},{12,4},{16,24},{20,28},{24,16},{28,20},{1,9},{5... | collective-permute-start | bytes 294920 | tf_op jit(solution)/shard_map/ppermute | solution.py:333
  11.6 1.8 %collective-permute-start.3 = (bf16[768,256]{1,0:T(8,128)(2,1)S(1)}, bf16[768,256]{1,0:T(8,128)(2,1)S(1)}, u32[]{:S(2)}, u32[]{:S(2)}) collective-permute-start(bf16[768,256]{1,0:T(8,128)(2,1)S(1)} %constant_dynamic-update-slice_fusion.kv), channel_id=1, source_target_pairs={{0,4},{4,0},{8,12},{12,8},{16,20},{20,16},{24,28},{28,24},{1,5},{5... | collective-permute-start | bytes 1179656 | tf_op jit(solution)/shard_map/ppermute | solution.py:333
  15.1 6.7 %collective-permute-start.4 = (bf16[64,1024]{1,0:T(8,128)(2,1)S(1)}, bf16[64,1024]{1,0:T(8,128)(2,1)S(1)}, u32[]{:S(2)}, u32[]{:S(2)}) collective-permute-start(bf16[64,1024]{1,0:T(8,128)(2,1)S(1)} %get-tuple-element.81), channel_id=1, source_target_pairs={{0,8},{4,12},{8,0},{12,4},{16,24},{20,28},{24,16},{28,20},{1,9},{5... | collective-permute-start | bytes 393224 | tf_op jit(solution)/shard_map/ppermute | solution.py:333
  16.6 6.6 %collective-permute-start.7 = (bf16[64,1024]{1,0:T(8,128)(2,1)S(1)}, bf16[64,1024]{1,0:T(8,128)(2,1)S(1)}, u32[]{:S(2)}, u32[]{:S(2)}) collective-permute-start(bf16[64,1024]{1,0:T(8,128)(2,1)S(1)} %get-tuple-element.82), channel_id=1, source_target_pairs={{0,16},{4,20},{8,24},{12,28},{16,0},{20,4},{24,8},{28,12},{1,17},{... | collective-permute-start | bytes 393224 | tf_op jit(solution)/shard_map/ppermute | solution.py:333
  17.2 6.8 %collective-permute-start.10 = (f32[8,128]{1,0:T(8,128)S(1)}, f32[8,128]{1,0:T(8,128)S(1)}, u32[]{:S(2)}, u32[]{:S(2)}) collective-permute-start(f32[8,128]{1,0:T(8,128)S(1)} %get-tuple-element.80), channel_id=1, source_target_pairs={{0,2},{1,3},{2,0},{3,1},{4,6},{5,7},{6,4},{7,5},{8,10},{9,11},{10,... | collective-permute-start | bytes 12296 | tf_op jit(solution)/shard_map/ppermute | solution.py:333
  20.0 7.7 %collective-permute-start.5 = (bf16[64,1024]{1,0:T(8,128)(2,1)S(1)}, bf16[64,1024]{1,0:T(8,128)(2,1)S(1)}, u32[]{:S(2)}, u32[]{:S(2)}) collective-permute-start(bf16[64,1024]{1,0:T(8,128)(2,1)S(1)} %get-tuple-element.82), channel_id=1, source_target_pairs={{0,8},{4,12},{8,0},{12,4},{16,24},{20,28},{24,16},{28,20},{1,9},{5... | collective-permute-start | bytes 393224 | tf_op jit(solution)/shard_map/ppermute | solution.py:333
  21.2 6.5 %collective-permute-start.6 = (bf16[64,1024]{1,0:T(8,128)(2,1)S(1)}, bf16[64,1024]{1,0:T(8,128)(2,1)S(1)}, u32[]{:S(2)}, u32[]{:S(2)}) collective-permute-start(bf16[64,1024]{1,0:T(8,128)(2,1)S(1)} %get-tuple-element.81), channel_id=1, source_target_pairs={{0,16},{4,20},{8,24},{12,28},{16,0},{20,4},{24,8},{28,12},{1,17},{... | collective-permute-start | bytes 393224 | tf_op jit(solution)/shard_map/ppermute | solution.py:333
  21.8 6.9 %collective-permute-start.8 = (bf16[64,1024]{1,0:T(8,128)(2,1)S(1)}, bf16[64,1024]{1,0:T(8,128)(2,1)S(1)}, u32[]{:S(2)}, u32[]{:S(2)}) collective-permute-start(bf16[64,1024]{1,0:T(8,128)(2,1)S(1)} %collective-permute-done.4), channel_id=1, source_target_pairs={{0,16},{4,20},{8,24},{12,28},{16,0},{20,4},{24,8},{28,12},{1,17},{... | collective-permute-start | bytes 393224 | tf_op jit(solution)/shard_map/ppermute | solution.py:333
  23.2 5.5 %collective-permute-start.9 = (bf16[64,1024]{1,0:T(8,128)(2,1)S(1)}, bf16[64,1024]{1,0:T(8,128)(2,1)S(1)}, u32[]{:S(2)}, u32[]{:S(2)}) collective-permute-start(bf16[64,1024]{1,0:T(8,128)(2,1)S(1)} %collective-permute-done.7), channel_id=1, source_target_pairs={{0,8},{4,12},{8,0},{12,4},{16,24},{20,28},{24,16},{28,20},{1,9},{5... | collective-permute-start | bytes 393224 | tf_op jit(solution)/shard_map/ppermute | solution.py:333
  24.0 3.7 %collective-permute-start.11 = (f32[16,128]{1,0:T(8,128)S(1)}, f32[16,128]{1,0:T(8,128)S(1)}, u32[]{:S(2)}, u32[]{:S(2)}) collective-permute-start(f32[16,128]{1,0:T(8,128)S(1)} %pad_maximum_fusion.2), channel_id=1, source_target_pairs={{0,1},{1,0},{2,3},{3,2},{4,5},{5,4},{6,7},{7,6},{8,9},{9,8},{10,11... | collective-permute-start | bytes 24584 | tf_op jit(solution)/shard_map/ppermute | solution.py:333
  28.8 2.7 %collective-permute-start.12 = (bf16[256,2048]{1,0:T(8,128)(2,1)S(1)}, bf16[256,2048]{1,0:T(8,128)(2,1)S(1)}, u32[]{:S(2)}, u32[]{:S(2)}) collective-permute-start(bf16[256,2048]{1,0:T(8,128)(2,1)S(1)} %maximum_maximum_fusion.heads_out), channel_id=1, source_target_pairs={{0,4},{4,0},{8,12},{12,8},{16,20},{20,16},{24,28},{28,24},{1,5},{5... | collective-permute-start | bytes 3145736 | tf_op jit(solution)/shard_map/ppermute | solution.py:333
  32.6 6.1 %collective-permute-start.17 = (bf16[128,256]{1,0:T(8,128)(2,1)S(1)}, bf16[128,256]{1,0:T(8,128)(2,1)S(1)}, u32[]{:S(2)}, u32[]{:S(2)}) collective-permute-start(bf16[128,256]{1,0:T(8,128)(2,1)S(1)} %get-tuple-element.97), channel_id=1, source_target_pairs={{0,1},{1,0},{2,3},{3,2},{4,5},{5,4},{6,7},{7,6},{8,9},{9,8},{10,11... | collective-permute-start | bytes 196616 | tf_op jit(solution)/shard_map/ppermute | solution.py:333
  34.3 6.8 %collective-permute-start.13 = (bf16[128,256]{1,0:T(8,128)(2,1)S(1)}, bf16[128,256]{1,0:T(8,128)(2,1)S(1)}, u32[]{:S(2)}, u32[]{:S(2)}) collective-permute-start(bf16[128,256]{1,0:T(8,128)(2,1)S(1)} %get-tuple-element.92), channel_id=1, source_target_pairs={{0,3},{1,2},{2,1},{3,0},{4,7},{5,6},{6,5},{7,4},{8,11},{9,10},{10,... | collective-permute-start | bytes 196616 | tf_op jit(solution)/shard_map/ppermute | solution.py:333
  35.9 6.9 %collective-permute-start.14 = (bf16[128,256]{1,0:T(8,128)(2,1)S(1)}, bf16[128,256]{1,0:T(8,128)(2,1)S(1)}, u32[]{:S(2)}, u32[]{:S(2)}) collective-permute-start(bf16[128,256]{1,0:T(8,128)(2,1)S(1)} %get-tuple-element.93), channel_id=1, source_target_pairs={{0,2},{1,3},{2,0},{3,1},{4,6},{5,7},{6,4},{7,5},{8,10},{9,11},{10,... | collective-permute-start | bytes 196616 | tf_op jit(solution)/shard_map/ppermute | solution.py:333
  36.2 8.2 %collective-permute-start.15 = (bf16[128,256]{1,0:T(8,128)(2,1)S(1)}, bf16[128,256]{1,0:T(8,128)(2,1)S(1)}, u32[]{:S(2)}, u32[]{:S(2)}) collective-permute-start(bf16[128,256]{1,0:T(8,128)(2,1)S(1)} %get-tuple-element.94), channel_id=1, source_target_pairs={{0,1},{1,0},{2,3},{3,2},{4,5},{5,4},{6,7},{7,6},{8,9},{9,8},{10,11... | collective-permute-start | bytes 196616 | tf_op jit(solution)/shard_map/ppermute | solution.py:333
  38.6 6.9 %collective-permute-start.16 = (bf16[128,256]{1,0:T(8,128)(2,1)S(1)}, bf16[128,256]{1,0:T(8,128)(2,1)S(1)}, u32[]{:S(2)}, u32[]{:S(2)}) collective-permute-start(bf16[128,256]{1,0:T(8,128)(2,1)S(1)} %get-tuple-element.95), channel_id=1, source_target_pairs={{0,1},{1,0},{2,3},{3,2},{4,5},{5,4},{6,7},{7,6},{8,9},{9,8},{10,11... | collective-permute-start | bytes 196616 | tf_op jit(solution)/shard_map/ppermute | solution.py:333
  38.7 6.8 %collective-permute-start.18 = (bf16[128,256]{1,0:T(8,128)(2,1)S(1)}, bf16[128,256]{1,0:T(8,128)(2,1)S(1)}, u32[]{:S(2)}, u32[]{:S(2)}) collective-permute-start(bf16[128,256]{1,0:T(8,128)(2,1)S(1)} %add_convert_fusion.2), channel_id=1, source_target_pairs={{0,2},{1,3},{2,0},{3,1},{4,6},{5,7},{6,4},{7,5},{8,10},{9,11},{10,... | collective-permute-start | bytes 196616 | tf_op jit(solution)/shard_map/ppermute | solution.py:333
  46.2 1.8 %collective-permute-start.19 = (bf16[64,3200]{1,0:T(8,128)(2,1)S(1)}, bf16[64,3200]{1,0:T(8,128)(2,1)S(1)}, u32[]{:S(2)}, u32[]{:S(2)}) collective-permute-start(bf16[64,3200]{1,0:T(8,128)(2,1)S(1)} %shard_map.147), channel_id=1, source_target_pairs={{0,4},{4,0},{8,12},{12,8},{16,20},{20,16},{24,28},{28,24},{1,5},{5... | collective-permute-start | bytes 1228808 | tf_op jit(solution)/shard_map/ppermute | solution.py:333
  46.3 8.7 %collective-permute-start.23 = (bf16[256,512]{1,0:T(8,128)(2,1)S(1)}, bf16[256,512]{1,0:T(8,128)(2,1)S(1)}, u32[]{:S(2)}, u32[]{:S(2)}) collective-permute-start(bf16[256,512]{1,0:T(8,128)(2,1)S(1)} %get-tuple-element.103), channel_id=1, source_target_pairs={{0,1},{1,0},{2,3},{3,2},{4,5},{5,4},{6,7},{7,6},{8,9},{9,8},{10,11... | collective-permute-start | bytes 786440 | tf_op jit(solution)/shard_map/ppermute | solution.py:333
  48.2 6.9 %collective-permute-start.20 = (bf16[16,3200]{1,0:T(8,128)(2,1)S(1)}, bf16[16,3200]{1,0:T(8,128)(2,1)S(1)}, u32[]{:S(2)}, u32[]{:S(2)}) collective-permute-start(bf16[16,3200]{1,0:T(8,128)(2,1)S(1)} %get-tuple-element.100), channel_id=1, source_target_pairs={{0,8},{4,12},{8,0},{12,4},{16,24},{20,28},{24,16},{28,20},{1,9},{5... | collective-permute-start | bytes 307208 | tf_op jit(solution)/shard_map/ppermute | solution.py:333
  49.0 6.1 %collective-permute-start.21 = (bf16[16,3200]{1,0:T(8,128)(2,1)S(1)}, bf16[16,3200]{1,0:T(8,128)(2,1)S(1)}, u32[]{:S(2)}, u32[]{:S(2)}) collective-permute-start(bf16[16,3200]{1,0:T(8,128)(2,1)S(1)} %get-tuple-element.101), channel_id=1, source_target_pairs={{0,16},{4,20},{8,24},{12,28},{16,0},{20,4},{24,8},{28,12},{1,17},{... | collective-permute-start | bytes 307208 | tf_op jit(solution)/shard_map/ppermute | solution.py:333
  50.3 5.6 %collective-permute-start.22 = (bf16[16,3200]{1,0:T(8,128)(2,1)S(1)}, bf16[16,3200]{1,0:T(8,128)(2,1)S(1)}, u32[]{:S(2)}, u32[]{:S(2)}) collective-permute-start(bf16[16,3200]{1,0:T(8,128)(2,1)S(1)} %get-tuple-element.102), channel_id=1, source_target_pairs={{0,24},{4,28},{8,16},{12,20},{16,8},{20,12},{24,0},{28,4},{1,25},{... | collective-permute-start | bytes 307208 | tf_op jit(solution)/shard_map/ppermute | solution.py:333
  55.9 9.2 %collective-permute-start.27 = (bf16[128,512]{1,0:T(8,128)(2,1)S(1)}, bf16[128,512]{1,0:T(8,128)(2,1)S(1)}, u32[]{:S(2)}, u32[]{:S(2)}) collective-permute-start(bf16[128,512]{1,0:T(8,128)(2,1)S(1)} %add_convert_fusion.1), channel_id=1, source_target_pairs={{0,2},{1,3},{2,0},{3,1},{4,6},{5,7},{6,4},{7,5},{8,10},{9,11},{10,... | collective-permute-start | bytes 393224 | tf_op jit(solution)/shard_map/ppermute | solution.py:333
  58.2 5.1 %collective-permute-start.24 = (bf16[16,1536]{1,0:T(8,128)(2,1)S(1)}, bf16[16,1536]{1,0:T(8,128)(2,1)S(1)}, u32[]{:S(2)}, u32[]{:S(2)}) collective-permute-start(bf16[16,1536]{1,0:T(8,128)(2,1)S(1)} %shard_map.149), channel_id=1, source_target_pairs={{0,24},{4,28},{8,16},{12,20},{16,8},{20,12},{24,0},{28,4},{1,25},{... | collective-permute-start | bytes 147464 | tf_op jit(solution)/shard_map/ppermute | solution.py:333
  59.7 4.1 %collective-permute-start.25 = (bf16[16,1536]{1,0:T(8,128)(2,1)S(1)}, bf16[16,1536]{1,0:T(8,128)(2,1)S(1)}, u32[]{:S(2)}, u32[]{:S(2)}) collective-permute-start(bf16[16,1536]{1,0:T(8,128)(2,1)S(1)} %shard_map.149), channel_id=1, source_target_pairs={{0,16},{4,20},{8,24},{12,28},{16,0},{20,4},{24,8},{28,12},{1,17},{... | collective-permute-start | bytes 147464 | tf_op jit(solution)/shard_map/ppermute | solution.py:333
  61.0 4.1 %collective-permute-start.26 = (bf16[16,1536]{1,0:T(8,128)(2,1)S(1)}, bf16[16,1536]{1,0:T(8,128)(2,1)S(1)}, u32[]{:S(2)}, u32[]{:S(2)}) collective-permute-start(bf16[16,1536]{1,0:T(8,128)(2,1)S(1)} %shard_map.149), channel_id=1, source_target_pairs={{0,8},{4,12},{8,0},{12,4},{16,24},{20,28},{24,16},{28,20},{1,9},{5... | collective-permute-start | bytes 147464 | tf_op jit(solution)/shard_map/ppermute | solution.py:333
  65.1 1.5 %collective-permute-start.28 = (bf16[64,1536]{1,0:T(8,128)(2,1)S(1)}, bf16[64,1536]{1,0:T(8,128)(2,1)S(1)}, u32[]{:S(2)}, u32[]{:S(2)}) collective-permute-start(bf16[64,1536]{1,0:T(8,128)(2,1)S(1)} %pad_maximum_fusion.active), channel_id=1, source_target_pairs={{0,4},{4,0},{8,12},{12,8},{16,20},{20,16},{24,28},{28,24},{1,5},{5... | collective-permute-start | bytes 589832 | tf_op jit(solution)/shard_map/ppermute | solution.py:333
  67.0 5.8 %collective-permute-start.29 = (bf16[32,512]{1,0:T(8,128)(2,1)S(1)}, bf16[32,512]{1,0:T(8,128)(2,1)S(1)}, u32[]{:S(2)}, u32[]{:S(2)}) collective-permute-start(bf16[32,512]{1,0:T(8,128)(2,1)S(1)} %get-tuple-element.117), channel_id=1, source_target_pairs={{0,3},{1,2},{2,1},{3,0},{4,7},{5,6},{6,5},{7,4},{8,11},{9,10},{10,... | collective-permute-start | bytes 98312 | tf_op jit(solution)/shard_map/ppermute | solution.py:333
  68.4 4.6 %collective-permute-start.30 = (bf16[32,512]{1,0:T(8,128)(2,1)S(1)}, bf16[32,512]{1,0:T(8,128)(2,1)S(1)}, u32[]{:S(2)}, u32[]{:S(2)}) collective-permute-start(bf16[32,512]{1,0:T(8,128)(2,1)S(1)} %get-tuple-element.118), channel_id=1, source_target_pairs={{0,1},{1,0},{2,3},{3,2},{4,5},{5,4},{6,7},{7,6},{8,9},{9,8},{10,11... | collective-permute-start | bytes 98312 | tf_op jit(solution)/shard_map/ppermute | solution.py:333
  68.5 5.2 %collective-permute-start.31 = (bf16[32,512]{1,0:T(8,128)(2,1)S(1)}, bf16[32,512]{1,0:T(8,128)(2,1)S(1)}, u32[]{:S(2)}, u32[]{:S(2)}) collective-permute-start(bf16[32,512]{1,0:T(8,128)(2,1)S(1)} %get-tuple-element.119), channel_id=1, source_target_pairs={{0,2},{1,3},{2,0},{3,1},{4,6},{5,7},{6,4},{7,5},{8,10},{9,11},{10,... | collective-permute-start | bytes 98312 | tf_op jit(solution)/shard_map/ppermute | solution.py:333
  (8 other events, 109.6 us)
